TPU v7x, 512 devices: a whole 4x4x16 slice. The times are simulated.
512 devices in a mesh: expert: 32 (over y_lo, z), cuts: 16 (over y_hi, x, core).
Axes of the slice: x: 4, y: 4 (y_hi: 2, y_lo: 2; y = y_hi * 2 + y_lo), z: 16, core: 2. Of those that a mesh axis runs over, the one named last changes fastest.
Arguments:
- tokens: bfloat16 [1024, 4096], P('expert', 'cuts'), may hold values from -6 to 6
- expert_ids: int32 [1024, 2], P('expert'), may hold values from 0 to 15, all different within a row; in each aligned block of 32 rows (0 to 31, 32 to 63, ...) at most 8 rows name the same one
- gate_weights: float32 [1024, 2], P('expert'), may hold values from 0.25 to 1
- old_up: bfloat16 [65536, 4096], P('expert', 'cuts'), may hold values from -0.09375 to 0.09375
- old_down: bfloat16 [65536, 4096], P('expert', 'cuts'), may hold values from -0.09375 to 0.09375
- old_rows: int32 [16], replicated, may hold values from 0 to 15, each once
- new_slots: int32 [16], replicated, may hold values from 0 to 15, each once
- cotangent: bfloat16 [1024, 4096], P('expert', 'cuts'), may hold values from -6 to 6
Outputs:
- mixed: bfloat16 [1024, 4096], P('expert', 'cuts')
- token_grad: bfloat16 [1024, 4096], P('expert', 'cuts')
- up_grad: bfloat16 [65536, 4096], P(('expert', 'cuts'))
- down_grad: bfloat16 [65536, 4096], P(('expert', 'cuts'))
Inputs may be any that keep to these rules, and one draw needn't show every extreme that they name: `expert_ids`: each row names two different experts; in each aligned block of 32 rows (the rows of one index of the expert axis) no expert is named more than 8 times, and in some blocks one expert exactly 8 times. `old_rows`: each number once. `new_slots`: each number once.
All inputs are finite; a program needn't handle non-finite values.
Results may differ from a plain program's by a relative error of at most 0.02.
Values may be sent and summed in bfloat16 or wider, within the bound.
No kernel may reach another device: no remote copies, remote signals or barrier semaphores. Data moves between devices by JAX's collectives and lax.ppermute only.
A program may use at most 64 MiB of HBM per device.

v0:
```python
import jax
import jax.numpy as jnp
from jax import lax
from jax.sharding import PartitionSpec as P


def local(tokens, expert_ids, gate_weights, old_up, old_down, old_rows, new_slots, cotangent):
    cut_count = lax.axis_size("cuts")
    group_count = lax.axis_size("expert")
    expert_count = group_count // 2
    tok_rows, block_width = tokens.shape
    half_units = old_up.shape[0]
    unit_width = half_units // cut_count
    capacity = 8 * tok_rows // group_count
    slot_rows = group_count * capacity
    up_pieces = jnp.take(old_up.reshape(cut_count, unit_width, block_width), new_slots, axis=0)
    down_pieces = jnp.take(old_down.reshape(cut_count, unit_width, block_width), new_slots, axis=0)
    up_recv, down_recv = (
        lax.all_to_all(up_pieces, "cuts", split_axis=0, concat_axis=0, tiled=True),
        lax.all_to_all(down_pieces, "cuts", split_axis=0, concat_axis=0, tiled=True),
    )
    cut_list = jnp.arange(cut_count, dtype=jnp.int32)
    inverse = jnp.sum(
        cut_list[:, None] * (old_rows[:, None] == cut_list[None, :]).astype(jnp.int32), axis=0
    )
    up_local = jnp.take(up_recv, inverse, axis=0)
    down_local = jnp.take(down_recv, inverse, axis=0)
    flat_ids = expert_ids.reshape(-1)
    flat_gate = gate_weights.reshape(-1)
    expert_hits = (flat_ids[:, None] == jnp.arange(expert_count, dtype=jnp.int32)[None, :]).astype(
        jnp.int32
    )
    slot_rank = jnp.sum((jnp.cumsum(expert_hits, axis=0) - expert_hits) * expert_hits, axis=1)
    target = flat_ids * capacity + slot_rank
    placer = (
        jnp.arange(expert_count * capacity, dtype=jnp.int32)[:, None] == target[None, :]
    ).astype(jnp.bfloat16)
    back_rows = (flat_gate[:, None] * jnp.repeat(cotangent, 2, axis=0).astype(jnp.float32)).astype(
        jnp.bfloat16
    )

    def fill_slots(entries):
        width = entries.shape[1]
        placed = jnp.dot(placer, entries, preferred_element_type=jnp.float32).astype(jnp.bfloat16)
        placed = placed.reshape(expert_count, 1, capacity, width)
        return jnp.broadcast_to(placed, (expert_count, 2, capacity, width)).reshape(
            group_count, capacity, width
        )

    sent_x, sent_back = (
        lax.all_to_all(
            fill_slots(jnp.repeat(tokens, 2, axis=0)),
            "expert",
            split_axis=0,
            concat_axis=0,
            tiled=True,
        ),
        lax.all_to_all(fill_slots(back_rows), "expert", split_axis=0, concat_axis=0, tiled=True),
    )
    routed_x, routed_back = (
        lax.all_gather(sent_x, "cuts", axis=2, tiled=True),
        lax.all_gather(sent_back, "cuts", axis=2, tiled=True),
    )
    routed_x = routed_x.reshape(slot_rows, cut_count, block_width)
    routed_back = routed_back.reshape(slot_rows, cut_count, block_width)
    pre_act = jnp.einsum("rpd,pud->ru", routed_x, up_local, preferred_element_type=jnp.float32)
    hidden = jax.nn.silu(pre_act).astype(jnp.bfloat16)
    out_terms = jnp.einsum("ru,pud->rpd", hidden, down_local, preferred_element_type=jnp.float32)
    out_share = lax.psum_scatter(
        out_terms.astype(jnp.bfloat16), "cuts", scatter_dimension=1, tiled=True
    )
    hidden_grad = jnp.einsum(
        "rpd,pud->ru", routed_back, down_local, preferred_element_type=jnp.float32
    )
    sigmoid_val = jax.nn.sigmoid(pre_act)
    pre_grad = (hidden_grad * sigmoid_val * (1.0 + pre_act * (1.0 - sigmoid_val))).astype(
        jnp.bfloat16
    )
    in_terms = jnp.einsum("ru,pud->rpd", pre_grad, up_local, preferred_element_type=jnp.float32)
    in_share = lax.psum_scatter(
        in_terms.astype(jnp.bfloat16), "cuts", scatter_dimension=1, tiled=True
    )
    up_grad = jnp.einsum("ru,rpd->upd", pre_grad, routed_x, preferred_element_type=jnp.float32)
    down_grad = jnp.einsum("ru,rpd->upd", hidden, routed_back, preferred_element_type=jnp.float32)
    up_grad = up_grad.reshape(unit_width, cut_count * block_width).astype(jnp.bfloat16)
    down_grad = down_grad.reshape(unit_width, cut_count * block_width).astype(jnp.bfloat16)
    out_send = out_share.reshape(group_count, capacity, block_width)
    in_send = in_share.reshape(group_count, capacity, block_width)
    out_back, in_back = (
        lax.all_to_all(out_send, "expert", split_axis=0, concat_axis=0, tiled=True),
        lax.all_to_all(in_send, "expert", split_axis=0, concat_axis=0, tiled=True),
    )
    out_halves = out_back.reshape(expert_count, 2, capacity, block_width)
    in_halves = in_back.reshape(expert_count, 2, capacity, block_width)
    out_rows = (
        out_halves[:, 0].astype(jnp.float32) + out_halves[:, 1].astype(jnp.float32)
    ).reshape(expert_count * capacity, block_width)
    in_rows = (in_halves[:, 0].astype(jnp.float32) + in_halves[:, 1].astype(jnp.float32)).reshape(
        expert_count * capacity, block_width
    )
    entry_out = jnp.take(out_rows, target, axis=0) * flat_gate[:, None]
    entry_in = jnp.take(in_rows, target, axis=0)
    mixed = jnp.sum(entry_out.reshape(tok_rows, 2, block_width), axis=1).astype(jnp.bfloat16)
    token_grad = jnp.sum(entry_in.reshape(tok_rows, 2, block_width), axis=1).astype(jnp.bfloat16)
    return (mixed, token_grad, up_grad, down_grad)


def solution(mesh):
    placed = (
        P("expert", "cuts"),
        P("expert", None),
        P("expert", None),
        P("expert", "cuts"),
        P("expert", "cuts"),
        P(),
        P(),
        P("expert", "cuts"),
    )
    return jax.shard_map(
        local,
        mesh=mesh,
        in_specs=placed,
        out_specs=(
            P("expert", "cuts"),
            P("expert", "cuts"),
            P(("expert", "cuts"), None),
            P(("expert", "cuts"), None),
        ),
        check_vma=False,
    )
```

profile of v0, /device:TPU:1, one launch (start us, length us, event | category | flops | bytes accessed | tf_op | source)
XLA Modules:
  0.0 406.8 jit_solution(12454544829041068551)
XLA Ops:
  7.2 0.0 copy-start
  7.2 0.0 all-gather.3.cloned.1.call-start
  7.2 0.8 copy.28
  8.1 0.1 reshape.93
  8.2 0.1 fusion.26
  8.2 0.1 reduce_window_sum.11
  8.3 0.2 select_reduce_fusion
  8.5 0.7 broadcast_in_dim.44
  9.3 0.1 fusion.19
  9.5 31.5 %all_to_all.30 = bf16[32,8,256]{2,1,0:T(8,128)(2,1)} all-to-all(bf16[32,8,256]{2,1,0:T(8,128)(2,1)S(1)} %bitcast.76), channel_id=1, replica_groups=mesh['expert'=32,'cuts'=16] {'expert'}, dimensions={0} | all-to-all | bytes 262144 | tf_op jit(solution)/shard_map/all_to_all | solution.py:51
  41.0 0.0 all-gather.3.cloned.1.call-update
  41.0 0.0 all-gather.5.cloned.1.call-start
  41.1 0.8 copy.32
  41.9 0.1 mul.56
  42.0 0.7 broadcast_in_dim.47
  42.8 0.2 fusion.20
  43.0 19.1 %all_to_all.31 = bf16[32,8,256]{2,1,0:T(8,128)(2,1)} all-to-all(bf16[32,8,256]{2,1,0:T(8,128)(2,1)S(1)} %bitcast.77), channel_id=1, replica_groups=mesh['expert'=32,'cuts'=16] {'expert'}, dimensions={0} | all-to-all | bytes 262144 | tf_op jit(solution)/shard_map/all_to_all | solution.py:58
  62.1 0.0 all-gather.5.cloned.1.call-update
  62.1 0.7 compare_select_fusion.2
  62.8 0.0 copy-done
  62.8 0.0 copy-start.5
  62.8 0.6 gather_fusion
  63.4 1.8 gather_fusion.2
  65.3 0.0 copy-done.5
  65.3 1.2 broadcast_select_fusion.3
  66.5 28.4 %all_to_all.32 = bf16[16,128,256]{2,1,0:T(8,128)(2,1)S(1)} all-to-all(bf16[16,128,256]{2,1,0:T(8,128)(2,1)S(1)} %get-tuple-element.10), channel_id=1, replica_groups=mesh['expert'=32,'cuts'=16] {'cuts'}, dimensions={0} | all-to-all | bytes 2097152 | tf_op jit(solution)/shard_map/all_to_all | solution.py:19
  94.9 4.5 %all-to-all-start.2 = ((bf16[16,128,256]{2,1,0:T(8,128)(2,1)}), bf16[16,128,256]{2,1,0:T(8,128)(2,1)S(1)}, u32[]{:S(2)}, u32[]{:S(2)}) async-start(bf16[16,128,256]{2,1,0:T(8,128)(2,1)} %get-tuple-element.11), calls=%async_computation.2 | async-start | bytes 2097152 | tf_op jit(solution)/shard_map/all_to_all | solution.py:20
  99.4 0.0 reduce-scatter.5.cloned.1.call-start
  99.5 0.0 copy-done.6
  99.5 0.1 select_reduce_fusion.1
  99.6 1.6 gather_fusion.1
  101.2 16.4 %all-to-all-done.2 = bf16[16,128,256]{2,1,0:T(8,128)(2,1)S(1)} async-done(((bf16[16,128,256]{2,1,0:T(8,128)(2,1)}), bf16[16,128,256]{2,1,0:T(8,128)(2,1)S(1)}, u32[]{:S(2)}, u32[]{:S(2)}) %all-to-all-start.2) | async-done | bytes 1048608 | tf_op jit(solution)/shard_map/all_to_all | solution.py:20
  117.6 1.6 gather_fusion.3
  119.1 2.2 copy.42
  121.4 52.3 %all-gather.5.cloned.1.call-done = bf16[32,8,4096]{2,1,0:T(8,128)(2,1)} async-done(((bf16[32,8,256]{2,1,0:T(8,128)(2,1)}), bf16[32,8,4096]{2,1,0:T(8,128)(2,1)}) %all-gather.5.cloned.1.call-update) | async-done | bytes 2097168 | tf_op jit(solution)/shard_map/all_gather | solution.py:62
  173.7 2.3 copy.43
  176.0 0.0 copy-start.1
  176.0 0.0 copy-done.4
  176.0 0.0 copy-start.3
  176.0 1.3 fusion.4
  177.4 0.0 copy-done.1
  177.4 0.6 copy-done.3
  178.0 1.4 fusion.16
  179.5 2.1 convolution_convert_fusion.2
  181.6 0.0 reduce-scatter.5.cloned.1.call-update
  181.6 0.0 reduce-scatter.3.cloned.1.call-start
  181.7 3.3 convolution_convert_fusion.3
  185.0 0.0 reduce-scatter.3.cloned.1.call-update
  185.0 87.4 %reduce-scatter.5.cloned.1.call-done = bf16[256,1,256]{2,0,1:T(8,128)(2,1)} async-done(((bf16[256,16,256]{2,0,1:T(8,128)(2,1)}), bf16[256,1,256]{2,0,1:T(8,128)(2,1)}) %reduce-scatter.5.cloned.1.call-update) | async-done | bytes 131088 | tf_op jit(solution)/shard_map/reduce_scatter | solution.py:80
  272.4 12.7 %all-to-all-start.5 = ((bf16[32,8,256]{2,1,0:T(8,128)(2,1)}), bf16[32,8,256]{2,1,0:T(8,128)(2,1)S(1)}, u32[]{:S(2)}, u32[]{:S(2)}) async-start(bf16[32,8,256]{2,1,0:T(8,128)(2,1)} %bitcast.79), calls=%async_computation.7 | async-start | bytes 262144 | tf_op jit(solution)/shard_map/all_to_all | solution.py:91
  285.0 2.8 copy.36
  287.9 4.3 %copy.37 = bf16[16,256,256]{2,1,0:T(8,128)(2,1)} copy(bf16[16,256,256]{1,0,2:T(8,128)(2,1)} %bitcast.68) | data formatting | bytes 4194304 | tf_op jit(solution)/shard_map/ru,rpd->upd/dot_general | solution.py:84
  292.2 3.5 convolution_convert_fusion
  295.7 74.6 %reduce-scatter.3.cloned.1.call-done = bf16[256,1,256]{2,0,1:T(8,128)(2,1)} async-done(((bf16[256,16,256]{2,0,1:T(8,128)(2,1)}), bf16[256,1,256]{2,0,1:T(8,128)(2,1)}) %reduce-scatter.3.cloned.1.call-update) | async-done | bytes 131088 | tf_op jit(solution)/shard_map/reduce_scatter | solution.py:69
  370.3 0.0 all-to-all-done.5
  370.3 12.7 %all-to-all-start.3 = ((bf16[32,8,256]{2,1,0:T(8,128)(2,1)}), bf16[32,8,256]{2,1,0:T(8,128)(2,1)S(1)}, u32[]{:S(2)}, u32[]{:S(2)}) async-start(bf16[32,8,256]{2,1,0:T(8,128)(2,1)} %bitcast.78), calls=%async_computation.4 | async-start | bytes 262144 | tf_op jit(solution)/shard_map/all_to_all | solution.py:90
  383.0 0.0 copy-done.2
  383.0 1.8 convolution_convert_fusion.1
  384.8 12.6 %all-to-all-done.3 = bf16[32,8,256]{2,1,0:T(8,128)(2,1)S(1)} async-done(((bf16[32,8,256]{2,1,0:T(8,128)(2,1)}), bf16[32,8,256]{2,1,0:T(8,128)(2,1)S(1)}, u32[]{:S(2)}, u32[]{:S(2)}) %all-to-all-start.3) | async-done | bytes 131104 | tf_op jit(solution)/shard_map/all_to_all | solution.py:90
  397.4 0.7 gather_fusion.5
  398.1 0.7 gather_fusion.4
  398.8 0.1 broadcast_select_fusion.8
  398.9 0.7 reduce_sum.38
  399.6 0.7 reduce_sum.39
  (20 shorter events, 0.3 us)
Async XLA Ops:
  7.2 55.6 %copy-start = (bf16[2048,256]{1,0:T(8,128)(2,1)S(1)}, bf16[2048,256]{1,0:T(8,128)(2,1)}, u32[]{:S(2)}) copy-start(bf16[2048,256]{1,0:T(8,128)(2,1)} %param.15) | copy-start | bytes 3145732
  7.2 112.0 %all-gather.3.cloned.1.call-start = ((), (), s32[]{:S(2)}) async-start(), calls=%async_computation.8 | async-start | bytes 2228224 | tf_op jit(solution)/shard_map/all_gather | solution.py:61
  41.0 132.6 %all-gather.5.cloned.1.call-start = ((), (), s32[]{:S(2)}) async-start(), calls=%async_computation.10 | async-start | bytes 2228224 | tf_op jit(solution)/shard_map/all_gather | solution.py:62
  62.8 2.5 copy-start.5
  66.5 33.0 %copy-start.6 = (s32[16]{0:T(128)S(1)}, s32[16]{0:T(128)}, u32[]{:S(2)}) copy-start(s32[16]{0:T(128)} %param.17) | copy-start | bytes 196
  94.9 22.7 %all-to-all-start.2 = ((bf16[16,128,256]{2,1,0:T(8,128)(2,1)}), bf16[16,128,256]{2,1,0:T(8,128)(2,1)S(1)}, u32[]{:S(2)}, u32[]{:S(2)}) async-start(bf16[16,128,256]{2,1,0:T(8,128)(2,1)} %get-tuple-element.11), calls=%async_computation.2 | async-start | bytes 2097152 | tf_op jit(solution)/shard_map/all_to_all | solution.py:20
  99.4 172.9 %reduce-scatter.5.cloned.1.call-start = ((), (), s32[]{:S(2)}) async-start(), calls=%async_computation.11 | async-start | bytes 2228224 | tf_op jit(solution)/shard_map/reduce_scatter | solution.py:80
  173.7 2.3 copy-start.4
  176.0 1.4 copy-start.1
  176.0 2.0 copy-start.3
  181.6 188.7 %reduce-scatter.3.cloned.1.call-start = ((), (), s32[]{:S(2)}) async-start(), calls=%async_computation.9 | async-start | bytes 2228224 | tf_op jit(solution)/shard_map/reduce_scatter | solution.py:69
  272.4 98.0 %all-to-all-start.5 = ((bf16[32,8,256]{2,1,0:T(8,128)(2,1)}), bf16[32,8,256]{2,1,0:T(8,128)(2,1)S(1)}, u32[]{:S(2)}, u32[]{:S(2)}) async-start(bf16[32,8,256]{2,1,0:T(8,128)(2,1)} %bitcast.79), calls=%async_computation.7 | async-start | bytes 262144 | tf_op jit(solution)/shard_map/all_to_all | solution.py:91
  292.2 90.9 %copy-start.2 = (bf16[16,256,256]{2,1,0:T(8,128)(2,1)S(1)}, bf16[16,256,256]{2,1,0:T(8,128)(2,1)}, u32[]{:S(2)}) copy-start(bf16[16,256,256]{2,1,0:T(8,128)(2,1)} %copy.36) | copy-start | bytes 6291460
  370.3 27.1 %all-to-all-start.3 = ((bf16[32,8,256]{2,1,0:T(8,128)(2,1)}), bf16[32,8,256]{2,1,0:T(8,128)(2,1)S(1)}, u32[]{:S(2)}, u32[]{:S(2)}) async-start(bf16[32,8,256]{2,1,0:T(8,128)(2,1)} %bitcast.78), calls=%async_computation.4 | async-start | bytes 262144 | tf_op jit(solution)/shard_map/all_to_all | solution.py:90
Sparse Core Ops, SparseCore 0:
  41.2 69.9 all-gather.2
  114.3 59.3 all-gather.4
  181.7 90.5 reduce-scatter.4
  277.0 93.2 reduce-scatter.2
where the time goes:
time: 409 us; the launch traced here: 407 us
  waiting for transfers between devices  243 us (59%)
  blocking collectives  79 us (19%)
  starting transfers between devices  30 us (7%)
  local copies, waits for them, and re-layouts  22.7 us (6%)
  between operations  14 us (3%)
  matrix products  13.9 us (3%)
    reduce_scatter x1, waiting for transfers between devices, local(): lax.psum_scatter(in_terms.astype(jnp.bfloat16), 'cuts', scatter_dimension...  87.4 us
    reduce_scatter x1, waiting for transfers between devices, local(): lax.psum_scatter(out_terms.astype(jnp.bfloat16), 'cuts', scatter_dimensio...  74.6 us
    all_gather x1, waiting for transfers between devices, local(): lax.all_gather(sent_back, 'cuts', axis=2, tiled=True)  52.3 us
    all_to_all x1, blocking collectives, local(): lax.all_to_all(fill_slots(jnp.repeat(tokens, 2, axis=0)), 'expert', split...  31.5 us
    all_to_all x1, blocking collectives, local(): lax.all_to_all(up_pieces, 'cuts', split_axis=0, concat_axis=0, tiled=True)  28.4 us
    all_to_all x1, blocking collectives, local(): lax.all_to_all(fill_slots(back_rows), 'expert', split_axis=0, concat_axis...  19.1 us
    all_to_all x1, waiting for transfers between devices, local(): lax.all_to_all(down_pieces, 'cuts', split_axis=0, concat_axis=0, tiled=True)  16.4 us
    all_to_all x1, starting transfers between devices, local(): lax.all_to_all(out_send, 'expert', split_axis=0, concat_axis=0, tiled=True)  12.7 us
  transfers between devices with their start and end apart: 7, of which 5 were waited for; matrix products, arithmetic and copies ran while one was open for 7% of the time, Pallas kernels for 0%

commit v1 on v0

v1 whole, which is shorter than its diff:
```python
import jax
import jax.numpy as jnp
from jax import lax
from jax.sharding import PartitionSpec as P

F32, BF16 = jnp.float32, jnp.bfloat16


def exchange(parts, axis):
    return lax.all_to_all(parts, axis, split_axis=0, concat_axis=0, tiled=True)


def everywhere(block, axis):
    return exchange(jnp.broadcast_to(block[None], (lax.axis_size(axis), *block.shape)), axis)


def local(tokens, expert_ids, gate_weights, old_up, old_down, old_rows, new_slots, cotangent):
    cut_count = lax.axis_size("cuts")
    group_count = lax.axis_size("expert")
    expert_count = group_count // 2
    tok_rows, block_width = tokens.shape
    half_units = old_up.shape[0]
    unit_width = half_units // cut_count
    capacity = 8 * tok_rows // group_count
    slot_rows = group_count * capacity
    cut = lax.axis_index("cuts")
    own_block = lax.dynamic_index_in_dim(old_rows, cut, keepdims=False)
    cut_list = jnp.arange(cut_count, dtype=jnp.int32)
    inverse = jnp.sum(
        cut_list[:, None] * (old_rows[:, None] == cut_list[None, :]).astype(jnp.int32), axis=0
    )
    own_source = jnp.sum(cut_list * (old_rows == cut).astype(jnp.int32))

    with jax.named_scope("token_blocks"):
        both = everywhere(jnp.concatenate([tokens, cotangent], axis=1), "cuts")
        both = lax.dynamic_index_in_dim(both, own_block, axis=0, keepdims=False)

    flat_ids = expert_ids.reshape(-1)
    expert_hits = (flat_ids[:, None] == jnp.arange(expert_count, dtype=jnp.int32)[None, :]).astype(
        jnp.int32
    )
    slot_rank = jnp.sum((jnp.cumsum(expert_hits, axis=0) - expert_hits) * expert_hits, axis=1)
    target = (flat_ids * capacity + slot_rank).reshape(tok_rows, 2)
    slots = expert_count * capacity
    slot_list = jnp.arange(slots, dtype=jnp.int32)
    matches = slot_list[:, None, None] == target[None]
    placer = jnp.any(matches, axis=2).astype(BF16)
    slot_gate = jnp.sum(jnp.where(matches, gate_weights[None], 0.0), axis=(1, 2))

    with jax.named_scope("dispatch"):
        placed = jnp.dot(placer, both, preferred_element_type=F32)
        scale = jnp.where(
            jnp.arange(2 * block_width)[None, :] < block_width, 1.0, slot_gate[:, None]
        )
        placed = (placed * scale).astype(BF16).reshape(expert_count, 1, capacity, 2 * block_width)
        placed = jnp.broadcast_to(placed, (expert_count, 2, capacity, 2 * block_width))
        routed = exchange(placed.reshape(group_count, capacity, 2 * block_width), "expert")
        routed = routed.reshape(slot_rows, 2 * block_width)
        routed_x, routed_back = routed[:, :block_width], routed[:, block_width:]

    def summed(weights, rows):
        part = lax.dot_general(
            weights, rows, (((1,), (1,)), ((), ())), preferred_element_type=F32
        ).astype(BF16)
        part = exchange(part.reshape(cut_count, unit_width, slot_rows), "cuts")
        return jnp.sum(part.astype(F32), axis=0)

    with jax.named_scope("pre_act"):
        pre_act = summed(old_up, routed_x)
    with jax.named_scope("hidden_grad"):
        hidden_grad = summed(old_down, routed_back)
    with jax.named_scope("hidden"):
        hidden = jax.nn.silu(pre_act).astype(BF16)
        hidden = everywhere(hidden, "cuts").reshape(half_units, slot_rows)
    with jax.named_scope("pre_grad"):
        sig = jax.nn.sigmoid(pre_act)
        pre_grad = (hidden_grad * sig * (1.0 + pre_act * (1.0 - sig))).astype(BF16)
        pre_grad = everywhere(pre_grad, "cuts").reshape(half_units, slot_rows)

    def rows_of(units, weights):
        return lax.dot_general(
            units, weights, (((0,), (0,)), ((), ())), preferred_element_type=F32
        ).astype(BF16)

    with jax.named_scope("give_back"):
        half_rows = jnp.concatenate(
            [rows_of(hidden, old_down), rows_of(pre_grad, old_up)], axis=1
        ).reshape(group_count, capacity, 2 * block_width)
        half_rows = exchange(half_rows, "expert").reshape(slot_rows, 2 * block_width)
        row_list = jnp.arange(slot_rows, dtype=jnp.int32)
        row_slot = row_list // (2 * capacity) * capacity + row_list % capacity
        picker = (target.reshape(-1)[:, None] == row_slot[None, :]).astype(BF16)
        entries = jnp.dot(picker, half_rows, preferred_element_type=F32)
        entries = entries.reshape(tok_rows, 2, 2 * block_width)
        mixed = jnp.sum(entries[:, :, :block_width] * gate_weights[:, :, None], axis=1)
        token_grad = jnp.sum(entries[:, :, block_width:], axis=1)
        result = jnp.concatenate([mixed, token_grad], axis=1).astype(BF16)
        result = everywhere(result, "cuts")
        result = lax.dynamic_index_in_dim(result, own_source, axis=0, keepdims=False)

    def new_slices(units, rows):
        grad = jnp.dot(units, rows, preferred_element_type=F32).astype(BF16)
        grad = jnp.take(grad.reshape(cut_count, unit_width, block_width), new_slots, axis=0)
        grad = jnp.take(exchange(grad, "cuts"), inverse, axis=0)
        return jnp.transpose(grad, (1, 0, 2)).reshape(unit_width, cut_count * block_width)

    with jax.named_scope("down_grad"):
        down_grad = new_slices(hidden, routed_back)
    with jax.named_scope("up_grad"):
        up_grad = new_slices(pre_grad, routed_x)
    return (result[:, :block_width], result[:, block_width:], up_grad, down_grad)


def solution(mesh):
    placed = (
        P("expert", "cuts"),
        P("expert", None),
        P("expert", None),
        P("expert", "cuts"),
        P("expert", "cuts"),
        P(),
        P(),
        P("expert", "cuts"),
    )
    return jax.shard_map(
        local,
        mesh=mesh,
        in_specs=placed,
        out_specs=(
            P("expert", "cuts"),
            P("expert", "cuts"),
            P(("expert", "cuts"), None),
            P(("expert", "cuts"), None),
        ),
        check_vma=False,
    )
```

time: 409 us -> 248 us (0.61)
  waiting for transfers between devices: 243 us -> 131 us
  blocking collectives: 79 us -> 32.3 us
  starting transfers between devices: 30 us -> 50.3 us
  between operations: 14 us -> 4.87 us
  matrix products: 13.9 us -> 6.83 us
  local copies, waits for them, and re-layouts: 22.7 us -> 17 us
    reduce_scatter x2 -> x0, waiting for transfers between devices: 162 us -> none  [the longest x1 87.4 us: local(): lax.psum_scatter(in_terms.astype(jnp.bfloat16), 'cuts', scatter_dimension...]
    all_to_all x3 -> x9, waiting for transfers between devices: 29 us -> 131 us  [exchange(): return lax.all_to_all(parts, axis, split_axis=0, concat_axis=0, tiled=True)]
    all_gather x2 -> x0, waiting for transfers between devices: 52.3 us -> none  [the longest x1 52.3 us: local(): lax.all_gather(sent_back, 'cuts', axis=2, tiled=True)]
    all_to_all x3 -> x1, blocking collectives: 79 us -> 32.3 us  [exchange(): return lax.all_to_all(parts, axis, split_axis=0, concat_axis=0, tiled=True)]
    all_to_all x3 -> x9, starting transfers between devices: 29.9 us -> 50.3 us  [exchange(): return lax.all_to_all(parts, axis, split_axis=0, concat_axis=0, tiled=True)]
    dot_general x2 -> x0, local copies, waits for them, and re-layouts: 7.12 us -> none  [the longest x1 4.3 us: local(): jnp.einsum('ru,rpd->upd', hidden, routed_back, preferred_element_type=jnp...]
    dot_general x8, matrix products: 13.9 us -> 6.83 us  [the longest x2 3.05 us: new_slices(): grad = jnp.dot(units, rows, preferred_element_type=F32).astype(BF16)]
    unnamed x18 -> x21, local copies, waits for them, and re-layouts: 6.8 us -> 0.13 us
  transfers between devices with their start and end apart: 7 -> 9, of which waited for: 5 -> 9; matrix products, arithmetic and copies ran while one was open for 7% -> 5% of each run, Pallas kernels for 0% -> 0%
where the time goes in v1:
time: 248 us; the launch traced here: 247 us
  waiting for transfers between devices  131 us (53%)
  starting transfers between devices  50.3 us (20%)
  blocking collectives  32.3 us (13%)
  local copies, waits for them, and re-layouts  17 us (7%)
  matrix products  6.83 us (3%)
  between operations  4.87 us (2%)
  other arithmetic  4.45 us (2%)
    all_to_all x9, waiting for transfers between devices, exchange(): return lax.all_to_all(parts, axis, split_axis=0, concat_axis=0, tiled=True)  131 us
    all_to_all x9, starting transfers between devices, exchange(): return lax.all_to_all(parts, axis, split_axis=0, concat_axis=0, tiled=True)  50.3 us
    all_to_all x1, blocking collectives, exchange(): return lax.all_to_all(parts, axis, split_axis=0, concat_axis=0, tiled=True)  32.3 us
  transfers between devices with their start and end apart: 9, of which 9 were waited for; matrix products, arithmetic and copies ran while one was open for 5% of the time, Pallas kernels for 0%

profile of v1, /device:TPU:1, one launch (start us, length us, event | category | flops | bytes accessed | tf_op | source)
XLA Modules:
  0.0 246.7 jit_solution(2394767012477286742)
XLA Ops:
  0.6 0.0 copy-start
  0.7 0.8 pad_maximum_fusion.1
  1.5 0.8 broadcast_in_dim.50
  2.3 10.2 %all-to-all-start = ((bf16[16,32,512]{2,1,0:T(8,128)(2,1)}), bf16[16,32,512]{2,1,0:T(8,128)(2,1)S(1)}, u32[]{:S(2)}, u32[]{:S(2)}) async-start(bf16[16,32,512]{2,1,0:T(8,128)(2,1)} %broadcast_in_dim.50), calls=%async_computation | async-start | bytes 1048576 | tf_op jit(solution)/shard_map/token_blocks/all_to_all | solution.py:10
  12.6 0.1 copy.56
  12.7 0.1 eq.67
  12.8 0.1 fusion.17
  12.9 0.1 reduce_window_sum.11
  13.0 0.2 select_reduce_fusion.1
  13.2 0.6 dynamic_slice.11
  15.1 0.1 reduce_sum.75
  15.2 0.1 copy.57
  15.9 0.1 fusion.14
  16.0 0.1 select_reduce_fusion
  16.1 8.0 %all-to-all-done = bf16[16,32,512]{2,1,0:T(8,128)(2,1)S(1)} async-done(((bf16[16,32,512]{2,1,0:T(8,128)(2,1)}), bf16[16,32,512]{2,1,0:T(8,128)(2,1)S(1)}, u32[]{:S(2)}, u32[]{:S(2)}) %all-to-all-start) | async-done | bytes 524320 | tf_op jit(solution)/shard_map/token_blocks/all_to_all | solution.py:10
  24.1 0.2 fusion.3
  24.3 32.3 %all_to_all.50 = bf16[32,8,512]{2,1,0:T(8,128)(2,1)S(1)} all-to-all(bf16[32,8,512]{2,1,0:T(8,128)(2,1)S(1)} %bitcast.59), channel_id=1, replica_groups=mesh['expert'=32,'cuts'=16] {'expert'}, dimensions={0} | all-to-all | bytes 524288 | tf_op jit(solution)/shard_map/dispatch/all_to_all | solution.py:10
  56.7 0.5 fusion
  57.2 1.2 copy.76
  58.4 7.9 %all-to-all-start.2 = ((bf16[16,128,256]{1,2,0:T(8,128)(2,1)}), bf16[16,128,256]{1,2,0:T(8,128)(2,1)S(1)}, u32[]{:S(2)}, u32[]{:S(2)}) async-start(bf16[16,128,256]{1,2,0:T(8,128)(2,1)} %bitcast.48), calls=%async_computation.2 | async-start | bytes 2097152 | tf_op jit(solution)/shard_map/pre_act/all_to_all | solution.py:10
  66.3 0.5 fusion.1
  66.7 1.2 copy.75
  68.0 15.6 %all-to-all-done.2 = bf16[16,128,256]{1,2,0:T(8,128)(2,1)S(1)} async-done(((bf16[16,128,256]{1,2,0:T(8,128)(2,1)}), bf16[16,128,256]{1,2,0:T(8,128)(2,1)S(1)}, u32[]{:S(2)}, u32[]{:S(2)}) %all-to-all-start.2) | async-done | bytes 1048608 | tf_op jit(solution)/shard_map/pre_act/all_to_all | solution.py:10
  83.6 4.2 %all-to-all-start.4 = ((bf16[16,128,256]{1,2,0:T(8,128)(2,1)}), bf16[16,128,256]{1,2,0:T(8,128)(2,1)S(1)}, u32[]{:S(2)}, u32[]{:S(2)}) async-start(bf16[16,128,256]{1,2,0:T(8,128)(2,1)} %bitcast.47), calls=%async_computation.4 | async-start | bytes 2097152 | tf_op jit(solution)/shard_map/hidden_grad/all_to_all | solution.py:10
  87.8 0.1 convert_reduce_fusion.1
  87.9 17.3 %all-to-all-done.4 = bf16[16,128,256]{1,2,0:T(8,128)(2,1)S(1)} async-done(((bf16[16,128,256]{1,2,0:T(8,128)(2,1)}), bf16[16,128,256]{1,2,0:T(8,128)(2,1)S(1)}, u32[]{:S(2)}, u32[]{:S(2)}) %all-to-all-start.4) | async-done | bytes 1048608 | tf_op jit(solution)/shard_map/hidden_grad/all_to_all | solution.py:10
  105.3 0.1 convert_reduce_fusion
  105.4 0.1 multiply_convert_fusion.1
  105.5 0.1 copy.60
  105.6 1.1 broadcast_in_dim.90
  106.7 4.2 %all-to-all-start.3 = ((bf16[16,128,256]{2,1,0:T(8,128)(2,1)}), bf16[16,128,256]{2,1,0:T(8,128)(2,1)S(1)}, u32[]{:S(2)}, u32[]{:S(2)}) async-start(bf16[16,128,256]{2,1,0:T(8,128)(2,1)} %broadcast_in_dim.90), calls=%async_computation.3 | async-start | bytes 2097152 | tf_op jit(solution)/shard_map/hidden/all_to_all | solution.py:10
  110.8 0.1 copy.63
  110.9 17.3 %all-to-all-done.3 = bf16[16,128,256]{2,1,0:T(8,128)(2,1)S(1)} async-done(((bf16[16,128,256]{2,1,0:T(8,128)(2,1)}), bf16[16,128,256]{2,1,0:T(8,128)(2,1)S(1)}, u32[]{:S(2)}, u32[]{:S(2)}) %all-to-all-start.3) | async-done | bytes 1048608 | tf_op jit(solution)/shard_map/hidden/all_to_all | solution.py:10
  128.3 1.2 broadcast_in_dim.91
  129.5 4.9 %all-to-all-start.5 = ((bf16[16,128,256]{2,1,0:T(8,128)(2,1)}), bf16[16,128,256]{2,1,0:T(8,128)(2,1)}, u32[]{:S(2)}, u32[]{:S(2)}) async-start(bf16[16,128,256]{2,1,0:T(8,128)(2,1)} %broadcast_in_dim.91), calls=%async_computation.5 | async-start | bytes 2097152 | tf_op jit(solution)/shard_map/pre_grad/all_to_all | solution.py:10
  134.4 0.4 convolution_convert_fusion
  134.8 17.1 %all-to-all-done.5 = bf16[16,128,256]{2,1,0:T(8,128)(2,1)} async-done(((bf16[16,128,256]{2,1,0:T(8,128)(2,1)}), bf16[16,128,256]{2,1,0:T(8,128)(2,1)}, u32[]{:S(2)}, u32[]{:S(2)}) %all-to-all-start.5) | async-done | bytes 1048608 | tf_op jit(solution)/shard_map/pre_grad/all_to_all | solution.py:10
  151.9 2.6 %convolution_convert_fusion.1 = bf16[2048,256]{1,0:T(8,128)(2,1)} fusion(bf16[2048,256]{1,0:T(8,128)(2,1)} %bitcast.8, bf16[256,512]{1,0:T(8,128)(2,1)S(1)} %bitcast.56), kind=kOutput, calls=%fused_computation.5 | convolution fusion | flops 268959744 | bytes 2228224 | tf_op jit(solution)/shard_map/up_grad/dot_general | solution.py:102
  154.5 0.6 gather_fusion.2
  155.2 1.8 gather_fusion
  157.0 1.6 broadcast_select_fusion
  158.6 4.2 %all-to-all-start.9 = ((bf16[16,128,256]{2,1,0:T(8,128)(2,1)}), bf16[16,128,256]{2,1,0:T(8,128)(2,1)S(1)}, u32[]{:S(2)}, u32[]{:S(2)}) async-start(bf16[16,128,256]{2,1,0:T(8,128)(2,1)} %get-tuple-element.13), calls=%async_computation.9 | async-start | bytes 2097152 | tf_op jit(solution)/shard_map/down_grad/all_to_all | solution.py:10
  162.8 1.9 convolution_convert_fusion.4
  164.7 0.5 convolution_convert_fusion.5
  165.3 0.8 copy.64
  166.1 14.1 %all-to-all-done.9 = bf16[16,128,256]{2,1,0:T(8,128)(2,1)S(1)} async-done(((bf16[16,128,256]{2,1,0:T(8,128)(2,1)}), bf16[16,128,256]{2,1,0:T(8,128)(2,1)S(1)}, u32[]{:S(2)}, u32[]{:S(2)}) %all-to-all-start.9) | async-done | bytes 1048608 | tf_op jit(solution)/shard_map/down_grad/all_to_all | solution.py:10
  180.2 3.9 %all-to-all-start.6 = ((bf16[32,8,512]{2,1,0:T(8,128)(2,1)}), bf16[32,8,512]{2,1,0:T(8,128)(2,1)S(1)}, u32[]{:S(2)}, u32[]{:S(2)}) async-start(bf16[32,8,512]{2,1,0:T(8,128)(2,1)} %bitcast.9), calls=%async_computation.6 | async-start | bytes 524288 | tf_op jit(solution)/shard_map/give_back/all_to_all | solution.py:10
  184.1 0.1 select_reduce_fusion.2
  184.2 20.2 %all-to-all-done.6 = bf16[32,8,512]{2,1,0:T(8,128)(2,1)S(1)} async-done(((bf16[32,8,512]{2,1,0:T(8,128)(2,1)}), bf16[32,8,512]{2,1,0:T(8,128)(2,1)S(1)}, u32[]{:S(2)}, u32[]{:S(2)}) %all-to-all-start.6) | async-done | bytes 262176 | tf_op jit(solution)/shard_map/give_back/all_to_all | solution.py:10
  204.4 6.3 %all-to-all-start.8 = ((bf16[16,128,256]{2,1,0:T(8,128)(2,1)}), bf16[16,128,256]{2,1,0:T(8,128)(2,1)S(1)}, u32[]{:S(2)}, u32[]{:S(2)}) async-start(bf16[16,128,256]{2,1,0:T(8,128)(2,1)} %get-tuple-element.14), calls=%async_computation.8 | async-start | bytes 2097152 | tf_op jit(solution)/shard_map/up_grad/all_to_all | solution.py:10
  210.7 0.2 fusion.4
  210.9 0.1 fusion.10
  211.0 17.1 %all-to-all-done.8 = bf16[16,128,256]{2,1,0:T(8,128)(2,1)S(1)} async-done(((bf16[16,128,256]{2,1,0:T(8,128)(2,1)}), bf16[16,128,256]{2,1,0:T(8,128)(2,1)S(1)}, u32[]{:S(2)}, u32[]{:S(2)}) %all-to-all-start.8) | async-done | bytes 1048608 | tf_op jit(solution)/shard_map/up_grad/all_to_all | solution.py:10
  228.2 0.9 broadcast_in_dim.92
  229.1 4.7 %all-to-all-start.7 = ((bf16[16,32,512]{2,1,0:T(8,128)(2,1)}), bf16[16,32,512]{2,1,0:T(8,128)(2,1)}, u32[]{:S(2)}, u32[]{:S(2)}) async-start(bf16[16,32,512]{2,1,0:T(8,128)(2,1)} %broadcast_in_dim.92), calls=%async_computation.7 | async-start | bytes 1048576 | tf_op jit(solution)/shard_map/give_back/all_to_all | solution.py:10
  233.7 0.6 fusion.20
  236.3 0.6 gather_fusion.3
  237.0 1.8 gather_fusion.1
  238.8 0.3 select_bitcast_fusion
  239.1 1.1 copy.71
  240.2 1.1 copy.72
  241.2 4.1 %all-to-all-done.7 = bf16[16,32,512]{2,1,0:T(8,128)(2,1)} async-done(((bf16[16,32,512]{2,1,0:T(8,128)(2,1)}), bf16[16,32,512]{2,1,0:T(8,128)(2,1)}, u32[]{:S(2)}, u32[]{:S(2)}) %all-to-all-start.7) | async-done | bytes 524320 | tf_op jit(solution)/shard_map/give_back/all_to_all | solution.py:10
  245.3 0.8 dynamic-slice_bitcast_fusion
  246.1 0.6 fusion.22
  (31 shorter events, 0.1 us)
Async XLA Ops:
  0.6 56.0 %copy-start = (bf16[2048,256]{1,0:T(8,128)(2,1)S(1)}, bf16[2048,256]{1,0:T(8,128)(2,1)}, u32[]{:S(2)}) copy-start(bf16[2048,256]{1,0:T(8,128)(2,1)} %param.13) | copy-start | bytes 3145732
  0.6 11.9 %copy-start.7 = (s32[32,2]{0,1:T(2,128)S(1)}, s32[32,2]{0,1:T(2,128)}, u32[]{:S(2)}) copy-start(s32[32,2]{0,1:T(2,128)} %param.11) | copy-start | bytes 772
  0.7 12.5 %copy-start.9 = (s32[16]{0:T(128)S(1)}, s32[16]{0:T(128)}, u32[]{:S(2)}) copy-start(s32[16]{0:T(128)} %param.15) | copy-start | bytes 196
  0.7 15.3 %copy-start.6 = (f32[32,2]{0,1:T(2,128)S(1)}, f32[32,2]{0,1:T(2,128)}, u32[]{:S(2)}) copy-start(f32[32,2]{0,1:T(2,128)} %param.12) | copy-start | bytes 772
  2.3 21.7 %all-to-all-start = ((bf16[16,32,512]{2,1,0:T(8,128)(2,1)}), bf16[16,32,512]{2,1,0:T(8,128)(2,1)S(1)}, u32[]{:S(2)}, u32[]{:S(2)}) async-start(bf16[16,32,512]{2,1,0:T(8,128)(2,1)} %broadcast_in_dim.50), calls=%async_computation | async-start | bytes 1048576 | tf_op jit(solution)/shard_map/token_blocks/all_to_all | solution.py:10
  58.4 7.9 %copy-start.4 = (bf16[2048,256]{1,0:T(8,128)(2,1)S(1)}, bf16[2048,256]{1,0:T(8,128)(2,1)}, u32[]{:S(2)}) copy-start(bf16[2048,256]{1,0:T(8,128)(2,1)} %param.14) | copy-start | bytes 3145732
  58.4 25.2 %all-to-all-start.2 = ((bf16[16,128,256]{1,2,0:T(8,128)(2,1)}), bf16[16,128,256]{1,2,0:T(8,128)(2,1)S(1)}, u32[]{:S(2)}, u32[]{:S(2)}) async-start(bf16[16,128,256]{1,2,0:T(8,128)(2,1)} %bitcast.48), calls=%async_computation.2 | async-start | bytes 2097152 | tf_op jit(solution)/shard_map/pre_act/all_to_all | solution.py:10
  83.6 21.6 %all-to-all-start.4 = ((bf16[16,128,256]{1,2,0:T(8,128)(2,1)}), bf16[16,128,256]{1,2,0:T(8,128)(2,1)S(1)}, u32[]{:S(2)}, u32[]{:S(2)}) async-start(bf16[16,128,256]{1,2,0:T(8,128)(2,1)} %bitcast.47), calls=%async_computation.4 | async-start | bytes 2097152 | tf_op jit(solution)/shard_map/hidden_grad/all_to_all | solution.py:10
  106.7 21.6 %all-to-all-start.3 = ((bf16[16,128,256]{2,1,0:T(8,128)(2,1)}), bf16[16,128,256]{2,1,0:T(8,128)(2,1)S(1)}, u32[]{:S(2)}, u32[]{:S(2)}) async-start(bf16[16,128,256]{2,1,0:T(8,128)(2,1)} %broadcast_in_dim.90), calls=%async_computation.3 | async-start | bytes 2097152 | tf_op jit(solution)/shard_map/hidden/all_to_all | solution.py:10
  128.3 6.1 %copy-start.2 = (bf16[16,128,256]{2,1,0:T(8,128)(2,1)}, bf16[16,128,256]{2,1,0:T(8,128)(2,1)S(1)}, u32[]{:S(2)}) copy-start(bf16[16,128,256]{2,1,0:T(8,128)(2,1)S(1)} %all-to-all-done.3) | copy-start | bytes 3145732
  129.5 4.9 %copy-start.8 = (s32[16]{0:T(128)S(1)}, s32[16]{0:T(128)}, u32[]{:S(2)}) copy-start(s32[16]{0:T(128)} %param.16) | copy-start | bytes 196
  129.5 22.5 %all-to-all-start.5 = ((bf16[16,128,256]{2,1,0:T(8,128)(2,1)}), bf16[16,128,256]{2,1,0:T(8,128)(2,1)}, u32[]{:S(2)}, u32[]{:S(2)}) async-start(bf16[16,128,256]{2,1,0:T(8,128)(2,1)} %broadcast_in_dim.91), calls=%async_computation.5 | async-start | bytes 2097152 | tf_op jit(solution)/shard_map/pre_grad/all_to_all | solution.py:10
  158.6 21.6 %all-to-all-start.9 = ((bf16[16,128,256]{2,1,0:T(8,128)(2,1)}), bf16[16,128,256]{2,1,0:T(8,128)(2,1)S(1)}, u32[]{:S(2)}, u32[]{:S(2)}) async-start(bf16[16,128,256]{2,1,0:T(8,128)(2,1)} %get-tuple-element.13), calls=%async_computation.9 | async-start | bytes 2097152 | tf_op jit(solution)/shard_map/down_grad/all_to_all | solution.py:10
  162.8 1.9 copy-start.3
  162.8 1.9 copy-start.5
  180.2 24.2 %all-to-all-start.6 = ((bf16[32,8,512]{2,1,0:T(8,128)(2,1)}), bf16[32,8,512]{2,1,0:T(8,128)(2,1)S(1)}, u32[]{:S(2)}, u32[]{:S(2)}) async-start(bf16[32,8,512]{2,1,0:T(8,128)(2,1)} %bitcast.9), calls=%async_computation.6 | async-start | bytes 524288 | tf_op jit(solution)/shard_map/give_back/all_to_all | solution.py:10
  204.4 23.8 %all-to-all-start.8 = ((bf16[16,128,256]{2,1,0:T(8,128)(2,1)}), bf16[16,128,256]{2,1,0:T(8,128)(2,1)S(1)}, u32[]{:S(2)}, u32[]{:S(2)}) async-start(bf16[16,128,256]{2,1,0:T(8,128)(2,1)} %get-tuple-element.14), calls=%async_computation.8 | async-start | bytes 2097152 | tf_op jit(solution)/shard_map/up_grad/all_to_all | solution.py:10
  228.2 8.2 %copy-start.1 = (bf16[16,128,256]{2,1,0:T(8,128)(2,1)}, bf16[16,128,256]{2,1,0:T(8,128)(2,1)S(1)}, u32[]{:S(2)}) copy-start(bf16[16,128,256]{2,1,0:T(8,128)(2,1)S(1)} %all-to-all-done.8) | copy-start | bytes 3145732
  229.1 16.3 %all-to-all-start.7 = ((bf16[16,32,512]{2,1,0:T(8,128)(2,1)}), bf16[16,32,512]{2,1,0:T(8,128)(2,1)}, u32[]{:S(2)}, u32[]{:S(2)}) async-start(bf16[16,32,512]{2,1,0:T(8,128)(2,1)} %broadcast_in_dim.92), calls=%async_computation.7 | async-start | bytes 1048576 | tf_op jit(solution)/shard_map/give_back/all_to_all | solution.py:10

commit v2 on v1

v2 whole, which is shorter than its diff:
```python
import jax
import jax.numpy as jnp
from jax import lax
from jax.sharding import Mesh, PartitionSpec as P

F32, BF16 = jnp.float32, jnp.bfloat16


def exchange(parts, axis):
    return lax.all_to_all(parts, axis, split_axis=0, concat_axis=0, tiled=True)


def everywhere(block, axis):
    return exchange(jnp.broadcast_to(block[None], (lax.axis_size(axis), *block.shape)), axis)


def swap(block):
    return lax.ppermute(block, "core", [(0, 1), (1, 0)])


def pick(blocks, index):
    return lax.dynamic_index_in_dim(blocks, index, axis=0, keepdims=False)


def rows_at(blocks, places):
    return jnp.take(blocks, places, axis=0, mode="clip")


def local(tokens, expert_ids, gate_weights, old_up, old_down, old_rows, new_slots, cotangent):
    chips = lax.axis_size("chip")
    cut_count = 2 * chips
    group_count = lax.axis_size("expert")
    expert_count = group_count // 2
    tok_rows, width = tokens.shape
    half_units = old_up.shape[0]
    unit_width = half_units // cut_count
    core_units = half_units // 2
    capacity = 8 * tok_rows // group_count
    slot_rows = group_count * capacity
    chip, core = lax.axis_index("chip"), lax.axis_index("core")
    cut = 2 * chip + core
    cut_list = jnp.arange(cut_count, dtype=jnp.int32)
    inverse = jnp.sum(
        cut_list[:, None] * (old_rows[:, None] == cut_list[None, :]).astype(jnp.int32), axis=0
    )
    own_block, other_block = pick(old_rows, cut), pick(old_rows, 2 * chip + 1 - core)
    own_source = pick(inverse, cut)
    other_source = pick(inverse, 2 * chip + 1 - core)

    def across(blocks, own, other):
        theirs = swap(pick(blocks, other // 2))
        return jnp.where(own % 2 == core, pick(blocks, own // 2), theirs)

    slot_pairs = new_slots.reshape(chips, 2)
    kept, given = slot_pairs[:, core], slot_pairs[:, 1 - core]

    def both_blocks(weights):
        blocks = weights.reshape(cut_count, unit_width, width)
        mine, theirs = rows_at(blocks, kept), swap(rows_at(blocks, given))
        return jnp.concatenate([mine, theirs], axis=2).reshape(core_units, 2 * width)

    with jax.named_scope("weights"):
        up, down = both_blocks(old_up), both_blocks(old_down)

    with jax.named_scope("token_blocks"):
        both = everywhere(jnp.concatenate([tokens, cotangent], axis=1), "chip")
        both = across(both, own_block, other_block)

    flat_ids = expert_ids.reshape(-1)
    expert_hits = (flat_ids[:, None] == jnp.arange(expert_count, dtype=jnp.int32)[None, :]).astype(
        jnp.int32
    )
    slot_rank = jnp.sum((jnp.cumsum(expert_hits, axis=0) - expert_hits) * expert_hits, axis=1)
    target = (flat_ids * capacity + slot_rank).reshape(tok_rows, 2)
    slots = expert_count * capacity
    slot_list = jnp.arange(slots, dtype=jnp.int32)
    matches = slot_list[:, None, None] == target[None]
    placer = jnp.any(matches, axis=2).astype(BF16)
    slot_gate = jnp.sum(jnp.where(matches, gate_weights[None], 0.0), axis=(1, 2))

    with jax.named_scope("dispatch"):
        placed = jnp.dot(placer, both, preferred_element_type=F32)
        scale = jnp.where(jnp.arange(2 * width)[None, :] < width, 1.0, slot_gate[:, None])
        placed = (placed * scale).astype(BF16).reshape(expert_count, 1, capacity, 2 * width)
        placed = jnp.broadcast_to(placed, (expert_count, 2, capacity, 2 * width))
        routed = exchange(placed.reshape(group_count, capacity, 2 * width), "expert")
        routed = routed.reshape(slot_rows, 2 * width)
        other = swap(routed)
        routed_x = jnp.concatenate([routed[:, :width], other[:, :width]], axis=1)
        routed_back = jnp.concatenate([routed[:, width:], other[:, width:]], axis=1)

    def partial(weights, rows):
        part = lax.dot_general(
            weights, rows, (((1,), (1,)), ((), ())), preferred_element_type=F32
        ).astype(BF16)
        return part.reshape(chips, unit_width, slot_rows)

    with jax.named_scope("hidden"):
        parts = jnp.concatenate([partial(up, routed_x), partial(down, routed_back)], axis=1)
        sums = jnp.sum(exchange(parts, "chip").astype(F32), axis=0)
        pre_act, hidden_grad = sums[:unit_width], sums[unit_width:]
        sig = jax.nn.sigmoid(pre_act)
        hidden = jax.nn.silu(pre_act).astype(BF16)
        pre_grad = (hidden_grad * sig * (1.0 + pre_act * (1.0 - sig))).astype(BF16)
        units = everywhere(jnp.concatenate([hidden, pre_grad], axis=0), "chip")
        hidden = units[:, :unit_width].reshape(core_units, slot_rows)
        pre_grad = units[:, unit_width:].reshape(core_units, slot_rows)

    def rows_of(units, weights):
        return lax.dot_general(
            units, weights, (((0,), (0,)), ((), ())), preferred_element_type=F32
        )

    with jax.named_scope("give_back"):
        out_part, in_part = rows_of(hidden, down), rows_of(pre_grad, up)
        theirs = swap(jnp.concatenate([out_part[:, width:], in_part[:, width:]], axis=1).astype(BF16))
        own = jnp.concatenate([out_part[:, :width], in_part[:, :width]], axis=1)
        half_rows = (own + theirs.astype(F32)).astype(BF16)
        half_rows = exchange(half_rows.reshape(group_count, capacity, 2 * width), "expert")
        row_list = jnp.arange(slot_rows, dtype=jnp.int32)
        row_slot = row_list // (2 * capacity) * capacity + row_list % capacity
        picker = (target.reshape(-1)[:, None] == row_slot[None, :]).astype(BF16)
        entries = jnp.dot(picker, half_rows.reshape(slot_rows, 2 * width), preferred_element_type=F32)
        entries = entries.reshape(tok_rows, 2, 2 * width)
        mixed = jnp.sum(entries[:, :, :width] * gate_weights[:, :, None], axis=1)
        token_grad = jnp.sum(entries[:, :, width:], axis=1)
        result = jnp.concatenate([mixed, token_grad], axis=1).astype(BF16)

    def outer(units, rows):
        grad = jnp.dot(units, rows, preferred_element_type=F32).astype(BF16)
        return grad.reshape(chips, unit_width, 2 * width)

    with jax.named_scope("new_slices"):
        result = jnp.broadcast_to(result[None], (chips, tok_rows, 2 * width))
        sent = jnp.concatenate([outer(pre_grad, routed_x), outer(hidden, routed_back), result], axis=1)
        got = exchange(sent, "chip")
        result = across(got[:, 2 * unit_width :], own_source, other_source)

        def place(grad):
            grad = grad.reshape(chips, unit_width, 2, width).transpose(0, 2, 1, 3)
            grad = grad.reshape(cut_count, unit_width, width)
            source = inverse // 2 * 2 + (inverse % 2 != core).astype(jnp.int32)
            grad = rows_at(grad, source)
            return jnp.transpose(grad, (1, 0, 2)).reshape(unit_width, cut_count * width)

        up_grad, down_grad = place(got[:, :unit_width]), place(got[:, unit_width : 2 * unit_width])
    return (result[:, :width], result[:, width:], up_grad, down_grad)


def solution(mesh):
    experts, cuts = mesh.devices.shape
    split = Mesh(mesh.devices.reshape(experts, cuts // 2, 2), ("expert", "chip", "core"))
    spread = P("expert", ("chip", "core"))
    return jax.shard_map(
        local,
        mesh=split,
        in_specs=(spread, P("expert", None), P("expert", None), spread, spread, P(), P(), spread),
        out_specs=(
            spread,
            spread,
            P(("expert", "chip", "core"), None),
            P(("expert", "chip", "core"), None),
        ),
        check_vma=False,
    )
```

time: 248 us -> 193 us (0.78)
  waiting for transfers between devices: 131 us -> 52.8 us
  blocking collectives: 32.3 us -> 41.5 us
  between operations: 4.87 us -> 11.6 us
  local copies, waits for them, and re-layouts: 17 us -> 22.6 us
  other arithmetic: 4.45 us -> 7.31 us
    all_to_all x9 -> x4, waiting for transfers between devices: 131 us -> 51.7 us  [exchange(): return lax.all_to_all(parts, axis, split_axis=0, concat_axis=0, tiled=True)]
    all_to_all x9 -> x4, starting transfers between devices: 50.3 us -> 28.5 us  [exchange(): return lax.all_to_all(parts, axis, split_axis=0, concat_axis=0, tiled=True)]
    ppermute x0 -> x6, starting transfers between devices: none -> 21.3 us  [swap(): return lax.ppermute(block, 'core', [(0, 1), (1, 0)])]
    all_to_all x1 -> x2, blocking collectives: 32.3 us -> 41.5 us  [exchange(): return lax.all_to_all(parts, axis, split_axis=0, concat_axis=0, tiled=True)]
    unnamed x21 -> x23, local copies, waits for them, and re-layouts: 0.13 us -> 5.21 us
    reshape x4 -> x1, local copies, waits for them, and re-layouts: 4.64 us -> 0.08 us  [local(): slot_pairs = new_slots.reshape(chips, 2)]
    broadcast_in_dim x4 -> x2, local copies, waits for them, and re-layouts: 4 us -> 0.79 us  [everywhere(): jnp.broadcast_to(block[None], (lax.axis_size(axis), *block.shape))]
    gather x4 -> x6, local copies, waits for them, and re-layouts: 4.91 us -> 6.89 us  [rows_at(): return jnp.take(blocks, places, axis=0, mode='clip')]
  transfers between devices with their start and end apart: 9 -> 10, of which waited for: 9 -> 4; matrix products, arithmetic and copies ran while one was open for 5% -> 13% of each run, Pallas kernels for 0% -> 0%
where the time goes in v2:
time: 193 us; the launch traced here: 192 us
  waiting for transfers between devices  52.8 us (27%)
  starting transfers between devices  49.7 us (26%)
  blocking collectives  41.5 us (22%)
  local copies, waits for them, and re-layouts  22.6 us (12%)
  between operations  11.6 us (6%)
  other arithmetic  7.31 us (4%)
  matrix products  6.33 us (3%)
    all_to_all x4, waiting for transfers between devices, exchange(): return lax.all_to_all(parts, axis, split_axis=0, concat_axis=0, tiled=True)  51.7 us
    all_to_all x2, blocking collectives, exchange(): return lax.all_to_all(parts, axis, split_axis=0, concat_axis=0, tiled=True)  41.5 us
    all_to_all x4, starting transfers between devices, exchange(): return lax.all_to_all(parts, axis, split_axis=0, concat_axis=0, tiled=True)  28.5 us
    ppermute x6, starting transfers between devices, swap(): return lax.ppermute(block, 'core', [(0, 1), (1, 0)])  21.3 us
    gather x6, local copies, waits for them, and re-layouts, rows_at(): return jnp.take(blocks, places, axis=0, mode='clip')  6.89 us
    unnamed x23, local copies, waits for them, and re-layouts  5.21 us
  transfers between devices with their start and end apart: 10, of which 4 were waited for; matrix products, arithmetic and copies ran while one was open for 13% of the time, Pallas kernels for 0%

profile of v2, /device:TPU:1, one launch (start us, length us, event | category | flops | bytes accessed | tf_op | source)
XLA Modules:
  0.0 191.9 jit_solution(16487280043292352197)
XLA Ops:
  0.7 0.9 pad_maximum_fusion.12
  1.6 0.7 broadcast_in_dim.49
  2.3 7.5 %all-to-all-start = ((bf16[8,32,512]{2,1,0:T(8,128)(2,1)}), bf16[8,32,512]{2,1,0:T(8,128)(2,1)S(1)}, u32[]{:S(2)}, u32[]{:S(2)}) async-start(bf16[8,32,512]{2,1,0:T(8,128)(2,1)} %broadcast_in_dim.49), calls=%async_computation | async-start | bytes 524288 | tf_op jit(solution)/shard_map/token_blocks/all_to_all | solution.py:10
  9.8 0.7 select_reduce_fusion.2
  10.5 1.4 fusion.32
  14.5 0.8 copy.59
  15.2 0.1 eq.78
  15.4 0.1 reduce_window_sum.11
  15.5 0.2 select_reduce_fusion.1
  15.7 0.1 reduce_sum.60
  15.9 0.7 multiply_add_fusion
  16.6 0.1 fusion.14
  16.7 0.8 select_reduce_fusion
  17.5 5.7 %collective-permute-start.1 = (bf16[32,512]{1,0:T(8,128)(2,1)S(1)}, bf16[32,512]{1,0:T(8,128)(2,1)S(1)}, u32[]{:S(2)}, u32[]{:S(2)}) collective-permute-start(bf16[32,512]{1,0:T(8,128)(2,1)S(1)} %dynamic-slice_bitcast_fusion.1), channel_id=1, source_target_pairs={{0,1},{1,0},{2,3},{3,2},{4,5},{5,4},{6,7},{7,6},{8,9},{9,8},{10,11... | collective-permute-start | bytes 98312 | tf_op jit(solution)/shard_map/token_blocks/ppermute | solution.py:18
  25.8 0.2 fusion.1
  26.0 0.7 broadcast_in_dim.82
  26.7 13.5 %all-to-all-start.1 = ((bf16[32,8,512]{2,1,0:T(8,128)(2,1)}), bf16[32,8,512]{2,1,0:T(8,128)(2,1)S(1)}, u32[]{:S(2)}, u32[]{:S(2)}) async-start(bf16[32,8,512]{2,1,0:T(8,128)(2,1)} %bitcast.8), calls=%async_computation.1 | async-start | bytes 524288 | tf_op jit(solution)/shard_map/dispatch/all_to_all | solution.py:10
  40.4 0.2 dynamic-slice_reduce_fusion
  40.6 1.4 gather_fusion.1
  42.0 2.2 %collective-permute-start = (bf16[8,128,256]{2,1,0:T(8,128)(2,1)}, bf16[8,128,256]{2,1,0:T(8,128)(2,1)}, u32[]{:S(2)}, u32[]{:S(2)}) collective-permute-start(bf16[8,128,256]{2,1,0:T(8,128)(2,1)} %gather_fusion.1), channel_id=1, source_target_pairs={{0,1},{1,0},{2,3},{3,2},{4,5},{5,4},{6,7},{7,6},{8,9},{9,8},{10,11... | collective-permute-start | bytes 1572872 | tf_op jit(solution)/shard_map/weights/ppermute | solution.py:18
  44.2 1.4 gather_fusion.3
  45.5 2.1 %collective-permute-start.3 = (bf16[8,128,256]{2,1,0:T(8,128)(2,1)}, bf16[8,128,256]{2,1,0:T(8,128)(2,1)}, u32[]{:S(2)}, u32[]{:S(2)}) collective-permute-start(bf16[8,128,256]{2,1,0:T(8,128)(2,1)} %gather_fusion.3), channel_id=1, source_target_pairs={{0,1},{1,0},{2,3},{3,2},{4,5},{5,4},{6,7},{7,6},{8,9},{9,8},{10,11... | collective-permute-start | bytes 1572872 | tf_op jit(solution)/shard_map/weights/ppermute | solution.py:18
  47.7 0.6 gather_fusion
  48.3 1.4 gather_fusion.2
  49.7 1.1 constant_dynamic-update-slice_fusion.3
  50.8 1.1 constant_dynamic-update-slice_fusion
  51.9 9.2 %all-to-all-done.1 = bf16[32,8,512]{2,1,0:T(8,128)(2,1)S(1)} async-done(((bf16[32,8,512]{2,1,0:T(8,128)(2,1)}), bf16[32,8,512]{2,1,0:T(8,128)(2,1)S(1)}, u32[]{:S(2)}, u32[]{:S(2)}) %all-to-all-start.1) | async-done | bytes 262176 | tf_op jit(solution)/shard_map/dispatch/all_to_all | solution.py:10
  61.1 4.3 %collective-permute-start.2 = (bf16[256,512]{1,0:T(8,128)(2,1)S(1)}, bf16[256,512]{1,0:T(8,128)(2,1)S(1)}, u32[]{:S(2)}, u32[]{:S(2)}) collective-permute-start(bf16[256,512]{1,0:T(8,128)(2,1)S(1)} %bitcast.82), channel_id=1, source_target_pairs={{0,1},{1,0},{2,3},{3,2},{4,5},{5,4},{6,7},{7,6},{8,9},{9,8},{10,11... | collective-permute-start | bytes 786440 | tf_op jit(solution)/shard_map/dispatch/ppermute | solution.py:18
  65.4 1.1 constant_dynamic-update-slice_fusion.2
  66.5 0.5 convolution_convert_fusion.2
  67.0 0.5 convolution_convert_fusion.3
  67.6 23.2 %all_to_all.30 = bf16[8,256,256]{2,1,0:T(8,128)(2,1)S(1)} all-to-all(bf16[8,256,256]{2,1,0:T(8,128)(2,1)S(1)} %pad_maximum_fusion.1), channel_id=1, replica_groups=mesh['expert'=32,'chip'=8,'core'=2] {'chip'}, dimensions={0} | all-to-all | bytes 2097152 | tf_op jit(solution)/shard_map/hidden/all_to_all | solution.py:10
  90.8 0.1 convert_reduce_fusion
  91.0 0.1 copy.61
  91.2 18.3 %all_to_all.31 = bf16[8,256,256]{1,2,0:T(8,128)(2,1)S(1)} all-to-all(bf16[8,256,256]{1,2,0:T(8,128)(2,1)S(1)} %broadcast_in_dim.83), channel_id=1, replica_groups=mesh['expert'=32,'chip'=8,'core'=2] {'chip'}, dimensions={0} | all-to-all | bytes 2097152 | tf_op jit(solution)/shard_map/hidden/all_to_all | solution.py:10
  109.5 1.7 convolution_bitcast_fusion
  111.2 0.4 convolution_bitcast_fusion.1
  111.7 4.2 %collective-permute-start.4 = (bf16[256,512]{1,0:T(8,128)(2,1)S(1)}, bf16[256,512]{1,0:T(8,128)(2,1)S(1)}, u32[]{:S(2)}, u32[]{:S(2)}) collective-permute-start(bf16[256,512]{1,0:T(8,128)(2,1)S(1)} %pad_maximum_fusion.6), channel_id=1, source_target_pairs={{0,1},{1,0},{2,3},{3,2},{4,5},{5,4},{6,7},{7,6},{8,9},{9,8},{10,11... | collective-permute-start | bytes 786440 | tf_op jit(solution)/shard_map/give_back/ppermute | solution.py:18
  116.0 1.1 collective-permute-done.4
  117.0 0.8 fusion.3
  117.8 3.9 %all-to-all-start.4 = ((bf16[32,8,512]{2,1,0:T(8,128)(2,1)}), bf16[32,8,512]{2,1,0:T(8,128)(2,1)S(1)}, u32[]{:S(2)}, u32[]{:S(2)}) async-start(bf16[32,8,512]{2,1,0:T(8,128)(2,1)} %fusion.3), calls=%async_computation.4 | async-start | bytes 524288 | tf_op jit(solution)/shard_map/give_back/all_to_all | solution.py:10
  121.7 0.3 fusion.28
  122.0 0.2 copy.63
  122.2 1.0 copy.62
  123.2 1.4 convolution_convert_fusion
  124.6 1.5 convolution_convert_fusion.1
  126.1 16.5 %all-to-all-done.4 = bf16[32,8,512]{2,1,0:T(8,128)(2,1)S(1)} async-done(((bf16[32,8,512]{2,1,0:T(8,128)(2,1)}), bf16[32,8,512]{2,1,0:T(8,128)(2,1)S(1)}, u32[]{:S(2)}, u32[]{:S(2)}) %all-to-all-start.4) | async-done | bytes 262176 | tf_op jit(solution)/shard_map/give_back/all_to_all | solution.py:10
  142.6 0.2 fusion.4
  142.8 0.1 fusion.8
  142.9 1.7 pad_maximum_fusion
  144.6 3.6 %all-to-all-start.5 = ((bf16[8,288,512]{2,1,0:T(8,128)(2,1)}), bf16[8,288,512]{2,1,0:T(8,128)(2,1)S(1)}, u32[]{:S(2)}, u32[]{:S(2)}) async-start(bf16[8,288,512]{2,1,0:T(8,128)(2,1)} %pad_maximum_fusion), calls=%async_computation.5 | async-start | bytes 4718592 | tf_op jit(solution)/shard_map/new_slices/all_to_all | solution.py:10
  153.5 26.0 %all-to-all-done.5 = bf16[8,288,512]{2,1,0:T(8,128)(2,1)S(1)} async-done(((bf16[8,288,512]{2,1,0:T(8,128)(2,1)}), bf16[8,288,512]{2,1,0:T(8,128)(2,1)S(1)}, u32[]{:S(2)}, u32[]{:S(2)}) %all-to-all-start.5) | async-done | bytes 2359328 | tf_op jit(solution)/shard_map/new_slices/all_to_all | solution.py:10
  179.5 0.7 copy-done.6
  180.2 2.7 %collective-permute-start.5 = (bf16[32,512]{1,0:T(8,128)(2,1)S(1)}, bf16[32,512]{1,0:T(8,128)(2,1)S(1)}, u32[]{:S(2)}, u32[]{:S(2)}) collective-permute-start(bf16[32,512]{1,0:T(8,128)(2,1)S(1)} %dynamic-slice_bitcast_fusion), channel_id=1, source_target_pairs={{0,1},{1,0},{2,3},{3,2},{4,5},{5,4},{6,7},{7,6},{8,9},{9,8},{10,11... | collective-permute-start | bytes 98312 | tf_op jit(solution)/shard_map/new_slices/ppermute | solution.py:18
  183.0 0.3 fusion.27
  183.2 0.1 pad_maximum_fusion.2
  183.4 1.6 gather_fusion.4
  185.0 1.6 copy.64
  186.6 1.3 copy.66
  187.9 0.6 gather_fusion.5
  188.5 0.7 copy.65
  189.2 1.3 copy.67
  190.5 0.8 bitcast_select_fusion
  191.3 0.6 fusion.31
  (50 shorter events, 0.9 us)
Async XLA Ops:
  0.6 40.0 %copy-start = (bf16[2048,256]{1,0:T(8,128)(2,1)S(1)}, bf16[2048,256]{1,0:T(8,128)(2,1)}, u32[]{:S(2)}) copy-start(bf16[2048,256]{1,0:T(8,128)(2,1)} %param.11) | copy-start | bytes 3145732
  0.6 39.6 %copy-start.8 = (s32[16]{0:T(128)S(1)}, s32[16]{0:T(128)}, u32[]{:S(2)}) copy-start(s32[16]{0:T(128)} %param.14) | copy-start | bytes 196
  0.7 43.5 %copy-start.2 = (bf16[2048,256]{1,0:T(8,128)(2,1)S(1)}, bf16[2048,256]{1,0:T(8,128)(2,1)}, u32[]{:S(2)}) copy-start(bf16[2048,256]{1,0:T(8,128)(2,1)} %param.12) | copy-start | bytes 3145732
  2.3 15.2 %all-to-all-start = ((bf16[8,32,512]{2,1,0:T(8,128)(2,1)}), bf16[8,32,512]{2,1,0:T(8,128)(2,1)S(1)}, u32[]{:S(2)}, u32[]{:S(2)}) async-start(bf16[8,32,512]{2,1,0:T(8,128)(2,1)} %broadcast_in_dim.49), calls=%async_computation | async-start | bytes 524288 | tf_op jit(solution)/shard_map/token_blocks/all_to_all | solution.py:10
  17.5 8.3 %collective-permute-start.1 = (bf16[32,512]{1,0:T(8,128)(2,1)S(1)}, bf16[32,512]{1,0:T(8,128)(2,1)S(1)}, u32[]{:S(2)}, u32[]{:S(2)}) collective-permute-start(bf16[32,512]{1,0:T(8,128)(2,1)S(1)} %dynamic-slice_bitcast_fusion.1), channel_id=1, source_target_pairs={{0,1},{1,0},{2,3},{3,2},{4,5},{5,4},{6,7},{7,6},{8,9},{9,8},{10,11... | collective-permute-start | bytes 98312 | tf_op jit(solution)/shard_map/token_blocks/ppermute | solution.py:18
  26.7 34.3 %all-to-all-start.1 = ((bf16[32,8,512]{2,1,0:T(8,128)(2,1)}), bf16[32,8,512]{2,1,0:T(8,128)(2,1)S(1)}, u32[]{:S(2)}, u32[]{:S(2)}) async-start(bf16[32,8,512]{2,1,0:T(8,128)(2,1)} %bitcast.8), calls=%async_computation.1 | async-start | bytes 524288 | tf_op jit(solution)/shard_map/dispatch/all_to_all | solution.py:10
  42.0 8.8 %collective-permute-start = (bf16[8,128,256]{2,1,0:T(8,128)(2,1)}, bf16[8,128,256]{2,1,0:T(8,128)(2,1)}, u32[]{:S(2)}, u32[]{:S(2)}) collective-permute-start(bf16[8,128,256]{2,1,0:T(8,128)(2,1)} %gather_fusion.1), channel_id=1, source_target_pairs={{0,1},{1,0},{2,3},{3,2},{4,5},{5,4},{6,7},{7,6},{8,9},{9,8},{10,11... | collective-permute-start | bytes 1572872 | tf_op jit(solution)/shard_map/weights/ppermute | solution.py:18
  45.5 19.8 %collective-permute-start.3 = (bf16[8,128,256]{2,1,0:T(8,128)(2,1)}, bf16[8,128,256]{2,1,0:T(8,128)(2,1)}, u32[]{:S(2)}, u32[]{:S(2)}) collective-permute-start(bf16[8,128,256]{2,1,0:T(8,128)(2,1)} %gather_fusion.3), channel_id=1, source_target_pairs={{0,1},{1,0},{2,3},{3,2},{4,5},{5,4},{6,7},{7,6},{8,9},{9,8},{10,11... | collective-permute-start | bytes 1572872 | tf_op jit(solution)/shard_map/weights/ppermute | solution.py:18
  51.9 15.6 %copy-start.1 = (bf16[8,128,512]{2,1,0:T(8,128)(2,1)}, bf16[8,128,512]{2,1,0:T(8,128)(2,1)S(1)}, u32[]{:S(2)}) copy-start(bf16[8,128,512]{2,1,0:T(8,128)(2,1)S(1)} %constant_dynamic-update-slice_fusion) | copy-start | bytes 3145732
  61.1 5.4 %collective-permute-start.2 = (bf16[256,512]{1,0:T(8,128)(2,1)S(1)}, bf16[256,512]{1,0:T(8,128)(2,1)S(1)}, u32[]{:S(2)}, u32[]{:S(2)}) collective-permute-start(bf16[256,512]{1,0:T(8,128)(2,1)S(1)} %bitcast.82), channel_id=1, source_target_pairs={{0,1},{1,0},{2,3},{3,2},{4,5},{5,4},{6,7},{7,6},{8,9},{9,8},{10,11... | collective-permute-start | bytes 786440 | tf_op jit(solution)/shard_map/dispatch/ppermute | solution.py:18
  66.5 1.0 copy-start.3
  66.5 1.1 copy-start.4
  66.5 1.1 copy-start.5
  111.7 5.4 %collective-permute-start.4 = (bf16[256,512]{1,0:T(8,128)(2,1)S(1)}, bf16[256,512]{1,0:T(8,128)(2,1)S(1)}, u32[]{:S(2)}, u32[]{:S(2)}) collective-permute-start(bf16[256,512]{1,0:T(8,128)(2,1)S(1)} %pad_maximum_fusion.6), channel_id=1, source_target_pairs={{0,1},{1,0},{2,3},{3,2},{4,5},{5,4},{6,7},{7,6},{8,9},{9,8},{10,11... | collective-permute-start | bytes 786440 | tf_op jit(solution)/shard_map/give_back/ppermute | solution.py:18
  117.8 24.8 %all-to-all-start.4 = ((bf16[32,8,512]{2,1,0:T(8,128)(2,1)}), bf16[32,8,512]{2,1,0:T(8,128)(2,1)S(1)}, u32[]{:S(2)}, u32[]{:S(2)}) async-start(bf16[32,8,512]{2,1,0:T(8,128)(2,1)} %fusion.3), calls=%async_computation.4 | async-start | bytes 524288 | tf_op jit(solution)/shard_map/give_back/all_to_all | solution.py:10
  122.2 20.6 %copy-start.7 = (f32[32,2]{0,1:T(2,128)S(1)}, f32[32,2]{0,1:T(2,128)}, u32[]{:S(2)}) copy-start(f32[32,2]{0,1:T(2,128)} %param.10) | copy-start | bytes 772
  144.6 34.9 %all-to-all-start.5 = ((bf16[8,288,512]{2,1,0:T(8,128)(2,1)}), bf16[8,288,512]{2,1,0:T(8,128)(2,1)S(1)}, u32[]{:S(2)}, u32[]{:S(2)}) async-start(bf16[8,288,512]{2,1,0:T(8,128)(2,1)} %pad_maximum_fusion), calls=%async_computation.5 | async-start | bytes 4718592 | tf_op jit(solution)/shard_map/new_slices/all_to_all | solution.py:10
  179.5 0.7 copy-start.6
  180.2 10.3 %collective-permute-start.5 = (bf16[32,512]{1,0:T(8,128)(2,1)S(1)}, bf16[32,512]{1,0:T(8,128)(2,1)S(1)}, u32[]{:S(2)}, u32[]{:S(2)}) collective-permute-start(bf16[32,512]{1,0:T(8,128)(2,1)S(1)} %dynamic-slice_bitcast_fusion), channel_id=1, source_target_pairs={{0,1},{1,0},{2,3},{3,2},{4,5},{5,4},{6,7},{7,6},{8,9},{9,8},{10,11... | collective-permute-start | bytes 98312 | tf_op jit(solution)/shard_map/new_slices/ppermute | solution.py:18

commit v3 on v2

v3 whole, which is shorter than its diff:
```python
import jax
import jax.numpy as jnp
from jax import lax
from jax.experimental import pallas as pl
from jax.experimental.pallas import tpu as pltpu
from jax.sharding import Mesh, PartitionSpec as P

F32, BF16 = jnp.float32, jnp.bfloat16
CHIP = ("y", "x")
CUTS = ("y", "x", "core")
VMEM = pl.BlockSpec(memory_space=pltpu.VMEM)


def exchange(parts, axis):
    return lax.all_to_all(parts, axis, split_axis=0, concat_axis=0, tiled=True)


def everywhere(block, axis):
    count = lax.axis_size(axis)
    return exchange(jnp.broadcast_to(block[None], (count, *block.shape)), axis)


def swap(block):
    return lax.ppermute(block, "core", [(0, 1), (1, 0)])


def pick(blocks, index):
    return lax.dynamic_index_in_dim(blocks, index, axis=0, keepdims=False)


def rows_at(blocks, places):
    return jnp.take(blocks, places, axis=0, mode="clip")


def transposed_dot(left, right):
    return lax.dot_general(left, right, (((0,), (0,)), ((), ())), preferred_element_type=F32)


def place_kernel(capacity, ids_ref, gate_ref, token_ref, cotangent_ref, rows_ref, picker_ref):
    tok_rows, width = token_ref.shape
    slot_rows = rows_ref.shape[0]
    ids, gates = ids_ref[...], gate_ref[...]
    lane = lax.broadcasted_iota(jnp.int32, (tok_rows, 128), 1)
    hits = [(ids[:, k : k + 1] == lane).astype(F32) for k in range(2)]
    earlier = lax.broadcasted_iota(jnp.int32, (tok_rows, tok_rows), 0) > (
        lax.broadcasted_iota(jnp.int32, (tok_rows, tok_rows), 1)
    )
    before = jnp.dot(
        earlier.astype(BF16), (hits[0] + hits[1]).astype(BF16), preferred_element_type=F32
    )
    row = lax.broadcasted_iota(jnp.int32, (tok_rows, slot_rows), 1)
    within = row & (capacity - 1)
    row_slot = ((row & -(2 * capacity)) >> 1) + within
    pickers = []
    for k in range(2):
        rank = jnp.sum(before * hits[k], axis=1, keepdims=True).astype(jnp.int32)
        target = ids[:, k : k + 1] * capacity + rank
        pickers.append((target == row_slot).astype(BF16))
        picker_ref[k] = pickers[k]
    rows_ref[:, :width] = transposed_dot(pickers[0] + pickers[1], token_ref[...]).astype(BF16)
    back = jnp.zeros((slot_rows, width), F32)
    for k in range(2):
        scaled = gates[:, k : k + 1] * cotangent_ref[...].astype(F32)
        back = back + transposed_dot(pickers[k], scaled.astype(BF16))
    rows_ref[:, width:] = back.astype(BF16)


def combine_kernel(rows_ref, picker_ref, gate_ref, result_ref):
    width = rows_ref.shape[1] // 2
    gates = gate_ref[...]
    rows = rows_ref[...]
    entries = [jnp.dot(picker_ref[k], rows, preferred_element_type=F32) for k in range(2)]
    mixed = gates[:, 0:1] * entries[0][:, :width] + gates[:, 1:2] * entries[1][:, :width]
    token_grad = entries[0][:, width:] + entries[1][:, width:]
    for copy in range(result_ref.shape[0]):
        result_ref[copy, :, :width] = mixed.astype(BF16)
        result_ref[copy, :, width:] = token_grad.astype(BF16)


def local(tokens, expert_ids, gate_weights, old_up, old_down, old_rows, new_slots, cotangent):
    chips = lax.axis_size(CHIP)
    cut_count = 2 * chips
    group_count = lax.axis_size("expert")
    tok_rows, width = tokens.shape
    half_units = old_up.shape[0]
    unit_width = half_units // cut_count
    core_units = half_units // 2
    capacity = 8 * tok_rows // group_count
    slot_rows = group_count * capacity
    chip, core = lax.axis_index(CHIP), lax.axis_index("core")
    cut = 2 * chip + core
    own_source = jnp.sum(
        jnp.arange(cut_count, dtype=jnp.int32) * (old_rows == cut).astype(jnp.int32)
    )

    with jax.named_scope("dispatch"):
        rows, pickers = pl.pallas_call(
            lambda *refs: place_kernel(capacity, *refs),
            out_shape=(
                jax.ShapeDtypeStruct((slot_rows, 2 * width), BF16),
                jax.ShapeDtypeStruct((2, tok_rows, slot_rows), BF16),
            ),
            in_specs=[VMEM] * 4,
            out_specs=(VMEM, VMEM),
        )(expert_ids, gate_weights, tokens, cotangent)
        rows = exchange(rows.reshape(group_count, capacity, 2 * width), "expert")
        rows = rows.reshape(slot_rows, 2 * width)

    slot_pairs = new_slots.reshape(chips, 2)
    kept, given = slot_pairs[:, core], slot_pairs[:, 1 - core]

    def both_blocks(weights):
        blocks = weights.reshape(cut_count, unit_width, width)
        mine, theirs = rows_at(blocks, kept), swap(rows_at(blocks, given))
        return jnp.concatenate([mine, theirs], axis=2).reshape(core_units, 2 * width)

    with jax.named_scope("weights"):
        up, down = both_blocks(old_up), both_blocks(old_down)

    with jax.named_scope("all_rows"):
        all_rows = everywhere(rows, CHIP)
        needed = [pick(old_rows, cut), pick(old_rows, 2 * chip + 1 - core)]
        mine = [pick(all_rows, block // 2) for block in needed]
        theirs = swap(jnp.concatenate([mine[1], mine[0]], axis=1))
        chosen = [
            jnp.where(block % 2 == core, mine[j], theirs[:, 2 * width * j : 2 * width * (j + 1)])
            for j, block in enumerate(needed)
        ]
        routed_x = jnp.concatenate([rows[:, :width] for rows in chosen], axis=1)
        routed_back = jnp.concatenate([rows[:, width:] for rows in chosen], axis=1)

    def partial(weights, rows):
        part = lax.dot_general(
            weights, rows, (((1,), (1,)), ((), ())), preferred_element_type=F32
        ).astype(BF16)
        return part.reshape(chips, unit_width, slot_rows)

    with jax.named_scope("hidden"):
        parts = jnp.concatenate([partial(up, routed_x), partial(down, routed_back)], axis=1)
        sums = jnp.sum(exchange(parts, CHIP).astype(F32), axis=0)
        pre_act, hidden_grad = sums[:unit_width], sums[unit_width:]
        sig = jax.nn.sigmoid(pre_act)
        hidden = jax.nn.silu(pre_act).astype(BF16)
        pre_grad = (hidden_grad * sig * (1.0 + pre_act * (1.0 - sig))).astype(BF16)
        own_units = jnp.concatenate([hidden, pre_grad], axis=0)
        other_units = swap(own_units)
        units = everywhere(own_units, CHIP)
        hidden = units[:, :unit_width].reshape(core_units, slot_rows)
        pre_grad = units[:, unit_width:].reshape(core_units, slot_rows)

    with jax.named_scope("give_back"):
        out_part, in_part = transposed_dot(hidden, down), transposed_dot(pre_grad, up)
        theirs = swap(jnp.concatenate([out_part[:, width:], in_part[:, width:]], axis=1).astype(BF16))
        own = jnp.concatenate([out_part[:, :width], in_part[:, :width]], axis=1)
        half_rows = (own + theirs.astype(F32)).astype(BF16)
        half_rows = exchange(half_rows.reshape(group_count, capacity, 2 * width), "expert")
        result = pl.pallas_call(
            combine_kernel,
            out_shape=jax.ShapeDtypeStruct((cut_count, tok_rows, 2 * width), BF16),
            in_specs=[VMEM] * 3,
            out_specs=VMEM,
        )(half_rows.reshape(slot_rows, 2 * width), pickers, gate_weights)

    with jax.named_scope("result"):
        result = pick(exchange(result, CUTS), own_source)

    with jax.named_scope("new_slices"):

        def outer(own, other, rows):
            units = jnp.concatenate([own, other], axis=0)
            return jnp.einsum("ur,brd->bud", units, rows, preferred_element_type=F32).astype(BF16)

        up_part = outer(own_units[unit_width:], other_units[unit_width:], all_rows[:, :, :width])
        down_part = outer(own_units[:unit_width], other_units[:unit_width], all_rows[:, :, width:])
        theirs = swap(jnp.concatenate([up_part[:, unit_width:], down_part[:, unit_width:]], axis=1))

        def place(own, other):
            pair = jnp.where(
                core == 0,
                jnp.concatenate([own, other], axis=2),
                jnp.concatenate([other, own], axis=2),
            )
            return jnp.transpose(pair, (1, 0, 2)).reshape(unit_width, cut_count * width)

        up_grad = place(up_part[:, :unit_width], theirs[:, :unit_width])
        down_grad = place(down_part[:, :unit_width], theirs[:, unit_width:])
    return (result[:, :width], result[:, width:], up_grad, down_grad)


def solution(mesh):
    experts, cuts = mesh.devices.shape
    split = Mesh(mesh.devices.reshape(experts, 2, cuts // 4, 2), ("expert", "y", "x", "core"))
    spread = P("expert", CUTS)
    return jax.shard_map(
        local,
        mesh=split,
        in_specs=(spread, P("expert", None), P("expert", None), spread, spread, P(), P(), spread),
        out_specs=(
            spread,
            spread,
            P(("expert", *CUTS), None),
            P(("expert", *CUTS), None),
        ),
        check_vma=False,
    )
```

time: 193 us -> 202 us (1.047)
  blocking collectives: 41.5 us -> 56.9 us
  starting transfers between devices: 49.7 us -> 42.1 us
  local copies, waits for them, and re-layouts: 22.6 us -> 28.1 us
  Pallas kernels: 0 us -> 4.16 us
  between operations: 11.6 us -> 8.28 us
  waiting for transfers between devices: 52.8 us -> 49.5 us
    all_to_all x2, blocking collectives: 41.5 us -> 56.9 us  [exchange(): return lax.all_to_all(parts, axis, split_axis=0, concat_axis=0, tiled=True)]
    pallas_call x0 -> x2, Pallas kernels: none -> 4.16 us  [the longest x1 2.13 us: local(): pl.pallas_call(lambda *refs: place_kernel(capacity, *refs), out_shape=(ja...]
    ppermute x6, starting transfers between devices: 21.3 us -> 17.2 us  [swap(): return lax.ppermute(block, 'core', [(0, 1), (1, 0)])]
    unnamed x23 -> x32, local copies, waits for them, and re-layouts: 5.21 us -> 9.08 us
    all_to_all x4, starting transfers between devices: 28.5 us -> 24.9 us  [exchange(): return lax.all_to_all(parts, axis, split_axis=0, concat_axis=0, tiled=True)]
    transpose x2 -> x0, local copies, waits for them, and re-layouts: 2.28 us -> none  [place(): return jnp.transpose(grad, (1, 0, 2)).reshape(unit_width, cut_count * width)]
    all_to_all x4, waiting for transfers between devices: 51.7 us -> 49.5 us  [exchange(): return lax.all_to_all(parts, axis, split_axis=0, concat_axis=0, tiled=True)]
    gather x6 -> x4, local copies, waits for them, and re-layouts: 6.89 us -> 7.96 us  [rows_at(): return jnp.take(blocks, places, axis=0, mode='clip')]
  transfers between devices with their start and end apart: 10 -> 10, of which waited for: 4 -> 4; matrix products, arithmetic and copies ran while one was open for 13% -> 13% of each run, Pallas kernels for 0% -> 1%
where the time goes in v3:
time: 202 us; the launch traced here: 201 us
  blocking collectives  56.9 us (28%)
  waiting for transfers between devices  49.5 us (25%)
  starting transfers between devices  42.1 us (21%)
  local copies, waits for them, and re-layouts  28.1 us (14%)
  between operations  8.28 us (4%)
  matrix products  6.17 us (3%)
  other arithmetic  5.62 us (3%)
  Pallas kernels  4.16 us (2%)
    all_to_all x2, blocking collectives, exchange(): return lax.all_to_all(parts, axis, split_axis=0, concat_axis=0, tiled=True)  56.9 us
    all_to_all x4, waiting for transfers between devices, exchange(): return lax.all_to_all(parts, axis, split_axis=0, concat_axis=0, tiled=True)  49.5 us
    all_to_all x4, starting transfers between devices, exchange(): return lax.all_to_all(parts, axis, split_axis=0, concat_axis=0, tiled=True)  24.9 us
    ppermute x6, starting transfers between devices, swap(): return lax.ppermute(block, 'core', [(0, 1), (1, 0)])  17.2 us
    unnamed x32, local copies, waits for them, and re-layouts  9.08 us
    gather x4, local copies, waits for them, and re-layouts, rows_at(): return jnp.take(blocks, places, axis=0, mode='clip')  7.96 us
  transfers between devices with their start and end apart: 10, of which 4 were waited for; matrix products, arithmetic and copies ran while one was open for 13% of the time, Pallas kernels for 1%

profile of v3, /device:TPU:1, one launch (start us, length us, event | category | flops | bytes accessed | tf_op | source)
XLA Modules:
  0.0 200.7 jit_solution(7754600610292519940)
XLA Ops:
  0.6 0.0 copy-start
  0.6 1.5 copy.20.refs_1_.gate_ref
  2.1 1.4 copy.19.refs_0_
  3.5 2.1 %dispatch.1 = (bf16[256,512]{1,0:T(8,128)(2,1)}, bf16[2,32,256]{2,1,0:T(8,128)(2,1)}) custom-call(s32[32,2]{1,0:T(8,128)} %copy.19.refs_0_, f32[32,2]{1,0:T(8,128)} %copy.20.refs_1_.gate_ref, bf16[32,256]{1,0:T(8,128)(2,1)} %refs_2_.1, bf16[32,256]{1,0:T(8,128)(2,1)} %refs_3_.1), custom_call_target="tpu_custom_call" | custom-call | tf_op jit(solution)/shard_map/dispatch/pallas_call | solution.py:97
  5.6 37.0 %all_to_all.30 = bf16[32,8,512]{2,1,0:T(8,128)(2,1)S(1)} all-to-all(bf16[32,8,512]{2,1,0:T(8,128)(2,1)} %bitcast.55), channel_id=1, replica_groups=mesh['expert'=32,'y'=2,'x'=4,'core'=2] {'expert'}, dimensions={0} | all-to-all | bytes 524288 | tf_op jit(solution)/shard_map/dispatch/all_to_all | solution.py:15
  42.6 0.1 copy.21
  42.8 1.5 broadcast_in_dim.19
  44.2 6.5 %all-to-all-start.1 = ((bf16[8,256,512]{1,2,0:T(8,128)(2,1)}), bf16[8,256,512]{1,2,0:T(8,128)(2,1)S(1)}, u32[]{:S(2)}, u32[]{:S(2)}) async-start(bf16[8,256,512]{1,2,0:T(8,128)(2,1)} %broadcast_in_dim.19), calls=%async_computation.1 | async-start | bytes 4194304 | tf_op jit(solution)/shard_map/all_rows/all_to_all | solution.py:15
  50.7 0.1 reshape.50
  50.8 0.2 dynamic-slice_reduce_fusion
  51.1 2.6 %gather_fusion.1 = bf16[8,128,256]{2,1,0:T(8,128)(2,1)} fusion(bf16[16,128,256]{2,1,0:T(8,128)(2,1)} %bitcast.51, s32[1024]{0:T(1024)S(1)} %pad_clamp_fusion), kind=kCustom, calls=%fused_computation.1 | custom fusion | bytes 1048608 | tf_op jit(solution)/shard_map/weights/jit(_take)/gather | solution.py:32
  53.7 5.4 %collective-permute-start = (bf16[8,128,256]{2,1,0:T(8,128)(2,1)}, bf16[8,128,256]{2,1,0:T(8,128)(2,1)}, u32[]{:S(2)}, u32[]{:S(2)}) collective-permute-start(bf16[8,128,256]{2,1,0:T(8,128)(2,1)} %gather_fusion.1), channel_id=1, source_target_pairs={{0,1},{1,0},{2,3},{3,2},{4,5},{5,4},{6,7},{7,6},{8,9},{9,8},{10,11... | collective-permute-start | bytes 1572872 | tf_op jit(solution)/shard_map/weights/ppermute | solution.py:24
  59.0 1.4 gather_fusion.3
  60.4 1.9 collective-permute-start.2
  62.4 0.6 fusion.33
  68.2 11.1 %all-to-all-done.1 = bf16[8,256,512]{1,2,0:T(8,128)(2,1)S(1)} async-done(((bf16[8,256,512]{1,2,0:T(8,128)(2,1)}), bf16[8,256,512]{1,2,0:T(8,128)(2,1)S(1)}, u32[]{:S(2)}, u32[]{:S(2)}) %all-to-all-start.1) | async-done | bytes 2097184 | tf_op jit(solution)/shard_map/all_rows/all_to_all | solution.py:15
  79.3 0.7 copy-done.5
  80.0 0.8 pad_maximum_fusion.2
  80.8 2.8 %collective-permute-start.1 = (bf16[256,1024]{0,1:T(8,128)(2,1)}, bf16[256,1024]{0,1:T(8,128)(2,1)}, u32[]{:S(2)}, u32[]{:S(2)}) collective-permute-start(bf16[256,1024]{0,1:T(8,128)(2,1)} %pad_maximum_fusion.2), channel_id=1, source_target_pairs={{0,1},{1,0},{2,3},{3,2},{4,5},{5,4},{6,7},{7,6},{8,9},{9,8},{10,11... | collective-permute-start | bytes 1572872 | tf_op jit(solution)/shard_map/all_rows/ppermute | solution.py:24
  83.6 1.4 gather_fusion.2
  85.0 2.6 %gather_fusion = bf16[8,128,256]{2,1,0:T(8,128)(2,1)} fusion(bf16[16,128,256]{2,1,0:T(8,128)(2,1)} %bitcast.52, s32[1024]{0:T(1024)S(1)} %pad_clamp_fusion.1), kind=kCustom, calls=%fused_computation | custom fusion | bytes 1048608 | tf_op jit(solution)/shard_map/weights/jit(_take)/gather | solution.py:32
  87.6 1.1 constant_dynamic-update-slice_fusion.1
  88.7 1.1 constant_dynamic-update-slice_fusion.3
  89.8 1.1 constant_dynamic-update-slice_fusion
  90.9 0.0 copy-start.3
  90.9 1.5 constant_dynamic-update-slice_fusion.2
  92.4 1.5 slice_select_fusion.1
  93.9 0.4 convolution_convert_fusion.3
  94.4 0.4 convolution_convert_fusion.2
  94.8 0.1 pad_maximum_fusion
  94.9 19.9 %all_to_all.31 = bf16[8,256,256]{2,1,0:T(8,128)(2,1)S(1)} all-to-all(bf16[8,256,256]{2,1,0:T(8,128)(2,1)S(1)} %pad_maximum_fusion), channel_id=1, replica_groups=mesh['expert'=32,'y'=2,'x'=4,'core'=2] {'y','x'}, dimensions={0} | all-to-all | bytes 2097152 | tf_op jit(solution)/shard_map/hidden/all_to_all | solution.py:15
  114.8 0.1 convert_reduce_fusion
  114.9 0.1 fusion.17
  115.0 2.6 %collective-permute-start.4 = (bf16[256,256]{1,0:T(8,128)(2,1)S(1)}, bf16[256,256]{1,0:T(8,128)(2,1)}, u32[]{:S(2)}, u32[]{:S(2)}) collective-permute-start(bf16[256,256]{1,0:T(8,128)(2,1)S(1)} %pad_maximum_fusion.5), channel_id=1, source_target_pairs={{0,1},{1,0},{2,3},{3,2},{4,5},{5,4},{6,7},{7,6},{8,9},{9,8},{10,11... | collective-permute-start | bytes 393224 | tf_op jit(solution)/shard_map/hidden/ppermute | solution.py:24
  117.6 0.1 copy.22
  117.7 1.0 broadcast_in_dim.20
  118.8 4.2 %all-to-all-start.3 = ((bf16[8,256,256]{1,2,0:T(8,128)(2,1)}), bf16[8,256,256]{1,2,0:T(8,128)(2,1)}, u32[]{:S(2)}, u32[]{:S(2)}) async-start(bf16[8,256,256]{1,2,0:T(8,128)(2,1)} %broadcast_in_dim.20), calls=%async_computation.3 | async-start | bytes 2097152 | tf_op jit(solution)/shard_map/hidden/all_to_all | solution.py:15
  123.0 0.9 fusion.31
  123.9 0.5 fusion.1
  124.4 1.2 fusion.26
  125.6 1.5 fusion
  127.1 13.4 %all-to-all-done.3 = bf16[8,256,256]{1,2,0:T(8,128)(2,1)} async-done(((bf16[8,256,256]{1,2,0:T(8,128)(2,1)}), bf16[8,256,256]{1,2,0:T(8,128)(2,1)}, u32[]{:S(2)}, u32[]{:S(2)}) %all-to-all-start.3) | async-done | bytes 1048608 | tf_op jit(solution)/shard_map/hidden/all_to_all | solution.py:15
  140.5 1.8 convolution_bitcast_fusion.1
  142.4 1.6 convolution_bitcast_fusion
  144.0 2.6 %collective-permute-start.3 = (bf16[256,512]{1,0:T(8,128)(2,1)S(1)}, bf16[256,512]{1,0:T(8,128)(2,1)S(1)}, u32[]{:S(2)}, u32[]{:S(2)}) collective-permute-start(bf16[256,512]{1,0:T(8,128)(2,1)S(1)} %pad_maximum_fusion.3), channel_id=1, source_target_pairs={{0,1},{1,0},{2,3},{3,2},{4,5},{5,4},{6,7},{7,6},{8,9},{9,8},{10,11... | collective-permute-start | bytes 786440 | tf_op jit(solution)/shard_map/give_back/ppermute | solution.py:24
  146.6 0.3 fusion.28
  146.9 1.1 pad_maximum_fusion.1
  148.0 1.9 collective-permute-start.5
  150.0 0.8 fusion.7
  150.8 7.4 %all-to-all-start.4 = ((bf16[32,8,512]{2,1,0:T(8,128)(2,1)}), bf16[32,8,512]{2,1,0:T(8,128)(2,1)S(1)}, u32[]{:S(2)}, u32[]{:S(2)}) async-start(bf16[32,8,512]{2,1,0:T(8,128)(2,1)} %fusion.7), calls=%async_computation.4 | async-start | bytes 524288 | tf_op jit(solution)/shard_map/give_back/all_to_all | solution.py:15
  158.2 0.6 fusion.21
  160.7 17.6 %all-to-all-done.4 = bf16[32,8,512]{2,1,0:T(8,128)(2,1)S(1)} async-done(((bf16[32,8,512]{2,1,0:T(8,128)(2,1)}), bf16[32,8,512]{2,1,0:T(8,128)(2,1)S(1)}, u32[]{:S(2)}, u32[]{:S(2)}) %all-to-all-start.4) | async-done | bytes 262176 | tf_op jit(solution)/shard_map/give_back/all_to_all | solution.py:15
  178.3 0.7 copy-done.10
  179.0 2.0 %give_back.1 = bf16[16,32,512]{2,1,0:T(8,128)(2,1)} custom-call(bf16[256,512]{1,0:T(8,128)(2,1)} %bitcast.49, bf16[2,32,256]{2,1,0:T(8,128)(2,1)} %get-tuple-element.7.picker_ref, f32[32,2]{1,0:T(8,128)} %copy.20.refs_1_.gate_ref), custom_call_target="tpu_custom_call" | custom-call | tf_op jit(solution)/shard_map/give_back/pallas_call | solution.py:157
  181.0 6.7 %all-to-all-start.5 = ((bf16[16,32,512]{2,1,0:T(8,128)(2,1)}), bf16[16,32,512]{2,1,0:T(8,128)(2,1)}, u32[]{:S(2)}, u32[]{:S(2)}) async-start(bf16[16,32,512]{2,1,0:T(8,128)(2,1)} %give_back.1), calls=%async_computation.5 | async-start | bytes 1048576 | tf_op jit(solution)/shard_map/result/all_to_all | solution.py:15
  187.8 1.0 fusion.27
  188.7 0.3 maximum_select_fusion
  189.0 0.0 copy-start.8
  189.0 1.3 copy.24
  190.4 0.3 maximum_select_fusion.1
  190.6 1.3 copy.25
  192.0 7.4 %all-to-all-done.5 = bf16[16,32,512]{2,1,0:T(8,128)(2,1)} async-done(((bf16[16,32,512]{2,1,0:T(8,128)(2,1)}), bf16[16,32,512]{2,1,0:T(8,128)(2,1)}, u32[]{:S(2)}, u32[]{:S(2)}) %all-to-all-start.5) | async-done | bytes 524320 | tf_op jit(solution)/shard_map/result/all_to_all | solution.py:15
  199.4 0.8 dynamic-slice_bitcast_fusion.2
  200.1 0.6 fusion.32
  (37 shorter events, 0.2 us)
Async XLA Ops:
  0.6 58.4 %copy-start = (bf16[2048,256]{1,0:T(8,128)(2,1)S(1)}, bf16[2048,256]{1,0:T(8,128)(2,1)}, u32[]{:S(2)}) copy-start(bf16[2048,256]{1,0:T(8,128)(2,1)} %param.12) | copy-start | bytes 3145732
  44.2 6.5 %copy-start.12 = (s32[16]{0:T(128)S(1)}, s32[16]{0:T(128)}, u32[]{:S(2)}) copy-start(s32[16]{0:T(128)} %param.14) | copy-start | bytes 196
  44.2 35.0 %all-to-all-start.1 = ((bf16[8,256,512]{1,2,0:T(8,128)(2,1)}), bf16[8,256,512]{1,2,0:T(8,128)(2,1)S(1)}, u32[]{:S(2)}, u32[]{:S(2)}) async-start(bf16[8,256,512]{1,2,0:T(8,128)(2,1)} %broadcast_in_dim.19), calls=%async_computation.1 | async-start | bytes 4194304 | tf_op jit(solution)/shard_map/all_rows/all_to_all | solution.py:15
  50.7 11.6 %copy-start.11 = (s32[16]{0:T(128)S(1)}, s32[16]{0:T(128)}, u32[]{:S(2)}) copy-start(s32[16]{0:T(128)} %param.13) | copy-start | bytes 196
  53.7 36.2 %collective-permute-start = (bf16[8,128,256]{2,1,0:T(8,128)(2,1)}, bf16[8,128,256]{2,1,0:T(8,128)(2,1)}, u32[]{:S(2)}, u32[]{:S(2)}) collective-permute-start(bf16[8,128,256]{2,1,0:T(8,128)(2,1)} %gather_fusion.1), channel_id=1, source_target_pairs={{0,1},{1,0},{2,3},{3,2},{4,5},{5,4},{6,7},{7,6},{8,9},{9,8},{10,11... | collective-permute-start | bytes 1572872 | tf_op jit(solution)/shard_map/weights/ppermute | solution.py:24
  60.4 30.5 %collective-permute-start.2 = (bf16[8,128,256]{2,1,0:T(8,128)(2,1)}, bf16[8,128,256]{2,1,0:T(8,128)(2,1)}, u32[]{:S(2)}, u32[]{:S(2)}) collective-permute-start(bf16[8,128,256]{2,1,0:T(8,128)(2,1)} %gather_fusion.3), channel_id=1, source_target_pairs={{0,1},{1,0},{2,3},{3,2},{4,5},{5,4},{6,7},{7,6},{8,9},{9,8},{10,11... | collective-permute-start | bytes 1572872 | tf_op jit(solution)/shard_map/weights/ppermute | solution.py:24
  79.3 0.7 copy-start.5
  80.8 11.6 %collective-permute-start.1 = (bf16[256,1024]{0,1:T(8,128)(2,1)}, bf16[256,1024]{0,1:T(8,128)(2,1)}, u32[]{:S(2)}, u32[]{:S(2)}) collective-permute-start(bf16[256,1024]{0,1:T(8,128)(2,1)} %pad_maximum_fusion.2), channel_id=1, source_target_pairs={{0,1},{1,0},{2,3},{3,2},{4,5},{5,4},{6,7},{7,6},{8,9},{9,8},{10,11... | collective-permute-start | bytes 1572872 | tf_op jit(solution)/shard_map/all_rows/ppermute | solution.py:24
  87.6 4.8 %copy-start.6 = (bf16[256,512]{0,1:T(8,128)(2,1)S(1)}, bf16[256,512]{0,1:T(8,128)(2,1)}, u32[]{:S(2)}) copy-start(bf16[256,512]{0,1:T(8,128)(2,1)} %copy-done.5) | copy-start | bytes 786436
  90.9 3.5 %copy-start.3 = (bf16[8,128,512]{2,1,0:T(8,128)(2,1)}, bf16[8,128,512]{2,1,0:T(8,128)(2,1)S(1)}, u32[]{:S(2)}) copy-start(bf16[8,128,512]{2,1,0:T(8,128)(2,1)S(1)} %constant_dynamic-update-slice_fusion) | copy-start | bytes 3145732
  92.4 2.0 copy-start.2
  115.0 8.0 %collective-permute-start.4 = (bf16[256,256]{1,0:T(8,128)(2,1)S(1)}, bf16[256,256]{1,0:T(8,128)(2,1)}, u32[]{:S(2)}, u32[]{:S(2)}) collective-permute-start(bf16[256,256]{1,0:T(8,128)(2,1)S(1)} %pad_maximum_fusion.5), channel_id=1, source_target_pairs={{0,1},{1,0},{2,3},{3,2},{4,5},{5,4},{6,7},{7,6},{8,9},{9,8},{10,11... | collective-permute-start | bytes 393224 | tf_op jit(solution)/shard_map/hidden/ppermute | solution.py:24
  118.8 21.7 %all-to-all-start.3 = ((bf16[8,256,256]{1,2,0:T(8,128)(2,1)}), bf16[8,256,256]{1,2,0:T(8,128)(2,1)}, u32[]{:S(2)}, u32[]{:S(2)}) async-start(bf16[8,256,256]{1,2,0:T(8,128)(2,1)} %broadcast_in_dim.20), calls=%async_computation.3 | async-start | bytes 2097152 | tf_op jit(solution)/shard_map/hidden/all_to_all | solution.py:15
  127.1 15.3 %copy-start.4 = (bf16[8,128,512]{2,1,0:T(8,128)(2,1)S(1)}, bf16[8,128,512]{2,1,0:T(8,128)(2,1)}, u32[]{:S(2)}) copy-start(bf16[8,128,512]{2,1,0:T(8,128)(2,1)} %copy-done.3) | copy-start | bytes 3145732
  142.3 4.3 %copy-start.1 = (bf16[8,256,256]{1,2,0:T(8,128)(2,1)S(1)}, bf16[8,256,256]{1,2,0:T(8,128)(2,1)}, u32[]{:S(2)}) copy-start(bf16[8,256,256]{1,2,0:T(8,128)(2,1)} %fusion) | copy-start | bytes 3145732
  142.4 4.6 %copy-start.9 = (bf16[8,128,256]{1,2,0:T(8,128)(2,1)S(1)}, bf16[8,128,256]{1,2,0:T(8,128)(2,1)}, u32[]{:S(2)}) copy-start(bf16[8,128,256]{1,2,0:T(8,128)(2,1)} %get-tuple-element.21) | copy-start | bytes 1572868
  144.0 6.0 %collective-permute-start.3 = (bf16[256,512]{1,0:T(8,128)(2,1)S(1)}, bf16[256,512]{1,0:T(8,128)(2,1)S(1)}, u32[]{:S(2)}, u32[]{:S(2)}) collective-permute-start(bf16[256,512]{1,0:T(8,128)(2,1)S(1)} %pad_maximum_fusion.3), channel_id=1, source_target_pairs={{0,1},{1,0},{2,3},{3,2},{4,5},{5,4},{6,7},{7,6},{8,9},{9,8},{10,11... | collective-permute-start | bytes 786440 | tf_op jit(solution)/shard_map/give_back/ppermute | solution.py:24
  148.0 39.7 %collective-permute-start.5 = (bf16[8,256,256]{1,2,0:T(8,128)(2,1)}, bf16[8,256,256]{1,2,0:T(8,128)(2,1)S(1)}, u32[]{:S(2)}, u32[]{:S(2)}) collective-permute-start(bf16[8,256,256]{1,2,0:T(8,128)(2,1)} %pad_maximum_fusion.1), channel_id=1, source_target_pairs={{0,1},{1,0},{2,3},{3,2},{4,5},{5,4},{6,7},{7,6},{8,9},{9,8},{10,11... | collective-permute-start | bytes 3145736 | tf_op jit(solution)/shard_map/new_slices/ppermute | solution.py:24
  150.8 27.5 %all-to-all-start.4 = ((bf16[32,8,512]{2,1,0:T(8,128)(2,1)}), bf16[32,8,512]{2,1,0:T(8,128)(2,1)S(1)}, u32[]{:S(2)}, u32[]{:S(2)}) async-start(bf16[32,8,512]{2,1,0:T(8,128)(2,1)} %fusion.7), calls=%async_computation.4 | async-start | bytes 524288 | tf_op jit(solution)/shard_map/give_back/all_to_all | solution.py:15
  178.3 0.7 copy-start.10
  181.0 18.3 %all-to-all-start.5 = ((bf16[16,32,512]{2,1,0:T(8,128)(2,1)}), bf16[16,32,512]{2,1,0:T(8,128)(2,1)}, u32[]{:S(2)}, u32[]{:S(2)}) async-start(bf16[16,32,512]{2,1,0:T(8,128)(2,1)} %give_back.1), calls=%async_computation.5 | async-start | bytes 1048576 | tf_op jit(solution)/shard_map/result/all_to_all | solution.py:15
  188.7 1.6 copy-start.7
  189.0 1.3 copy-start.8

commit v4 on v3

--- a/solution.py
+++ b/solution.py
@@ -15,11 +15,6 @@
     return lax.all_to_all(parts, axis, split_axis=0, concat_axis=0, tiled=True)
 
 
-def everywhere(block, axis):
-    count = lax.axis_size(axis)
-    return exchange(jnp.broadcast_to(block[None], (count, *block.shape)), axis)
-
-
 def swap(block):
     return lax.ppermute(block, "core", [(0, 1), (1, 0)])
 
@@ -36,9 +31,17 @@
     return lax.dot_general(left, right, (((0,), (0,)), ((), ())), preferred_element_type=F32)
 
 
-def place_kernel(capacity, ids_ref, gate_ref, token_ref, cotangent_ref, rows_ref, picker_ref):
-    tok_rows, width = token_ref.shape
+def copies_kernel(token_ref, cotangent_ref, copies_ref):
+    width = token_ref.shape[1]
+    for copy in range(copies_ref.shape[0]):
+        copies_ref[copy, :, :width] = token_ref[...]
+        copies_ref[copy, :, width:] = cotangent_ref[...]
+
+
+def place_kernel(capacity, block_ref, ids_ref, gate_ref, blocks_ref, rows_ref, picker_ref):
+    tok_rows, width = blocks_ref.shape[1], blocks_ref.shape[2] // 2
     slot_rows = rows_ref.shape[0]
+    block = blocks_ref[block_ref[0]]
     ids, gates = ids_ref[...], gate_ref[...]
     lane = lax.broadcasted_iota(jnp.int32, (tok_rows, 128), 1)
     hits = [(ids[:, k : k + 1] == lane).astype(F32) for k in range(2)]
@@ -57,12 +60,26 @@
         target = ids[:, k : k + 1] * capacity + rank
         pickers.append((target == row_slot).astype(BF16))
         picker_ref[k] = pickers[k]
-    rows_ref[:, :width] = transposed_dot(pickers[0] + pickers[1], token_ref[...]).astype(BF16)
+    rows_ref[:, :width] = transposed_dot(pickers[0] + pickers[1], block[:, :width]).astype(BF16)
     back = jnp.zeros((slot_rows, width), F32)
     for k in range(2):
-        scaled = gates[:, k : k + 1] * cotangent_ref[...].astype(F32)
+        scaled = gates[:, k : k + 1] * block[:, width:].astype(F32)
         back = back + transposed_dot(pickers[k], scaled.astype(BF16))
     rows_ref[:, width:] = back.astype(BF16)
+
+
+def units_kernel(parts_ref, units_ref, copies_ref):
+    width = parts_ref.shape[1] // 2
+    sums = jnp.sum(parts_ref[...].astype(F32), axis=0)
+    pre_act, hidden_grad = sums[:width], sums[width:]
+    sig = jax.nn.sigmoid(pre_act)
+    hidden = (pre_act * sig).astype(BF16)
+    pre_grad = (hidden_grad * sig * (1.0 + pre_act * (1.0 - sig))).astype(BF16)
+    units_ref[:width] = hidden
+    units_ref[width:] = pre_grad
+    for copy in range(copies_ref.shape[0]):
+        copies_ref[copy, :width] = hidden
+        copies_ref[copy, width:] = pre_grad
 
 
 def combine_kernel(rows_ref, picker_ref, gate_ref, result_ref):
@@ -89,9 +106,19 @@
     slot_rows = group_count * capacity
     chip, core = lax.axis_index(CHIP), lax.axis_index("core")
     cut = 2 * chip + core
-    own_source = jnp.sum(
-        jnp.arange(cut_count, dtype=jnp.int32) * (old_rows == cut).astype(jnp.int32)
-    )
+    cut_list = jnp.arange(cut_count, dtype=jnp.int32)
+    inverse = jnp.sum(
+        cut_list[:, None] * (old_rows[:, None] == cut_list[None, :]).astype(jnp.int32), axis=0
+    )
+
+    with jax.named_scope("token_blocks"):
+        blocks = pl.pallas_call(
+            copies_kernel,
+            out_shape=jax.ShapeDtypeStruct((cut_count, tok_rows, 2 * width), BF16),
+            in_specs=[VMEM] * 2,
+            out_specs=VMEM,
+        )(tokens, cotangent)
+        blocks = exchange(blocks, CUTS)
 
     with jax.named_scope("dispatch"):
         rows, pickers = pl.pallas_call(
@@ -100,11 +127,17 @@
                 jax.ShapeDtypeStruct((slot_rows, 2 * width), BF16),
                 jax.ShapeDtypeStruct((2, tok_rows, slot_rows), BF16),
             ),
-            in_specs=[VMEM] * 4,
+            in_specs=[pl.BlockSpec(memory_space=pltpu.SMEM)] + [VMEM] * 3,
             out_specs=(VMEM, VMEM),
-        )(expert_ids, gate_weights, tokens, cotangent)
+        )(pick(old_rows, cut).reshape(1), expert_ids, gate_weights, blocks)
         rows = exchange(rows.reshape(group_count, capacity, 2 * width), "expert")
         rows = rows.reshape(slot_rows, 2 * width)
+        other = swap(rows)
+        routed_x = jnp.concatenate([rows[:, :width], other[:, :width]], axis=1)
+        routed_back = jnp.concatenate([rows[:, width:], other[:, width:]], axis=1)
+
+    with jax.named_scope("all_rows"):
+        all_rows = lax.all_gather(rows, CHIP)
 
     slot_pairs = new_slots.reshape(chips, 2)
     kept, given = slot_pairs[:, core], slot_pairs[:, 1 - core]
@@ -116,18 +149,6 @@
 
     with jax.named_scope("weights"):
         up, down = both_blocks(old_up), both_blocks(old_down)
-
-    with jax.named_scope("all_rows"):
-        all_rows = everywhere(rows, CHIP)
-        needed = [pick(old_rows, cut), pick(old_rows, 2 * chip + 1 - core)]
-        mine = [pick(all_rows, block // 2) for block in needed]
-        theirs = swap(jnp.concatenate([mine[1], mine[0]], axis=1))
-        chosen = [
-            jnp.where(block % 2 == core, mine[j], theirs[:, 2 * width * j : 2 * width * (j + 1)])
-            for j, block in enumerate(needed)
-        ]
-        routed_x = jnp.concatenate([rows[:, :width] for rows in chosen], axis=1)
-        routed_back = jnp.concatenate([rows[:, width:] for rows in chosen], axis=1)
 
     def partial(weights, rows):
         part = lax.dot_general(
@@ -137,22 +158,25 @@
 
     with jax.named_scope("hidden"):
         parts = jnp.concatenate([partial(up, routed_x), partial(down, routed_back)], axis=1)
-        sums = jnp.sum(exchange(parts, CHIP).astype(F32), axis=0)
-        pre_act, hidden_grad = sums[:unit_width], sums[unit_width:]
-        sig = jax.nn.sigmoid(pre_act)
-        hidden = jax.nn.silu(pre_act).astype(BF16)
-        pre_grad = (hidden_grad * sig * (1.0 + pre_act * (1.0 - sig))).astype(BF16)
-        own_units = jnp.concatenate([hidden, pre_grad], axis=0)
+        own_units, copies = pl.pallas_call(
+            units_kernel,
+            out_shape=(
+                jax.ShapeDtypeStruct((2 * unit_width, slot_rows), BF16),
+                jax.ShapeDtypeStruct((chips, 2 * unit_width, slot_rows), BF16),
+            ),
+            in_specs=[VMEM],
+            out_specs=(VMEM, VMEM),
+        )(exchange(parts, CHIP))
         other_units = swap(own_units)
-        units = everywhere(own_units, CHIP)
+        units = exchange(copies, CHIP)
         hidden = units[:, :unit_width].reshape(core_units, slot_rows)
         pre_grad = units[:, unit_width:].reshape(core_units, slot_rows)
 
     with jax.named_scope("give_back"):
-        out_part, in_part = transposed_dot(hidden, down), transposed_dot(pre_grad, up)
-        theirs = swap(jnp.concatenate([out_part[:, width:], in_part[:, width:]], axis=1).astype(BF16))
-        own = jnp.concatenate([out_part[:, :width], in_part[:, :width]], axis=1)
-        half_rows = (own + theirs.astype(F32)).astype(BF16)
+        theirs = [transposed_dot(hidden, down[:, width:]), transposed_dot(pre_grad, up[:, width:])]
+        theirs = swap(jnp.concatenate([part.astype(BF16) for part in theirs], axis=1))
+        own = [transposed_dot(hidden, down[:, :width]), transposed_dot(pre_grad, up[:, :width])]
+        half_rows = (jnp.concatenate(own, axis=1) + theirs.astype(F32)).astype(BF16)
         half_rows = exchange(half_rows.reshape(group_count, capacity, 2 * width), "expert")
         result = pl.pallas_call(
             combine_kernel,
@@ -162,7 +186,7 @@
         )(half_rows.reshape(slot_rows, 2 * width), pickers, gate_weights)
 
     with jax.named_scope("result"):
-        result = pick(exchange(result, CUTS), own_source)
+        result = pick(exchange(result, CUTS), pick(inverse, cut))
 
     with jax.named_scope("new_slices"):
 
@@ -174,13 +198,11 @@
         down_part = outer(own_units[:unit_width], other_units[:unit_width], all_rows[:, :, width:])
         theirs = swap(jnp.concatenate([up_part[:, unit_width:], down_part[:, unit_width:]], axis=1))
 
+        source = inverse // 2 + jnp.where(inverse % 2 == core, 0, chips)
+
         def place(own, other):
-            pair = jnp.where(
-                core == 0,
-                jnp.concatenate([own, other], axis=2),
-                jnp.concatenate([other, own], axis=2),
-            )
-            return jnp.transpose(pair, (1, 0, 2)).reshape(unit_width, cut_count * width)
+            grad = rows_at(jnp.concatenate([own, other], axis=0), source)
+            return jnp.transpose(grad, (1, 0, 2)).reshape(unit_width, cut_count * width)
 
         up_grad = place(up_part[:, :unit_width], theirs[:, :unit_width])
         down_grad = place(down_part[:, :unit_width], theirs[:, unit_width:])

time: 202 us -> 195 us (0.965)
  blocking collectives: 56.9 us -> 23.5 us
  starting transfers between devices: 42.1 us -> 56.8 us
  between operations: 8.28 us -> 16.4 us
  waiting for transfers between devices: 49.5 us -> 56 us
  local copies, waits for them, and re-layouts: 28.1 us -> 22.2 us
  Pallas kernels: 4.16 us -> 9.24 us
    all_to_all x2 -> x1, blocking collectives: 56.9 us -> 23.5 us  [exchange(): return lax.all_to_all(parts, axis, split_axis=0, concat_axis=0, tiled=True)]
    all_to_all x4 -> x5, starting transfers between devices: 24.9 us -> 37.1 us  [exchange(): return lax.all_to_all(parts, axis, split_axis=0, concat_axis=0, tiled=True)]
    pallas_call x0 -> x2, Pallas kernels: none -> 4.15 us  [the longest x1 2.43 us: local(): pl.pallas_call(units_kernel, out_shape=(jax.ShapeDtypeStruct((2 * unit_wi...]
    all_gather x0 -> x1, waiting for transfers between devices: none -> 3.71 us  [local(): all_rows = lax.all_gather(rows, CHIP)]
    gather x4 -> x6, local copies, waits for them, and re-layouts: 7.96 us -> 5.13 us  [rows_at(): return jnp.take(blocks, places, axis=0, mode='clip')]
    concatenate x3 -> x0, local copies, waits for them, and re-layouts: 2.64 us -> none  [the longest x2 2.54 us: both_blocks(): jnp.concatenate([mine, theirs], axis=2).reshape(core_units, 2 * width)]
    broadcast_in_dim x3 -> x0, local copies, waits for them, and re-layouts: 2.64 us -> none  [everywhere(): return exchange(jnp.broadcast_to(block[None], (count, *block.shape)), axis)]
    concatenate x3 -> x5, other arithmetic: 0.85 us -> 3.43 us  [the longest x2 3.22 us: both_blocks(): jnp.concatenate([mine, theirs], axis=2).reshape(core_units, 2 * width)]
  transfers between devices with their start and end apart: 10 -> 12, of which waited for: 4 -> 8; matrix products, arithmetic and copies ran while one was open for 13% -> 12% of each run, Pallas kernels for 1% -> 2%
where the time goes in v4:
time: 195 us; the launch traced here: 193 us
  starting transfers between devices  56.8 us (29%)
  waiting for transfers between devices  56 us (29%)
  blocking collectives  23.5 us (12%)
  local copies, waits for them, and re-layouts  22.2 us (11%)
  between operations  16.4 us (8%)
  Pallas kernels  9.24 us (5%)
  other arithmetic  4.71 us (2%)
  matrix products  4.57 us (2%)
    all_to_all x5, waiting for transfers between devices, exchange(): return lax.all_to_all(parts, axis, split_axis=0, concat_axis=0, tiled=True)  50.9 us
    all_to_all x5, starting transfers between devices, exchange(): return lax.all_to_all(parts, axis, split_axis=0, concat_axis=0, tiled=True)  37.1 us
    all_to_all x1, blocking collectives, exchange(): return lax.all_to_all(parts, axis, split_axis=0, concat_axis=0, tiled=True)  23.5 us
    ppermute x6, starting transfers between devices, swap(): return lax.ppermute(block, 'core', [(0, 1), (1, 0)])  19.7 us
    unnamed x32, local copies, waits for them, and re-layouts  8.11 us
    gather x6, local copies, waits for them, and re-layouts, rows_at(): return jnp.take(blocks, places, axis=0, mode='clip')  5.13 us
  transfers between devices with their start and end apart: 12, of which 8 were waited for; matrix products, arithmetic and copies ran while one was open for 12% of the time, Pallas kernels for 2%

profile of v4, /device:TPU:1, one launch (start us, length us, event | category | flops | bytes accessed | tf_op | source)
XLA Modules:
  0.0 193.4 jit_solution(14648446616649043352)
XLA Ops:
  7.2 1.7 token_blocks.1
  8.9 10.2 %all-to-all-start = ((bf16[16,32,512]{2,1,0:T(8,128)(2,1)}), bf16[16,32,512]{2,1,0:T(8,128)(2,1)S(1)}, u32[]{:S(2)}, u32[]{:S(2)}) async-start(bf16[16,32,512]{2,1,0:T(8,128)(2,1)} %token_blocks.1), calls=%async_computation | async-start | bytes 1048576 | tf_op jit(solution)/shard_map/token_blocks/all_to_all | solution.py:15
  19.2 1.4 copy.32.refs_1_
  20.5 1.4 copy.33.refs_2_.gate_ref
  21.9 1.2 dynamic_slice.19.refs_0_
  23.1 7.5 %all-to-all-done.refs_3_ = bf16[16,32,512]{2,1,0:T(8,128)(2,1)S(1)} async-done(((bf16[16,32,512]{2,1,0:T(8,128)(2,1)}), bf16[16,32,512]{2,1,0:T(8,128)(2,1)S(1)}, u32[]{:S(2)}, u32[]{:S(2)}) %all-to-all-start) | async-done | bytes 524320 | tf_op jit(solution)/shard_map/token_blocks/all_to_all | solution.py:15
  30.6 0.8 copy-done.2
  31.4 3.1 %dispatch.1 = (bf16[256,512]{1,0:T(8,128)(2,1)}, bf16[2,32,256]{2,1,0:T(8,128)(2,1)}) custom-call(s32[1]{0:T(128)} %dynamic_slice.19.refs_0_, s32[32,2]{1,0:T(8,128)} %copy.32.refs_1_, f32[32,2]{1,0:T(8,128)} %copy.33.refs_2_.gate_ref, bf16[16,32,512]{2,1,0:T(8,128)(2,1)} %copy-done.2), custom_call_target="tpu_custom_call" | custom-call | tf_op jit(solution)/shard_map/dispatch/pallas_call | solution.py:124
  34.5 13.6 %all-to-all-start.1 = ((bf16[32,8,512]{2,1,0:T(8,128)(2,1)}), bf16[32,8,512]{2,1,0:T(8,128)(2,1)S(1)}, u32[]{:S(2)}, u32[]{:S(2)}) async-start(bf16[32,8,512]{2,1,0:T(8,128)(2,1)} %bitcast.77), calls=%async_computation.1 | async-start | bytes 524288 | tf_op jit(solution)/shard_map/dispatch/all_to_all | solution.py:15
  48.2 0.2 dynamic-slice_reduce_fusion.1
  48.5 1.4 gather_fusion.3
  49.8 3.3 %collective-permute-start.2 = (bf16[8,128,256]{2,1,0:T(8,128)(2,1)}, bf16[8,128,256]{2,1,0:T(8,128)(2,1)}, u32[]{:S(2)}, u32[]{:S(2)}) collective-permute-start(bf16[8,128,256]{2,1,0:T(8,128)(2,1)} %gather_fusion.3), channel_id=1, source_target_pairs={{0,1},{1,0},{2,3},{3,2},{4,5},{5,4},{6,7},{7,6},{8,9},{9,8},{10,11... | collective-permute-start | bytes 1572872 | tf_op jit(solution)/shard_map/weights/ppermute | solution.py:19
  53.1 1.4 gather_fusion.1
  54.5 1.9 collective-permute-start
  56.4 0.6 gather_fusion.2
  57.0 0.6 gather_fusion
  57.6 1.1 pad_maximum_fusion.1
  58.8 8.4 %all-to-all-done.1 = bf16[32,8,512]{2,1,0:T(8,128)(2,1)S(1)} async-done(((bf16[32,8,512]{2,1,0:T(8,128)(2,1)}), bf16[32,8,512]{2,1,0:T(8,128)(2,1)S(1)}, u32[]{:S(2)}, u32[]{:S(2)}) %all-to-all-start.1) | async-done | bytes 262176 | tf_op jit(solution)/shard_map/dispatch/all_to_all | solution.py:15
  67.2 6.1 %collective-permute-start.1 = (bf16[256,512]{1,0:T(8,128)(2,1)S(1)}, bf16[256,512]{1,0:T(8,128)(2,1)}, u32[]{:S(2)}, u32[]{:S(2)}) collective-permute-start(bf16[256,512]{1,0:T(8,128)(2,1)S(1)} %bitcast.59), channel_id=1, source_target_pairs={{0,1},{1,0},{2,3},{3,2},{4,5},{5,4},{6,7},{7,6},{8,9},{9,8},{10,11... | collective-permute-start | bytes 786440 | tf_op jit(solution)/shard_map/dispatch/ppermute | solution.py:19
  73.3 2.1 %pad_maximum_fusion = bf16[8,128,512]{2,1,0:T(8,128)(2,1)} fusion(bf16[8,128,256]{2,1,0:T(8,128)(2,1)} %collective-permute-done, bf16[8,128,256]{2,1,0:T(8,128)(2,1)S(1)} %gather_fusion), kind=kLoop, calls=%fused_computation.16 | loop fusion | flops 2097152 | bytes 2097152 | tf_op jit(solution)/shard_map/weights/concatenate | solution.py:148
  75.5 1.1 fusion.31
  76.5 1.0 fusion.32
  77.5 0.5 convolution_convert_fusion.2
  78.0 0.5 convolution_convert_fusion.3
  78.6 23.5 %all_to_all.30.parts_ref = bf16[8,256,256]{2,1,0:T(8,128)(2,1)} all-to-all(bf16[8,256,256]{2,1,0:T(8,128)(2,1)S(1)} %pad_maximum_fusion.2), channel_id=1, replica_groups=mesh['expert'=32,'y'=2,'x'=4,'core'=2] {'y','x'}, dimensions={0} | all-to-all | bytes 2097152 | tf_op jit(solution)/shard_map/hidden/all_to_all | solution.py:15
  102.1 2.4 %hidden.1 = (bf16[256,256]{1,0:T(8,128)(2,1)}, bf16[8,256,256]{2,1,0:T(8,128)(2,1)}) custom-call(bf16[8,256,256]{2,1,0:T(8,128)(2,1)} %all_to_all.30.parts_ref), custom_call_target="tpu_custom_call" | custom-call | tf_op jit(solution)/shard_map/hidden/pallas_call | solution.py:161
  104.5 3.7 %all-to-all-start.3 = ((bf16[8,256,256]{2,1,0:T(8,128)(2,1)}), bf16[8,256,256]{2,1,0:T(8,128)(2,1)S(1)}, u32[]{:S(2)}, u32[]{:S(2)}) async-start(bf16[8,256,256]{2,1,0:T(8,128)(2,1)} %get-tuple-element.9), calls=%async_computation.3 | async-start | bytes 2097152 | tf_op jit(solution)/shard_map/hidden/all_to_all | solution.py:15
  108.2 2.4 %collective-permute-start.4 = (bf16[256,256]{1,0:T(8,128)(2,1)S(1)}, bf16[256,256]{1,0:T(8,128)(2,1)S(1)}, u32[]{:S(2)}, u32[]{:S(2)}) collective-permute-start(bf16[256,256]{1,0:T(8,128)(2,1)S(1)} %copy-done.11), channel_id=1, source_target_pairs={{0,1},{1,0},{2,3},{3,2},{4,5},{5,4},{6,7},{7,6},{8,9},{9,8},{10,11... | collective-permute-start | bytes 393224 | tf_op jit(solution)/shard_map/hidden/ppermute | solution.py:19
  110.6 0.9 collective-permute-done.4
  111.6 16.7 %all-to-all-done.3 = bf16[8,256,256]{2,1,0:T(8,128)(2,1)S(1)} async-done(((bf16[8,256,256]{2,1,0:T(8,128)(2,1)}), bf16[8,256,256]{2,1,0:T(8,128)(2,1)S(1)}, u32[]{:S(2)}, u32[]{:S(2)}) %all-to-all-start.3) | async-done | bytes 1048608 | tf_op jit(solution)/shard_map/hidden/all_to_all | solution.py:15
  128.3 0.1 fusion.30
  128.4 1.1 copy-done.8
  129.5 0.4 convolution_convert_fusion.4
  129.9 0.4 convolution_convert_fusion.5
  130.3 2.7 %collective-permute-start.3 = (bf16[256,512]{0,1:T(8,128)(2,1)S(1)}, bf16[256,512]{0,1:T(8,128)(2,1)S(1)}, u32[]{:S(2)}, u32[]{:S(2)}) collective-permute-start(bf16[256,512]{0,1:T(8,128)(2,1)S(1)} %pad_maximum_fusion.6), channel_id=1, source_target_pairs={{0,1},{1,0},{2,3},{3,2},{4,5},{5,4},{6,7},{7,6},{8,9},{9,8},{10,11... | collective-permute-start | bytes 786440 | tf_op jit(solution)/shard_map/give_back/ppermute | solution.py:19
  133.0 0.3 fusion.6
  133.3 0.3 fusion.8
  133.7 0.4 collective-permute-done.3
  134.2 0.8 copy.34
  135.0 3.9 %all-to-all-start.4 = ((bf16[32,8,512]{2,1,0:T(8,128)(2,1)}), bf16[32,8,512]{2,1,0:T(8,128)(2,1)S(1)}, u32[]{:S(2)}, u32[]{:S(2)}) async-start(bf16[32,8,512]{2,1,0:T(8,128)(2,1)} %bitcast.10), calls=%async_computation.4 | async-start | bytes 524288 | tf_op jit(solution)/shard_map/give_back/all_to_all | solution.py:15
  138.9 3.7 %all-gather.2.cloned.1.call-done = bf16[8,256,512]{2,1,0:T(8,128)(2,1)} async-done(((bf16[1,256,512]{2,1,0:T(8,128)(2,1)}), bf16[8,256,512]{2,1,0:T(8,128)(2,1)}) %all-gather.2.cloned.1.call-update) | async-done | bytes 2097168 | tf_op jit(solution)/shard_map/all_rows/all_gather | solution.py:140
  142.6 1.8 fusion.1
  144.4 0.1 copy-done.3
  144.5 0.4 fusion
  145.0 1.0 fusion.27
  146.0 1.0 pad_maximum_fusion.3
  147.0 3.3 %collective-permute-start.5 = (bf16[8,256,256]{2,1,0:T(8,128)(2,1)}, bf16[8,256,256]{2,1,0:T(8,128)(2,1)S(1)}, u32[]{:S(2)}, u32[]{:S(2)}) collective-permute-start(bf16[8,256,256]{2,1,0:T(8,128)(2,1)} %pad_maximum_fusion.3), channel_id=1, source_target_pairs={{0,1},{1,0},{2,3},{3,2},{4,5},{5,4},{6,7},{7,6},{8,9},{9,8},{10,11... | collective-permute-start | bytes 3145736 | tf_op jit(solution)/shard_map/new_slices/ppermute | solution.py:19
  150.3 9.5 %all-to-all-done.4 = bf16[32,8,512]{2,1,0:T(8,128)(2,1)S(1)} async-done(((bf16[32,8,512]{2,1,0:T(8,128)(2,1)}), bf16[32,8,512]{2,1,0:T(8,128)(2,1)S(1)}, u32[]{:S(2)}, u32[]{:S(2)}) %all-to-all-start.4) | async-done | bytes 262176 | tf_op jit(solution)/shard_map/give_back/all_to_all | solution.py:15
  159.8 0.7 copy-done.6
  160.5 2.0 %give_back.1 = bf16[16,32,512]{2,1,0:T(8,128)(2,1)} custom-call(bf16[256,512]{1,0:T(8,128)(2,1)} %bitcast.62, bf16[2,32,256]{2,1,0:T(8,128)(2,1)} %get-tuple-element.10.picker_ref, f32[32,2]{1,0:T(8,128)} %copy.33.refs_2_.gate_ref), custom_call_target="tpu_custom_call" | custom-call | tf_op jit(solution)/shard_map/give_back/pallas_call | solution.py:181
  162.5 5.7 %all-to-all-start.5 = ((bf16[16,32,512]{2,1,0:T(8,128)(2,1)}), bf16[16,32,512]{2,1,0:T(8,128)(2,1)S(1)}, u32[]{:S(2)}, u32[]{:S(2)}) async-start(bf16[16,32,512]{2,1,0:T(8,128)(2,1)} %give_back.1), calls=%async_computation.5 | async-start | bytes 1048576 | tf_op jit(solution)/shard_map/result/all_to_all | solution.py:15
  168.3 0.1 select_reduce_fusion
  168.4 0.6 dynamic_slice.20
  170.9 8.7 %all-to-all-done.5 = bf16[16,32,512]{2,1,0:T(8,128)(2,1)S(1)} async-done(((bf16[16,32,512]{2,1,0:T(8,128)(2,1)}), bf16[16,32,512]{2,1,0:T(8,128)(2,1)S(1)}, u32[]{:S(2)}, u32[]{:S(2)}) %all-to-all-start.5) | async-done | bytes 524320 | tf_op jit(solution)/shard_map/result/all_to_all | solution.py:15
  179.7 0.6 fusion.35
  180.3 0.9 fusion.28
  181.2 0.1 pad_maximum_fusion.4
  181.2 0.6 gather_fusion.4
  181.9 0.7 copy.36
  182.6 1.3 copy.38
  183.9 0.1 pad_maximum_fusion.5
  184.0 0.6 gather_fusion.5
  184.6 0.7 copy.37
  185.3 1.3 copy.39
  (41 shorter events, 0.4 us)
Async XLA Ops:
  7.2 41.3 %copy-start = (bf16[2048,256]{1,0:T(8,128)(2,1)S(1)}, bf16[2048,256]{1,0:T(8,128)(2,1)}, u32[]{:S(2)}) copy-start(bf16[2048,256]{1,0:T(8,128)(2,1)} %param.12) | copy-start | bytes 3145732
  7.2 41.0 %copy-start.12 = (s32[16]{0:T(128)S(1)}, s32[16]{0:T(128)}, u32[]{:S(2)}) copy-start(s32[16]{0:T(128)} %param.14) | copy-start | bytes 196
  7.2 45.9 %copy-start.9 = (bf16[2048,256]{1,0:T(8,128)(2,1)S(1)}, bf16[2048,256]{1,0:T(8,128)(2,1)}, u32[]{:S(2)}) copy-start(bf16[2048,256]{1,0:T(8,128)(2,1)} %param.11) | copy-start | bytes 3145732
  8.9 21.7 %all-to-all-start = ((bf16[16,32,512]{2,1,0:T(8,128)(2,1)}), bf16[16,32,512]{2,1,0:T(8,128)(2,1)S(1)}, u32[]{:S(2)}, u32[]{:S(2)}) async-start(bf16[16,32,512]{2,1,0:T(8,128)(2,1)} %token_blocks.1), calls=%async_computation | async-start | bytes 1048576 | tf_op jit(solution)/shard_map/token_blocks/all_to_all | solution.py:15
  30.6 0.8 copy-start.2
  34.5 22.5 %copy-start.10 = (bf16[2048,256]{1,0:T(8,128)(2,1)S(1)}, bf16[2048,256]{1,0:T(8,128)(2,1)}, u32[]{:S(2)}) copy-start(bf16[2048,256]{1,0:T(8,128)(2,1)} %param.11) | copy-start | bytes 3145732
  34.5 32.7 %all-to-all-start.1 = ((bf16[32,8,512]{2,1,0:T(8,128)(2,1)}), bf16[32,8,512]{2,1,0:T(8,128)(2,1)S(1)}, u32[]{:S(2)}, u32[]{:S(2)}) async-start(bf16[32,8,512]{2,1,0:T(8,128)(2,1)} %bitcast.77), calls=%async_computation.1 | async-start | bytes 524288 | tf_op jit(solution)/shard_map/dispatch/all_to_all | solution.py:15
  48.1 94.5 %all-gather.2.cloned.1.call-start = ((), (), s32[]{:S(2)}) async-start(), calls=%async_computation.6 | async-start | bytes 2359296 | tf_op jit(solution)/shard_map/all_rows/all_gather | solution.py:140
  49.8 7.8 %collective-permute-start.2 = (bf16[8,128,256]{2,1,0:T(8,128)(2,1)}, bf16[8,128,256]{2,1,0:T(8,128)(2,1)}, u32[]{:S(2)}, u32[]{:S(2)}) collective-permute-start(bf16[8,128,256]{2,1,0:T(8,128)(2,1)} %gather_fusion.3), channel_id=1, source_target_pairs={{0,1},{1,0},{2,3},{3,2},{4,5},{5,4},{6,7},{7,6},{8,9},{9,8},{10,11... | collective-permute-start | bytes 1572872 | tf_op jit(solution)/shard_map/weights/ppermute | solution.py:19
  54.5 18.8 %collective-permute-start = (bf16[8,128,256]{2,1,0:T(8,128)(2,1)}, bf16[8,128,256]{2,1,0:T(8,128)(2,1)}, u32[]{:S(2)}, u32[]{:S(2)}) collective-permute-start(bf16[8,128,256]{2,1,0:T(8,128)(2,1)} %gather_fusion.1), channel_id=1, source_target_pairs={{0,1},{1,0},{2,3},{3,2},{4,5},{5,4},{6,7},{7,6},{8,9},{9,8},{10,11... | collective-permute-start | bytes 1572872 | tf_op jit(solution)/shard_map/weights/ppermute | solution.py:19
  67.2 8.2 %copy-start.1 = (bf16[32,8,512]{2,1,0:T(8,128)(2,1)}, bf16[32,8,512]{2,1,0:T(8,128)(2,1)S(1)}, u32[]{:S(2)}) copy-start(bf16[32,8,512]{2,1,0:T(8,128)(2,1)S(1)} %all-to-all-done.1) | copy-start | bytes 786436
  67.2 9.3 %collective-permute-start.1 = (bf16[256,512]{1,0:T(8,128)(2,1)S(1)}, bf16[256,512]{1,0:T(8,128)(2,1)}, u32[]{:S(2)}, u32[]{:S(2)}) collective-permute-start(bf16[256,512]{1,0:T(8,128)(2,1)S(1)} %bitcast.59), channel_id=1, source_target_pairs={{0,1},{1,0},{2,3},{3,2},{4,5},{5,4},{6,7},{7,6},{8,9},{9,8},{10,11... | collective-permute-start | bytes 786440 | tf_op jit(solution)/shard_map/dispatch/ppermute | solution.py:19
  75.4 2.6 %copy-start.7 = (bf16[8,128,512]{2,1,0:T(8,128)(2,1)S(1)}, bf16[8,128,512]{2,1,0:T(8,128)(2,1)}, u32[]{:S(2)}) copy-start(bf16[8,128,512]{2,1,0:T(8,128)(2,1)} %pad_maximum_fusion) | copy-start | bytes 3145732
  104.5 3.7 %copy-start.11 = (bf16[256,256]{1,0:T(8,128)(2,1)S(1)}, bf16[256,256]{1,0:T(8,128)(2,1)}, u32[]{:S(2)}) copy-start(bf16[256,256]{1,0:T(8,128)(2,1)} %get-tuple-element.11) | copy-start | bytes 393220
  104.5 23.8 %all-to-all-start.3 = ((bf16[8,256,256]{2,1,0:T(8,128)(2,1)}), bf16[8,256,256]{2,1,0:T(8,128)(2,1)S(1)}, u32[]{:S(2)}, u32[]{:S(2)}) async-start(bf16[8,256,256]{2,1,0:T(8,128)(2,1)} %get-tuple-element.9), calls=%async_computation.3 | async-start | bytes 2097152 | tf_op jit(solution)/shard_map/hidden/all_to_all | solution.py:15
  108.2 3.4 %collective-permute-start.4 = (bf16[256,256]{1,0:T(8,128)(2,1)S(1)}, bf16[256,256]{1,0:T(8,128)(2,1)S(1)}, u32[]{:S(2)}, u32[]{:S(2)}) collective-permute-start(bf16[256,256]{1,0:T(8,128)(2,1)S(1)} %copy-done.11), channel_id=1, source_target_pairs={{0,1},{1,0},{2,3},{3,2},{4,5},{5,4},{6,7},{7,6},{8,9},{9,8},{10,11... | collective-permute-start | bytes 393224 | tf_op jit(solution)/shard_map/hidden/ppermute | solution.py:19
  128.3 1.2 copy-start.8
  130.3 3.8 %collective-permute-start.3 = (bf16[256,512]{0,1:T(8,128)(2,1)S(1)}, bf16[256,512]{0,1:T(8,128)(2,1)S(1)}, u32[]{:S(2)}, u32[]{:S(2)}) collective-permute-start(bf16[256,512]{0,1:T(8,128)(2,1)S(1)} %pad_maximum_fusion.6), channel_id=1, source_target_pairs={{0,1},{1,0},{2,3},{3,2},{4,5},{5,4},{6,7},{7,6},{8,9},{9,8},{10,11... | collective-permute-start | bytes 786440 | tf_op jit(solution)/shard_map/give_back/ppermute | solution.py:19
  135.0 24.8 %all-to-all-start.4 = ((bf16[32,8,512]{2,1,0:T(8,128)(2,1)}), bf16[32,8,512]{2,1,0:T(8,128)(2,1)S(1)}, u32[]{:S(2)}, u32[]{:S(2)}) async-start(bf16[32,8,512]{2,1,0:T(8,128)(2,1)} %bitcast.10), calls=%async_computation.4 | async-start | bytes 524288 | tf_op jit(solution)/shard_map/give_back/all_to_all | solution.py:15
  142.6 1.9 copy-start.3
  146.0 22.3 %copy-start.13 = (s32[16]{0:T(128)S(1)}, s32[16]{0:T(128)}, u32[]{:S(2)}) copy-start(s32[16]{0:T(128)} %param.13) | copy-start | bytes 196
  147.0 33.3 %collective-permute-start.5 = (bf16[8,256,256]{2,1,0:T(8,128)(2,1)}, bf16[8,256,256]{2,1,0:T(8,128)(2,1)S(1)}, u32[]{:S(2)}, u32[]{:S(2)}) collective-permute-start(bf16[8,256,256]{2,1,0:T(8,128)(2,1)} %pad_maximum_fusion.3), channel_id=1, source_target_pairs={{0,1},{1,0},{2,3},{3,2},{4,5},{5,4},{6,7},{7,6},{8,9},{9,8},{10,11... | collective-permute-start | bytes 3145736 | tf_op jit(solution)/shard_map/new_slices/ppermute | solution.py:19
  159.8 0.7 copy-start.6
  162.5 17.1 %all-to-all-start.5 = ((bf16[16,32,512]{2,1,0:T(8,128)(2,1)}), bf16[16,32,512]{2,1,0:T(8,128)(2,1)S(1)}, u32[]{:S(2)}, u32[]{:S(2)}) async-start(bf16[16,32,512]{2,1,0:T(8,128)(2,1)} %give_back.1), calls=%async_computation.5 | async-start | bytes 1048576 | tf_op jit(solution)/shard_map/result/all_to_all | solution.py:15
  182.5 1.3 copy-start.4
  182.6 1.3 copy-start.5
Sparse Core Ops, SparseCore 0:
  75.6 67.0 all-gather.1

commit v5 on v2

v5 whole, which is shorter than its diff:
```python
import jax
import jax.numpy as jnp
from jax import lax
from jax.experimental import pallas as pl
from jax.experimental.pallas import tpu as pltpu
from jax.sharding import Mesh, PartitionSpec as P

F32, BF16 = jnp.float32, jnp.bfloat16
CHIP = ("y", "x")
CUTS = ("y", "x", "core")
VMEM = pl.BlockSpec(memory_space=pltpu.VMEM)
ANY = pl.BlockSpec(memory_space=pl.ANY)
LARGE = pltpu.CompilerParams(vmem_limit_bytes=24 * 2**20)


def exchange(parts, axis):
    return lax.all_to_all(parts, axis, split_axis=0, concat_axis=0, tiled=True)


def everywhere(block, axis):
    return exchange(jnp.broadcast_to(block[None], (lax.axis_size(axis), *block.shape)), axis)


def swap(block):
    return lax.ppermute(block, "core", [(0, 1), (1, 0)])


def pick(blocks, index):
    return lax.dynamic_index_in_dim(blocks, index, axis=0, keepdims=False)


def rows_at(blocks, places):
    return jnp.take(blocks, places, axis=0, mode="clip")


def pair_kernel(own_ref, other_ref, after_ref, pair_ref):
    pair_ref[0] = own_ref[...]
    pair_ref[1] = other_ref[...]


def gradient_kernel(*refs):
    own_units, other_units, *rows = refs[:6]
    up_ref, down_ref, their_up, their_down = refs[7:]
    unit_width, width = up_ref.shape[1:]
    units = [
        jnp.concatenate([own_units[part], other_units[part]], axis=0)
        for part in (pl.ds(0, unit_width), pl.ds(unit_width, unit_width))
    ]
    for s, pair in enumerate(rows):
        for t in range(2):
            down = jnp.dot(units[0], pair[t, :, width:], preferred_element_type=F32).astype(BF16)
            up = jnp.dot(units[1], pair[t, :, :width], preferred_element_type=F32).astype(BF16)
            up_ref[2 * s + t] = up[:unit_width]
            down_ref[2 * s + t] = down[:unit_width]
            their_up[2 * s + t] = up[unit_width:]
            their_down[2 * s + t] = down[unit_width:]


def layout_kernel(source_ref, own_up, own_down, their_up, their_down, up_ref, down_ref):
    blocks, unit_width, width = own_up.shape
    for p in range(2 * blocks):
        columns = pl.ds(p * width, width)
        source = source_ref[p]

        @pl.when(source < blocks)
        def _():
            up_ref[:, columns] = own_up[source]
            down_ref[:, columns] = own_down[source]

        @pl.when(source >= blocks)
        def _():
            up_ref[:, columns] = their_up[source - blocks]
            down_ref[:, columns] = their_down[source - blocks]


def local(tokens, expert_ids, gate_weights, old_up, old_down, old_rows, new_slots, cotangent):
    chips = lax.axis_size(CHIP)
    cut_count = 2 * chips
    group_count = lax.axis_size("expert")
    expert_count = group_count // 2
    tok_rows, width = tokens.shape
    half_units = old_up.shape[0]
    unit_width = half_units // cut_count
    core_units = half_units // 2
    capacity = 8 * tok_rows // group_count
    slot_rows = group_count * capacity
    chip, core = lax.axis_index(CHIP), lax.axis_index("core")
    cut = 2 * chip + core
    cut_list = jnp.arange(cut_count, dtype=jnp.int32)
    inverse = jnp.sum(
        cut_list[:, None] * (old_rows[:, None] == cut_list[None, :]).astype(jnp.int32), axis=0
    )
    slot_pairs = new_slots.reshape(chips, 2)
    kept, given = slot_pairs[:, core], slot_pairs[:, 1 - core]

    def both_blocks(weights):
        blocks = weights.reshape(cut_count, unit_width, width)
        mine, theirs = rows_at(blocks, kept), swap(rows_at(blocks, given))
        return jnp.concatenate([mine, theirs], axis=2).reshape(core_units, 2 * width)

    with jax.named_scope("weights"):
        up, down = both_blocks(old_up), both_blocks(old_down)

    with jax.named_scope("token_blocks"):
        both = everywhere(jnp.concatenate([tokens, cotangent], axis=1), CUTS)
        both = pick(both, pick(old_rows, cut))

    flat_ids = expert_ids.reshape(-1)
    expert_hits = (flat_ids[:, None] == jnp.arange(expert_count, dtype=jnp.int32)[None, :]).astype(
        jnp.int32
    )
    slot_rank = jnp.sum((jnp.cumsum(expert_hits, axis=0) - expert_hits) * expert_hits, axis=1)
    target = (flat_ids * capacity + slot_rank).reshape(tok_rows, 2)
    slots = expert_count * capacity
    slot_list = jnp.arange(slots, dtype=jnp.int32)
    matches = slot_list[:, None, None] == target[None]
    placer = jnp.any(matches, axis=2).astype(BF16)
    slot_gate = jnp.sum(jnp.where(matches, gate_weights[None], 0.0), axis=(1, 2))

    with jax.named_scope("dispatch"):
        placed = jnp.dot(placer, both, preferred_element_type=F32)
        scale = jnp.where(jnp.arange(2 * width)[None, :] < width, 1.0, slot_gate[:, None])
        placed = (placed * scale).astype(BF16).reshape(expert_count, 1, capacity, 2 * width)
        placed = jnp.broadcast_to(placed, (expert_count, 2, capacity, 2 * width))
        routed = exchange(placed.reshape(group_count, capacity, 2 * width), "expert")
        routed = routed.reshape(slot_rows, 2 * width)
        other = swap(routed)
        routed_x = jnp.concatenate([routed[:, :width], other[:, :width]], axis=1)
        routed_back = jnp.concatenate([routed[:, width:], other[:, width:]], axis=1)

    def partial(weights, rows):
        part = lax.dot_general(
            weights, rows, (((1,), (1,)), ((), ())), preferred_element_type=F32
        ).astype(BF16)
        return part.reshape(chips, unit_width, slot_rows)

    with jax.named_scope("hidden"):
        parts = jnp.concatenate([partial(up, routed_x), partial(down, routed_back)], axis=1)
        sums = jnp.sum(exchange(parts, CHIP).astype(F32), axis=0)
        pre_act, hidden_grad = sums[:unit_width], sums[unit_width:]
        sig = jax.nn.sigmoid(pre_act)
        hidden = jax.nn.silu(pre_act).astype(BF16)
        pre_grad = (hidden_grad * sig * (1.0 + pre_act * (1.0 - sig))).astype(BF16)
        own_units = jnp.concatenate([hidden, pre_grad], axis=0)
        other_units = swap(own_units)
        early_rows, own_units = lax.optimization_barrier((routed, own_units))
        rows_y = lax.ppermute(early_rows, "y", [(0, 1), (1, 0)])
        units = everywhere(own_units, CHIP)
        units, rows_y, other_units = lax.optimization_barrier((units, rows_y, other_units))
        hidden = units[:, :unit_width].reshape(core_units, slot_rows)
        pre_grad = units[:, unit_width:].reshape(core_units, slot_rows)

    def rows_of(units, weights):
        return lax.dot_general(
            units, weights, (((0,), (0,)), ((), ())), preferred_element_type=F32
        )

    with jax.named_scope("give_back"):
        theirs = [rows_of(hidden, down[:, width:]), rows_of(pre_grad, up[:, width:])]
        theirs = swap(jnp.concatenate([part.astype(BF16) for part in theirs], axis=1))
        own = [rows_of(hidden, down[:, :width]), rows_of(pre_grad, up[:, :width])]
        half_rows = (jnp.concatenate(own, axis=1) + theirs.astype(F32)).astype(BF16)
        sent_rows = half_rows.reshape(group_count, capacity, 2 * width)
        half_rows = exchange(sent_rows, "expert")
        row_list = jnp.arange(slot_rows, dtype=jnp.int32)
        row_slot = row_list // (2 * capacity) * capacity + row_list % capacity
        picker = (target.reshape(-1)[:, None] == row_slot[None, :]).astype(BF16)
        entries = jnp.dot(picker, half_rows.reshape(slot_rows, 2 * width), preferred_element_type=F32)
        entries = entries.reshape(tok_rows, 2, 2 * width)
        mixed = jnp.sum(entries[:, :, :width] * gate_weights[:, :, None], axis=1)
        token_grad = jnp.sum(entries[:, :, width:], axis=1)
        result = jnp.concatenate([mixed, token_grad], axis=1).astype(BF16)

    with jax.named_scope("result"):
        own_result = result
        result = pick(everywhere(own_result, CUTS), pick(inverse, cut))

    with jax.named_scope("all_rows"):
        pair = pl.pallas_call(
            pair_kernel,
            out_shape=jax.ShapeDtypeStruct((2, slot_rows, 2 * width), BF16),
            in_specs=[VMEM, VMEM, ANY],
            out_specs=VMEM,
        )(routed, rows_y, sent_rows)
        column = lax.axis_size("x")
        pairs = [pair] + [
            lax.ppermute(pair, "x", [(i, (i + s) % column) for i in range(column)])
            for s in range(1, column)
        ]

    with jax.named_scope("new_slices"):
        block = jax.ShapeDtypeStruct((chips, unit_width, width), BF16)
        up_part, down_part, their_up, their_down = pl.pallas_call(
            gradient_kernel,
            out_shape=(block,) * 4,
            in_specs=[VMEM] * 6 + [ANY],
            out_specs=(VMEM,) * 4,
            compiler_params=LARGE,
        )(own_units, other_units, *pairs, own_result)
        source = inverse // 2
        back = (lax.axis_index("x") - source % column) % column
        source = 2 * back + (source // column != lax.axis_index("y")).astype(jnp.int32)
        source = source + jnp.where(inverse % 2 == core, 0, chips)
        grad = jax.ShapeDtypeStruct((unit_width, cut_count * width), BF16)
        up_grad, down_grad = pl.pallas_call(
            layout_kernel,
            out_shape=(grad, grad),
            in_specs=[pl.BlockSpec(memory_space=pltpu.SMEM)] + [VMEM] * 4,
            out_specs=(VMEM, VMEM),
            compiler_params=LARGE,
        )(source, up_part, down_part, swap(their_up), swap(their_down))
    return (result[:, :width], result[:, width:], up_grad, down_grad)


def solution(mesh):
    experts, cuts = mesh.devices.shape
    split = Mesh(mesh.devices.reshape(experts, 2, cuts // 4, 2), ("expert", "y", "x", "core"))
    spread = P("expert", CUTS)
    return jax.shard_map(
        local,
        mesh=split,
        in_specs=(spread, P("expert", None), P("expert", None), spread, spread, P(), P(), spread),
        out_specs=(
            spread,
            spread,
            P(("expert", *CUTS), None),
            P(("expert", *CUTS), None),
        ),
        check_vma=False,
    )
```

time: 193 us -> 174 us (0.902)
  starting transfers between devices: 49.7 us -> 76.7 us
  blocking collectives: 41.5 us -> 20.4 us
  waiting for transfers between devices: 52.8 us -> 36.6 us
  between operations: 11.6 us -> 5.07 us
  Pallas kernels: 0 us -> 5.72 us
  local copies, waits for them, and re-layouts: 22.6 us -> 17.9 us
  other arithmetic: 7.31 us -> 5.15 us
    all_to_all x4 -> x5, waiting for transfers between devices: 51.7 us -> 23.5 us  [exchange(): return lax.all_to_all(parts, axis, split_axis=0, concat_axis=0, tiled=True)]
    all_to_all x2 -> x1, blocking collectives: 41.5 us -> 20.4 us  [exchange(): return lax.all_to_all(parts, axis, split_axis=0, concat_axis=0, tiled=True)]
    ppermute x0 -> x4, starting transfers between devices: none -> 15.4 us  [the longest x3 10.6 us: local(): lax.ppermute(pair, 'x', [(i, (i + s) % column) for i in range(column)])]
    ppermute x0 -> x4, waiting for transfers between devices: none -> 11.1 us  [the longest x1 11.1 us: local(): rows_y = lax.ppermute(early_rows, 'y', [(0, 1), (1, 0)])]
    all_to_all x4 -> x5, starting transfers between devices: 28.5 us -> 38.5 us  [exchange(): return lax.all_to_all(parts, axis, split_axis=0, concat_axis=0, tiled=True)]
    pallas_call x0 -> x3, Pallas kernels: none -> 5.72 us  [the longest x1 2.18 us: local(): pl.pallas_call(layout_kernel, out_shape=(grad, grad), in_specs=[pl.BlockS...]
    dot_general x2 -> x0, matrix products: 2.89 us -> none  [outer(): grad = jnp.dot(units, rows, preferred_element_type=F32).astype(BF16)]
    gather x6 -> x4, local copies, waits for them, and re-layouts: 6.89 us -> 4.34 us  [rows_at(): return jnp.take(blocks, places, axis=0, mode='clip')]
  transfers between devices with their start and end apart: 10 -> 16, of which waited for: 4 -> 7; matrix products, arithmetic and copies ran while one was open for 13% -> 8% of each run, Pallas kernels for 0% -> 2%
where the time goes in v5:
time: 174 us; the launch traced here: 172 us
  starting transfers between devices  76.7 us (44%)
  waiting for transfers between devices  36.6 us (21%)
  blocking collectives  20.4 us (12%)
  local copies, waits for them, and re-layouts  17.9 us (10%)
  Pallas kernels  5.72 us (3%)
  other arithmetic  5.15 us (3%)
  between operations  5.07 us (3%)
  matrix products  4.83 us (3%)
    all_to_all x5, starting transfers between devices, exchange(): return lax.all_to_all(parts, axis, split_axis=0, concat_axis=0, tiled=True)  38.5 us
    all_to_all x5, waiting for transfers between devices, exchange(): return lax.all_to_all(parts, axis, split_axis=0, concat_axis=0, tiled=True)  23.5 us
    ppermute x7, starting transfers between devices, swap(): return lax.ppermute(block, 'core', [(0, 1), (1, 0)])  22.9 us
    all_to_all x1, blocking collectives, exchange(): return lax.all_to_all(parts, axis, split_axis=0, concat_axis=0, tiled=True)  20.4 us
    ppermute x1, waiting for transfers between devices, local(): rows_y = lax.ppermute(early_rows, 'y', [(0, 1), (1, 0)])  11.1 us
    ppermute x3, starting transfers between devices, local(): lax.ppermute(pair, 'x', [(i, (i + s) % column) for i in range(column)])  10.6 us
    unnamed x35, local copies, waits for them, and re-layouts  5.97 us
    ppermute x1, starting transfers between devices, local(): rows_y = lax.ppermute(early_rows, 'y', [(0, 1), (1, 0)])  4.77 us
  transfers between devices with their start and end apart: 16, of which 7 were waited for; matrix products, arithmetic and copies ran while one was open for 8% of the time, Pallas kernels for 2%

profile of v5, /device:TPU:1, one launch (start us, length us, event | category | flops | bytes accessed | tf_op | source)
XLA Modules:
  0.0 172.3 jit_solution(9976779260727266407)
XLA Ops:
  0.7 0.8 pad_maximum_fusion.5
  1.5 0.8 broadcast_in_dim.78
  2.3 10.4 %all-to-all-start = ((bf16[16,32,512]{2,1,0:T(8,128)(2,1)}), bf16[16,32,512]{2,1,0:T(8,128)(2,1)S(1)}, u32[]{:S(2)}, u32[]{:S(2)}) async-start(bf16[16,32,512]{2,1,0:T(8,128)(2,1)} %broadcast_in_dim.78), calls=%async_computation | async-start | bytes 1048576 | tf_op jit(solution)/shard_map/token_blocks/all_to_all | solution.py:17
  12.8 0.1 eq.71
  13.0 0.1 reduce_window_sum.11
  13.1 0.2 select_reduce_fusion.1
  13.3 0.6 dynamic_slice.20
  15.2 0.1 reduce_sum.57
  16.1 0.1 select_reduce_fusion
  16.2 8.0 %all-to-all-done = bf16[16,32,512]{2,1,0:T(8,128)(2,1)S(1)} async-done(((bf16[16,32,512]{2,1,0:T(8,128)(2,1)}), bf16[16,32,512]{2,1,0:T(8,128)(2,1)S(1)}, u32[]{:S(2)}, u32[]{:S(2)}) %all-to-all-start) | async-done | bytes 524320 | tf_op jit(solution)/shard_map/token_blocks/all_to_all | solution.py:17
  24.2 0.2 fusion.1
  24.5 0.7 broadcast_in_dim.85
  25.2 13.4 %all-to-all-start.1 = ((bf16[32,8,512]{2,1,0:T(8,128)(2,1)}), bf16[32,8,512]{2,1,0:T(8,128)(2,1)S(1)}, u32[]{:S(2)}, u32[]{:S(2)}) async-start(bf16[32,8,512]{2,1,0:T(8,128)(2,1)} %bitcast.3), calls=%async_computation.1 | async-start | bytes 524288 | tf_op jit(solution)/shard_map/dispatch/all_to_all | solution.py:17
  38.7 0.2 dynamic-slice_reduce_fusion.1
  38.9 1.4 gather_fusion.1
  40.3 3.3 %collective-permute-start = (bf16[8,128,256]{2,1,0:T(8,128)(2,1)}, bf16[8,128,256]{2,1,0:T(8,128)(2,1)}, u32[]{:S(2)}, u32[]{:S(2)}) collective-permute-start(bf16[8,128,256]{2,1,0:T(8,128)(2,1)} %gather_fusion.1), channel_id=1, source_target_pairs={{0,1},{1,0},{2,3},{3,2},{4,5},{5,4},{6,7},{7,6},{8,9},{9,8},{10,11... | collective-permute-start | bytes 1572872 | tf_op jit(solution)/shard_map/weights/ppermute | solution.py:25
  43.6 0.6 gather_fusion.3
  44.2 1.9 %collective-permute-start.2 = (bf16[8,128,256]{2,1,0:T(8,128)(2,1)S(1)}, bf16[8,128,256]{2,1,0:T(8,128)(2,1)}, u32[]{:S(2)}, u32[]{:S(2)}) collective-permute-start(bf16[8,128,256]{2,1,0:T(8,128)(2,1)S(1)} %gather_fusion.3), channel_id=1, source_target_pairs={{0,1},{1,0},{2,3},{3,2},{4,5},{5,4},{6,7},{7,6},{8,9},{9,8},{10,11... | collective-permute-start | bytes 1572872 | tf_op jit(solution)/shard_map/weights/ppermute | solution.py:25
  46.1 0.6 gather_fusion
  46.7 1.8 %gather_fusion.2 = bf16[8,128,256]{2,1,0:T(8,128)(2,1)S(1)} fusion(bf16[16,128,256]{2,1,0:T(8,128)(2,1)} %bitcast.44, s32[1024]{0:T(1024)S(1)} %pad_clamp_fusion.1), kind=kCustom, calls=%fused_computation.2 | custom fusion | bytes 1048608 | tf_op jit(solution)/shard_map/weights/jit(_take)/gather | solution.py:33
  48.5 2.1 %pad_maximum_fusion = bf16[8,128,512]{2,1,0:T(8,128)(2,1)} fusion(bf16[8,128,256]{2,1,0:T(8,128)(2,1)} %collective-permute-done, bf16[8,128,256]{2,1,0:T(8,128)(2,1)S(1)} %gather_fusion), kind=kLoop, calls=%fused_computation.12 | loop fusion | flops 2097152 | bytes 2097152 | tf_op jit(solution)/shard_map/weights/concatenate | solution.py:99
  50.6 7.1 %all-to-all-done.1 = bf16[32,8,512]{2,1,0:T(8,128)(2,1)S(1)} async-done(((bf16[32,8,512]{2,1,0:T(8,128)(2,1)}), bf16[32,8,512]{2,1,0:T(8,128)(2,1)S(1)}, u32[]{:S(2)}, u32[]{:S(2)}) %all-to-all-start.1) | async-done | bytes 262176 | tf_op jit(solution)/shard_map/dispatch/all_to_all | solution.py:17
  57.7 6.1 %collective-permute-start.1 = (bf16[256,512]{1,0:T(8,128)(2,1)S(1)}, bf16[256,512]{1,0:T(8,128)(2,1)S(1)}, u32[]{:S(2)}, u32[]{:S(2)}) collective-permute-start(bf16[256,512]{1,0:T(8,128)(2,1)S(1)} %bitcast.34), channel_id=1, source_target_pairs={{0,1},{1,0},{2,3},{3,2},{4,5},{5,4},{6,7},{7,6},{8,9},{9,8},{10,11... | collective-permute-start | bytes 786440 | tf_op jit(solution)/shard_map/dispatch/ppermute | solution.py:25
  63.9 1.1 pad_maximum_fusion.1
  65.1 1.5 copy-done.7
  66.6 0.5 convolution_convert_fusion.1
  67.1 0.5 convolution_convert_fusion
  67.6 20.4 %all_to_all.30 = bf16[8,256,256]{2,1,0:T(8,128)(2,1)S(1)} all-to-all(bf16[8,256,256]{2,1,0:T(8,128)(2,1)S(1)} %pad_maximum_fusion.2), channel_id=1, replica_groups=mesh['expert'=32,'y'=2,'x'=4,'core'=2] {'y','x'}, dimensions={0} | all-to-all | bytes 2097152 | tf_op jit(solution)/shard_map/hidden/all_to_all | solution.py:17
  88.0 0.1 convert_reduce_fusion
  88.2 1.0 broadcast_in_dim.86
  89.3 3.6 %all-to-all-start.3 = ((bf16[8,256,256]{2,1,0:T(8,128)(2,1)}), bf16[8,256,256]{2,1,0:T(8,128)(2,1)S(1)}, u32[]{:S(2)}, u32[]{:S(2)}) async-start(bf16[8,256,256]{2,1,0:T(8,128)(2,1)} %broadcast_in_dim.86), calls=%async_computation.3 | async-start | bytes 2097152 | tf_op jit(solution)/shard_map/hidden/all_to_all | solution.py:17
  92.9 4.8 %collective-permute-start.3 = (bf16[256,512]{1,0:T(8,128)(2,1)S(1)}, bf16[256,512]{1,0:T(8,128)(2,1)S(1)}, u32[]{:S(2)}, u32[]{:S(2)}) collective-permute-start(bf16[256,512]{1,0:T(8,128)(2,1)S(1)} %bitcast.36), channel_id=1, source_target_pairs={{0,8},{8,0},{1,9},{9,1},{2,10},{10,2},{3,11},{11,3},{4,12},{12,4},... | collective-permute-start | bytes 786440 | tf_op jit(solution)/shard_map/hidden/ppermute | solution.py:147
  97.6 3.3 %collective-permute-start.4 = (bf16[256,256]{1,0:T(8,128)(2,1)S(1)}, bf16[256,256]{1,0:T(8,128)(2,1)S(1)}, u32[]{:S(2)}, u32[]{:S(2)}) collective-permute-start(bf16[256,256]{1,0:T(8,128)(2,1)S(1)} %pad_maximum_fusion.4.refs_0_), channel_id=1, source_target_pairs={{0,1},{1,0},{2,3},{3,2},{4,5},{5,4},{6,7},{7,6},{8,9},{9,8},{10,11... | collective-permute-start | bytes 393224 | tf_op jit(solution)/shard_map/hidden/ppermute | solution.py:25
  100.9 1.0 collective-permute-done.4.refs_1_
  101.9 11.1 %collective-permute-done.3.other_ref = bf16[256,512]{1,0:T(8,128)(2,1)S(1)} collective-permute-done((bf16[256,512]{1,0:T(8,128)(2,1)S(1)}, bf16[256,512]{1,0:T(8,128)(2,1)S(1)}, u32[]{:S(2)}, u32[]{:S(2)}) %collective-permute-start.3) | collective-permute-done | bytes 262176 | tf_op jit(solution)/shard_map/hidden/ppermute | solution.py:147
  113.0 0.6 copy-done.12
  113.6 1.5 convolution_convert_fusion.3
  115.1 0.4 convolution_convert_fusion.2
  115.5 3.4 %collective-permute-start.5 = (bf16[256,512]{0,1:T(8,128)(2,1)S(1)}, bf16[256,512]{0,1:T(8,128)(2,1)S(1)}, u32[]{:S(2)}, u32[]{:S(2)}) collective-permute-start(bf16[256,512]{0,1:T(8,128)(2,1)S(1)} %pad_maximum_fusion.3), channel_id=1, source_target_pairs={{0,1},{1,0},{2,3},{3,2},{4,5},{5,4},{6,7},{7,6},{8,9},{9,8},{10,11... | collective-permute-start | bytes 786440 | tf_op jit(solution)/shard_map/give_back/ppermute | solution.py:25
  119.0 0.3 fusion.6
  119.3 0.3 fusion.4
  119.7 0.4 collective-permute-done.5
  120.1 0.8 copy.32
  121.0 4.6 %all-to-all-start.4 = ((bf16[32,8,512]{2,1,0:T(8,128)(2,1)}), bf16[32,8,512]{2,1,0:T(8,128)(2,1)}, u32[]{:S(2)}, u32[]{:S(2)}) async-start(bf16[32,8,512]{2,1,0:T(8,128)(2,1)} %bitcast.13.after_ref), calls=%async_computation.4 | async-start | bytes 524288 | tf_op jit(solution)/shard_map/give_back/all_to_all | solution.py:17
  125.6 1.9 %all_rows.1.refs_2_ = bf16[2,256,512]{2,1,0:T(8,128)(2,1)} custom-call(bf16[256,512]{1,0:T(8,128)(2,1)} %bitcast.37, bf16[256,512]{1,0:T(8,128)(2,1)} %copy-done.12, bf16[32,8,512]{2,1,0:T(8,128)(2,1)} %bitcast.13.after_ref), custom_call_target="tpu_custom_call" | custom-call | tf_op jit(solution)/shard_map/all_rows/pallas_call | solution.py:179
  127.5 3.2 %collective-permute-start.6 = (bf16[2,256,512]{2,1,0:T(8,128)(2,1)}, bf16[2,256,512]{2,1,0:T(8,128)(2,1)S(1)}, u32[]{:S(2)}, u32[]{:S(2)}) collective-permute-start(bf16[2,256,512]{2,1,0:T(8,128)(2,1)} %all_rows.1.refs_2_), channel_id=1, source_target_pairs={{0,2},{2,4},{4,6},{6,0},{1,3},{3,5},{5,7},{7,1},{8,10},{10,12},{12... | collective-permute-start | bytes 1572872 | tf_op jit(solution)/shard_map/all_rows/ppermute | solution.py:187
  130.7 4.3 %collective-permute-start.7 = (bf16[2,256,512]{2,1,0:T(8,128)(2,1)}, bf16[2,256,512]{2,1,0:T(8,128)(2,1)S(1)}, u32[]{:S(2)}, u32[]{:S(2)}) collective-permute-start(bf16[2,256,512]{2,1,0:T(8,128)(2,1)} %all_rows.1.refs_2_), channel_id=1, source_target_pairs={{0,4},{2,6},{4,0},{6,2},{1,5},{3,7},{5,1},{7,3},{8,12},{10,14},{12... | collective-permute-start | bytes 1572872 | tf_op jit(solution)/shard_map/all_rows/ppermute | solution.py:187
  135.0 3.1 %collective-permute-start.8 = (bf16[2,256,512]{2,1,0:T(8,128)(2,1)}, bf16[2,256,512]{2,1,0:T(8,128)(2,1)S(1)}, u32[]{:S(2)}, u32[]{:S(2)}) collective-permute-start(bf16[2,256,512]{2,1,0:T(8,128)(2,1)} %all_rows.1.refs_2_), channel_id=1, source_target_pairs={{0,6},{2,0},{4,2},{6,4},{1,7},{3,1},{5,3},{7,5},{8,14},{10,8},{12,... | collective-permute-start | bytes 1572872 | tf_op jit(solution)/shard_map/all_rows/ppermute | solution.py:187
  138.1 8.4 %all-to-all-done.4 = bf16[32,8,512]{2,1,0:T(8,128)(2,1)} async-done(((bf16[32,8,512]{2,1,0:T(8,128)(2,1)}), bf16[32,8,512]{2,1,0:T(8,128)(2,1)}, u32[]{:S(2)}, u32[]{:S(2)}) %all-to-all-start.4) | async-done | bytes 262176 | tf_op jit(solution)/shard_map/give_back/all_to_all | solution.py:17
  146.5 1.2 fusion.15
  147.7 0.8 broadcast_in_dim.87
  148.6 6.5 %all-to-all-start.5 = ((bf16[16,32,512]{2,1,0:T(8,128)(2,1)}), bf16[16,32,512]{2,1,0:T(8,128)(2,1)}, u32[]{:S(2)}, u32[]{:S(2)}) async-start(bf16[16,32,512]{2,1,0:T(8,128)(2,1)} %broadcast_in_dim.87), calls=%async_computation.5 | async-start | bytes 1048576 | tf_op jit(solution)/shard_map/result/all_to_all | solution.py:17
  155.2 0.6 dynamic_slice.24
  157.7 0.8 copy-done.2
  158.5 0.8 copy-done.4
  159.4 1.0 copy-done.3
  160.4 1.0 copy-done.5
  161.4 1.7 new_slices.2
  163.1 3.0 %collective-permute-start.10 = (bf16[8,128,256]{2,1,0:T(8,128)(2,1)}, bf16[8,128,256]{2,1,0:T(8,128)(2,1)S(1)}, u32[]{:S(2)}, u32[]{:S(2)}) collective-permute-start(bf16[8,128,256]{2,1,0:T(8,128)(2,1)} %get-tuple-element.23), channel_id=1, source_target_pairs={{0,1},{1,0},{2,3},{3,2},{4,5},{5,4},{6,7},{7,6},{8,9},{9,8},{10,11... | collective-permute-start | bytes 1572872 | tf_op jit(solution)/shard_map/new_slices/ppermute | solution.py:25
  166.1 1.9 %collective-permute-start.9 = (bf16[8,128,256]{2,1,0:T(8,128)(2,1)}, bf16[8,128,256]{2,1,0:T(8,128)(2,1)S(1)}, u32[]{:S(2)}, u32[]{:S(2)}) collective-permute-start(bf16[8,128,256]{2,1,0:T(8,128)(2,1)} %get-tuple-element.22), channel_id=1, source_target_pairs={{0,1},{1,0},{2,3},{3,2},{4,5},{5,4},{6,7},{7,6},{8,9},{9,8},{10,11... | collective-permute-start | bytes 1572872 | tf_op jit(solution)/shard_map/new_slices/ppermute | solution.py:25
  168.1 0.8 dynamic-slice_bitcast_fusion
  168.9 0.6 fusion.40
  169.5 0.7 collective-permute-done.9.their_up
  170.2 2.2 %new_slices.3 = (bf16[128,4096]{1,0:T(8,128)(2,1)}, bf16[128,4096]{1,0:T(8,128)(2,1)}) custom-call(s32[16]{0:T(128)S(1)} %fusion.33.source_ref, bf16[8,128,256]{2,1,0:T(8,128)(2,1)S(1)} %get-tuple-element.20.own_up, bf16[8,128,256]{2,1,0:T(8,128)(2,1)S(1)} %get-tuple-element.21.own_down, bf16[8,128,256]{2,1,0:T(8,128)(2,1)S(1)} %collective-permute-done.9.their_up, ...), custom_call_target="tpu_custom_call" | custom-call | tf_op jit(solution)/shard_map/new_slices/pallas_call | solution.py:205
  (59 shorter events, 1.1 us)
Async XLA Ops:
  0.6 38.3 %copy-start = (bf16[2048,256]{1,0:T(8,128)(2,1)S(1)}, bf16[2048,256]{1,0:T(8,128)(2,1)}, u32[]{:S(2)}) copy-start(bf16[2048,256]{1,0:T(8,128)(2,1)} %param.11) | copy-start | bytes 3145732
  0.6 12.1 %copy-start.14 = (s32[32,2]{0,1:T(2,128)S(1)}, s32[32,2]{0,1:T(2,128)}, u32[]{:S(2)}) copy-start(s32[32,2]{0,1:T(2,128)} %param.9) | copy-start | bytes 772
  0.7 12.6 %copy-start.16 = (s32[16]{0:T(128)S(1)}, s32[16]{0:T(128)}, u32[]{:S(2)}) copy-start(s32[16]{0:T(128)} %param.13) | copy-start | bytes 196
  0.7 15.5 %copy-start.13 = (f32[32,2]{0,1:T(2,128)S(1)}, f32[32,2]{0,1:T(2,128)}, u32[]{:S(2)}) copy-start(f32[32,2]{0,1:T(2,128)} %param.10) | copy-start | bytes 772
  2.3 36.3 %copy-start.15 = (s32[16]{0:T(128)S(1)}, s32[16]{0:T(128)}, u32[]{:S(2)}) copy-start(s32[16]{0:T(128)} %param.14) | copy-start | bytes 196
  2.3 21.9 %all-to-all-start = ((bf16[16,32,512]{2,1,0:T(8,128)(2,1)}), bf16[16,32,512]{2,1,0:T(8,128)(2,1)S(1)}, u32[]{:S(2)}, u32[]{:S(2)}) async-start(bf16[16,32,512]{2,1,0:T(8,128)(2,1)} %broadcast_in_dim.78), calls=%async_computation | async-start | bytes 1048576 | tf_op jit(solution)/shard_map/token_blocks/all_to_all | solution.py:17
  24.4 19.1 %copy-start.11 = (bf16[2048,256]{1,0:T(8,128)(2,1)S(1)}, bf16[2048,256]{1,0:T(8,128)(2,1)}, u32[]{:S(2)}) copy-start(bf16[2048,256]{1,0:T(8,128)(2,1)} %param.12) | copy-start | bytes 3145732
  25.2 32.5 %all-to-all-start.1 = ((bf16[32,8,512]{2,1,0:T(8,128)(2,1)}), bf16[32,8,512]{2,1,0:T(8,128)(2,1)S(1)}, u32[]{:S(2)}, u32[]{:S(2)}) async-start(bf16[32,8,512]{2,1,0:T(8,128)(2,1)} %bitcast.3), calls=%async_computation.1 | async-start | bytes 524288 | tf_op jit(solution)/shard_map/dispatch/all_to_all | solution.py:17
  40.3 8.2 %collective-permute-start = (bf16[8,128,256]{2,1,0:T(8,128)(2,1)}, bf16[8,128,256]{2,1,0:T(8,128)(2,1)}, u32[]{:S(2)}, u32[]{:S(2)}) collective-permute-start(bf16[8,128,256]{2,1,0:T(8,128)(2,1)} %gather_fusion.1), channel_id=1, source_target_pairs={{0,1},{1,0},{2,3},{3,2},{4,5},{5,4},{6,7},{7,6},{8,9},{9,8},{10,11... | collective-permute-start | bytes 1572872 | tf_op jit(solution)/shard_map/weights/ppermute | solution.py:25
  44.2 19.7 %collective-permute-start.2 = (bf16[8,128,256]{2,1,0:T(8,128)(2,1)S(1)}, bf16[8,128,256]{2,1,0:T(8,128)(2,1)}, u32[]{:S(2)}, u32[]{:S(2)}) collective-permute-start(bf16[8,128,256]{2,1,0:T(8,128)(2,1)S(1)} %gather_fusion.3), channel_id=1, source_target_pairs={{0,1},{1,0},{2,3},{3,2},{4,5},{5,4},{6,7},{7,6},{8,9},{9,8},{10,11... | collective-permute-start | bytes 1572872 | tf_op jit(solution)/shard_map/weights/ppermute | solution.py:25
  57.7 35.1 %copy-start.6 = (bf16[32,8,512]{2,1,0:T(8,128)(2,1)}, bf16[32,8,512]{2,1,0:T(8,128)(2,1)S(1)}, u32[]{:S(2)}) copy-start(bf16[32,8,512]{2,1,0:T(8,128)(2,1)S(1)} %all-to-all-done.1) | copy-start | bytes 786436
  57.7 7.3 %collective-permute-start.1 = (bf16[256,512]{1,0:T(8,128)(2,1)S(1)}, bf16[256,512]{1,0:T(8,128)(2,1)S(1)}, u32[]{:S(2)}, u32[]{:S(2)}) collective-permute-start(bf16[256,512]{1,0:T(8,128)(2,1)S(1)} %bitcast.34), channel_id=1, source_target_pairs={{0,1},{1,0},{2,3},{3,2},{4,5},{5,4},{6,7},{7,6},{8,9},{9,8},{10,11... | collective-permute-start | bytes 786440 | tf_op jit(solution)/shard_map/dispatch/ppermute | solution.py:25
  65.0 2.6 %copy-start.9 = (bf16[8,128,512]{2,1,0:T(8,128)(2,1)}, bf16[8,128,512]{2,1,0:T(8,128)(2,1)S(1)}, u32[]{:S(2)}) copy-start(bf16[8,128,512]{2,1,0:T(8,128)(2,1)S(1)} %pad_maximum_fusion.1) | copy-start | bytes 3145732
  65.0 1.6 copy-start.7
  89.3 23.7 %all-to-all-start.3 = ((bf16[8,256,256]{2,1,0:T(8,128)(2,1)}), bf16[8,256,256]{2,1,0:T(8,128)(2,1)S(1)}, u32[]{:S(2)}, u32[]{:S(2)}) async-start(bf16[8,256,256]{2,1,0:T(8,128)(2,1)} %broadcast_in_dim.86), calls=%async_computation.3 | async-start | bytes 2097152 | tf_op jit(solution)/shard_map/hidden/all_to_all | solution.py:17
  92.9 20.1 %collective-permute-start.3 = (bf16[256,512]{1,0:T(8,128)(2,1)S(1)}, bf16[256,512]{1,0:T(8,128)(2,1)S(1)}, u32[]{:S(2)}, u32[]{:S(2)}) collective-permute-start(bf16[256,512]{1,0:T(8,128)(2,1)S(1)} %bitcast.36), channel_id=1, source_target_pairs={{0,8},{8,0},{1,9},{9,1},{2,10},{10,2},{3,11},{11,3},{4,12},{12,4},... | collective-permute-start | bytes 786440 | tf_op jit(solution)/shard_map/hidden/ppermute | solution.py:147
  97.6 4.2 %collective-permute-start.4 = (bf16[256,256]{1,0:T(8,128)(2,1)S(1)}, bf16[256,256]{1,0:T(8,128)(2,1)S(1)}, u32[]{:S(2)}, u32[]{:S(2)}) collective-permute-start(bf16[256,256]{1,0:T(8,128)(2,1)S(1)} %pad_maximum_fusion.4.refs_0_), channel_id=1, source_target_pairs={{0,1},{1,0},{2,3},{3,2},{4,5},{5,4},{6,7},{7,6},{8,9},{9,8},{10,11... | collective-permute-start | bytes 393224 | tf_op jit(solution)/shard_map/hidden/ppermute | solution.py:25
  112.9 0.7 copy-start.12
  113.6 1.5 copy-start.8
  115.1 3.8 %copy-start.10 = (bf16[8,128,512]{2,1,0:T(8,128)(2,1)S(1)}, bf16[8,128,512]{2,1,0:T(8,128)(2,1)}, u32[]{:S(2)}) copy-start(bf16[8,128,512]{2,1,0:T(8,128)(2,1)} %copy-done.9) | copy-start | bytes 3145732
  115.5 4.6 %collective-permute-start.5 = (bf16[256,512]{0,1:T(8,128)(2,1)S(1)}, bf16[256,512]{0,1:T(8,128)(2,1)S(1)}, u32[]{:S(2)}, u32[]{:S(2)}) collective-permute-start(bf16[256,512]{0,1:T(8,128)(2,1)S(1)} %pad_maximum_fusion.3), channel_id=1, source_target_pairs={{0,1},{1,0},{2,3},{3,2},{4,5},{5,4},{6,7},{7,6},{8,9},{9,8},{10,11... | collective-permute-start | bytes 786440 | tf_op jit(solution)/shard_map/give_back/ppermute | solution.py:25
  121.0 25.5 %all-to-all-start.4 = ((bf16[32,8,512]{2,1,0:T(8,128)(2,1)}), bf16[32,8,512]{2,1,0:T(8,128)(2,1)}, u32[]{:S(2)}, u32[]{:S(2)}) async-start(bf16[32,8,512]{2,1,0:T(8,128)(2,1)} %bitcast.13.after_ref), calls=%async_computation.4 | async-start | bytes 524288 | tf_op jit(solution)/shard_map/give_back/all_to_all | solution.py:17
  127.5 31.9 %copy-start.1 = (bf16[2,256,512]{2,1,0:T(8,128)(2,1)S(1)}, bf16[2,256,512]{2,1,0:T(8,128)(2,1)}, u32[]{:S(2)}) copy-start(bf16[2,256,512]{2,1,0:T(8,128)(2,1)} %all_rows.1.refs_2_) | copy-start | bytes 1572868
  127.5 30.2 %collective-permute-start.6 = (bf16[2,256,512]{2,1,0:T(8,128)(2,1)}, bf16[2,256,512]{2,1,0:T(8,128)(2,1)S(1)}, u32[]{:S(2)}, u32[]{:S(2)}) collective-permute-start(bf16[2,256,512]{2,1,0:T(8,128)(2,1)} %all_rows.1.refs_2_), channel_id=1, source_target_pairs={{0,2},{2,4},{4,6},{6,0},{1,3},{3,5},{5,7},{7,1},{8,10},{10,12},{12... | collective-permute-start | bytes 1572872 | tf_op jit(solution)/shard_map/all_rows/ppermute | solution.py:187
  130.7 27.0 %collective-permute-start.7 = (bf16[2,256,512]{2,1,0:T(8,128)(2,1)}, bf16[2,256,512]{2,1,0:T(8,128)(2,1)S(1)}, u32[]{:S(2)}, u32[]{:S(2)}) collective-permute-start(bf16[2,256,512]{2,1,0:T(8,128)(2,1)} %all_rows.1.refs_2_), channel_id=1, source_target_pairs={{0,4},{2,6},{4,0},{6,2},{1,5},{3,7},{5,1},{7,3},{8,12},{10,14},{12... | collective-permute-start | bytes 1572872 | tf_op jit(solution)/shard_map/all_rows/ppermute | solution.py:187
  135.0 23.5 %collective-permute-start.8 = (bf16[2,256,512]{2,1,0:T(8,128)(2,1)}, bf16[2,256,512]{2,1,0:T(8,128)(2,1)S(1)}, u32[]{:S(2)}, u32[]{:S(2)}) collective-permute-start(bf16[2,256,512]{2,1,0:T(8,128)(2,1)} %all_rows.1.refs_2_), channel_id=1, source_target_pairs={{0,6},{2,0},{4,2},{6,4},{1,7},{3,1},{5,3},{7,5},{8,14},{10,8},{12,... | collective-permute-start | bytes 1572872 | tf_op jit(solution)/shard_map/all_rows/ppermute | solution.py:187
  148.6 19.5 %all-to-all-start.5 = ((bf16[16,32,512]{2,1,0:T(8,128)(2,1)}), bf16[16,32,512]{2,1,0:T(8,128)(2,1)}, u32[]{:S(2)}, u32[]{:S(2)}) async-start(bf16[16,32,512]{2,1,0:T(8,128)(2,1)} %broadcast_in_dim.87), calls=%async_computation.5 | async-start | bytes 1048576 | tf_op jit(solution)/shard_map/result/all_to_all | solution.py:17
  157.7 0.8 copy-start.2
  158.5 0.8 copy-start.4
  159.4 1.0 copy-start.3
  160.4 1.0 copy-start.5
  163.1 6.4 %collective-permute-start.10 = (bf16[8,128,256]{2,1,0:T(8,128)(2,1)}, bf16[8,128,256]{2,1,0:T(8,128)(2,1)S(1)}, u32[]{:S(2)}, u32[]{:S(2)}) collective-permute-start(bf16[8,128,256]{2,1,0:T(8,128)(2,1)} %get-tuple-element.23), channel_id=1, source_target_pairs={{0,1},{1,0},{2,3},{3,2},{4,5},{5,4},{6,7},{7,6},{8,9},{9,8},{10,11... | collective-permute-start | bytes 1572872 | tf_op jit(solution)/shard_map/new_slices/ppermute | solution.py:25
  166.1 4.0 %collective-permute-start.9 = (bf16[8,128,256]{2,1,0:T(8,128)(2,1)}, bf16[8,128,256]{2,1,0:T(8,128)(2,1)S(1)}, u32[]{:S(2)}, u32[]{:S(2)}) collective-permute-start(bf16[8,128,256]{2,1,0:T(8,128)(2,1)} %get-tuple-element.22), channel_id=1, source_target_pairs={{0,1},{1,0},{2,3},{3,2},{4,5},{5,4},{6,7},{7,6},{8,9},{9,8},{10,11... | collective-permute-start | bytes 1572872 | tf_op jit(solution)/shard_map/new_slices/ppermute | solution.py:25

commit v6 on v5

--- a/solution.py
+++ b/solution.py
@@ -25,6 +25,10 @@
     return lax.ppermute(block, "core", [(0, 1), (1, 0)])
 
 
+def swap_y(block):
+    return lax.ppermute(block, "y", [(0, 1), (1, 0)])
+
+
 def pick(blocks, index):
     return lax.dynamic_index_in_dim(blocks, index, axis=0, keepdims=False)
 
@@ -33,44 +37,52 @@
     return jnp.take(blocks, places, axis=0, mode="clip")
 
 
-def pair_kernel(own_ref, other_ref, after_ref, pair_ref):
-    pair_ref[0] = own_ref[...]
-    pair_ref[1] = other_ref[...]
-
-
-def gradient_kernel(*refs):
-    own_units, other_units, *rows = refs[:6]
-    up_ref, down_ref, their_up, their_down = refs[7:]
+def pair_kernel(own_ref, x_ref, back_ref, after_ref, pair_ref, sems):
+    width = x_ref.shape[1]
+    copies = [
+        pltpu.make_async_copy(own_ref, pair_ref.at[0], sems.at[0]),
+        pltpu.make_async_copy(x_ref, pair_ref.at[1, :, pl.ds(0, width)], sems.at[1]),
+        pltpu.make_async_copy(back_ref, pair_ref.at[1, :, pl.ds(width, width)], sems.at[2]),
+    ]
+    for copy in copies:
+        copy.start()
+    for copy in copies:
+        copy.wait()
+
+
+def gradient_kernel(own_units, other_units, first, second, after_ref, up_ref, down_ref, theirs_ref):
     unit_width, width = up_ref.shape[1:]
-    units = [
+    hidden, pre_grad = [
         jnp.concatenate([own_units[part], other_units[part]], axis=0)
         for part in (pl.ds(0, unit_width), pl.ds(unit_width, unit_width))
     ]
-    for s, pair in enumerate(rows):
-        for t in range(2):
-            down = jnp.dot(units[0], pair[t, :, width:], preferred_element_type=F32).astype(BF16)
-            up = jnp.dot(units[1], pair[t, :, :width], preferred_element_type=F32).astype(BF16)
-            up_ref[2 * s + t] = up[:unit_width]
-            down_ref[2 * s + t] = down[:unit_width]
-            their_up[2 * s + t] = up[unit_width:]
-            their_down[2 * s + t] = down[unit_width:]
-
-
-def layout_kernel(source_ref, own_up, own_down, their_up, their_down, up_ref, down_ref):
-    blocks, unit_width, width = own_up.shape
-    for p in range(2 * blocks):
+    for j, rows in enumerate((first, second)):
+        up = jnp.dot(pre_grad, rows[0, :, :width], preferred_element_type=F32).astype(BF16)
+        down = jnp.dot(hidden, rows[0, :, width:], preferred_element_type=F32).astype(BF16)
+        up_ref[j] = up[:unit_width]
+        down_ref[j] = down[:unit_width]
+        theirs_ref[j, :unit_width] = up[unit_width:]
+        theirs_ref[j, unit_width:] = down[unit_width:]
+
+
+def layout_kernel(source_ref, *refs):
+    groups, (up_ref, down_ref) = (refs[:3], refs[3:6]), refs[6:]
+    blocks, unit_width, width = refs[0].shape
+    for p in range(4 * blocks):
         columns = pl.ds(p * width, width)
         source = source_ref[p]
-
-        @pl.when(source < blocks)
-        def _():
-            up_ref[:, columns] = own_up[source]
-            down_ref[:, columns] = own_down[source]
-
-        @pl.when(source >= blocks)
-        def _():
-            up_ref[:, columns] = their_up[source - blocks]
-            down_ref[:, columns] = their_down[source - blocks]
+        place = source % blocks
+        for g, (own_up, own_down, theirs) in enumerate(groups):
+
+            @pl.when(source // blocks == 2 * g)
+            def _():
+                up_ref[:, columns] = own_up[place]
+                down_ref[:, columns] = own_down[place]
+
+            @pl.when(source // blocks == 2 * g + 1)
+            def _():
+                up_ref[:, columns] = theirs[place, :unit_width]
+                down_ref[:, columns] = theirs[place, unit_width:]
 
 
 def local(tokens, expert_ids, gate_weights, old_up, old_down, old_rows, new_slots, cotangent):
@@ -136,17 +148,20 @@
 
     with jax.named_scope("hidden"):
         parts = jnp.concatenate([partial(up, routed_x), partial(down, routed_back)], axis=1)
-        sums = jnp.sum(exchange(parts, CHIP).astype(F32), axis=0)
+        later_x, parts = lax.optimization_barrier((routed[:, :width], parts))
+        x_y = swap_y(later_x)
+        parts, x_y = lax.optimization_barrier((exchange(parts, CHIP), x_y))
+        sums = jnp.sum(parts.astype(F32), axis=0)
         pre_act, hidden_grad = sums[:unit_width], sums[unit_width:]
         sig = jax.nn.sigmoid(pre_act)
         hidden = jax.nn.silu(pre_act).astype(BF16)
         pre_grad = (hidden_grad * sig * (1.0 + pre_act * (1.0 - sig))).astype(BF16)
         own_units = jnp.concatenate([hidden, pre_grad], axis=0)
         other_units = swap(own_units)
-        early_rows, own_units = lax.optimization_barrier((routed, own_units))
-        rows_y = lax.ppermute(early_rows, "y", [(0, 1), (1, 0)])
+        later_back, own_units = lax.optimization_barrier((routed[:, width:], own_units))
+        back_y = swap_y(later_back)
         units = everywhere(own_units, CHIP)
-        units, rows_y, other_units = lax.optimization_barrier((units, rows_y, other_units))
+        units, back_y, other_units = lax.optimization_barrier((units, back_y, other_units))
         hidden = units[:, :unit_width].reshape(core_units, slot_rows)
         pre_grad = units[:, unit_width:].reshape(core_units, slot_rows)
 
@@ -179,9 +194,10 @@
         pair = pl.pallas_call(
             pair_kernel,
             out_shape=jax.ShapeDtypeStruct((2, slot_rows, 2 * width), BF16),
-            in_specs=[VMEM, VMEM, ANY],
-            out_specs=VMEM,
-        )(routed, rows_y, sent_rows)
+            in_specs=[ANY] * 4,
+            out_specs=ANY,
+            scratch_shapes=[pltpu.SemaphoreType.DMA((3,))],
+        )(routed, x_y, back_y, sent_rows)
         column = lax.axis_size("x")
         pairs = [pair] + [
             lax.ppermute(pair, "x", [(i, (i + s) % column) for i in range(column)])
@@ -189,26 +205,42 @@
         ]
 
     with jax.named_scope("new_slices"):
-        block = jax.ShapeDtypeStruct((chips, unit_width, width), BF16)
-        up_part, down_part, their_up, their_down = pl.pallas_call(
-            gradient_kernel,
-            out_shape=(block,) * 4,
-            in_specs=[VMEM] * 6 + [ANY],
-            out_specs=(VMEM,) * 4,
-            compiler_params=LARGE,
-        )(own_units, other_units, *pairs, own_result)
+        units_spec = pl.BlockSpec((2 * unit_width, slot_rows), lambda t: (0, 0))
+        rows_spec = pl.BlockSpec((1, slot_rows, 2 * width), lambda t: (t, 0, 0))
+        part_spec = pl.BlockSpec((2, unit_width, width), lambda t: (t, 0, 0))
+        part = jax.ShapeDtypeStruct((chips // 2, unit_width, width), BF16)
+        held = []
+        for g in range(2):
+            up_part, down_part, theirs = pl.pallas_call(
+                gradient_kernel,
+                grid=(2,),
+                out_shape=(
+                    part,
+                    part,
+                    jax.ShapeDtypeStruct((chips // 2, 2 * unit_width, width), BF16),
+                ),
+                in_specs=[units_spec, units_spec, rows_spec, rows_spec, ANY],
+                out_specs=(
+                    part_spec,
+                    part_spec,
+                    pl.BlockSpec((2, 2 * unit_width, width), lambda t: (t, 0, 0)),
+                ),
+                compiler_params=LARGE,
+            )(own_units, other_units, *pairs[2 * g : 2 * g + 2], own_result)
+            held += [up_part, down_part, swap(theirs)]
         source = inverse // 2
         back = (lax.axis_index("x") - source % column) % column
-        source = 2 * back + (source // column != lax.axis_index("y")).astype(jnp.int32)
-        source = source + jnp.where(inverse % 2 == core, 0, chips)
+        other_y = (source // column != lax.axis_index("y")).astype(jnp.int32)
+        other_core = (inverse % 2 != core).astype(jnp.int32)
+        source = 8 * (back // 2) + 4 * other_core + 2 * other_y + back % 2
         grad = jax.ShapeDtypeStruct((unit_width, cut_count * width), BF16)
         up_grad, down_grad = pl.pallas_call(
             layout_kernel,
             out_shape=(grad, grad),
-            in_specs=[pl.BlockSpec(memory_space=pltpu.SMEM)] + [VMEM] * 4,
+            in_specs=[pl.BlockSpec(memory_space=pltpu.SMEM)] + [VMEM] * 6,
             out_specs=(VMEM, VMEM),
             compiler_params=LARGE,
-        )(source, up_part, down_part, swap(their_up), swap(their_down))
+        )(source, *held)
     return (result[:, :width], result[:, width:], up_grad, down_grad)
 
 

time: 174 us -> 189 us (1.086)
  blocking collectives: 20.4 us -> 0 us
  Pallas kernels: 5.72 us -> 22.1 us
  starting transfers between devices: 76.7 us -> 91.7 us
  waiting for transfers between devices: 36.6 us -> 42 us
    all_to_all x1 -> x0, blocking collectives: 20.4 us -> none  [exchange(): return lax.all_to_all(parts, axis, split_axis=0, concat_axis=0, tiled=True)]
    pallas_call x1, Pallas kernels: 1.86 us -> 17 us  [local(): pl.pallas_call(pair_kernel, out_shape=jax.ShapeDtypeStruct((2, slot_rows,...]
    ppermute x1 -> x2, waiting for transfers between devices: 11.1 us -> 20.7 us  [swap_y(): return lax.ppermute(block, 'y', [(0, 1), (1, 0)])]
    ppermute x7, starting transfers between devices: 22.9 us -> 31.5 us  [swap(): return lax.ppermute(block, 'core', [(0, 1), (1, 0)])]
    all_to_all x5 -> x6, waiting for transfers between devices: 23.5 us -> 18.3 us  [exchange(): return lax.all_to_all(parts, axis, split_axis=0, concat_axis=0, tiled=True)]
    ppermute x1 -> x2, starting transfers between devices: 4.77 us -> 9.64 us  [swap_y(): return lax.ppermute(block, 'y', [(0, 1), (1, 0)])]
    all_to_all x5 -> x6, starting transfers between devices: 38.5 us -> 41.3 us  [exchange(): return lax.all_to_all(parts, axis, split_axis=0, concat_axis=0, tiled=True)]
    ppermute x3, waiting for transfers between devices: 0.01 us -> 1.99 us  [local(): lax.ppermute(pair, 'x', [(i, (i + s) % column) for i in range(column)])]
  transfers between devices with their start and end apart: 16 -> 18, of which waited for: 7 -> 8; matrix products, arithmetic and copies ran while one was open for 8% -> 7% of each run, Pallas kernels for 2% -> 11%
where the time goes in v6:
time: 189 us; the launch traced here: 186 us
  starting transfers between devices  91.7 us (49%)
  waiting for transfers between devices  42 us (22%)
  Pallas kernels  22.1 us (12%)
  local copies, waits for them, and re-layouts  16.7 us (9%)
  other arithmetic  5.18 us (3%)
  between operations  5.04 us (3%)
  matrix products  3.66 us (2%)
    all_to_all x6, starting transfers between devices, exchange(): return lax.all_to_all(parts, axis, split_axis=0, concat_axis=0, tiled=True)  41.3 us
    ppermute x7, starting transfers between devices, swap(): return lax.ppermute(block, 'core', [(0, 1), (1, 0)])  31.5 us
    ppermute x2, waiting for transfers between devices, swap_y(): return lax.ppermute(block, 'y', [(0, 1), (1, 0)])  20.7 us
    all_to_all x6, waiting for transfers between devices, exchange(): return lax.all_to_all(parts, axis, split_axis=0, concat_axis=0, tiled=True)  18.3 us
    pallas_call x1, Pallas kernels, local(): pl.pallas_call(pair_kernel, out_shape=jax.ShapeDtypeStruct((2, slot_rows,...  17 us
    ppermute x2, starting transfers between devices, swap_y(): return lax.ppermute(block, 'y', [(0, 1), (1, 0)])  9.64 us
    ppermute x3, starting transfers between devices, local(): lax.ppermute(pair, 'x', [(i, (i + s) % column) for i in range(column)])  9.27 us
    unnamed x37, local copies, waits for them, and re-layouts  4.55 us
  transfers between devices with their start and end apart: 18, of which 8 were waited for; matrix products, arithmetic and copies ran while one was open for 7% of the time, Pallas kernels for 11%

profile of v6, /device:TPU:1, one launch (start us, length us, event | category | flops | bytes accessed | tf_op | source)
XLA Modules:
  0.0 186.4 jit_solution(6990065651451048913)
XLA Ops:
  0.7 0.8 pad_maximum_fusion.5
  1.5 0.8 broadcast_in_dim.47
  2.3 10.4 %all-to-all-start = ((bf16[16,32,512]{2,1,0:T(8,128)(2,1)}), bf16[16,32,512]{2,1,0:T(8,128)(2,1)S(1)}, u32[]{:S(2)}, u32[]{:S(2)}) async-start(bf16[16,32,512]{2,1,0:T(8,128)(2,1)} %broadcast_in_dim.47), calls=%async_computation | async-start | bytes 1048576 | tf_op jit(solution)/shard_map/token_blocks/all_to_all | solution.py:17
  13.1 0.2 select_reduce_fusion.1
  13.3 0.6 dynamic_slice.20
  16.2 8.0 %all-to-all-done = bf16[16,32,512]{2,1,0:T(8,128)(2,1)S(1)} async-done(((bf16[16,32,512]{2,1,0:T(8,128)(2,1)}), bf16[16,32,512]{2,1,0:T(8,128)(2,1)S(1)}, u32[]{:S(2)}, u32[]{:S(2)}) %all-to-all-start) | async-done | bytes 524320 | tf_op jit(solution)/shard_map/token_blocks/all_to_all | solution.py:17
  24.2 0.2 fusion.1
  24.5 0.7 broadcast_in_dim.79
  25.2 13.4 %all-to-all-start.1 = ((bf16[32,8,512]{2,1,0:T(8,128)(2,1)}), bf16[32,8,512]{2,1,0:T(8,128)(2,1)S(1)}, u32[]{:S(2)}, u32[]{:S(2)}) async-start(bf16[32,8,512]{2,1,0:T(8,128)(2,1)} %bitcast.3), calls=%async_computation.1 | async-start | bytes 524288 | tf_op jit(solution)/shard_map/dispatch/all_to_all | solution.py:17
  38.7 0.2 dynamic-slice_reduce_fusion.1
  38.9 1.4 gather_fusion.1
  40.3 3.3 %collective-permute-start = (bf16[8,128,256]{2,1,0:T(8,128)(2,1)}, bf16[8,128,256]{2,1,0:T(8,128)(2,1)}, u32[]{:S(2)}, u32[]{:S(2)}) collective-permute-start(bf16[8,128,256]{2,1,0:T(8,128)(2,1)} %gather_fusion.1), channel_id=1, source_target_pairs={{0,1},{1,0},{2,3},{3,2},{4,5},{5,4},{6,7},{7,6},{8,9},{9,8},{10,11... | collective-permute-start | bytes 1572872 | tf_op jit(solution)/shard_map/weights/ppermute | solution.py:25
  43.6 1.4 gather_fusion.3
  44.9 1.9 %collective-permute-start.2 = (bf16[8,128,256]{2,1,0:T(8,128)(2,1)}, bf16[8,128,256]{2,1,0:T(8,128)(2,1)}, u32[]{:S(2)}, u32[]{:S(2)}) collective-permute-start(bf16[8,128,256]{2,1,0:T(8,128)(2,1)} %gather_fusion.3), channel_id=1, source_target_pairs={{0,1},{1,0},{2,3},{3,2},{4,5},{5,4},{6,7},{7,6},{8,9},{9,8},{10,11... | collective-permute-start | bytes 1572872 | tf_op jit(solution)/shard_map/weights/ppermute | solution.py:25
  46.9 0.6 gather_fusion
  47.5 0.6 gather_fusion.2
  48.1 1.1 pad_maximum_fusion
  49.2 8.5 %all-to-all-done.1 = bf16[32,8,512]{2,1,0:T(8,128)(2,1)S(1)} async-done(((bf16[32,8,512]{2,1,0:T(8,128)(2,1)}), bf16[32,8,512]{2,1,0:T(8,128)(2,1)S(1)}, u32[]{:S(2)}, u32[]{:S(2)}) %all-to-all-start.1) | async-done | bytes 262176 | tf_op jit(solution)/shard_map/dispatch/all_to_all | solution.py:17
  57.7 6.1 %collective-permute-start.1 = (bf16[256,512]{1,0:T(8,128)(2,1)S(1)}, bf16[256,512]{1,0:T(8,128)(2,1)S(1)}, u32[]{:S(2)}, u32[]{:S(2)}) collective-permute-start(bf16[256,512]{1,0:T(8,128)(2,1)S(1)} %bitcast.34), channel_id=1, source_target_pairs={{0,1},{1,0},{2,3},{3,2},{4,5},{5,4},{6,7},{7,6},{8,9},{9,8},{10,11... | collective-permute-start | bytes 786440 | tf_op jit(solution)/shard_map/dispatch/ppermute | solution.py:25
  63.8 1.1 pad_maximum_fusion.1
  65.0 0.7 fusion.39
  65.7 0.5 convolution_convert_fusion.1
  66.2 1.4 convolution_convert_fusion
  67.6 1.0 pad_maximum_fusion.2
  68.7 3.6 %all-to-all-start.2 = ((bf16[8,256,256]{2,1,0:T(8,128)(2,1)}), bf16[8,256,256]{2,1,0:T(8,128)(2,1)S(1)}, u32[]{:S(2)}, u32[]{:S(2)}) async-start(bf16[8,256,256]{2,1,0:T(8,128)(2,1)} %pad_maximum_fusion.2), calls=%async_computation.2 | async-start | bytes 2097152 | tf_op jit(solution)/shard_map/hidden/all_to_all | solution.py:17
  72.2 4.8 %collective-permute-start.3 = (bf16[256,256]{1,0:T(8,128)(2,1)S(1)}, bf16[256,256]{1,0:T(8,128)(2,1)S(1)}, u32[]{:S(2)}, u32[]{:S(2)}) collective-permute-start(bf16[256,256]{1,0:T(8,128)(2,1)S(1)} %get-tuple-element.22), channel_id=1, source_target_pairs={{0,8},{8,0},{1,9},{9,1},{2,10},{10,2},{3,11},{11,3},{4,12},{12,4},... | collective-permute-start | bytes 393224 | tf_op jit(solution)/shard_map/hidden/ppermute | solution.py:29
  77.0 13.2 %collective-permute-done.3.x_ref = bf16[256,256]{1,0:T(8,128)(2,1)S(1)} collective-permute-done((bf16[256,256]{1,0:T(8,128)(2,1)S(1)}, bf16[256,256]{1,0:T(8,128)(2,1)S(1)}, u32[]{:S(2)}, u32[]{:S(2)}) %collective-permute-start.3) | collective-permute-done | bytes 131104 | tf_op jit(solution)/shard_map/hidden/ppermute | solution.py:29
  90.2 0.1 convert_reduce_fusion
  90.4 1.0 broadcast_in_dim.80
  91.4 4.4 %all-to-all-start.3 = ((bf16[8,256,256]{2,1,0:T(8,128)(2,1)}), bf16[8,256,256]{2,1,0:T(8,128)(2,1)S(1)}, u32[]{:S(2)}, u32[]{:S(2)}) async-start(bf16[8,256,256]{2,1,0:T(8,128)(2,1)} %broadcast_in_dim.80), calls=%async_computation.3 | async-start | bytes 2097152 | tf_op jit(solution)/shard_map/hidden/all_to_all | solution.py:17
  95.8 4.9 %collective-permute-start.4 = (bf16[256,256]{1,0:T(8,128)(2,1)}, bf16[256,256]{1,0:T(8,128)(2,1)S(1)}, u32[]{:S(2)}, u32[]{:S(2)}) collective-permute-start(bf16[256,256]{1,0:T(8,128)(2,1)} %get-tuple-element.25), channel_id=1, source_target_pairs={{0,8},{8,0},{1,9},{9,1},{2,10},{10,2},{3,11},{11,3},{4,12},{12,4},... | collective-permute-start | bytes 393224 | tf_op jit(solution)/shard_map/hidden/ppermute | solution.py:29
  100.7 3.2 %collective-permute-start.5 = (bf16[256,256]{1,0:T(8,128)(2,1)S(1)}, bf16[256,256]{1,0:T(8,128)(2,1)S(1)}, u32[]{:S(2)}, u32[]{:S(2)}) collective-permute-start(bf16[256,256]{1,0:T(8,128)(2,1)S(1)} %pad_maximum_fusion.4.own_units), channel_id=1, source_target_pairs={{0,1},{1,0},{2,3},{3,2},{4,5},{5,4},{6,7},{7,6},{8,9},{9,8},{10,11... | collective-permute-start | bytes 393224 | tf_op jit(solution)/shard_map/hidden/ppermute | solution.py:25
  103.9 7.5 %collective-permute-done.4.back_ref = bf16[256,256]{1,0:T(8,128)(2,1)S(1)} collective-permute-done((bf16[256,256]{1,0:T(8,128)(2,1)}, bf16[256,256]{1,0:T(8,128)(2,1)S(1)}, u32[]{:S(2)}, u32[]{:S(2)}) %collective-permute-start.4) | collective-permute-done | bytes 131104 | tf_op jit(solution)/shard_map/hidden/ppermute | solution.py:29
  111.4 1.8 all-to-all-done.3
  113.3 1.1 copy-done.10
  114.4 0.3 convolution_convert_fusion.3
  114.7 0.4 convolution_convert_fusion.2
  115.1 3.5 %collective-permute-start.6 = (bf16[256,512]{0,1:T(8,128)(2,1)S(1)}, bf16[256,512]{0,1:T(8,128)(2,1)S(1)}, u32[]{:S(2)}, u32[]{:S(2)}) collective-permute-start(bf16[256,512]{0,1:T(8,128)(2,1)S(1)} %pad_maximum_fusion.3), channel_id=1, source_target_pairs={{0,1},{1,0},{2,3},{3,2},{4,5},{5,4},{6,7},{7,6},{8,9},{9,8},{10,11... | collective-permute-start | bytes 786440 | tf_op jit(solution)/shard_map/give_back/ppermute | solution.py:25
  118.6 0.3 fusion.6
  119.0 0.3 fusion.4
  119.3 0.4 collective-permute-done.6
  119.8 0.8 copy.32
  120.6 3.9 %all-to-all-start.4 = ((bf16[32,8,512]{2,1,0:T(8,128)(2,1)}), bf16[32,8,512]{2,1,0:T(8,128)(2,1)S(1)}, u32[]{:S(2)}, u32[]{:S(2)}) async-start(bf16[32,8,512]{2,1,0:T(8,128)(2,1)} %bitcast.13.after_ref), calls=%async_computation.4 | async-start | bytes 524288 | tf_op jit(solution)/shard_map/give_back/all_to_all | solution.py:17
  124.5 17.0 %all_rows.1.first = bf16[2,256,512]{2,1,0:T(8,128)(2,1)} custom-call(bf16[256,512]{1,0:T(8,128)(2,1)} %bitcast.36, bf16[256,256]{1,0:T(8,128)(2,1)} %copy-done.12, bf16[256,256]{1,0:T(8,128)(2,1)} %copy-done.13, bf16[32,8,512]{2,1,0:T(8,128)(2,1)} %bitcast.13.after_ref), custom_call_target="tpu_custom_call" | custom-call | tf_op jit(solution)/shard_map/all_rows/pallas_call | solution.py:194
  141.6 4.3 %collective-permute-start.10 = (bf16[2,256,512]{2,1,0:T(8,128)(2,1)}, bf16[2,256,512]{2,1,0:T(8,128)(2,1)S(1)}, u32[]{:S(2)}, u32[]{:S(2)}) collective-permute-start(bf16[2,256,512]{2,1,0:T(8,128)(2,1)} %all_rows.1.first), channel_id=1, source_target_pairs={{0,6},{2,0},{4,2},{6,4},{1,7},{3,1},{5,3},{7,5},{8,14},{10,8},{12,... | collective-permute-start | bytes 1572872 | tf_op jit(solution)/shard_map/all_rows/ppermute | solution.py:203
  145.9 2.5 %collective-permute-start.9 = (bf16[2,256,512]{2,1,0:T(8,128)(2,1)}, bf16[2,256,512]{2,1,0:T(8,128)(2,1)S(1)}, u32[]{:S(2)}, u32[]{:S(2)}) collective-permute-start(bf16[2,256,512]{2,1,0:T(8,128)(2,1)} %all_rows.1.first), channel_id=1, source_target_pairs={{0,4},{2,6},{4,0},{6,2},{1,5},{3,7},{5,1},{7,3},{8,12},{10,14},{12... | collective-permute-start | bytes 1572872 | tf_op jit(solution)/shard_map/all_rows/ppermute | solution.py:203
  148.4 2.5 %collective-permute-start.7 = (bf16[2,256,512]{2,1,0:T(8,128)(2,1)}, bf16[2,256,512]{2,1,0:T(8,128)(2,1)S(1)}, u32[]{:S(2)}, u32[]{:S(2)}) collective-permute-start(bf16[2,256,512]{2,1,0:T(8,128)(2,1)} %all_rows.1.first), channel_id=1, source_target_pairs={{0,2},{2,4},{4,6},{6,0},{1,3},{3,5},{5,7},{7,1},{8,10},{10,12},{12... | collective-permute-start | bytes 1572872 | tf_op jit(solution)/shard_map/all_rows/ppermute | solution.py:203
  150.9 0.2 fusion.15
  151.2 0.8 broadcast_in_dim.81
  152.0 5.7 %all-to-all-start.5 = ((bf16[16,32,512]{2,1,0:T(8,128)(2,1)}), bf16[16,32,512]{2,1,0:T(8,128)(2,1)}, u32[]{:S(2)}, u32[]{:S(2)}) async-start(bf16[16,32,512]{2,1,0:T(8,128)(2,1)} %broadcast_in_dim.81), calls=%async_computation.5 | async-start | bytes 1048576 | tf_op jit(solution)/shard_map/result/all_to_all | solution.py:17
  157.8 0.6 dynamic_slice.24
  160.3 2.0 %collective-permute-done.9.first = bf16[2,256,512]{2,1,0:T(8,128)(2,1)S(1)} collective-permute-done((bf16[2,256,512]{2,1,0:T(8,128)(2,1)}, bf16[2,256,512]{2,1,0:T(8,128)(2,1)S(1)}, u32[]{:S(2)}, u32[]{:S(2)}) %collective-permute-start.9) | collective-permute-done | bytes 524320 | tf_op jit(solution)/shard_map/all_rows/ppermute | solution.py:203
  162.3 1.3 new_slices.4
  163.7 0.7 copy-done.2
  164.3 11.6 %collective-permute-start.11 = (bf16[4,256,256]{2,1,0:T(8,128)(2,1)}, bf16[4,256,256]{2,1,0:T(8,128)(2,1)S(1)}, u32[]{:S(2)}, u32[]{:S(2)}) collective-permute-start(bf16[4,256,256]{2,1,0:T(8,128)(2,1)} %get-tuple-element.35), channel_id=1, source_target_pairs={{0,1},{1,0},{2,3},{3,2},{4,5},{5,4},{6,7},{7,6},{8,9},{9,8},{10,11... | collective-permute-start | bytes 1572872 | tf_op jit(solution)/shard_map/new_slices/ppermute | solution.py:25
  176.0 1.3 new_slices.3
  177.4 0.7 copy-done.6
  178.1 1.9 %collective-permute-start.8 = (bf16[4,256,256]{2,1,0:T(8,128)(2,1)}, bf16[4,256,256]{2,1,0:T(8,128)(2,1)S(1)}, u32[]{:S(2)}, u32[]{:S(2)}) collective-permute-start(bf16[4,256,256]{2,1,0:T(8,128)(2,1)} %get-tuple-element.32), channel_id=1, source_target_pairs={{0,1},{1,0},{2,3},{3,2},{4,5},{5,4},{6,7},{7,6},{8,9},{9,8},{10,11... | collective-permute-start | bytes 1572872 | tf_op jit(solution)/shard_map/new_slices/ppermute | solution.py:25
  180.1 0.8 dynamic-slice_bitcast_fusion
  180.8 0.6 fusion.40
  181.4 0.6 collective-permute-done.8.refs_2_
  182.1 0.9 copy-done.5
  183.0 0.9 copy-done.7
  184.0 2.4 %new_slices.5 = (bf16[128,4096]{1,0:T(8,128)(2,1)}, bf16[128,4096]{1,0:T(8,128)(2,1)}) custom-call(s32[16]{0:T(128)S(1)} %fusion.30.source_ref, bf16[4,128,256]{2,1,0:T(8,128)(2,1)S(1)} %get-tuple-element.30.refs_0_, bf16[4,128,256]{2,1,0:T(8,128)(2,1)S(1)} %copy-done.7, bf16[4,256,256]{2,1,0:T(8,128)(2,1)S(1)} %collective-permute-done.8.refs_2_, ...), custom_call_target="tpu_custom_call" | custom-call | tf_op jit(solution)/shard_map/new_slices/pallas_call | solution.py:237
  (65 shorter events, 1.4 us)
Async XLA Ops:
  0.6 38.3 %copy-start = (bf16[2048,256]{1,0:T(8,128)(2,1)S(1)}, bf16[2048,256]{1,0:T(8,128)(2,1)}, u32[]{:S(2)}) copy-start(bf16[2048,256]{1,0:T(8,128)(2,1)} %param.11) | copy-start | bytes 3145732
  0.6 12.1 %copy-start.15 = (s32[32,2]{0,1:T(2,128)S(1)}, s32[32,2]{0,1:T(2,128)}, u32[]{:S(2)}) copy-start(s32[32,2]{0,1:T(2,128)} %param.9) | copy-start | bytes 772
  0.7 12.6 %copy-start.17 = (s32[16]{0:T(128)S(1)}, s32[16]{0:T(128)}, u32[]{:S(2)}) copy-start(s32[16]{0:T(128)} %param.13) | copy-start | bytes 196
  0.7 15.5 %copy-start.14 = (f32[32,2]{0,1:T(2,128)S(1)}, f32[32,2]{0,1:T(2,128)}, u32[]{:S(2)}) copy-start(f32[32,2]{0,1:T(2,128)} %param.10) | copy-start | bytes 772
  2.3 36.3 %copy-start.16 = (s32[16]{0:T(128)S(1)}, s32[16]{0:T(128)}, u32[]{:S(2)}) copy-start(s32[16]{0:T(128)} %param.14) | copy-start | bytes 196
  2.3 21.9 %all-to-all-start = ((bf16[16,32,512]{2,1,0:T(8,128)(2,1)}), bf16[16,32,512]{2,1,0:T(8,128)(2,1)S(1)}, u32[]{:S(2)}, u32[]{:S(2)}) async-start(bf16[16,32,512]{2,1,0:T(8,128)(2,1)} %broadcast_in_dim.47), calls=%async_computation | async-start | bytes 1048576 | tf_op jit(solution)/shard_map/token_blocks/all_to_all | solution.py:17
  24.4 19.1 %copy-start.11 = (bf16[2048,256]{1,0:T(8,128)(2,1)S(1)}, bf16[2048,256]{1,0:T(8,128)(2,1)}, u32[]{:S(2)}) copy-start(bf16[2048,256]{1,0:T(8,128)(2,1)} %param.12) | copy-start | bytes 3145732
  25.2 32.5 %all-to-all-start.1 = ((bf16[32,8,512]{2,1,0:T(8,128)(2,1)}), bf16[32,8,512]{2,1,0:T(8,128)(2,1)S(1)}, u32[]{:S(2)}, u32[]{:S(2)}) async-start(bf16[32,8,512]{2,1,0:T(8,128)(2,1)} %bitcast.3), calls=%async_computation.1 | async-start | bytes 524288 | tf_op jit(solution)/shard_map/dispatch/all_to_all | solution.py:17
  40.3 7.8 %collective-permute-start = (bf16[8,128,256]{2,1,0:T(8,128)(2,1)}, bf16[8,128,256]{2,1,0:T(8,128)(2,1)}, u32[]{:S(2)}, u32[]{:S(2)}) collective-permute-start(bf16[8,128,256]{2,1,0:T(8,128)(2,1)} %gather_fusion.1), channel_id=1, source_target_pairs={{0,1},{1,0},{2,3},{3,2},{4,5},{5,4},{6,7},{7,6},{8,9},{9,8},{10,11... | collective-permute-start | bytes 1572872 | tf_op jit(solution)/shard_map/weights/ppermute | solution.py:25
  44.9 18.9 %collective-permute-start.2 = (bf16[8,128,256]{2,1,0:T(8,128)(2,1)}, bf16[8,128,256]{2,1,0:T(8,128)(2,1)}, u32[]{:S(2)}, u32[]{:S(2)}) collective-permute-start(bf16[8,128,256]{2,1,0:T(8,128)(2,1)} %gather_fusion.3), channel_id=1, source_target_pairs={{0,1},{1,0},{2,3},{3,2},{4,5},{5,4},{6,7},{7,6},{8,9},{9,8},{10,11... | collective-permute-start | bytes 1572872 | tf_op jit(solution)/shard_map/weights/ppermute | solution.py:25
  57.7 7.3 %copy-start.8 = (bf16[32,8,512]{2,1,0:T(8,128)(2,1)}, bf16[32,8,512]{2,1,0:T(8,128)(2,1)S(1)}, u32[]{:S(2)}) copy-start(bf16[32,8,512]{2,1,0:T(8,128)(2,1)S(1)} %all-to-all-done.1) | copy-start | bytes 786436
  57.7 8.0 %collective-permute-start.1 = (bf16[256,512]{1,0:T(8,128)(2,1)S(1)}, bf16[256,512]{1,0:T(8,128)(2,1)S(1)}, u32[]{:S(2)}, u32[]{:S(2)}) collective-permute-start(bf16[256,512]{1,0:T(8,128)(2,1)S(1)} %bitcast.34), channel_id=1, source_target_pairs={{0,1},{1,0},{2,3},{3,2},{4,5},{5,4},{6,7},{7,6},{8,9},{9,8},{10,11... | collective-permute-start | bytes 786440 | tf_op jit(solution)/shard_map/dispatch/ppermute | solution.py:25
  65.0 1.2 copy-start.9
  68.7 21.5 %all-to-all-start.2 = ((bf16[8,256,256]{2,1,0:T(8,128)(2,1)}), bf16[8,256,256]{2,1,0:T(8,128)(2,1)S(1)}, u32[]{:S(2)}, u32[]{:S(2)}) async-start(bf16[8,256,256]{2,1,0:T(8,128)(2,1)} %pad_maximum_fusion.2), calls=%async_computation.2 | async-start | bytes 2097152 | tf_op jit(solution)/shard_map/hidden/all_to_all | solution.py:17
  72.2 17.9 %collective-permute-start.3 = (bf16[256,256]{1,0:T(8,128)(2,1)S(1)}, bf16[256,256]{1,0:T(8,128)(2,1)S(1)}, u32[]{:S(2)}, u32[]{:S(2)}) collective-permute-start(bf16[256,256]{1,0:T(8,128)(2,1)S(1)} %get-tuple-element.22), channel_id=1, source_target_pairs={{0,8},{8,0},{1,9},{9,1},{2,10},{10,2},{3,11},{11,3},{4,12},{12,4},... | collective-permute-start | bytes 393224 | tf_op jit(solution)/shard_map/hidden/ppermute | solution.py:29
  90.2 1.3 copy-start.12
  91.4 21.7 %all-to-all-start.3 = ((bf16[8,256,256]{2,1,0:T(8,128)(2,1)}), bf16[8,256,256]{2,1,0:T(8,128)(2,1)S(1)}, u32[]{:S(2)}, u32[]{:S(2)}) async-start(bf16[8,256,256]{2,1,0:T(8,128)(2,1)} %broadcast_in_dim.80), calls=%async_computation.3 | async-start | bytes 2097152 | tf_op jit(solution)/shard_map/hidden/all_to_all | solution.py:17
  95.8 15.6 %collective-permute-start.4 = (bf16[256,256]{1,0:T(8,128)(2,1)}, bf16[256,256]{1,0:T(8,128)(2,1)S(1)}, u32[]{:S(2)}, u32[]{:S(2)}) collective-permute-start(bf16[256,256]{1,0:T(8,128)(2,1)} %get-tuple-element.25), channel_id=1, source_target_pairs={{0,8},{8,0},{1,9},{9,1},{2,10},{10,2},{3,11},{11,3},{4,12},{12,4},... | collective-permute-start | bytes 393224 | tf_op jit(solution)/shard_map/hidden/ppermute | solution.py:29
  100.7 10.7 %collective-permute-start.5 = (bf16[256,256]{1,0:T(8,128)(2,1)S(1)}, bf16[256,256]{1,0:T(8,128)(2,1)S(1)}, u32[]{:S(2)}, u32[]{:S(2)}) collective-permute-start(bf16[256,256]{1,0:T(8,128)(2,1)S(1)} %pad_maximum_fusion.4.own_units), channel_id=1, source_target_pairs={{0,1},{1,0},{2,3},{3,2},{4,5},{5,4},{6,7},{7,6},{8,9},{9,8},{10,11... | collective-permute-start | bytes 393224 | tf_op jit(solution)/shard_map/hidden/ppermute | solution.py:25
  111.4 1.9 %copy-start.13 = (bf16[256,256]{1,0:T(8,128)(2,1)}, bf16[256,256]{1,0:T(8,128)(2,1)S(1)}, u32[]{:S(2)}) copy-start(bf16[256,256]{1,0:T(8,128)(2,1)S(1)} %collective-permute-done.4.back_ref) | copy-start | bytes 393220
  113.1 1.2 copy-start.10
  115.1 4.6 %collective-permute-start.6 = (bf16[256,512]{0,1:T(8,128)(2,1)S(1)}, bf16[256,512]{0,1:T(8,128)(2,1)S(1)}, u32[]{:S(2)}, u32[]{:S(2)}) collective-permute-start(bf16[256,512]{0,1:T(8,128)(2,1)S(1)} %pad_maximum_fusion.3), channel_id=1, source_target_pairs={{0,1},{1,0},{2,3},{3,2},{4,5},{5,4},{6,7},{7,6},{8,9},{9,8},{10,11... | collective-permute-start | bytes 786440 | tf_op jit(solution)/shard_map/give_back/ppermute | solution.py:25
  120.6 30.2 %all-to-all-start.4 = ((bf16[32,8,512]{2,1,0:T(8,128)(2,1)}), bf16[32,8,512]{2,1,0:T(8,128)(2,1)S(1)}, u32[]{:S(2)}, u32[]{:S(2)}) async-start(bf16[32,8,512]{2,1,0:T(8,128)(2,1)} %bitcast.13.after_ref), calls=%async_computation.4 | async-start | bytes 524288 | tf_op jit(solution)/shard_map/give_back/all_to_all | solution.py:17
  141.6 18.8 %collective-permute-start.10 = (bf16[2,256,512]{2,1,0:T(8,128)(2,1)}, bf16[2,256,512]{2,1,0:T(8,128)(2,1)S(1)}, u32[]{:S(2)}, u32[]{:S(2)}) collective-permute-start(bf16[2,256,512]{2,1,0:T(8,128)(2,1)} %all_rows.1.first), channel_id=1, source_target_pairs={{0,6},{2,0},{4,2},{6,4},{1,7},{3,1},{5,3},{7,5},{8,14},{10,8},{12,... | collective-permute-start | bytes 1572872 | tf_op jit(solution)/shard_map/all_rows/ppermute | solution.py:203
  145.9 16.5 %collective-permute-start.9 = (bf16[2,256,512]{2,1,0:T(8,128)(2,1)}, bf16[2,256,512]{2,1,0:T(8,128)(2,1)S(1)}, u32[]{:S(2)}, u32[]{:S(2)}) collective-permute-start(bf16[2,256,512]{2,1,0:T(8,128)(2,1)} %all_rows.1.first), channel_id=1, source_target_pairs={{0,4},{2,6},{4,0},{6,2},{1,5},{3,7},{5,1},{7,3},{8,12},{10,14},{12... | collective-permute-start | bytes 1572872 | tf_op jit(solution)/shard_map/all_rows/ppermute | solution.py:203
  148.4 27.6 %collective-permute-start.7 = (bf16[2,256,512]{2,1,0:T(8,128)(2,1)}, bf16[2,256,512]{2,1,0:T(8,128)(2,1)S(1)}, u32[]{:S(2)}, u32[]{:S(2)}) collective-permute-start(bf16[2,256,512]{2,1,0:T(8,128)(2,1)} %all_rows.1.first), channel_id=1, source_target_pairs={{0,2},{2,4},{4,6},{6,0},{1,3},{3,5},{5,7},{7,1},{8,10},{10,12},{12... | collective-permute-start | bytes 1572872 | tf_op jit(solution)/shard_map/all_rows/ppermute | solution.py:203
  152.0 24.0 %copy-start.1 = (bf16[2,256,512]{2,1,0:T(8,128)(2,1)S(1)}, bf16[2,256,512]{2,1,0:T(8,128)(2,1)}, u32[]{:S(2)}) copy-start(bf16[2,256,512]{2,1,0:T(8,128)(2,1)} %all_rows.1.first) | copy-start | bytes 1572868
  152.0 28.1 %all-to-all-start.5 = ((bf16[16,32,512]{2,1,0:T(8,128)(2,1)}), bf16[16,32,512]{2,1,0:T(8,128)(2,1)}, u32[]{:S(2)}, u32[]{:S(2)}) async-start(bf16[16,32,512]{2,1,0:T(8,128)(2,1)} %broadcast_in_dim.81), calls=%async_computation.5 | async-start | bytes 1048576 | tf_op jit(solution)/shard_map/result/all_to_all | solution.py:17
  163.6 0.7 copy-start.2
  164.3 13.0 %copy-start.4 = (bf16[4,128,256]{2,1,0:T(8,128)(2,1)}, bf16[4,128,256]{2,1,0:T(8,128)(2,1)S(1)}, u32[]{:S(2)}) copy-start(bf16[4,128,256]{2,1,0:T(8,128)(2,1)S(1)} %get-tuple-element.34.refs_4_) | copy-start | bytes 786436
  164.3 17.7 %copy-start.3 = (bf16[4,128,256]{2,1,0:T(8,128)(2,1)S(1)}, bf16[4,128,256]{2,1,0:T(8,128)(2,1)}, u32[]{:S(2)}) copy-start(bf16[4,128,256]{2,1,0:T(8,128)(2,1)} %copy-done.2) | copy-start | bytes 786436
  164.3 17.1 %collective-permute-start.11 = (bf16[4,256,256]{2,1,0:T(8,128)(2,1)}, bf16[4,256,256]{2,1,0:T(8,128)(2,1)S(1)}, u32[]{:S(2)}, u32[]{:S(2)}) collective-permute-start(bf16[4,256,256]{2,1,0:T(8,128)(2,1)} %get-tuple-element.35), channel_id=1, source_target_pairs={{0,1},{1,0},{2,3},{3,2},{4,5},{5,4},{6,7},{7,6},{8,9},{9,8},{10,11... | collective-permute-start | bytes 1572872 | tf_op jit(solution)/shard_map/new_slices/ppermute | solution.py:25
  177.4 0.7 copy-start.6
  178.1 4.0 %collective-permute-start.8 = (bf16[4,256,256]{2,1,0:T(8,128)(2,1)}, bf16[4,256,256]{2,1,0:T(8,128)(2,1)S(1)}, u32[]{:S(2)}, u32[]{:S(2)}) collective-permute-start(bf16[4,256,256]{2,1,0:T(8,128)(2,1)} %get-tuple-element.32), channel_id=1, source_target_pairs={{0,1},{1,0},{2,3},{3,2},{4,5},{5,4},{6,7},{7,6},{8,9},{9,8},{10,11... | collective-permute-start | bytes 1572872 | tf_op jit(solution)/shard_map/new_slices/ppermute | solution.py:25
  182.1 1.0 copy-start.5
  183.0 0.9 copy-start.7

commit v7 on v6

--- a/solution.py
+++ b/solution.py
@@ -25,29 +25,12 @@
     return lax.ppermute(block, "core", [(0, 1), (1, 0)])
 
 
-def swap_y(block):
-    return lax.ppermute(block, "y", [(0, 1), (1, 0)])
-
-
 def pick(blocks, index):
     return lax.dynamic_index_in_dim(blocks, index, axis=0, keepdims=False)
 
 
 def rows_at(blocks, places):
     return jnp.take(blocks, places, axis=0, mode="clip")
-
-
-def pair_kernel(own_ref, x_ref, back_ref, after_ref, pair_ref, sems):
-    width = x_ref.shape[1]
-    copies = [
-        pltpu.make_async_copy(own_ref, pair_ref.at[0], sems.at[0]),
-        pltpu.make_async_copy(x_ref, pair_ref.at[1, :, pl.ds(0, width)], sems.at[1]),
-        pltpu.make_async_copy(back_ref, pair_ref.at[1, :, pl.ds(width, width)], sems.at[2]),
-    ]
-    for copy in copies:
-        copy.start()
-    for copy in copies:
-        copy.wait()
 
 
 def gradient_kernel(own_units, other_units, first, second, after_ref, up_ref, down_ref, theirs_ref):
@@ -148,20 +131,17 @@
 
     with jax.named_scope("hidden"):
         parts = jnp.concatenate([partial(up, routed_x), partial(down, routed_back)], axis=1)
-        later_x, parts = lax.optimization_barrier((routed[:, :width], parts))
-        x_y = swap_y(later_x)
-        parts, x_y = lax.optimization_barrier((exchange(parts, CHIP), x_y))
-        sums = jnp.sum(parts.astype(F32), axis=0)
+        sums = jnp.sum(exchange(parts, CHIP).astype(F32), axis=0)
         pre_act, hidden_grad = sums[:unit_width], sums[unit_width:]
         sig = jax.nn.sigmoid(pre_act)
         hidden = jax.nn.silu(pre_act).astype(BF16)
         pre_grad = (hidden_grad * sig * (1.0 + pre_act * (1.0 - sig))).astype(BF16)
         own_units = jnp.concatenate([hidden, pre_grad], axis=0)
         other_units = swap(own_units)
-        later_back, own_units = lax.optimization_barrier((routed[:, width:], own_units))
-        back_y = swap_y(later_back)
+        later_rows, own_units = lax.optimization_barrier((routed, own_units))
+        rows_y = lax.ppermute(later_rows, "y", [(0, 1), (1, 0)])
         units = everywhere(own_units, CHIP)
-        units, back_y, other_units = lax.optimization_barrier((units, back_y, other_units))
+        units, rows_y, other_units = lax.optimization_barrier((units, rows_y, other_units))
         hidden = units[:, :unit_width].reshape(core_units, slot_rows)
         pre_grad = units[:, unit_width:].reshape(core_units, slot_rows)
 
@@ -191,13 +171,7 @@
         result = pick(everywhere(own_result, CUTS), pick(inverse, cut))
 
     with jax.named_scope("all_rows"):
-        pair = pl.pallas_call(
-            pair_kernel,
-            out_shape=jax.ShapeDtypeStruct((2, slot_rows, 2 * width), BF16),
-            in_specs=[ANY] * 4,
-            out_specs=ANY,
-            scratch_shapes=[pltpu.SemaphoreType.DMA((3,))],
-        )(routed, x_y, back_y, sent_rows)
+        pair = jnp.stack(lax.optimization_barrier((routed, rows_y, sent_rows))[:2])
         column = lax.axis_size("x")
         pairs = [pair] + [
             lax.ppermute(pair, "x", [(i, (i + s) % column) for i in range(column)])

time: 189 us -> 173 us (0.915)
  blocking collectives: 0 us -> 20.4 us
  Pallas kernels: 22.1 us -> 5.15 us
  starting transfers between devices: 91.7 us -> 75.4 us
    all_to_all x0 -> x1, blocking collectives: none -> 20.4 us  [exchange(): return lax.all_to_all(parts, axis, split_axis=0, concat_axis=0, tiled=True)]
    pallas_call x1 -> x0, Pallas kernels: 17 us -> none  [local(): pl.pallas_call(pair_kernel, out_shape=jax.ShapeDtypeStruct((2, slot_rows,...]
    ppermute x2 -> x1, waiting for transfers between devices: 20.7 us -> 11 us  [local(): rows_y = lax.ppermute(later_rows, 'y', [(0, 1), (1, 0)])]
    all_to_all x6 -> x5, waiting for transfers between devices: 18.3 us -> 27.8 us  [exchange(): return lax.all_to_all(parts, axis, split_axis=0, concat_axis=0, tiled=True)]
    ppermute x7, starting transfers between devices: 31.5 us -> 22.3 us  [swap(): return lax.ppermute(block, 'core', [(0, 1), (1, 0)])]
    ppermute x2 -> x1, starting transfers between devices: 9.64 us -> 4.78 us  [local(): rows_y = lax.ppermute(later_rows, 'y', [(0, 1), (1, 0)])]
    all_to_all x6 -> x5, starting transfers between devices: 41.3 us -> 38.5 us  [exchange(): return lax.all_to_all(parts, axis, split_axis=0, concat_axis=0, tiled=True)]
    ppermute x3, waiting for transfers between devices: 1.99 us -> 0.01 us  [local(): lax.ppermute(pair, 'x', [(i, (i + s) % column) for i in range(column)])]
  transfers between devices with their start and end apart: 18 -> 16, of which waited for: 8 -> 7; matrix products, arithmetic and copies ran while one was open for 7% -> 8% of each run, Pallas kernels for 11% -> 2%
where the time goes in v7:
time: 173 us; the launch traced here: 172 us
  starting transfers between devices  75.4 us (44%)
  waiting for transfers between devices  40.2 us (23%)
  blocking collectives  20.4 us (12%)
  local copies, waits for them, and re-layouts  16.6 us (10%)
  other arithmetic  5.22 us (3%)
  Pallas kernels  5.15 us (3%)
  between operations  5.05 us (3%)
  matrix products  3.71 us (2%)
    all_to_all x5, starting transfers between devices, exchange(): return lax.all_to_all(parts, axis, split_axis=0, concat_axis=0, tiled=True)  38.5 us
    all_to_all x5, waiting for transfers between devices, exchange(): return lax.all_to_all(parts, axis, split_axis=0, concat_axis=0, tiled=True)  27.8 us
    ppermute x7, starting transfers between devices, swap(): return lax.ppermute(block, 'core', [(0, 1), (1, 0)])  22.3 us
    all_to_all x1, blocking collectives, exchange(): return lax.all_to_all(parts, axis, split_axis=0, concat_axis=0, tiled=True)  20.4 us
    ppermute x1, waiting for transfers between devices, local(): rows_y = lax.ppermute(later_rows, 'y', [(0, 1), (1, 0)])  11 us
    ppermute x3, starting transfers between devices, local(): lax.ppermute(pair, 'x', [(i, (i + s) % column) for i in range(column)])  9.88 us
    ppermute x1, starting transfers between devices, local(): rows_y = lax.ppermute(later_rows, 'y', [(0, 1), (1, 0)])  4.78 us
    unnamed x29, local copies, waits for them, and re-layouts  4.69 us
  transfers between devices with their start and end apart: 16, of which 7 were waited for; matrix products, arithmetic and copies ran while one was open for 8% of the time, Pallas kernels for 2%

profile of v7, /device:TPU:1, one launch (start us, length us, event | category | flops | bytes accessed | tf_op | source)
XLA Modules:
  0.0 171.7 jit_solution(14747573722023927109)
XLA Ops:
  0.7 0.8 pad_maximum_fusion.6
  1.5 0.8 broadcast_in_dim.47
  2.3 10.4 %all-to-all-start = ((bf16[16,32,512]{2,1,0:T(8,128)(2,1)}), bf16[16,32,512]{2,1,0:T(8,128)(2,1)S(1)}, u32[]{:S(2)}, u32[]{:S(2)}) async-start(bf16[16,32,512]{2,1,0:T(8,128)(2,1)} %broadcast_in_dim.47), calls=%async_computation | async-start | bytes 1048576 | tf_op jit(solution)/shard_map/token_blocks/all_to_all | solution.py:17
  12.7 0.1 copy.30
  12.8 0.1 eq.66
  13.0 0.1 reduce_window_sum.11
  13.1 0.2 select_reduce_fusion.1
  13.3 0.6 dynamic_slice.20
  15.2 0.1 reduce_sum.57
  16.1 0.1 select_reduce_fusion
  16.2 8.0 %all-to-all-done = bf16[16,32,512]{2,1,0:T(8,128)(2,1)S(1)} async-done(((bf16[16,32,512]{2,1,0:T(8,128)(2,1)}), bf16[16,32,512]{2,1,0:T(8,128)(2,1)S(1)}, u32[]{:S(2)}, u32[]{:S(2)}) %all-to-all-start) | async-done | bytes 524320 | tf_op jit(solution)/shard_map/token_blocks/all_to_all | solution.py:17
  24.2 0.2 fusion.1
  24.5 0.7 broadcast_in_dim.79
  25.2 13.4 %all-to-all-start.1 = ((bf16[32,8,512]{2,1,0:T(8,128)(2,1)}), bf16[32,8,512]{2,1,0:T(8,128)(2,1)S(1)}, u32[]{:S(2)}, u32[]{:S(2)}) async-start(bf16[32,8,512]{2,1,0:T(8,128)(2,1)} %bitcast.3), calls=%async_computation.1 | async-start | bytes 524288 | tf_op jit(solution)/shard_map/dispatch/all_to_all | solution.py:17
  38.7 0.2 dynamic-slice_reduce_fusion.1
  38.9 1.4 gather_fusion.1
  40.3 3.3 %collective-permute-start = (bf16[8,128,256]{2,1,0:T(8,128)(2,1)}, bf16[8,128,256]{2,1,0:T(8,128)(2,1)}, u32[]{:S(2)}, u32[]{:S(2)}) collective-permute-start(bf16[8,128,256]{2,1,0:T(8,128)(2,1)} %gather_fusion.1), channel_id=1, source_target_pairs={{0,1},{1,0},{2,3},{3,2},{4,5},{5,4},{6,7},{7,6},{8,9},{9,8},{10,11... | collective-permute-start | bytes 1572872 | tf_op jit(solution)/shard_map/weights/ppermute | solution.py:25
  43.6 0.6 gather_fusion.3
  44.2 1.9 %collective-permute-start.2 = (bf16[8,128,256]{2,1,0:T(8,128)(2,1)S(1)}, bf16[8,128,256]{2,1,0:T(8,128)(2,1)}, u32[]{:S(2)}, u32[]{:S(2)}) collective-permute-start(bf16[8,128,256]{2,1,0:T(8,128)(2,1)S(1)} %gather_fusion.3), channel_id=1, source_target_pairs={{0,1},{1,0},{2,3},{3,2},{4,5},{5,4},{6,7},{7,6},{8,9},{9,8},{10,11... | collective-permute-start | bytes 1572872 | tf_op jit(solution)/shard_map/weights/ppermute | solution.py:25
  46.1 0.6 gather_fusion
  46.7 1.8 %gather_fusion.2 = bf16[8,128,256]{2,1,0:T(8,128)(2,1)S(1)} fusion(bf16[16,128,256]{2,1,0:T(8,128)(2,1)} %bitcast.46, s32[1024]{0:T(1024)S(1)} %pad_clamp_fusion.1), kind=kCustom, calls=%fused_computation.2 | custom fusion | bytes 1048608 | tf_op jit(solution)/shard_map/weights/jit(_take)/gather | solution.py:33
  48.5 2.1 %pad_maximum_fusion = bf16[8,128,512]{2,1,0:T(8,128)(2,1)} fusion(bf16[8,128,256]{2,1,0:T(8,128)(2,1)} %collective-permute-done, bf16[8,128,256]{2,1,0:T(8,128)(2,1)S(1)} %gather_fusion), kind=kLoop, calls=%fused_computation.12 | loop fusion | flops 2097152 | bytes 2097152 | tf_op jit(solution)/shard_map/weights/concatenate | solution.py:94
  50.6 7.1 %all-to-all-done.1 = bf16[32,8,512]{2,1,0:T(8,128)(2,1)S(1)} async-done(((bf16[32,8,512]{2,1,0:T(8,128)(2,1)}), bf16[32,8,512]{2,1,0:T(8,128)(2,1)S(1)}, u32[]{:S(2)}, u32[]{:S(2)}) %all-to-all-start.1) | async-done | bytes 262176 | tf_op jit(solution)/shard_map/dispatch/all_to_all | solution.py:17
  57.7 6.1 %collective-permute-start.1 = (bf16[256,512]{1,0:T(8,128)(2,1)S(1)}, bf16[256,512]{1,0:T(8,128)(2,1)S(1)}, u32[]{:S(2)}, u32[]{:S(2)}) collective-permute-start(bf16[256,512]{1,0:T(8,128)(2,1)S(1)} %bitcast.36), channel_id=1, source_target_pairs={{0,1},{1,0},{2,3},{3,2},{4,5},{5,4},{6,7},{7,6},{8,9},{9,8},{10,11... | collective-permute-start | bytes 786440 | tf_op jit(solution)/shard_map/dispatch/ppermute | solution.py:25
  63.8 1.1 pad_maximum_fusion.1
  65.1 1.5 copy-done.5
  66.6 0.5 convolution_convert_fusion.1
  67.1 0.5 convolution_convert_fusion
  67.6 20.4 %all_to_all.30 = bf16[8,256,256]{2,1,0:T(8,128)(2,1)S(1)} all-to-all(bf16[8,256,256]{2,1,0:T(8,128)(2,1)S(1)} %pad_maximum_fusion.2), channel_id=1, replica_groups=mesh['expert'=32,'y'=2,'x'=4,'core'=2] {'y','x'}, dimensions={0} | all-to-all | bytes 2097152 | tf_op jit(solution)/shard_map/hidden/all_to_all | solution.py:17
  88.0 0.1 convert_reduce_fusion
  88.2 1.0 broadcast_in_dim.80
  89.3 3.6 %all-to-all-start.3 = ((bf16[8,256,256]{2,1,0:T(8,128)(2,1)}), bf16[8,256,256]{2,1,0:T(8,128)(2,1)S(1)}, u32[]{:S(2)}, u32[]{:S(2)}) async-start(bf16[8,256,256]{2,1,0:T(8,128)(2,1)} %broadcast_in_dim.80), calls=%async_computation.3 | async-start | bytes 2097152 | tf_op jit(solution)/shard_map/hidden/all_to_all | solution.py:17
  92.8 4.8 %collective-permute-start.3 = (bf16[256,512]{1,0:T(8,128)(2,1)S(1)}, bf16[256,512]{1,0:T(8,128)(2,1)S(1)}, u32[]{:S(2)}, u32[]{:S(2)}) collective-permute-start(bf16[256,512]{1,0:T(8,128)(2,1)S(1)} %bitcast.38), channel_id=1, source_target_pairs={{0,8},{8,0},{1,9},{9,1},{2,10},{10,2},{3,11},{11,3},{4,12},{12,4},... | collective-permute-start | bytes 786440 | tf_op jit(solution)/shard_map/hidden/ppermute | solution.py:142
  97.6 3.3 %collective-permute-start.4 = (bf16[256,256]{1,0:T(8,128)(2,1)S(1)}, bf16[256,256]{1,0:T(8,128)(2,1)S(1)}, u32[]{:S(2)}, u32[]{:S(2)}) collective-permute-start(bf16[256,256]{1,0:T(8,128)(2,1)S(1)} %pad_maximum_fusion.5.own_units), channel_id=1, source_target_pairs={{0,1},{1,0},{2,3},{3,2},{4,5},{5,4},{6,7},{7,6},{8,9},{9,8},{10,11... | collective-permute-start | bytes 393224 | tf_op jit(solution)/shard_map/hidden/ppermute | solution.py:25
  100.9 1.0 collective-permute-done.4.other_units
  101.9 11.0 %collective-permute-done.3 = bf16[256,512]{1,0:T(8,128)(2,1)S(1)} collective-permute-done((bf16[256,512]{1,0:T(8,128)(2,1)S(1)}, bf16[256,512]{1,0:T(8,128)(2,1)S(1)}, u32[]{:S(2)}, u32[]{:S(2)}) %collective-permute-start.3) | collective-permute-done | bytes 262176 | tf_op jit(solution)/shard_map/hidden/ppermute | solution.py:142
  112.9 0.1 fusion.37
  113.0 1.1 copy-done.8
  114.2 0.3 convolution_convert_fusion.3
  114.5 0.4 convolution_convert_fusion.2
  114.9 3.4 %collective-permute-start.5 = (bf16[256,512]{0,1:T(8,128)(2,1)S(1)}, bf16[256,512]{0,1:T(8,128)(2,1)S(1)}, u32[]{:S(2)}, u32[]{:S(2)}) collective-permute-start(bf16[256,512]{0,1:T(8,128)(2,1)S(1)} %pad_maximum_fusion.4), channel_id=1, source_target_pairs={{0,1},{1,0},{2,3},{3,2},{4,5},{5,4},{6,7},{7,6},{8,9},{9,8},{10,11... | collective-permute-start | bytes 786440 | tf_op jit(solution)/shard_map/give_back/ppermute | solution.py:25
  118.3 0.4 fusion.6
  118.7 0.3 fusion.4
  119.0 0.4 collective-permute-done.5
  119.5 0.8 copy.32
  120.4 4.6 %all-to-all-start.4 = ((bf16[32,8,512]{2,1,0:T(8,128)(2,1)}), bf16[32,8,512]{2,1,0:T(8,128)(2,1)}, u32[]{:S(2)}, u32[]{:S(2)}) async-start(bf16[32,8,512]{2,1,0:T(8,128)(2,1)} %bitcast.13), calls=%async_computation.4 | async-start | bytes 524288 | tf_op jit(solution)/shard_map/give_back/all_to_all | solution.py:17
  125.0 4.6 %collective-permute-start.8 = (bf16[2,256,512]{2,1,0:T(8,128)(2,1)S(1)}, bf16[2,256,512]{2,1,0:T(8,128)(2,1)S(1)}, u32[]{:S(2)}, u32[]{:S(2)}) collective-permute-start(bf16[2,256,512]{2,1,0:T(8,128)(2,1)S(1)} %pad_maximum_fusion.3.first), channel_id=1, source_target_pairs={{0,4},{2,6},{4,0},{6,2},{1,5},{3,7},{5,1},{7,3},{8,12},{10,14},{12... | collective-permute-start | bytes 1572872 | tf_op jit(solution)/shard_map/all_rows/ppermute | solution.py:177
  129.7 2.8 %collective-permute-start.9 = (bf16[2,256,512]{2,1,0:T(8,128)(2,1)S(1)}, bf16[2,256,512]{2,1,0:T(8,128)(2,1)S(1)}, u32[]{:S(2)}, u32[]{:S(2)}) collective-permute-start(bf16[2,256,512]{2,1,0:T(8,128)(2,1)S(1)} %pad_maximum_fusion.3.first), channel_id=1, source_target_pairs={{0,6},{2,0},{4,2},{6,4},{1,7},{3,1},{5,3},{7,5},{8,14},{10,8},{12,... | collective-permute-start | bytes 1572872 | tf_op jit(solution)/shard_map/all_rows/ppermute | solution.py:177
  132.5 2.5 %collective-permute-start.6 = (bf16[2,256,512]{2,1,0:T(8,128)(2,1)S(1)}, bf16[2,256,512]{2,1,0:T(8,128)(2,1)S(1)}, u32[]{:S(2)}, u32[]{:S(2)}) collective-permute-start(bf16[2,256,512]{2,1,0:T(8,128)(2,1)S(1)} %pad_maximum_fusion.3.first), channel_id=1, source_target_pairs={{0,2},{2,4},{4,6},{6,0},{1,3},{3,5},{5,7},{7,1},{8,10},{10,12},{12... | collective-permute-start | bytes 1572872 | tf_op jit(solution)/shard_map/all_rows/ppermute | solution.py:177
  134.9 10.9 %all-to-all-done.4 = bf16[32,8,512]{2,1,0:T(8,128)(2,1)} async-done(((bf16[32,8,512]{2,1,0:T(8,128)(2,1)}), bf16[32,8,512]{2,1,0:T(8,128)(2,1)}, u32[]{:S(2)}, u32[]{:S(2)}) %all-to-all-start.4) | async-done | bytes 262176 | tf_op jit(solution)/shard_map/give_back/all_to_all | solution.py:17
  145.9 1.1 fusion.15
  147.1 0.8 broadcast_in_dim.81
  147.9 6.5 %all-to-all-start.5 = ((bf16[16,32,512]{2,1,0:T(8,128)(2,1)}), bf16[16,32,512]{2,1,0:T(8,128)(2,1)}, u32[]{:S(2)}, u32[]{:S(2)}) async-start(bf16[16,32,512]{2,1,0:T(8,128)(2,1)} %broadcast_in_dim.81), calls=%async_computation.5 | async-start | bytes 1048576 | tf_op jit(solution)/shard_map/result/all_to_all | solution.py:17
  154.5 0.6 dynamic_slice.24
  157.1 1.4 new_slices.4
  158.5 2.0 %collective-permute-start.10 = (bf16[4,256,256]{2,1,0:T(8,128)(2,1)}, bf16[4,256,256]{2,1,0:T(8,128)(2,1)S(1)}, u32[]{:S(2)}, u32[]{:S(2)}) collective-permute-start(bf16[4,256,256]{2,1,0:T(8,128)(2,1)} %get-tuple-element.31), channel_id=1, source_target_pairs={{0,1},{1,0},{2,3},{3,2},{4,5},{5,4},{6,7},{7,6},{8,9},{9,8},{10,11... | collective-permute-start | bytes 1572872 | tf_op jit(solution)/shard_map/new_slices/ppermute | solution.py:25
  160.5 1.3 new_slices.3
  161.9 2.3 %collective-permute-start.7 = (bf16[4,256,256]{2,1,0:T(8,128)(2,1)}, bf16[4,256,256]{2,1,0:T(8,128)(2,1)S(1)}, u32[]{:S(2)}, u32[]{:S(2)}) collective-permute-start(bf16[4,256,256]{2,1,0:T(8,128)(2,1)} %get-tuple-element.28), channel_id=1, source_target_pairs={{0,1},{1,0},{2,3},{3,2},{4,5},{5,4},{6,7},{7,6},{8,9},{9,8},{10,11... | collective-permute-start | bytes 1572872 | tf_op jit(solution)/shard_map/new_slices/ppermute | solution.py:25
  164.2 1.8 %all-to-all-done.5 = bf16[16,32,512]{2,1,0:T(8,128)(2,1)} async-done(((bf16[16,32,512]{2,1,0:T(8,128)(2,1)}), bf16[16,32,512]{2,1,0:T(8,128)(2,1)}, u32[]{:S(2)}, u32[]{:S(2)}) %all-to-all-start.5) | async-done | bytes 524320 | tf_op jit(solution)/shard_map/result/all_to_all | solution.py:17
  166.0 0.8 dynamic-slice_bitcast_fusion
  166.7 0.6 fusion.40
  167.3 0.9 copy-done.2
  168.3 0.9 copy-done.4
  169.2 2.4 %new_slices.5 = (bf16[128,4096]{1,0:T(8,128)(2,1)}, bf16[128,4096]{1,0:T(8,128)(2,1)}) custom-call(s32[16]{0:T(128)S(1)} %fusion.30.source_ref, bf16[4,128,256]{2,1,0:T(8,128)(2,1)S(1)} %get-tuple-element.26.refs_0_, bf16[4,128,256]{2,1,0:T(8,128)(2,1)S(1)} %get-tuple-element.27.refs_1_, bf16[4,256,256]{2,1,0:T(8,128)(2,1)S(1)} %collective-permute-done.7.refs_2_, ...), custom_call_target="tpu_custom_call" | custom-call | tf_op jit(solution)/shard_map/new_slices/pallas_call | solution.py:211
  (54 shorter events, 0.9 us)
Async XLA Ops:
  0.6 38.3 %copy-start = (bf16[2048,256]{1,0:T(8,128)(2,1)S(1)}, bf16[2048,256]{1,0:T(8,128)(2,1)}, u32[]{:S(2)}) copy-start(bf16[2048,256]{1,0:T(8,128)(2,1)} %param.11) | copy-start | bytes 3145732
  0.6 12.1 %copy-start.11 = (s32[32,2]{0,1:T(2,128)S(1)}, s32[32,2]{0,1:T(2,128)}, u32[]{:S(2)}) copy-start(s32[32,2]{0,1:T(2,128)} %param.9) | copy-start | bytes 772
  0.7 12.6 %copy-start.13 = (s32[16]{0:T(128)S(1)}, s32[16]{0:T(128)}, u32[]{:S(2)}) copy-start(s32[16]{0:T(128)} %param.13) | copy-start | bytes 196
  0.7 15.5 %copy-start.10 = (f32[32,2]{0,1:T(2,128)S(1)}, f32[32,2]{0,1:T(2,128)}, u32[]{:S(2)}) copy-start(f32[32,2]{0,1:T(2,128)} %param.10) | copy-start | bytes 772
  2.3 36.3 %copy-start.12 = (s32[16]{0:T(128)S(1)}, s32[16]{0:T(128)}, u32[]{:S(2)}) copy-start(s32[16]{0:T(128)} %param.14) | copy-start | bytes 196
  2.3 21.9 %all-to-all-start = ((bf16[16,32,512]{2,1,0:T(8,128)(2,1)}), bf16[16,32,512]{2,1,0:T(8,128)(2,1)S(1)}, u32[]{:S(2)}, u32[]{:S(2)}) async-start(bf16[16,32,512]{2,1,0:T(8,128)(2,1)} %broadcast_in_dim.47), calls=%async_computation | async-start | bytes 1048576 | tf_op jit(solution)/shard_map/token_blocks/all_to_all | solution.py:17
  24.4 19.1 %copy-start.9 = (bf16[2048,256]{1,0:T(8,128)(2,1)S(1)}, bf16[2048,256]{1,0:T(8,128)(2,1)}, u32[]{:S(2)}) copy-start(bf16[2048,256]{1,0:T(8,128)(2,1)} %param.12) | copy-start | bytes 3145732
  25.2 32.5 %all-to-all-start.1 = ((bf16[32,8,512]{2,1,0:T(8,128)(2,1)}), bf16[32,8,512]{2,1,0:T(8,128)(2,1)S(1)}, u32[]{:S(2)}, u32[]{:S(2)}) async-start(bf16[32,8,512]{2,1,0:T(8,128)(2,1)} %bitcast.3), calls=%async_computation.1 | async-start | bytes 524288 | tf_op jit(solution)/shard_map/dispatch/all_to_all | solution.py:17
  40.3 8.2 %collective-permute-start = (bf16[8,128,256]{2,1,0:T(8,128)(2,1)}, bf16[8,128,256]{2,1,0:T(8,128)(2,1)}, u32[]{:S(2)}, u32[]{:S(2)}) collective-permute-start(bf16[8,128,256]{2,1,0:T(8,128)(2,1)} %gather_fusion.1), channel_id=1, source_target_pairs={{0,1},{1,0},{2,3},{3,2},{4,5},{5,4},{6,7},{7,6},{8,9},{9,8},{10,11... | collective-permute-start | bytes 1572872 | tf_op jit(solution)/shard_map/weights/ppermute | solution.py:25
  44.2 19.7 %collective-permute-start.2 = (bf16[8,128,256]{2,1,0:T(8,128)(2,1)S(1)}, bf16[8,128,256]{2,1,0:T(8,128)(2,1)}, u32[]{:S(2)}, u32[]{:S(2)}) collective-permute-start(bf16[8,128,256]{2,1,0:T(8,128)(2,1)S(1)} %gather_fusion.3), channel_id=1, source_target_pairs={{0,1},{1,0},{2,3},{3,2},{4,5},{5,4},{6,7},{7,6},{8,9},{9,8},{10,11... | collective-permute-start | bytes 1572872 | tf_op jit(solution)/shard_map/weights/ppermute | solution.py:25
  57.7 7.3 %collective-permute-start.1 = (bf16[256,512]{1,0:T(8,128)(2,1)S(1)}, bf16[256,512]{1,0:T(8,128)(2,1)S(1)}, u32[]{:S(2)}, u32[]{:S(2)}) collective-permute-start(bf16[256,512]{1,0:T(8,128)(2,1)S(1)} %bitcast.36), channel_id=1, source_target_pairs={{0,1},{1,0},{2,3},{3,2},{4,5},{5,4},{6,7},{7,6},{8,9},{9,8},{10,11... | collective-permute-start | bytes 786440 | tf_op jit(solution)/shard_map/dispatch/ppermute | solution.py:25
  65.0 2.1 %copy-start.7 = (bf16[8,128,512]{2,1,0:T(8,128)(2,1)}, bf16[8,128,512]{2,1,0:T(8,128)(2,1)S(1)}, u32[]{:S(2)}) copy-start(bf16[8,128,512]{2,1,0:T(8,128)(2,1)S(1)} %pad_maximum_fusion.1) | copy-start | bytes 3145732
  65.0 1.6 copy-start.5
  89.3 23.6 %all-to-all-start.3 = ((bf16[8,256,256]{2,1,0:T(8,128)(2,1)}), bf16[8,256,256]{2,1,0:T(8,128)(2,1)S(1)}, u32[]{:S(2)}, u32[]{:S(2)}) async-start(bf16[8,256,256]{2,1,0:T(8,128)(2,1)} %broadcast_in_dim.80), calls=%async_computation.3 | async-start | bytes 2097152 | tf_op jit(solution)/shard_map/hidden/all_to_all | solution.py:17
  92.8 20.1 %collective-permute-start.3 = (bf16[256,512]{1,0:T(8,128)(2,1)S(1)}, bf16[256,512]{1,0:T(8,128)(2,1)S(1)}, u32[]{:S(2)}, u32[]{:S(2)}) collective-permute-start(bf16[256,512]{1,0:T(8,128)(2,1)S(1)} %bitcast.38), channel_id=1, source_target_pairs={{0,8},{8,0},{1,9},{9,1},{2,10},{10,2},{3,11},{11,3},{4,12},{12,4},... | collective-permute-start | bytes 786440 | tf_op jit(solution)/shard_map/hidden/ppermute | solution.py:142
  97.6 4.2 %collective-permute-start.4 = (bf16[256,256]{1,0:T(8,128)(2,1)S(1)}, bf16[256,256]{1,0:T(8,128)(2,1)S(1)}, u32[]{:S(2)}, u32[]{:S(2)}) collective-permute-start(bf16[256,256]{1,0:T(8,128)(2,1)S(1)} %pad_maximum_fusion.5.own_units), channel_id=1, source_target_pairs={{0,1},{1,0},{2,3},{3,2},{4,5},{5,4},{6,7},{7,6},{8,9},{9,8},{10,11... | collective-permute-start | bytes 393224 | tf_op jit(solution)/shard_map/hidden/ppermute | solution.py:25
  112.9 1.2 copy-start.8
  113.0 1.5 copy-start.6
  114.9 4.6 %collective-permute-start.5 = (bf16[256,512]{0,1:T(8,128)(2,1)S(1)}, bf16[256,512]{0,1:T(8,128)(2,1)S(1)}, u32[]{:S(2)}, u32[]{:S(2)}) collective-permute-start(bf16[256,512]{0,1:T(8,128)(2,1)S(1)} %pad_maximum_fusion.4), channel_id=1, source_target_pairs={{0,1},{1,0},{2,3},{3,2},{4,5},{5,4},{6,7},{7,6},{8,9},{9,8},{10,11... | collective-permute-start | bytes 786440 | tf_op jit(solution)/shard_map/give_back/ppermute | solution.py:25
  120.4 25.5 %all-to-all-start.4 = ((bf16[32,8,512]{2,1,0:T(8,128)(2,1)}), bf16[32,8,512]{2,1,0:T(8,128)(2,1)}, u32[]{:S(2)}, u32[]{:S(2)}) async-start(bf16[32,8,512]{2,1,0:T(8,128)(2,1)} %bitcast.13), calls=%async_computation.4 | async-start | bytes 524288 | tf_op jit(solution)/shard_map/give_back/all_to_all | solution.py:17
  125.0 32.0 %collective-permute-start.8 = (bf16[2,256,512]{2,1,0:T(8,128)(2,1)S(1)}, bf16[2,256,512]{2,1,0:T(8,128)(2,1)S(1)}, u32[]{:S(2)}, u32[]{:S(2)}) collective-permute-start(bf16[2,256,512]{2,1,0:T(8,128)(2,1)S(1)} %pad_maximum_fusion.3.first), channel_id=1, source_target_pairs={{0,4},{2,6},{4,0},{6,2},{1,5},{3,7},{5,1},{7,3},{8,12},{10,14},{12... | collective-permute-start | bytes 1572872 | tf_op jit(solution)/shard_map/all_rows/ppermute | solution.py:177
  129.7 27.4 %collective-permute-start.9 = (bf16[2,256,512]{2,1,0:T(8,128)(2,1)S(1)}, bf16[2,256,512]{2,1,0:T(8,128)(2,1)S(1)}, u32[]{:S(2)}, u32[]{:S(2)}) collective-permute-start(bf16[2,256,512]{2,1,0:T(8,128)(2,1)S(1)} %pad_maximum_fusion.3.first), channel_id=1, source_target_pairs={{0,6},{2,0},{4,2},{6,4},{1,7},{3,1},{5,3},{7,5},{8,14},{10,8},{12,... | collective-permute-start | bytes 1572872 | tf_op jit(solution)/shard_map/all_rows/ppermute | solution.py:177
  132.5 28.1 %collective-permute-start.6 = (bf16[2,256,512]{2,1,0:T(8,128)(2,1)S(1)}, bf16[2,256,512]{2,1,0:T(8,128)(2,1)S(1)}, u32[]{:S(2)}, u32[]{:S(2)}) collective-permute-start(bf16[2,256,512]{2,1,0:T(8,128)(2,1)S(1)} %pad_maximum_fusion.3.first), channel_id=1, source_target_pairs={{0,2},{2,4},{4,6},{6,0},{1,3},{3,5},{5,7},{7,1},{8,10},{10,12},{12... | collective-permute-start | bytes 1572872 | tf_op jit(solution)/shard_map/all_rows/ppermute | solution.py:177
  147.9 18.0 %all-to-all-start.5 = ((bf16[16,32,512]{2,1,0:T(8,128)(2,1)}), bf16[16,32,512]{2,1,0:T(8,128)(2,1)}, u32[]{:S(2)}, u32[]{:S(2)}) async-start(bf16[16,32,512]{2,1,0:T(8,128)(2,1)} %broadcast_in_dim.81), calls=%async_computation.5 | async-start | bytes 1048576 | tf_op jit(solution)/shard_map/result/all_to_all | solution.py:17
  158.5 3.4 %copy-start.1 = (bf16[4,128,256]{2,1,0:T(8,128)(2,1)}, bf16[4,128,256]{2,1,0:T(8,128)(2,1)S(1)}, u32[]{:S(2)}) copy-start(bf16[4,128,256]{2,1,0:T(8,128)(2,1)S(1)} %get-tuple-element.29.refs_3_) | copy-start | bytes 786436
  158.5 3.4 %copy-start.3 = (bf16[4,128,256]{2,1,0:T(8,128)(2,1)}, bf16[4,128,256]{2,1,0:T(8,128)(2,1)S(1)}, u32[]{:S(2)}) copy-start(bf16[4,128,256]{2,1,0:T(8,128)(2,1)S(1)} %get-tuple-element.30.refs_4_) | copy-start | bytes 786436
  158.5 8.9 %collective-permute-start.10 = (bf16[4,256,256]{2,1,0:T(8,128)(2,1)}, bf16[4,256,256]{2,1,0:T(8,128)(2,1)S(1)}, u32[]{:S(2)}, u32[]{:S(2)}) collective-permute-start(bf16[4,256,256]{2,1,0:T(8,128)(2,1)} %get-tuple-element.31), channel_id=1, source_target_pairs={{0,1},{1,0},{2,3},{3,2},{4,5},{5,4},{6,7},{7,6},{8,9},{9,8},{10,11... | collective-permute-start | bytes 1572872 | tf_op jit(solution)/shard_map/new_slices/ppermute | solution.py:25
  161.9 5.5 %collective-permute-start.7 = (bf16[4,256,256]{2,1,0:T(8,128)(2,1)}, bf16[4,256,256]{2,1,0:T(8,128)(2,1)S(1)}, u32[]{:S(2)}, u32[]{:S(2)}) collective-permute-start(bf16[4,256,256]{2,1,0:T(8,128)(2,1)} %get-tuple-element.28), channel_id=1, source_target_pairs={{0,1},{1,0},{2,3},{3,2},{4,5},{5,4},{6,7},{7,6},{8,9},{9,8},{10,11... | collective-permute-start | bytes 1572872 | tf_op jit(solution)/shard_map/new_slices/ppermute | solution.py:25
  167.3 1.0 copy-start.2
  168.3 0.9 copy-start.4

commit v8 on v7

--- a/solution.py
+++ b/solution.py
@@ -76,29 +76,26 @@
     tok_rows, width = tokens.shape
     half_units = old_up.shape[0]
     unit_width = half_units // cut_count
-    core_units = half_units // 2
     capacity = 8 * tok_rows // group_count
     slot_rows = group_count * capacity
     chip, core = lax.axis_index(CHIP), lax.axis_index("core")
-    cut = 2 * chip + core
+    cut, other_cut = 2 * chip + core, 2 * chip + 1 - core
     cut_list = jnp.arange(cut_count, dtype=jnp.int32)
     inverse = jnp.sum(
         cut_list[:, None] * (old_rows[:, None] == cut_list[None, :]).astype(jnp.int32), axis=0
     )
-    slot_pairs = new_slots.reshape(chips, 2)
-    kept, given = slot_pairs[:, core], slot_pairs[:, 1 - core]
-
-    def both_blocks(weights):
-        blocks = weights.reshape(cut_count, unit_width, width)
-        mine, theirs = rows_at(blocks, kept), swap(rows_at(blocks, given))
-        return jnp.concatenate([mine, theirs], axis=2).reshape(core_units, 2 * width)
 
     with jax.named_scope("weights"):
-        up, down = both_blocks(old_up), both_blocks(old_down)
+        shape = (chips, 2 * unit_width, width)
+        up = [old_up.reshape(shape), swap(old_up).reshape(shape)]
+        down = [old_down.reshape(shape), swap(old_down).reshape(shape)]
 
     with jax.named_scope("token_blocks"):
-        both = everywhere(jnp.concatenate([tokens, cotangent], axis=1), CUTS)
-        both = pick(both, pick(old_rows, cut))
+        blocks = everywhere(jnp.concatenate([tokens, cotangent], axis=1), CUTS)
+        own, other = pick(blocks, pick(old_rows, cut)), pick(blocks, pick(old_rows, other_cut))
+        both = jnp.concatenate(
+            [own[:, :width], other[:, :width], own[:, width:], other[:, width:]], axis=1
+        )
 
     flat_ids = expert_ids.reshape(-1)
     expert_hits = (flat_ids[:, None] == jnp.arange(expert_count, dtype=jnp.int32)[None, :]).astype(
@@ -106,69 +103,95 @@
     )
     slot_rank = jnp.sum((jnp.cumsum(expert_hits, axis=0) - expert_hits) * expert_hits, axis=1)
     target = (flat_ids * capacity + slot_rank).reshape(tok_rows, 2)
-    slots = expert_count * capacity
-    slot_list = jnp.arange(slots, dtype=jnp.int32)
+    held_slots = capacity // 2
+    core_rows = slot_rows // 2
+    slot_list = 2 * jnp.arange(expert_count * held_slots, dtype=jnp.int32) + core
     matches = slot_list[:, None, None] == target[None]
     placer = jnp.any(matches, axis=2).astype(BF16)
     slot_gate = jnp.sum(jnp.where(matches, gate_weights[None], 0.0), axis=(1, 2))
 
     with jax.named_scope("dispatch"):
         placed = jnp.dot(placer, both, preferred_element_type=F32)
-        scale = jnp.where(jnp.arange(2 * width)[None, :] < width, 1.0, slot_gate[:, None])
-        placed = (placed * scale).astype(BF16).reshape(expert_count, 1, capacity, 2 * width)
-        placed = jnp.broadcast_to(placed, (expert_count, 2, capacity, 2 * width))
-        routed = exchange(placed.reshape(group_count, capacity, 2 * width), "expert")
-        routed = routed.reshape(slot_rows, 2 * width)
-        other = swap(routed)
-        routed_x = jnp.concatenate([routed[:, :width], other[:, :width]], axis=1)
-        routed_back = jnp.concatenate([routed[:, width:], other[:, width:]], axis=1)
-
-    def partial(weights, rows):
-        part = lax.dot_general(
-            weights, rows, (((1,), (1,)), ((), ())), preferred_element_type=F32
+        scale = jnp.where(jnp.arange(4 * width)[None, :] < 2 * width, 1.0, slot_gate[:, None])
+        placed = (placed * scale).astype(BF16).reshape(expert_count, 1, held_slots, 4 * width)
+        placed = jnp.broadcast_to(placed, (expert_count, 2, held_slots, 4 * width))
+        rows = exchange(placed.reshape(group_count, held_slots, 4 * width), "expert")
+        rows = rows.reshape(core_rows, 4 * width)
+
+    def partial(weights, first):
+        return sum(
+            jnp.einsum(
+                "rd,pud->pru",
+                rows[:, first + j * width : first + (j + 1) * width],
+                weights[j],
+                preferred_element_type=F32,
+            )
+            for j in range(2)
         ).astype(BF16)
-        return part.reshape(chips, unit_width, slot_rows)
 
     with jax.named_scope("hidden"):
-        parts = jnp.concatenate([partial(up, routed_x), partial(down, routed_back)], axis=1)
+        parts = jnp.concatenate([partial(up, 0), partial(down, 2 * width)], axis=2)
         sums = jnp.sum(exchange(parts, CHIP).astype(F32), axis=0)
-        pre_act, hidden_grad = sums[:unit_width], sums[unit_width:]
+        pre_act, hidden_grad = sums[:, : 2 * unit_width], sums[:, 2 * unit_width :]
         sig = jax.nn.sigmoid(pre_act)
         hidden = jax.nn.silu(pre_act).astype(BF16)
         pre_grad = (hidden_grad * sig * (1.0 + pre_act * (1.0 - sig))).astype(BF16)
-        own_units = jnp.concatenate([hidden, pre_grad], axis=0)
-        other_units = swap(own_units)
+        own_units = jnp.concatenate([hidden, pre_grad], axis=1)
+
+        others = swap(
+            jnp.concatenate([rows[:, width : 2 * width], rows[:, 3 * width :]], axis=1)
+        )
+        routed = jnp.concatenate([rows[:, :width], rows[:, 2 * width : 3 * width]], axis=1)
+        routed = jnp.concatenate([routed, others], axis=0)
         later_rows, own_units = lax.optimization_barrier((routed, own_units))
         rows_y = lax.ppermute(later_rows, "y", [(0, 1), (1, 0)])
         units = everywhere(own_units, CHIP)
-        units, rows_y, other_units = lax.optimization_barrier((units, rows_y, other_units))
-        hidden = units[:, :unit_width].reshape(core_units, slot_rows)
-        pre_grad = units[:, unit_width:].reshape(core_units, slot_rows)
+        units, rows_y = lax.optimization_barrier((units, rows_y))
+        hidden, pre_grad = units[:, :, : 2 * unit_width], units[:, :, 2 * unit_width :]
 
     def rows_of(units, weights):
-        return lax.dot_general(
-            units, weights, (((0,), (0,)), ((), ())), preferred_element_type=F32
+        return jnp.einsum("pru,pud->rd", units, weights, preferred_element_type=F32).astype(BF16)
+
+    with jax.named_scope("give_back"):
+        half_rows = jnp.concatenate(
+            [rows_of(part, weights[j]) for j in range(2) for part, weights in ((hidden, down), (pre_grad, up))],
+            axis=1,
         )
-
-    with jax.named_scope("give_back"):
-        theirs = [rows_of(hidden, down[:, width:]), rows_of(pre_grad, up[:, width:])]
-        theirs = swap(jnp.concatenate([part.astype(BF16) for part in theirs], axis=1))
-        own = [rows_of(hidden, down[:, :width]), rows_of(pre_grad, up[:, :width])]
-        half_rows = (jnp.concatenate(own, axis=1) + theirs.astype(F32)).astype(BF16)
-        sent_rows = half_rows.reshape(group_count, capacity, 2 * width)
+        sent_rows = half_rows.reshape(group_count, held_slots, 4 * width)
         half_rows = exchange(sent_rows, "expert")
-        row_list = jnp.arange(slot_rows, dtype=jnp.int32)
-        row_slot = row_list // (2 * capacity) * capacity + row_list % capacity
+        row_list = jnp.arange(core_rows, dtype=jnp.int32)
+        row_slot = row_list // capacity * capacity + row_list % held_slots * 2 + core
         picker = (target.reshape(-1)[:, None] == row_slot[None, :]).astype(BF16)
-        entries = jnp.dot(picker, half_rows.reshape(slot_rows, 2 * width), preferred_element_type=F32)
-        entries = entries.reshape(tok_rows, 2, 2 * width)
-        mixed = jnp.sum(entries[:, :, :width] * gate_weights[:, :, None], axis=1)
-        token_grad = jnp.sum(entries[:, :, width:], axis=1)
-        result = jnp.concatenate([mixed, token_grad], axis=1).astype(BF16)
+        entries = jnp.dot(picker, half_rows.reshape(core_rows, 4 * width), preferred_element_type=F32)
+        is_out = jnp.arange(4 * width) // width % 2 == 0
+        factor = jnp.where(is_out[None, None, :], gate_weights[:, :, None], 1.0)
+        own_result = jnp.sum(entries.reshape(tok_rows, 2, 4 * width) * factor, axis=1).astype(BF16)
 
     with jax.named_scope("result"):
-        own_result = result
-        result = pick(everywhere(own_result, CUTS), pick(inverse, cut))
+        got = everywhere(own_result, CHIP)
+
+        def share(place):
+            source = pick(inverse, place)
+            first = jnp.where(source % 2 == core, 0, 2 * width)
+            return lax.dynamic_slice(got, (source // 2, 0, first), (1, tok_rows, 2 * width))[0]
+
+        result = (share(cut).astype(F32) + swap(share(other_cut)).astype(F32)).astype(BF16)
+
+    with jax.named_scope("slot_units"):
+
+        def of_slot(place):
+            block = pick(new_slots, place)
+            return [
+                lax.dynamic_slice(
+                    units, (block // 2, 0, first + block % 2 * unit_width), (1, core_rows, unit_width)
+                )[0]
+                for first in (0, 2 * unit_width)
+            ]
+
+        mine = of_slot(cut) + of_slot(other_cut)
+        theirs = swap(jnp.concatenate(mine[2:] + mine[:2], axis=1))
+        slot_units = jnp.concatenate([jnp.concatenate(mine, axis=1), theirs], axis=0).T
+        own_units, other_units = slot_units[: 2 * unit_width], slot_units[2 * unit_width :]
 
     with jax.named_scope("all_rows"):
         pair = jnp.stack(lax.optimization_barrier((routed, rows_y, sent_rows))[:2])

time: 173 us -> 175 us (1.012)
  blocking collectives: 20.4 us -> 0 us
  waiting for transfers between devices: 40.2 us -> 52.2 us
  between operations: 5.05 us -> 15.5 us
  local copies, waits for them, and re-layouts: 16.6 us -> 11.4 us
  starting transfers between devices: 75.4 us -> 79.2 us
  matrix products: 3.71 us -> 6.69 us
    all_to_all x1 -> x0, blocking collectives: 20.4 us -> none  [exchange(): return lax.all_to_all(parts, axis, split_axis=0, concat_axis=0, tiled=True)]
    ppermute x3, waiting for transfers between devices: 0.01 us -> 4.65 us  [local(): lax.ppermute(pair, 'x', [(i, (i + s) % column) for i in range(column)])]
    gather x4 -> x0, local copies, waits for them, and re-layouts: 4.34 us -> none  [rows_at(): return jnp.take(blocks, places, axis=0, mode='clip')]
    ppermute x1, waiting for transfers between devices: 11 us -> 15.3 us  [local(): rows_y = lax.ppermute(later_rows, 'y', [(0, 1), (1, 0)])]
    all_to_all x5 -> x6, waiting for transfers between devices: 27.8 us -> 31.3 us  [exchange(): return lax.all_to_all(parts, axis, split_axis=0, concat_axis=0, tiled=True)]
    dot_general x7 -> x9, matrix products: 3.48 us -> 6.46 us  [the longest x4 3.12 us: partial(): jnp.einsum('rd,pud->pru', rows[:, first + j * width:first + (j + 1) * wid...]
    all_to_all x5 -> x6, starting transfers between devices: 38.5 us -> 41.1 us  [exchange(): return lax.all_to_all(parts, axis, split_axis=0, concat_axis=0, tiled=True)]
    unnamed x29 -> x23, local copies, waits for them, and re-layouts: 4.69 us -> 2.42 us
  transfers between devices with their start and end apart: 16 -> 17, of which waited for: 7 -> 6; matrix products, arithmetic and copies ran while one was open for 8% -> 6% of each run, Pallas kernels for 2% -> 1%
where the time goes in v8:
time: 175 us; the launch traced here: 174 us
  starting transfers between devices  79.2 us (45%)
  waiting for transfers between devices  52.2 us (30%)
  between operations  15.5 us (9%)
  local copies, waits for them, and re-layouts  11.4 us (7%)
  matrix products  6.69 us (4%)
  Pallas kernels  4.41 us (3%)
  other arithmetic  4.14 us (2%)
    all_to_all x6, starting transfers between devices, exchange(): return lax.all_to_all(parts, axis, split_axis=0, concat_axis=0, tiled=True)  41.1 us
    all_to_all x6, waiting for transfers between devices, exchange(): return lax.all_to_all(parts, axis, split_axis=0, concat_axis=0, tiled=True)  31.3 us
    ppermute x7, starting transfers between devices, swap(): return lax.ppermute(block, 'core', [(0, 1), (1, 0)])  22.5 us
    ppermute x1, waiting for transfers between devices, local(): rows_y = lax.ppermute(later_rows, 'y', [(0, 1), (1, 0)])  15.3 us
    ppermute x3, starting transfers between devices, local(): lax.ppermute(pair, 'x', [(i, (i + s) % column) for i in range(column)])  10.9 us
    ppermute x1, starting transfers between devices, local(): rows_y = lax.ppermute(later_rows, 'y', [(0, 1), (1, 0)])  4.77 us
    ppermute x3, waiting for transfers between devices, local(): lax.ppermute(pair, 'x', [(i, (i + s) % column) for i in range(column)])  4.65 us
  transfers between devices with their start and end apart: 17, of which 6 were waited for; matrix products, arithmetic and copies ran while one was open for 6% of the time, Pallas kernels for 1%

profile of v8, /device:TPU:1, one launch (start us, length us, event | category | flops | bytes accessed | tf_op | source)
XLA Modules:
  0.0 173.5 jit_solution(2600454704694264708)
XLA Ops:
  0.7 0.8 pad_maximum_fusion.7
  1.4 0.8 broadcast_in_dim.88
  2.3 10.2 %all-to-all-start = ((bf16[16,32,512]{2,1,0:T(8,128)(2,1)}), bf16[16,32,512]{2,1,0:T(8,128)(2,1)S(1)}, u32[]{:S(2)}, u32[]{:S(2)}) async-start(bf16[16,32,512]{2,1,0:T(8,128)(2,1)} %broadcast_in_dim.88), calls=%async_computation | async-start | bytes 1048576 | tf_op jit(solution)/shard_map/token_blocks/all_to_all | solution.py:17
  12.5 0.1 copy.39
  12.6 0.1 eq.89
  12.8 0.1 reduce_window_sum.11
  12.9 0.2 select_reduce_fusion
  13.1 0.6 fusion.61
  16.3 0.1 reduce_sum.48
  17.9 0.1 fusion.30
  18.0 6.0 %all-to-all-done = bf16[16,32,512]{2,1,0:T(8,128)(2,1)S(1)} async-done(((bf16[16,32,512]{2,1,0:T(8,128)(2,1)}), bf16[16,32,512]{2,1,0:T(8,128)(2,1)S(1)}, u32[]{:S(2)}, u32[]{:S(2)}) %all-to-all-start) | async-done | bytes 524320 | tf_op jit(solution)/shard_map/token_blocks/all_to_all | solution.py:17
  24.0 0.2 fusion.5
  24.3 0.8 broadcast_in_dim.95
  25.1 13.6 %all-to-all-start.1 = ((bf16[32,4,1024]{2,1,0:T(4,128)(2,1)}), bf16[32,4,1024]{2,1,0:T(4,128)(2,1)}, u32[]{:S(2)}, u32[]{:S(2)}) async-start(bf16[32,4,1024]{2,1,0:T(4,128)(2,1)} %bitcast.4), calls=%async_computation.1 | async-start | bytes 524288 | tf_op jit(solution)/shard_map/dispatch/all_to_all | solution.py:17
  38.7 3.3 %collective-permute-start.1 = (bf16[2048,256]{1,0:T(8,128)(2,1)S(1)}, bf16[2048,256]{1,0:T(8,128)(2,1)S(1)}, u32[]{:S(2)}, u32[]{:S(2)}) collective-permute-start(bf16[2048,256]{1,0:T(8,128)(2,1)S(1)} %copy-done.1), channel_id=1, source_target_pairs={{0,1},{1,0},{2,3},{3,2},{4,5},{5,4},{6,7},{7,6},{8,9},{9,8},{10,11... | collective-permute-start | bytes 3145736 | tf_op jit(solution)/shard_map/weights/ppermute | solution.py:25
  41.9 1.9 %collective-permute-start.2 = (bf16[2048,256]{1,0:T(8,128)(2,1)S(1)}, bf16[2048,256]{1,0:T(8,128)(2,1)}, u32[]{:S(2)}, u32[]{:S(2)}) collective-permute-start(bf16[2048,256]{1,0:T(8,128)(2,1)S(1)} %copy-done), channel_id=1, source_target_pairs={{0,1},{1,0},{2,3},{3,2},{4,5},{5,4},{6,7},{7,6},{8,9},{9,8},{10,11... | collective-permute-start | bytes 3145736 | tf_op jit(solution)/shard_map/weights/ppermute | solution.py:25
  43.9 13.9 %all-to-all-done.1 = bf16[32,4,1024]{2,1,0:T(4,128)(2,1)} async-done(((bf16[32,4,1024]{2,1,0:T(4,128)(2,1)}), bf16[32,4,1024]{2,1,0:T(4,128)(2,1)}, u32[]{:S(2)}, u32[]{:S(2)}) %all-to-all-start.1) | async-done | bytes 262176 | tf_op jit(solution)/shard_map/dispatch/all_to_all | solution.py:17
  57.7 1.0 reshape.136
  58.8 0.5 fusion.28
  59.2 0.5 fusion.25
  59.7 0.5 fusion.3
  60.2 0.5 copy-done.3
  60.7 1.7 fusion.2
  62.4 1.1 pad_maximum_fusion
  63.5 4.9 %all-to-all-start.2 = ((bf16[8,128,512]{2,1,0:T(8,128)(2,1)}), bf16[8,128,512]{2,1,0:T(8,128)(2,1)S(1)}, u32[]{:S(2)}, u32[]{:S(2)}) async-start(bf16[8,128,512]{2,1,0:T(8,128)(2,1)} %pad_maximum_fusion), calls=%async_computation.2 | async-start | bytes 2097152 | tf_op jit(solution)/shard_map/hidden/all_to_all | solution.py:17
  68.4 4.8 %collective-permute-start = (bf16[128,512]{1,0:T(8,128)(2,1)S(1)}, bf16[128,512]{1,0:T(8,128)(2,1)S(1)}, u32[]{:S(2)}, u32[]{:S(2)}) collective-permute-start(bf16[128,512]{1,0:T(8,128)(2,1)S(1)} %pad_maximum_fusion.4), channel_id=1, source_target_pairs={{0,1},{1,0},{2,3},{3,2},{4,5},{5,4},{6,7},{7,6},{8,9},{9,8},{10,11... | collective-permute-start | bytes 393224 | tf_op jit(solution)/shard_map/hidden/ppermute | solution.py:25
  73.2 1.0 collective-permute-done
  74.2 11.5 %all-to-all-done.2 = bf16[8,128,512]{2,1,0:T(8,128)(2,1)S(1)} async-done(((bf16[8,128,512]{2,1,0:T(8,128)(2,1)}), bf16[8,128,512]{2,1,0:T(8,128)(2,1)S(1)}, u32[]{:S(2)}, u32[]{:S(2)}) %all-to-all-start.2) | async-done | bytes 1048608 | tf_op jit(solution)/shard_map/hidden/all_to_all | solution.py:17
  85.7 0.1 convert_reduce_fusion
  85.9 1.1 broadcast_in_dim.96
  87.0 3.6 %all-to-all-start.3 = ((bf16[8,128,512]{2,1,0:T(8,128)(2,1)}), bf16[8,128,512]{2,1,0:T(8,128)(2,1)S(1)}, u32[]{:S(2)}, u32[]{:S(2)}) async-start(bf16[8,128,512]{2,1,0:T(8,128)(2,1)} %broadcast_in_dim.96), calls=%async_computation.3 | async-start | bytes 2097152 | tf_op jit(solution)/shard_map/hidden/all_to_all | solution.py:17
  90.5 4.8 %collective-permute-start.3 = (bf16[256,512]{1,0:T(8,128)(2,1)S(1)}, bf16[256,512]{1,0:T(8,128)(2,1)S(1)}, u32[]{:S(2)}, u32[]{:S(2)}) collective-permute-start(bf16[256,512]{1,0:T(8,128)(2,1)S(1)} %pad_maximum_fusion.2), channel_id=1, source_target_pairs={{0,8},{8,0},{1,9},{9,1},{2,10},{10,2},{3,11},{11,3},{4,12},{12,4},... | collective-permute-start | bytes 786440 | tf_op jit(solution)/shard_map/hidden/ppermute | solution.py:147
  95.3 15.3 %collective-permute-done.3 = bf16[256,512]{1,0:T(8,128)(2,1)S(1)} collective-permute-done((bf16[256,512]{1,0:T(8,128)(2,1)S(1)}, bf16[256,512]{1,0:T(8,128)(2,1)S(1)}, u32[]{:S(2)}, u32[]{:S(2)}) %collective-permute-start.3) | collective-permute-done | bytes 262176 | tf_op jit(solution)/shard_map/hidden/ppermute | solution.py:147
  110.6 1.5 fusion.8
  112.1 0.3 fusion.6
  112.5 0.9 copy-done.2
  113.4 0.3 fusion.7
  113.7 0.9 copy-done.4
  114.6 0.3 fusion.9
  114.9 0.8 reshape.141
  115.8 4.5 %all-to-all-start.4 = ((bf16[32,4,1024]{2,1,0:T(4,128)(2,1)}), bf16[32,4,1024]{2,1,0:T(4,128)(2,1)S(1)}, u32[]{:S(2)}, u32[]{:S(2)}) async-start(bf16[32,4,1024]{2,1,0:T(4,128)(2,1)} %reshape.141), calls=%async_computation.4 | async-start | bytes 524288 | tf_op jit(solution)/shard_map/give_back/all_to_all | solution.py:17
  120.4 0.7 fusion.59
  126.3 0.5 fusion.43
  126.8 5.6 %collective-permute-start.8 = (bf16[2,256,512]{2,1,0:T(8,128)(2,1)S(1)}, bf16[2,256,512]{2,1,0:T(8,128)(2,1)S(1)}, u32[]{:S(2)}, u32[]{:S(2)}) collective-permute-start(bf16[2,256,512]{2,1,0:T(8,128)(2,1)S(1)} %pad_maximum_fusion.1.first), channel_id=1, source_target_pairs={{0,4},{2,6},{4,0},{6,2},{1,5},{3,7},{5,1},{7,3},{8,12},{10,14},{12... | collective-permute-start | bytes 1572872 | tf_op jit(solution)/shard_map/all_rows/ppermute | solution.py:200
  132.4 2.0 %collective-permute-start.9 = (bf16[2,256,512]{2,1,0:T(8,128)(2,1)S(1)}, bf16[2,256,512]{2,1,0:T(8,128)(2,1)S(1)}, u32[]{:S(2)}, u32[]{:S(2)}) collective-permute-start(bf16[2,256,512]{2,1,0:T(8,128)(2,1)S(1)} %pad_maximum_fusion.1.first), channel_id=1, source_target_pairs={{0,6},{2,0},{4,2},{6,4},{1,7},{3,1},{5,3},{7,5},{8,14},{10,8},{12,... | collective-permute-start | bytes 1572872 | tf_op jit(solution)/shard_map/all_rows/ppermute | solution.py:200
  134.4 3.3 %collective-permute-start.6 = (bf16[2,256,512]{2,1,0:T(8,128)(2,1)S(1)}, bf16[2,256,512]{2,1,0:T(8,128)(2,1)S(1)}, u32[]{:S(2)}, u32[]{:S(2)}) collective-permute-start(bf16[2,256,512]{2,1,0:T(8,128)(2,1)S(1)} %pad_maximum_fusion.1.first), channel_id=1, source_target_pairs={{0,2},{2,4},{4,6},{6,0},{1,3},{3,5},{5,7},{7,1},{8,10},{10,12},{12... | collective-permute-start | bytes 1572872 | tf_op jit(solution)/shard_map/all_rows/ppermute | solution.py:200
  137.8 0.1 copy.41
  137.9 0.1 copy.42
  138.0 0.1 copy.43
  138.2 0.1 copy.44
  138.3 3.5 %collective-permute-start.5 = (bf16[128,512]{0,1:T(8,128)(2,1)S(1)}, bf16[128,512]{0,1:T(8,128)(2,1)S(1)}, u32[]{:S(2)}, u32[]{:S(2)}) collective-permute-start(bf16[128,512]{0,1:T(8,128)(2,1)S(1)} %pad_maximum_fusion.6), channel_id=1, source_target_pairs={{0,1},{1,0},{2,3},{3,2},{4,5},{5,4},{6,7},{7,6},{8,9},{9,8},{10,11... | collective-permute-start | bytes 393224 | tf_op jit(solution)/shard_map/slot_units/ppermute | solution.py:25
  141.9 0.9 fusion.4.after_ref
  142.8 0.9 broadcast_in_dim.100
  143.7 4.3 %all-to-all-start.5 = ((bf16[8,32,1024]{2,1,0:T(8,128)(2,1)}), bf16[8,32,1024]{2,1,0:T(8,128)(2,1)}, u32[]{:S(2)}, u32[]{:S(2)}) async-start(bf16[8,32,1024]{2,1,0:T(8,128)(2,1)} %broadcast_in_dim.100), calls=%async_computation.5 | async-start | bytes 1048576 | tf_op jit(solution)/shard_map/result/all_to_all | solution.py:17
  150.7 4.6 %collective-permute-done.9.second = bf16[2,256,512]{2,1,0:T(8,128)(2,1)S(1)} collective-permute-done((bf16[2,256,512]{2,1,0:T(8,128)(2,1)S(1)}, bf16[2,256,512]{2,1,0:T(8,128)(2,1)S(1)}, u32[]{:S(2)}, u32[]{:S(2)}) %collective-permute-start.9) | collective-permute-done | bytes 524320 | tf_op jit(solution)/shard_map/all_rows/ppermute | solution.py:200
  155.3 0.6 new_slices.4
  155.9 4.7 %collective-permute-start.10 = (bf16[4,256,256]{2,1,0:T(8,128)(2,1)S(1)}, bf16[4,256,256]{2,1,0:T(8,128)(2,1)S(1)}, u32[]{:S(2)}, u32[]{:S(2)}) collective-permute-start(bf16[4,256,256]{2,1,0:T(8,128)(2,1)S(1)} %get-tuple-element.29), channel_id=1, source_target_pairs={{0,1},{1,0},{2,3},{3,2},{4,5},{5,4},{6,7},{7,6},{8,9},{9,8},{10,11... | collective-permute-start | bytes 1572872 | tf_op jit(solution)/shard_map/new_slices/ppermute | solution.py:25
  160.7 1.3 new_slices.3
  162.0 1.9 %collective-permute-start.7 = (bf16[4,256,256]{2,1,0:T(8,128)(2,1)}, bf16[4,256,256]{2,1,0:T(8,128)(2,1)S(1)}, u32[]{:S(2)}, u32[]{:S(2)}) collective-permute-start(bf16[4,256,256]{2,1,0:T(8,128)(2,1)} %get-tuple-element.26), channel_id=1, source_target_pairs={{0,1},{1,0},{2,3},{3,2},{4,5},{5,4},{6,7},{7,6},{8,9},{9,8},{10,11... | collective-permute-start | bytes 1572872 | tf_op jit(solution)/shard_map/new_slices/ppermute | solution.py:25
  164.0 0.8 dynamic-slice_bitcast_fusion
  164.7 2.4 %collective-permute-start.4 = (bf16[32,512]{1,0:T(8,128)(2,1)S(1)}, bf16[32,512]{1,0:T(8,128)(2,1)S(1)}, u32[]{:S(2)}, u32[]{:S(2)}) collective-permute-start(bf16[32,512]{1,0:T(8,128)(2,1)S(1)} %dynamic-slice_bitcast_fusion), channel_id=1, source_target_pairs={{0,1},{1,0},{2,3},{3,2},{4,5},{5,4},{6,7},{7,6},{8,9},{9,8},{10,11... | collective-permute-start | bytes 98312 | tf_op jit(solution)/shard_map/result/ppermute | solution.py:25
  169.7 0.8 fusion.23
  170.5 0.6 fusion.56
  171.1 2.4 %new_slices.5 = (bf16[128,4096]{1,0:T(8,128)(2,1)}, bf16[128,4096]{1,0:T(8,128)(2,1)}) custom-call(s32[16]{0:T(128)S(1)} %fusion.40.source_ref, bf16[4,128,256]{2,1,0:T(8,128)(2,1)S(1)} %get-tuple-element.24.refs_0_, bf16[4,128,256]{2,1,0:T(8,128)(2,1)S(1)} %get-tuple-element.25.refs_1_, bf16[4,256,256]{2,1,0:T(8,128)(2,1)S(1)} %collective-permute-done.7.refs_2_, ...), custom_call_target="tpu_custom_call" | custom-call | tf_op jit(solution)/shard_map/new_slices/pallas_call | solution.py:234
  (54 shorter events, 0.9 us)
Async XLA Ops:
  0.6 11.9 %copy-start.7 = (s32[32,2]{0,1:T(2,128)S(1)}, s32[32,2]{0,1:T(2,128)}, u32[]{:S(2)}) copy-start(s32[32,2]{0,1:T(2,128)} %param.9) | copy-start | bytes 772
  0.6 12.5 %copy-start.8 = (s32[16]{0:T(128)S(1)}, s32[16]{0:T(128)}, u32[]{:S(2)}) copy-start(s32[16]{0:T(128)} %param.13) | copy-start | bytes 196
  0.7 17.2 %copy-start.10 = (f32[32,2]{0,1:T(2,128)S(1)}, f32[32,2]{0,1:T(2,128)}, u32[]{:S(2)}) copy-start(f32[32,2]{0,1:T(2,128)} %param.10) | copy-start | bytes 772
  2.3 21.7 %all-to-all-start = ((bf16[16,32,512]{2,1,0:T(8,128)(2,1)}), bf16[16,32,512]{2,1,0:T(8,128)(2,1)S(1)}, u32[]{:S(2)}, u32[]{:S(2)}) async-start(bf16[16,32,512]{2,1,0:T(8,128)(2,1)} %broadcast_in_dim.88), calls=%async_computation | async-start | bytes 1048576 | tf_op jit(solution)/shard_map/token_blocks/all_to_all | solution.py:17
  12.6 26.0 %copy-start.1 = (bf16[2048,256]{1,0:T(8,128)(2,1)S(1)}, bf16[2048,256]{1,0:T(8,128)(2,1)}, u32[]{:S(2)}) copy-start(bf16[2048,256]{1,0:T(8,128)(2,1)} %param.11) | copy-start | bytes 3145732
  12.7 29.2 %copy-start = (bf16[2048,256]{1,0:T(8,128)(2,1)S(1)}, bf16[2048,256]{1,0:T(8,128)(2,1)}, u32[]{:S(2)}) copy-start(bf16[2048,256]{1,0:T(8,128)(2,1)} %param.12) | copy-start | bytes 3145732
  25.1 32.7 %all-to-all-start.1 = ((bf16[32,4,1024]{2,1,0:T(4,128)(2,1)}), bf16[32,4,1024]{2,1,0:T(4,128)(2,1)}, u32[]{:S(2)}, u32[]{:S(2)}) async-start(bf16[32,4,1024]{2,1,0:T(4,128)(2,1)} %bitcast.4), calls=%async_computation.1 | async-start | bytes 524288 | tf_op jit(solution)/shard_map/dispatch/all_to_all | solution.py:17
  38.7 21.1 %collective-permute-start.1 = (bf16[2048,256]{1,0:T(8,128)(2,1)S(1)}, bf16[2048,256]{1,0:T(8,128)(2,1)S(1)}, u32[]{:S(2)}, u32[]{:S(2)}) collective-permute-start(bf16[2048,256]{1,0:T(8,128)(2,1)S(1)} %copy-done.1), channel_id=1, source_target_pairs={{0,1},{1,0},{2,3},{3,2},{4,5},{5,4},{6,7},{7,6},{8,9},{9,8},{10,11... | collective-permute-start | bytes 3145736 | tf_op jit(solution)/shard_map/weights/ppermute | solution.py:25
  41.9 18.8 %collective-permute-start.2 = (bf16[2048,256]{1,0:T(8,128)(2,1)S(1)}, bf16[2048,256]{1,0:T(8,128)(2,1)}, u32[]{:S(2)}, u32[]{:S(2)}) collective-permute-start(bf16[2048,256]{1,0:T(8,128)(2,1)S(1)} %copy-done), channel_id=1, source_target_pairs={{0,1},{1,0},{2,3},{3,2},{4,5},{5,4},{6,7},{7,6},{8,9},{9,8},{10,11... | collective-permute-start | bytes 3145736 | tf_op jit(solution)/shard_map/weights/ppermute | solution.py:25
  59.7 1.0 copy-start.3
  63.5 22.2 %all-to-all-start.2 = ((bf16[8,128,512]{2,1,0:T(8,128)(2,1)}), bf16[8,128,512]{2,1,0:T(8,128)(2,1)S(1)}, u32[]{:S(2)}, u32[]{:S(2)}) async-start(bf16[8,128,512]{2,1,0:T(8,128)(2,1)} %pad_maximum_fusion), calls=%async_computation.2 | async-start | bytes 2097152 | tf_op jit(solution)/shard_map/hidden/all_to_all | solution.py:17
  68.4 5.7 %collective-permute-start = (bf16[128,512]{1,0:T(8,128)(2,1)S(1)}, bf16[128,512]{1,0:T(8,128)(2,1)S(1)}, u32[]{:S(2)}, u32[]{:S(2)}) collective-permute-start(bf16[128,512]{1,0:T(8,128)(2,1)S(1)} %pad_maximum_fusion.4), channel_id=1, source_target_pairs={{0,1},{1,0},{2,3},{3,2},{4,5},{5,4},{6,7},{7,6},{8,9},{9,8},{10,11... | collective-permute-start | bytes 393224 | tf_op jit(solution)/shard_map/hidden/ppermute | solution.py:25
  74.2 16.3 %copy-start.5 = (bf16[256,512]{1,0:T(8,128)(2,1)}, bf16[256,512]{1,0:T(8,128)(2,1)S(1)}, u32[]{:S(2)}) copy-start(bf16[256,512]{1,0:T(8,128)(2,1)S(1)} %pad_maximum_fusion.2) | copy-start | bytes 786436
  87.0 23.6 %all-to-all-start.3 = ((bf16[8,128,512]{2,1,0:T(8,128)(2,1)}), bf16[8,128,512]{2,1,0:T(8,128)(2,1)S(1)}, u32[]{:S(2)}, u32[]{:S(2)}) async-start(bf16[8,128,512]{2,1,0:T(8,128)(2,1)} %broadcast_in_dim.96), calls=%async_computation.3 | async-start | bytes 2097152 | tf_op jit(solution)/shard_map/hidden/all_to_all | solution.py:17
  90.5 20.1 %collective-permute-start.3 = (bf16[256,512]{1,0:T(8,128)(2,1)S(1)}, bf16[256,512]{1,0:T(8,128)(2,1)S(1)}, u32[]{:S(2)}, u32[]{:S(2)}) collective-permute-start(bf16[256,512]{1,0:T(8,128)(2,1)S(1)} %pad_maximum_fusion.2), channel_id=1, source_target_pairs={{0,8},{8,0},{1,9},{9,1},{2,10},{10,2},{3,11},{11,3},{4,12},{12,4},... | collective-permute-start | bytes 786440 | tf_op jit(solution)/shard_map/hidden/ppermute | solution.py:147
  112.1 1.2 copy-start.2
  113.4 1.2 copy-start.4
  114.9 5.5 %copy-start.9 = (s32[16]{0:T(128)S(1)}, s32[16]{0:T(128)}, u32[]{:S(2)}) copy-start(s32[16]{0:T(128)} %param.14) | copy-start | bytes 196
  114.9 11.9 %copy-start.6 = (bf16[256,512]{1,0:T(8,128)(2,1)S(1)}, bf16[256,512]{1,0:T(8,128)(2,1)}, u32[]{:S(2)}) copy-start(bf16[256,512]{1,0:T(8,128)(2,1)} %copy-done.5) | copy-start | bytes 786436
  115.8 26.1 %all-to-all-start.4 = ((bf16[32,4,1024]{2,1,0:T(4,128)(2,1)}), bf16[32,4,1024]{2,1,0:T(4,128)(2,1)S(1)}, u32[]{:S(2)}, u32[]{:S(2)}) async-start(bf16[32,4,1024]{2,1,0:T(4,128)(2,1)} %reshape.141), calls=%async_computation.4 | async-start | bytes 524288 | tf_op jit(solution)/shard_map/give_back/all_to_all | solution.py:17
  126.8 23.8 %collective-permute-start.8 = (bf16[2,256,512]{2,1,0:T(8,128)(2,1)S(1)}, bf16[2,256,512]{2,1,0:T(8,128)(2,1)S(1)}, u32[]{:S(2)}, u32[]{:S(2)}) collective-permute-start(bf16[2,256,512]{2,1,0:T(8,128)(2,1)S(1)} %pad_maximum_fusion.1.first), channel_id=1, source_target_pairs={{0,4},{2,6},{4,0},{6,2},{1,5},{3,7},{5,1},{7,3},{8,12},{10,14},{12... | collective-permute-start | bytes 1572872 | tf_op jit(solution)/shard_map/all_rows/ppermute | solution.py:200
  132.4 22.9 %collective-permute-start.9 = (bf16[2,256,512]{2,1,0:T(8,128)(2,1)S(1)}, bf16[2,256,512]{2,1,0:T(8,128)(2,1)S(1)}, u32[]{:S(2)}, u32[]{:S(2)}) collective-permute-start(bf16[2,256,512]{2,1,0:T(8,128)(2,1)S(1)} %pad_maximum_fusion.1.first), channel_id=1, source_target_pairs={{0,6},{2,0},{4,2},{6,4},{1,7},{3,1},{5,3},{7,5},{8,14},{10,8},{12,... | collective-permute-start | bytes 1572872 | tf_op jit(solution)/shard_map/all_rows/ppermute | solution.py:200
  134.4 26.3 %collective-permute-start.6 = (bf16[2,256,512]{2,1,0:T(8,128)(2,1)S(1)}, bf16[2,256,512]{2,1,0:T(8,128)(2,1)S(1)}, u32[]{:S(2)}, u32[]{:S(2)}) collective-permute-start(bf16[2,256,512]{2,1,0:T(8,128)(2,1)S(1)} %pad_maximum_fusion.1.first), channel_id=1, source_target_pairs={{0,2},{2,4},{4,6},{6,0},{1,3},{3,5},{5,7},{7,1},{8,10},{10,12},{12... | collective-permute-start | bytes 1572872 | tf_op jit(solution)/shard_map/all_rows/ppermute | solution.py:200
  138.3 12.3 %collective-permute-start.5 = (bf16[128,512]{0,1:T(8,128)(2,1)S(1)}, bf16[128,512]{0,1:T(8,128)(2,1)S(1)}, u32[]{:S(2)}, u32[]{:S(2)}) collective-permute-start(bf16[128,512]{0,1:T(8,128)(2,1)S(1)} %pad_maximum_fusion.6), channel_id=1, source_target_pairs={{0,1},{1,0},{2,3},{3,2},{4,5},{5,4},{6,7},{7,6},{8,9},{9,8},{10,11... | collective-permute-start | bytes 393224 | tf_op jit(solution)/shard_map/slot_units/ppermute | solution.py:25
  143.7 20.3 %all-to-all-start.5 = ((bf16[8,32,1024]{2,1,0:T(8,128)(2,1)}), bf16[8,32,1024]{2,1,0:T(8,128)(2,1)}, u32[]{:S(2)}, u32[]{:S(2)}) async-start(bf16[8,32,1024]{2,1,0:T(8,128)(2,1)} %broadcast_in_dim.100), calls=%async_computation.5 | async-start | bytes 1048576 | tf_op jit(solution)/shard_map/result/all_to_all | solution.py:17
  155.9 15.2 %collective-permute-start.10 = (bf16[4,256,256]{2,1,0:T(8,128)(2,1)S(1)}, bf16[4,256,256]{2,1,0:T(8,128)(2,1)S(1)}, u32[]{:S(2)}, u32[]{:S(2)}) collective-permute-start(bf16[4,256,256]{2,1,0:T(8,128)(2,1)S(1)} %get-tuple-element.29), channel_id=1, source_target_pairs={{0,1},{1,0},{2,3},{3,2},{4,5},{5,4},{6,7},{7,6},{8,9},{9,8},{10,11... | collective-permute-start | bytes 1572872 | tf_op jit(solution)/shard_map/new_slices/ppermute | solution.py:25
  162.0 9.1 %collective-permute-start.7 = (bf16[4,256,256]{2,1,0:T(8,128)(2,1)}, bf16[4,256,256]{2,1,0:T(8,128)(2,1)S(1)}, u32[]{:S(2)}, u32[]{:S(2)}) collective-permute-start(bf16[4,256,256]{2,1,0:T(8,128)(2,1)} %get-tuple-element.26), channel_id=1, source_target_pairs={{0,1},{1,0},{2,3},{3,2},{4,5},{5,4},{6,7},{7,6},{8,9},{9,8},{10,11... | collective-permute-start | bytes 1572872 | tf_op jit(solution)/shard_map/new_slices/ppermute | solution.py:25
  164.7 5.0 %collective-permute-start.4 = (bf16[32,512]{1,0:T(8,128)(2,1)S(1)}, bf16[32,512]{1,0:T(8,128)(2,1)S(1)}, u32[]{:S(2)}, u32[]{:S(2)}) collective-permute-start(bf16[32,512]{1,0:T(8,128)(2,1)S(1)} %dynamic-slice_bitcast_fusion), channel_id=1, source_target_pairs={{0,1},{1,0},{2,3},{3,2},{4,5},{5,4},{6,7},{7,6},{8,9},{9,8},{10,11... | collective-permute-start | bytes 98312 | tf_op jit(solution)/shard_map/result/ppermute | solution.py:25

commit v9 on v8

--- a/solution.py
+++ b/solution.py
@@ -118,6 +118,26 @@
         rows = exchange(placed.reshape(group_count, held_slots, 4 * width), "expert")
         rows = rows.reshape(core_rows, 4 * width)
 
+    def found(place):
+        source = pick(inverse, place)
+        return source // 2, jnp.where(source % 2 == core, 0, 2 * width)
+
+    def slot(place):
+        block = pick(new_slots, place)
+        return block // 2, block % 2 * unit_width
+
+    column = lax.axis_size("x")
+    source = inverse // 2
+    back = (lax.axis_index("x") - source % column) % column
+    other_y = (source // column != lax.axis_index("y")).astype(jnp.int32)
+    other_core = (inverse % 2 != core).astype(jnp.int32)
+    source = 8 * (back // 2) + 4 * other_core + 2 * other_y + back % 2
+    row_list = jnp.arange(core_rows, dtype=jnp.int32)
+    row_slot = row_list // capacity * capacity + row_list % held_slots * 2 + core
+    picker = (target.reshape(-1)[:, None] == row_slot[None, :]).astype(BF16)
+    places = [*found(cut), *found(other_cut), *slot(cut), *slot(other_cut)]
+    rows, source, picker, places = lax.optimization_barrier((rows, source, picker, places))
+
     def partial(weights, first):
         return sum(
             jnp.einsum(
@@ -159,9 +179,6 @@
         )
         sent_rows = half_rows.reshape(group_count, held_slots, 4 * width)
         half_rows = exchange(sent_rows, "expert")
-        row_list = jnp.arange(core_rows, dtype=jnp.int32)
-        row_slot = row_list // capacity * capacity + row_list % held_slots * 2 + core
-        picker = (target.reshape(-1)[:, None] == row_slot[None, :]).astype(BF16)
         entries = jnp.dot(picker, half_rows.reshape(core_rows, 4 * width), preferred_element_type=F32)
         is_out = jnp.arange(4 * width) // width % 2 == 0
         factor = jnp.where(is_out[None, None, :], gate_weights[:, :, None], 1.0)
@@ -170,32 +187,27 @@
     with jax.named_scope("result"):
         got = everywhere(own_result, CHIP)
 
-        def share(place):
-            source = pick(inverse, place)
-            first = jnp.where(source % 2 == core, 0, 2 * width)
-            return lax.dynamic_slice(got, (source // 2, 0, first), (1, tok_rows, 2 * width))[0]
-
-        result = (share(cut).astype(F32) + swap(share(other_cut)).astype(F32)).astype(BF16)
+        def share(chip_from, first):
+            return lax.dynamic_slice(got, (chip_from, 0, first), (1, tok_rows, 2 * width))[0]
+
+        own_share, their_share = share(*places[0:2]), swap(share(*places[2:4]))
 
     with jax.named_scope("slot_units"):
 
-        def of_slot(place):
-            block = pick(new_slots, place)
+        def of_slot(chip_from, first):
+            size = (1, core_rows, unit_width)
             return [
-                lax.dynamic_slice(
-                    units, (block // 2, 0, first + block % 2 * unit_width), (1, core_rows, unit_width)
-                )[0]
-                for first in (0, 2 * unit_width)
+                lax.dynamic_slice(units, (chip_from, 0, first + part), size)[0]
+                for part in (0, 2 * unit_width)
             ]
 
-        mine = of_slot(cut) + of_slot(other_cut)
+        mine = of_slot(*places[4:6]) + of_slot(*places[6:8])
         theirs = swap(jnp.concatenate(mine[2:] + mine[:2], axis=1))
         slot_units = jnp.concatenate([jnp.concatenate(mine, axis=1), theirs], axis=0).T
         own_units, other_units = slot_units[: 2 * unit_width], slot_units[2 * unit_width :]
 
     with jax.named_scope("all_rows"):
         pair = jnp.stack(lax.optimization_barrier((routed, rows_y, sent_rows))[:2])
-        column = lax.axis_size("x")
         pairs = [pair] + [
             lax.ppermute(pair, "x", [(i, (i + s) % column) for i in range(column)])
             for s in range(1, column)
@@ -225,11 +237,6 @@
                 compiler_params=LARGE,
             )(own_units, other_units, *pairs[2 * g : 2 * g + 2], own_result)
             held += [up_part, down_part, swap(theirs)]
-        source = inverse // 2
-        back = (lax.axis_index("x") - source % column) % column
-        other_y = (source // column != lax.axis_index("y")).astype(jnp.int32)
-        other_core = (inverse % 2 != core).astype(jnp.int32)
-        source = 8 * (back // 2) + 4 * other_core + 2 * other_y + back % 2
         grad = jax.ShapeDtypeStruct((unit_width, cut_count * width), BF16)
         up_grad, down_grad = pl.pallas_call(
             layout_kernel,
@@ -238,6 +245,10 @@
             out_specs=(VMEM, VMEM),
             compiler_params=LARGE,
         )(source, *held)
+        their_share, up_grad, down_grad = lax.optimization_barrier(
+            (their_share, up_grad, down_grad)
+        )
+    result = (own_share.astype(F32) + their_share.astype(F32)).astype(BF16)
     return (result[:, :width], result[:, width:], up_grad, down_grad)
 
 

time: 175 us -> 173 us (0.989)
  waiting for transfers between devices: 52.2 us -> 46.8 us
  starting transfers between devices: 79.2 us -> 83.6 us
    all_to_all x6, waiting for transfers between devices: 31.3 us -> 23.4 us  [exchange(): return lax.all_to_all(parts, axis, split_axis=0, concat_axis=0, tiled=True)]
    all_to_all x6, starting transfers between devices: 41.1 us -> 47.9 us  [exchange(): return lax.all_to_all(parts, axis, split_axis=0, concat_axis=0, tiled=True)]
    ppermute x3, waiting for transfers between devices: 4.65 us -> 6.94 us  [local(): lax.ppermute(pair, 'x', [(i, (i + s) % column) for i in range(column)])]
  transfers between devices with their start and end apart: 17 -> 17, of which waited for: 6 -> 7; matrix products, arithmetic and copies ran while one was open for 6% -> 5% of each run, Pallas kernels for 1% -> 3%
where the time goes in v9:
time: 173 us; the launch traced here: 171 us
  starting transfers between devices  83.6 us (48%)
  waiting for transfers between devices  46.8 us (27%)
  between operations  15.5 us (9%)
  local copies, waits for them, and re-layouts  10.1 us (6%)
  matrix products  6 us (3%)
  other arithmetic  4.74 us (3%)
  Pallas kernels  4.41 us (3%)
    all_to_all x6, starting transfers between devices, exchange(): return lax.all_to_all(parts, axis, split_axis=0, concat_axis=0, tiled=True)  47.9 us
    all_to_all x6, waiting for transfers between devices, exchange(): return lax.all_to_all(parts, axis, split_axis=0, concat_axis=0, tiled=True)  23.4 us
    ppermute x7, starting transfers between devices, swap(): return lax.ppermute(block, 'core', [(0, 1), (1, 0)])  21 us
    ppermute x1, waiting for transfers between devices, local(): rows_y = lax.ppermute(later_rows, 'y', [(0, 1), (1, 0)])  15.5 us
    ppermute x3, starting transfers between devices, local(): lax.ppermute(pair, 'x', [(i, (i + s) % column) for i in range(column)])  9.87 us
    ppermute x3, waiting for transfers between devices, local(): lax.ppermute(pair, 'x', [(i, (i + s) % column) for i in range(column)])  6.94 us
    ppermute x1, starting transfers between devices, local(): rows_y = lax.ppermute(later_rows, 'y', [(0, 1), (1, 0)])  4.78 us
  transfers between devices with their start and end apart: 17, of which 7 were waited for; matrix products, arithmetic and copies ran while one was open for 5% of the time, Pallas kernels for 3%

profile of v9, /device:TPU:1, one launch (start us, length us, event | category | flops | bytes accessed | tf_op | source)
XLA Modules:
  0.0 171.1 jit_solution(7894650607438570040)
XLA Ops:
  0.7 0.8 pad_maximum_fusion.7
  1.4 0.8 broadcast_in_dim.88
  2.3 10.2 %all-to-all-start = ((bf16[16,32,512]{2,1,0:T(8,128)(2,1)}), bf16[16,32,512]{2,1,0:T(8,128)(2,1)S(1)}, u32[]{:S(2)}, u32[]{:S(2)}) async-start(bf16[16,32,512]{2,1,0:T(8,128)(2,1)} %broadcast_in_dim.88), calls=%async_computation | async-start | bytes 1048576 | tf_op jit(solution)/shard_map/token_blocks/all_to_all | solution.py:17
  12.5 0.1 copy.38
  12.6 0.1 eq.83
  12.8 0.1 reduce_window_sum.11
  12.9 0.2 select_reduce_fusion
  13.1 0.6 fusion.59
  16.3 0.1 reduce_sum.48
  17.9 0.1 fusion.30
  18.0 6.0 %all-to-all-done = bf16[16,32,512]{2,1,0:T(8,128)(2,1)S(1)} async-done(((bf16[16,32,512]{2,1,0:T(8,128)(2,1)}), bf16[16,32,512]{2,1,0:T(8,128)(2,1)S(1)}, u32[]{:S(2)}, u32[]{:S(2)}) %all-to-all-start) | async-done | bytes 524320 | tf_op jit(solution)/shard_map/token_blocks/all_to_all | solution.py:17
  24.0 0.2 fusion.5
  24.3 0.8 broadcast_in_dim.95
  25.1 13.6 %all-to-all-start.1 = ((bf16[32,4,1024]{2,1,0:T(4,128)(2,1)}), bf16[32,4,1024]{2,1,0:T(4,128)(2,1)}, u32[]{:S(2)}, u32[]{:S(2)}) async-start(bf16[32,4,1024]{2,1,0:T(4,128)(2,1)} %bitcast.4), calls=%async_computation.1 | async-start | bytes 524288 | tf_op jit(solution)/shard_map/dispatch/all_to_all | solution.py:17
  38.7 3.3 %collective-permute-start.1 = (bf16[2048,256]{1,0:T(8,128)(2,1)S(1)}, bf16[2048,256]{1,0:T(8,128)(2,1)S(1)}, u32[]{:S(2)}, u32[]{:S(2)}) collective-permute-start(bf16[2048,256]{1,0:T(8,128)(2,1)S(1)} %copy-done.1), channel_id=1, source_target_pairs={{0,1},{1,0},{2,3},{3,2},{4,5},{5,4},{6,7},{7,6},{8,9},{9,8},{10,11... | collective-permute-start | bytes 3145736 | tf_op jit(solution)/shard_map/weights/ppermute | solution.py:25
  41.9 1.9 %collective-permute-start.2 = (bf16[2048,256]{1,0:T(8,128)(2,1)S(1)}, bf16[2048,256]{1,0:T(8,128)(2,1)}, u32[]{:S(2)}, u32[]{:S(2)}) collective-permute-start(bf16[2048,256]{1,0:T(8,128)(2,1)S(1)} %copy-done), channel_id=1, source_target_pairs={{0,1},{1,0},{2,3},{3,2},{4,5},{5,4},{6,7},{7,6},{8,9},{9,8},{10,11... | collective-permute-start | bytes 3145736 | tf_op jit(solution)/shard_map/weights/ppermute | solution.py:25
  44.0 0.6 fusion.57
  55.1 2.7 %all-to-all-done.1 = bf16[32,4,1024]{2,1,0:T(4,128)(2,1)} async-done(((bf16[32,4,1024]{2,1,0:T(4,128)(2,1)}), bf16[32,4,1024]{2,1,0:T(4,128)(2,1)}, u32[]{:S(2)}, u32[]{:S(2)}) %all-to-all-start.1) | async-done | bytes 262176 | tf_op jit(solution)/shard_map/dispatch/all_to_all | solution.py:17
  57.7 1.0 reshape.123
  58.8 0.5 fusion.28
  59.2 0.5 fusion.25
  59.7 0.5 fusion.3
  60.2 1.7 fusion.2
  61.9 1.1 pad_maximum_fusion
  63.0 4.9 %all-to-all-start.2 = ((bf16[8,128,512]{2,1,0:T(8,128)(2,1)}), bf16[8,128,512]{2,1,0:T(8,128)(2,1)S(1)}, u32[]{:S(2)}, u32[]{:S(2)}) async-start(bf16[8,128,512]{2,1,0:T(8,128)(2,1)} %pad_maximum_fusion), calls=%async_computation.2 | async-start | bytes 2097152 | tf_op jit(solution)/shard_map/hidden/all_to_all | solution.py:17
  68.0 4.8 %collective-permute-start = (bf16[128,512]{1,0:T(8,128)(2,1)S(1)}, bf16[128,512]{1,0:T(8,128)(2,1)S(1)}, u32[]{:S(2)}, u32[]{:S(2)}) collective-permute-start(bf16[128,512]{1,0:T(8,128)(2,1)S(1)} %pad_maximum_fusion.4), channel_id=1, source_target_pairs={{0,1},{1,0},{2,3},{3,2},{4,5},{5,4},{6,7},{7,6},{8,9},{9,8},{10,11... | collective-permute-start | bytes 393224 | tf_op jit(solution)/shard_map/hidden/ppermute | solution.py:25
  72.7 1.0 collective-permute-done
  73.7 11.5 %all-to-all-done.2 = bf16[8,128,512]{2,1,0:T(8,128)(2,1)S(1)} async-done(((bf16[8,128,512]{2,1,0:T(8,128)(2,1)}), bf16[8,128,512]{2,1,0:T(8,128)(2,1)S(1)}, u32[]{:S(2)}, u32[]{:S(2)}) %all-to-all-start.2) | async-done | bytes 1048608 | tf_op jit(solution)/shard_map/hidden/all_to_all | solution.py:17
  85.2 0.1 convert_reduce_fusion
  85.4 1.1 broadcast_in_dim.96
  86.5 3.6 %all-to-all-start.3 = ((bf16[8,128,512]{2,1,0:T(8,128)(2,1)}), bf16[8,128,512]{2,1,0:T(8,128)(2,1)S(1)}, u32[]{:S(2)}, u32[]{:S(2)}) async-start(bf16[8,128,512]{2,1,0:T(8,128)(2,1)} %broadcast_in_dim.96), calls=%async_computation.3 | async-start | bytes 2097152 | tf_op jit(solution)/shard_map/hidden/all_to_all | solution.py:17
  90.0 4.8 %collective-permute-start.3 = (bf16[256,512]{1,0:T(8,128)(2,1)S(1)}, bf16[256,512]{1,0:T(8,128)(2,1)}, u32[]{:S(2)}, u32[]{:S(2)}) collective-permute-start(bf16[256,512]{1,0:T(8,128)(2,1)S(1)} %pad_maximum_fusion.2), channel_id=1, source_target_pairs={{0,8},{8,0},{1,9},{9,1},{2,10},{10,2},{3,11},{11,3},{4,12},{12,4},... | collective-permute-start | bytes 786440 | tf_op jit(solution)/shard_map/hidden/ppermute | solution.py:167
  94.8 15.5 %collective-permute-done.3 = bf16[256,512]{1,0:T(8,128)(2,1)} collective-permute-done((bf16[256,512]{1,0:T(8,128)(2,1)S(1)}, bf16[256,512]{1,0:T(8,128)(2,1)}, u32[]{:S(2)}, u32[]{:S(2)}) %collective-permute-start.3) | collective-permute-done | bytes 262176 | tf_op jit(solution)/shard_map/hidden/ppermute | solution.py:167
  110.3 1.5 fusion.8
  111.8 0.3 fusion.6
  112.2 0.9 copy-done.2
  113.1 0.3 fusion.7
  113.4 0.3 fusion.9
  113.7 0.8 reshape.128
  114.5 8.7 %all-to-all-start.4 = ((bf16[32,4,1024]{2,1,0:T(4,128)(2,1)}), bf16[32,4,1024]{2,1,0:T(4,128)(2,1)S(1)}, u32[]{:S(2)}, u32[]{:S(2)}) async-start(bf16[32,4,1024]{2,1,0:T(4,128)(2,1)} %reshape.128), calls=%async_computation.4 | async-start | bytes 524288 | tf_op jit(solution)/shard_map/give_back/all_to_all | solution.py:17
  123.3 0.1 constant_dynamic-slice_fusion
  123.4 0.1 copy.41
  123.6 0.1 copy.42
  123.7 0.1 copy.43
  123.8 0.1 copy.44
  124.0 3.7 %collective-permute-start.5 = (bf16[128,512]{0,1:T(8,128)(2,1)S(1)}, bf16[128,512]{0,1:T(8,128)(2,1)S(1)}, u32[]{:S(2)}, u32[]{:S(2)}) collective-permute-start(bf16[128,512]{0,1:T(8,128)(2,1)S(1)} %pad_maximum_fusion.6), channel_id=1, source_target_pairs={{0,1},{1,0},{2,3},{3,2},{4,5},{5,4},{6,7},{7,6},{8,9},{9,8},{10,11... | collective-permute-start | bytes 393224 | tf_op jit(solution)/shard_map/slot_units/ppermute | solution.py:25
  127.7 1.0 pad_maximum_fusion.1.first
  128.7 4.6 %collective-permute-start.8 = (bf16[2,256,512]{2,1,0:T(8,128)(2,1)S(1)}, bf16[2,256,512]{2,1,0:T(8,128)(2,1)S(1)}, u32[]{:S(2)}, u32[]{:S(2)}) collective-permute-start(bf16[2,256,512]{2,1,0:T(8,128)(2,1)S(1)} %pad_maximum_fusion.1.first), channel_id=1, source_target_pairs={{0,4},{2,6},{4,0},{6,2},{1,5},{3,7},{5,1},{7,3},{8,12},{10,14},{12... | collective-permute-start | bytes 1572872 | tf_op jit(solution)/shard_map/all_rows/ppermute | solution.py:212
  133.3 2.8 %collective-permute-start.9 = (bf16[2,256,512]{2,1,0:T(8,128)(2,1)S(1)}, bf16[2,256,512]{2,1,0:T(8,128)(2,1)S(1)}, u32[]{:S(2)}, u32[]{:S(2)}) collective-permute-start(bf16[2,256,512]{2,1,0:T(8,128)(2,1)S(1)} %pad_maximum_fusion.1.first), channel_id=1, source_target_pairs={{0,6},{2,0},{4,2},{6,4},{1,7},{3,1},{5,3},{7,5},{8,14},{10,8},{12,... | collective-permute-start | bytes 1572872 | tf_op jit(solution)/shard_map/all_rows/ppermute | solution.py:212
  136.1 2.5 %collective-permute-start.6 = (bf16[2,256,512]{2,1,0:T(8,128)(2,1)S(1)}, bf16[2,256,512]{2,1,0:T(8,128)(2,1)S(1)}, u32[]{:S(2)}, u32[]{:S(2)}) collective-permute-start(bf16[2,256,512]{2,1,0:T(8,128)(2,1)S(1)} %pad_maximum_fusion.1.first), channel_id=1, source_target_pairs={{0,2},{2,4},{4,6},{6,0},{1,3},{3,5},{5,7},{7,1},{8,10},{10,12},{12... | collective-permute-start | bytes 1572872 | tf_op jit(solution)/shard_map/all_rows/ppermute | solution.py:212
  138.6 3.3 %all-to-all-done.4 = bf16[32,4,1024]{2,1,0:T(4,128)(2,1)S(1)} async-done(((bf16[32,4,1024]{2,1,0:T(4,128)(2,1)}), bf16[32,4,1024]{2,1,0:T(4,128)(2,1)S(1)}, u32[]{:S(2)}, u32[]{:S(2)}) %all-to-all-start.4) | async-done | bytes 262176 | tf_op jit(solution)/shard_map/give_back/all_to_all | solution.py:17
  142.0 0.2 fusion.4.after_ref
  142.2 0.9 broadcast_in_dim.100
  143.0 6.9 %all-to-all-start.5 = ((bf16[8,32,1024]{2,1,0:T(8,128)(2,1)}), bf16[8,32,1024]{2,1,0:T(8,128)(2,1)}, u32[]{:S(2)}, u32[]{:S(2)}) async-start(bf16[8,32,1024]{2,1,0:T(8,128)(2,1)} %broadcast_in_dim.100), calls=%async_computation.5 | async-start | bytes 1048576 | tf_op jit(solution)/shard_map/result/all_to_all | solution.py:17
  150.0 6.9 %collective-permute-done.9.second = bf16[2,256,512]{2,1,0:T(8,128)(2,1)S(1)} collective-permute-done((bf16[2,256,512]{2,1,0:T(8,128)(2,1)S(1)}, bf16[2,256,512]{2,1,0:T(8,128)(2,1)S(1)}, u32[]{:S(2)}, u32[]{:S(2)}) %collective-permute-start.9) | collective-permute-done | bytes 524320 | tf_op jit(solution)/shard_map/all_rows/ppermute | solution.py:212
  156.9 0.6 new_slices.4
  157.5 3.1 %collective-permute-start.10 = (bf16[4,256,256]{2,1,0:T(8,128)(2,1)S(1)}, bf16[4,256,256]{2,1,0:T(8,128)(2,1)S(1)}, u32[]{:S(2)}, u32[]{:S(2)}) collective-permute-start(bf16[4,256,256]{2,1,0:T(8,128)(2,1)S(1)} %get-tuple-element.54), channel_id=1, source_target_pairs={{0,1},{1,0},{2,3},{3,2},{4,5},{5,4},{6,7},{7,6},{8,9},{9,8},{10,11... | collective-permute-start | bytes 1572872 | tf_op jit(solution)/shard_map/new_slices/ppermute | solution.py:25
  160.6 1.3 new_slices.3
  162.0 1.9 %collective-permute-start.7 = (bf16[4,256,256]{2,1,0:T(8,128)(2,1)}, bf16[4,256,256]{2,1,0:T(8,128)(2,1)S(1)}, u32[]{:S(2)}, u32[]{:S(2)}) collective-permute-start(bf16[4,256,256]{2,1,0:T(8,128)(2,1)} %get-tuple-element.51), channel_id=1, source_target_pairs={{0,1},{1,0},{2,3},{3,2},{4,5},{5,4},{6,7},{7,6},{8,9},{9,8},{10,11... | collective-permute-start | bytes 1572872 | tf_op jit(solution)/shard_map/new_slices/ppermute | solution.py:25
  163.9 0.9 dynamic-slice_bitcast_fusion
  164.8 2.4 %collective-permute-start.4 = (bf16[32,512]{1,0:T(8,128)(2,1)S(1)}, bf16[32,512]{1,0:T(8,128)(2,1)S(1)}, u32[]{:S(2)}, u32[]{:S(2)}) collective-permute-start(bf16[32,512]{1,0:T(8,128)(2,1)S(1)} %dynamic-slice_bitcast_fusion), channel_id=1, source_target_pairs={{0,1},{1,0},{2,3},{3,2},{4,5},{5,4},{6,7},{7,6},{8,9},{9,8},{10,11... | collective-permute-start | bytes 98312 | tf_op jit(solution)/shard_map/result/ppermute | solution.py:25
  167.2 2.4 %new_slices.5 = (bf16[128,4096]{1,0:T(8,128)(2,1)}, bf16[128,4096]{1,0:T(8,128)(2,1)}) custom-call(s32[16]{0:T(128)S(1)} %fusion.38.source_ref, bf16[4,128,256]{2,1,0:T(8,128)(2,1)S(1)} %get-tuple-element.49.refs_0_, bf16[4,128,256]{2,1,0:T(8,128)(2,1)S(1)} %get-tuple-element.50.refs_1_, bf16[4,256,256]{2,1,0:T(8,128)(2,1)S(1)} %collective-permute-done.7.refs_2_, ...), custom_call_target="tpu_custom_call" | custom-call | tf_op jit(solution)/shard_map/new_slices/pallas_call | solution.py:241
  169.6 0.9 fusion.23
  170.5 0.6 fusion.54
  (48 shorter events, 0.9 us)
Async XLA Ops:
  0.6 11.9 %copy-start.3 = (s32[32,2]{0,1:T(2,128)S(1)}, s32[32,2]{0,1:T(2,128)}, u32[]{:S(2)}) copy-start(s32[32,2]{0,1:T(2,128)} %param.9) | copy-start | bytes 772
  0.6 12.5 %copy-start.4 = (s32[16]{0:T(128)S(1)}, s32[16]{0:T(128)}, u32[]{:S(2)}) copy-start(s32[16]{0:T(128)} %param.13) | copy-start | bytes 196
  0.7 17.3 %copy-start.6 = (f32[32,2]{0,1:T(2,128)S(1)}, f32[32,2]{0,1:T(2,128)}, u32[]{:S(2)}) copy-start(f32[32,2]{0,1:T(2,128)} %param.10) | copy-start | bytes 772
  2.3 21.7 %all-to-all-start = ((bf16[16,32,512]{2,1,0:T(8,128)(2,1)}), bf16[16,32,512]{2,1,0:T(8,128)(2,1)S(1)}, u32[]{:S(2)}, u32[]{:S(2)}) async-start(bf16[16,32,512]{2,1,0:T(8,128)(2,1)} %broadcast_in_dim.88), calls=%async_computation | async-start | bytes 1048576 | tf_op jit(solution)/shard_map/token_blocks/all_to_all | solution.py:17
  12.6 26.0 %copy-start.1 = (bf16[2048,256]{1,0:T(8,128)(2,1)S(1)}, bf16[2048,256]{1,0:T(8,128)(2,1)}, u32[]{:S(2)}) copy-start(bf16[2048,256]{1,0:T(8,128)(2,1)} %param.11) | copy-start | bytes 3145732
  12.7 29.2 %copy-start = (bf16[2048,256]{1,0:T(8,128)(2,1)S(1)}, bf16[2048,256]{1,0:T(8,128)(2,1)}, u32[]{:S(2)}) copy-start(bf16[2048,256]{1,0:T(8,128)(2,1)} %param.12) | copy-start | bytes 3145732
  12.7 31.2 %copy-start.5 = (s32[16]{0:T(128)S(1)}, s32[16]{0:T(128)}, u32[]{:S(2)}) copy-start(s32[16]{0:T(128)} %param.14) | copy-start | bytes 196
  25.1 32.7 %all-to-all-start.1 = ((bf16[32,4,1024]{2,1,0:T(4,128)(2,1)}), bf16[32,4,1024]{2,1,0:T(4,128)(2,1)}, u32[]{:S(2)}, u32[]{:S(2)}) async-start(bf16[32,4,1024]{2,1,0:T(4,128)(2,1)} %bitcast.4), calls=%async_computation.1 | async-start | bytes 524288 | tf_op jit(solution)/shard_map/dispatch/all_to_all | solution.py:17
  38.7 21.1 %collective-permute-start.1 = (bf16[2048,256]{1,0:T(8,128)(2,1)S(1)}, bf16[2048,256]{1,0:T(8,128)(2,1)S(1)}, u32[]{:S(2)}, u32[]{:S(2)}) collective-permute-start(bf16[2048,256]{1,0:T(8,128)(2,1)S(1)} %copy-done.1), channel_id=1, source_target_pairs={{0,1},{1,0},{2,3},{3,2},{4,5},{5,4},{6,7},{7,6},{8,9},{9,8},{10,11... | collective-permute-start | bytes 3145736 | tf_op jit(solution)/shard_map/weights/ppermute | solution.py:25
  41.9 18.3 %collective-permute-start.2 = (bf16[2048,256]{1,0:T(8,128)(2,1)S(1)}, bf16[2048,256]{1,0:T(8,128)(2,1)}, u32[]{:S(2)}, u32[]{:S(2)}) collective-permute-start(bf16[2048,256]{1,0:T(8,128)(2,1)S(1)} %copy-done), channel_id=1, source_target_pairs={{0,1},{1,0},{2,3},{3,2},{4,5},{5,4},{6,7},{7,6},{8,9},{9,8},{10,11... | collective-permute-start | bytes 3145736 | tf_op jit(solution)/shard_map/weights/ppermute | solution.py:25
  63.0 22.2 %all-to-all-start.2 = ((bf16[8,128,512]{2,1,0:T(8,128)(2,1)}), bf16[8,128,512]{2,1,0:T(8,128)(2,1)S(1)}, u32[]{:S(2)}, u32[]{:S(2)}) async-start(bf16[8,128,512]{2,1,0:T(8,128)(2,1)} %pad_maximum_fusion), calls=%async_computation.2 | async-start | bytes 2097152 | tf_op jit(solution)/shard_map/hidden/all_to_all | solution.py:17
  68.0 5.7 %collective-permute-start = (bf16[128,512]{1,0:T(8,128)(2,1)S(1)}, bf16[128,512]{1,0:T(8,128)(2,1)S(1)}, u32[]{:S(2)}, u32[]{:S(2)}) collective-permute-start(bf16[128,512]{1,0:T(8,128)(2,1)S(1)} %pad_maximum_fusion.4), channel_id=1, source_target_pairs={{0,1},{1,0},{2,3},{3,2},{4,5},{5,4},{6,7},{7,6},{8,9},{9,8},{10,11... | collective-permute-start | bytes 393224 | tf_op jit(solution)/shard_map/hidden/ppermute | solution.py:25
  86.5 23.8 %all-to-all-start.3 = ((bf16[8,128,512]{2,1,0:T(8,128)(2,1)}), bf16[8,128,512]{2,1,0:T(8,128)(2,1)S(1)}, u32[]{:S(2)}, u32[]{:S(2)}) async-start(bf16[8,128,512]{2,1,0:T(8,128)(2,1)} %broadcast_in_dim.96), calls=%async_computation.3 | async-start | bytes 2097152 | tf_op jit(solution)/shard_map/hidden/all_to_all | solution.py:17
  90.0 20.3 %collective-permute-start.3 = (bf16[256,512]{1,0:T(8,128)(2,1)S(1)}, bf16[256,512]{1,0:T(8,128)(2,1)}, u32[]{:S(2)}, u32[]{:S(2)}) collective-permute-start(bf16[256,512]{1,0:T(8,128)(2,1)S(1)} %pad_maximum_fusion.2), channel_id=1, source_target_pairs={{0,8},{8,0},{1,9},{9,1},{2,10},{10,2},{3,11},{11,3},{4,12},{12,4},... | collective-permute-start | bytes 786440 | tf_op jit(solution)/shard_map/hidden/ppermute | solution.py:167
  111.8 1.2 copy-start.2
  114.5 27.4 %all-to-all-start.4 = ((bf16[32,4,1024]{2,1,0:T(4,128)(2,1)}), bf16[32,4,1024]{2,1,0:T(4,128)(2,1)S(1)}, u32[]{:S(2)}, u32[]{:S(2)}) async-start(bf16[32,4,1024]{2,1,0:T(4,128)(2,1)} %reshape.128), calls=%async_computation.4 | async-start | bytes 524288 | tf_op jit(solution)/shard_map/give_back/all_to_all | solution.py:17
  124.0 14.6 %collective-permute-start.5 = (bf16[128,512]{0,1:T(8,128)(2,1)S(1)}, bf16[128,512]{0,1:T(8,128)(2,1)S(1)}, u32[]{:S(2)}, u32[]{:S(2)}) collective-permute-start(bf16[128,512]{0,1:T(8,128)(2,1)S(1)} %pad_maximum_fusion.6), channel_id=1, source_target_pairs={{0,1},{1,0},{2,3},{3,2},{4,5},{5,4},{6,7},{7,6},{8,9},{9,8},{10,11... | collective-permute-start | bytes 393224 | tf_op jit(solution)/shard_map/slot_units/ppermute | solution.py:25
  128.7 21.3 %collective-permute-start.8 = (bf16[2,256,512]{2,1,0:T(8,128)(2,1)S(1)}, bf16[2,256,512]{2,1,0:T(8,128)(2,1)S(1)}, u32[]{:S(2)}, u32[]{:S(2)}) collective-permute-start(bf16[2,256,512]{2,1,0:T(8,128)(2,1)S(1)} %pad_maximum_fusion.1.first), channel_id=1, source_target_pairs={{0,4},{2,6},{4,0},{6,2},{1,5},{3,7},{5,1},{7,3},{8,12},{10,14},{12... | collective-permute-start | bytes 1572872 | tf_op jit(solution)/shard_map/all_rows/ppermute | solution.py:212
  133.3 23.6 %collective-permute-start.9 = (bf16[2,256,512]{2,1,0:T(8,128)(2,1)S(1)}, bf16[2,256,512]{2,1,0:T(8,128)(2,1)S(1)}, u32[]{:S(2)}, u32[]{:S(2)}) collective-permute-start(bf16[2,256,512]{2,1,0:T(8,128)(2,1)S(1)} %pad_maximum_fusion.1.first), channel_id=1, source_target_pairs={{0,6},{2,0},{4,2},{6,4},{1,7},{3,1},{5,3},{7,5},{8,14},{10,8},{12,... | collective-permute-start | bytes 1572872 | tf_op jit(solution)/shard_map/all_rows/ppermute | solution.py:212
  136.1 24.5 %collective-permute-start.6 = (bf16[2,256,512]{2,1,0:T(8,128)(2,1)S(1)}, bf16[2,256,512]{2,1,0:T(8,128)(2,1)S(1)}, u32[]{:S(2)}, u32[]{:S(2)}) collective-permute-start(bf16[2,256,512]{2,1,0:T(8,128)(2,1)S(1)} %pad_maximum_fusion.1.first), channel_id=1, source_target_pairs={{0,2},{2,4},{4,6},{6,0},{1,3},{3,5},{5,7},{7,1},{8,10},{10,12},{12... | collective-permute-start | bytes 1572872 | tf_op jit(solution)/shard_map/all_rows/ppermute | solution.py:212
  143.0 20.9 %all-to-all-start.5 = ((bf16[8,32,1024]{2,1,0:T(8,128)(2,1)}), bf16[8,32,1024]{2,1,0:T(8,128)(2,1)}, u32[]{:S(2)}, u32[]{:S(2)}) async-start(bf16[8,32,1024]{2,1,0:T(8,128)(2,1)} %broadcast_in_dim.100), calls=%async_computation.5 | async-start | bytes 1048576 | tf_op jit(solution)/shard_map/result/all_to_all | solution.py:17
  157.5 9.7 %collective-permute-start.10 = (bf16[4,256,256]{2,1,0:T(8,128)(2,1)S(1)}, bf16[4,256,256]{2,1,0:T(8,128)(2,1)S(1)}, u32[]{:S(2)}, u32[]{:S(2)}) collective-permute-start(bf16[4,256,256]{2,1,0:T(8,128)(2,1)S(1)} %get-tuple-element.54), channel_id=1, source_target_pairs={{0,1},{1,0},{2,3},{3,2},{4,5},{5,4},{6,7},{7,6},{8,9},{9,8},{10,11... | collective-permute-start | bytes 1572872 | tf_op jit(solution)/shard_map/new_slices/ppermute | solution.py:25
  162.0 5.2 %collective-permute-start.7 = (bf16[4,256,256]{2,1,0:T(8,128)(2,1)}, bf16[4,256,256]{2,1,0:T(8,128)(2,1)S(1)}, u32[]{:S(2)}, u32[]{:S(2)}) collective-permute-start(bf16[4,256,256]{2,1,0:T(8,128)(2,1)} %get-tuple-element.51), channel_id=1, source_target_pairs={{0,1},{1,0},{2,3},{3,2},{4,5},{5,4},{6,7},{7,6},{8,9},{9,8},{10,11... | collective-permute-start | bytes 1572872 | tf_op jit(solution)/shard_map/new_slices/ppermute | solution.py:25
  164.8 4.9 %collective-permute-start.4 = (bf16[32,512]{1,0:T(8,128)(2,1)S(1)}, bf16[32,512]{1,0:T(8,128)(2,1)S(1)}, u32[]{:S(2)}, u32[]{:S(2)}) collective-permute-start(bf16[32,512]{1,0:T(8,128)(2,1)S(1)} %dynamic-slice_bitcast_fusion), channel_id=1, source_target_pairs={{0,1},{1,0},{2,3},{3,2},{4,5},{5,4},{6,7},{7,6},{8,9},{9,8},{10,11... | collective-permute-start | bytes 98312 | tf_op jit(solution)/shard_map/result/ppermute | solution.py:25

commit v10 on v9

--- a/solution.py
+++ b/solution.py
@@ -85,10 +85,13 @@
         cut_list[:, None] * (old_rows[:, None] == cut_list[None, :]).astype(jnp.int32), axis=0
     )
 
+    def in_slots(weights):
+        blocks = rows_at(weights.reshape(cut_count, unit_width, width), new_slots)
+        shape = (chips, 2 * unit_width, width)
+        return [blocks.reshape(shape), swap(blocks).reshape(shape)]
+
     with jax.named_scope("weights"):
-        shape = (chips, 2 * unit_width, width)
-        up = [old_up.reshape(shape), swap(old_up).reshape(shape)]
-        down = [old_down.reshape(shape), swap(old_down).reshape(shape)]
+        up, down = in_slots(old_up), in_slots(old_down)
 
     with jax.named_scope("token_blocks"):
         blocks = everywhere(jnp.concatenate([tokens, cotangent], axis=1), CUTS)
@@ -122,10 +125,6 @@
         source = pick(inverse, place)
         return source // 2, jnp.where(source % 2 == core, 0, 2 * width)
 
-    def slot(place):
-        block = pick(new_slots, place)
-        return block // 2, block % 2 * unit_width
-
     column = lax.axis_size("x")
     source = inverse // 2
     back = (lax.axis_index("x") - source % column) % column
@@ -135,7 +134,7 @@
     row_list = jnp.arange(core_rows, dtype=jnp.int32)
     row_slot = row_list // capacity * capacity + row_list % held_slots * 2 + core
     picker = (target.reshape(-1)[:, None] == row_slot[None, :]).astype(BF16)
-    places = [*found(cut), *found(other_cut), *slot(cut), *slot(other_cut)]
+    places = [*found(cut), *found(other_cut)]
     rows, source, picker, places = lax.optimization_barrier((rows, source, picker, places))
 
     def partial(weights, first):
@@ -165,8 +164,13 @@
         routed = jnp.concatenate([routed, others], axis=0)
         later_rows, own_units = lax.optimization_barrier((routed, own_units))
         rows_y = lax.ppermute(later_rows, "y", [(0, 1), (1, 0)])
+        halves = [own_units[:, i * unit_width : (i + 1) * unit_width] for i in range(4)]
+        mine = [jnp.where(core == 0, halves[i], halves[i + 1]) for i in (0, 2)]
+        mine += [jnp.where(core == 0, halves[i + 1], halves[i]) for i in (0, 2)]
+        theirs = swap(jnp.concatenate(mine[2:] + mine[:2], axis=1))
+        slot_units = jnp.concatenate([jnp.concatenate(mine, axis=1), theirs], axis=0).T
         units = everywhere(own_units, CHIP)
-        units, rows_y = lax.optimization_barrier((units, rows_y))
+        units, rows_y, slot_units = lax.optimization_barrier((units, rows_y, slot_units))
         hidden, pre_grad = units[:, :, : 2 * unit_width], units[:, :, 2 * unit_width :]
 
     def rows_of(units, weights):
@@ -192,20 +196,6 @@
 
         own_share, their_share = share(*places[0:2]), swap(share(*places[2:4]))
 
-    with jax.named_scope("slot_units"):
-
-        def of_slot(chip_from, first):
-            size = (1, core_rows, unit_width)
-            return [
-                lax.dynamic_slice(units, (chip_from, 0, first + part), size)[0]
-                for part in (0, 2 * unit_width)
-            ]
-
-        mine = of_slot(*places[4:6]) + of_slot(*places[6:8])
-        theirs = swap(jnp.concatenate(mine[2:] + mine[:2], axis=1))
-        slot_units = jnp.concatenate([jnp.concatenate(mine, axis=1), theirs], axis=0).T
-        own_units, other_units = slot_units[: 2 * unit_width], slot_units[2 * unit_width :]
-
     with jax.named_scope("all_rows"):
         pair = jnp.stack(lax.optimization_barrier((routed, rows_y, sent_rows))[:2])
         pairs = [pair] + [
@@ -214,6 +204,7 @@
         ]
 
     with jax.named_scope("new_slices"):
+        own_units, other_units = slot_units[: 2 * unit_width], slot_units[2 * unit_width :]
         units_spec = pl.BlockSpec((2 * unit_width, slot_rows), lambda t: (0, 0))
         rows_spec = pl.BlockSpec((1, slot_rows, 2 * width), lambda t: (t, 0, 0))
         part_spec = pl.BlockSpec((2, unit_width, width), lambda t: (t, 0, 0))

time: 173 us -> 176 us (1.017)
  local copies, waits for them, and re-layouts: 10.1 us -> 16.6 us
  waiting for transfers between devices: 46.8 us -> 40.9 us
  between operations: 15.5 us -> 10.5 us
  matrix products: 6 us -> 9.28 us
  starting transfers between devices: 83.6 us -> 85.7 us
    ppermute x3, waiting for transfers between devices: 6.94 us -> 0.01 us  [local(): lax.ppermute(pair, 'x', [(i, (i + s) % column) for i in range(column)])]
    all_to_all x6, waiting for transfers between devices: 23.4 us -> 28.7 us  [exchange(): return lax.all_to_all(parts, axis, split_axis=0, concat_axis=0, tiled=True)]
    ppermute x1, waiting for transfers between devices: 15.5 us -> 10.2 us  [local(): rows_y = lax.ppermute(later_rows, 'y', [(0, 1), (1, 0)])]
    unnamed x15 -> x29, local copies, waits for them, and re-layouts: 1.02 us -> 5.32 us
    ppermute x7, starting transfers between devices: 21 us -> 24.3 us  [swap(): return lax.ppermute(block, 'core', [(0, 1), (1, 0)])]
    all_to_all x6, starting transfers between devices: 47.9 us -> 45.1 us  [exchange(): return lax.all_to_all(parts, axis, split_axis=0, concat_axis=0, tiled=True)]
    gather x0 -> x2, local copies, waits for them, and re-layouts: none -> 2.45 us  [rows_at(): return jnp.take(blocks, places, axis=0, mode='clip')]
  transfers between devices with their start and end apart: 17 -> 17, of which waited for: 7 -> 7; matrix products, arithmetic and copies ran while one was open for 5% -> 8% of each run, Pallas kernels for 3% -> 3%
where the time goes in v10:
time: 176 us; the launch traced here: 174 us
  starting transfers between devices  85.7 us (49%)
  waiting for transfers between devices  40.9 us (23%)
  local copies, waits for them, and re-layouts  16.6 us (9%)
  between operations  10.5 us (6%)
  matrix products  9.28 us (5%)
  other arithmetic  6.12 us (3%)
  Pallas kernels  5.15 us (3%)
    all_to_all x6, starting transfers between devices, exchange(): return lax.all_to_all(parts, axis, split_axis=0, concat_axis=0, tiled=True)  45.1 us
    all_to_all x6, waiting for transfers between devices, exchange(): return lax.all_to_all(parts, axis, split_axis=0, concat_axis=0, tiled=True)  28.7 us
    ppermute x7, starting transfers between devices, swap(): return lax.ppermute(block, 'core', [(0, 1), (1, 0)])  24.3 us
    ppermute x3, starting transfers between devices, local(): lax.ppermute(pair, 'x', [(i, (i + s) % column) for i in range(column)])  11.5 us
    ppermute x1, waiting for transfers between devices, local(): rows_y = lax.ppermute(later_rows, 'y', [(0, 1), (1, 0)])  10.2 us
    unnamed x29, local copies, waits for them, and re-layouts  5.32 us
    ppermute x1, starting transfers between devices, local(): rows_y = lax.ppermute(later_rows, 'y', [(0, 1), (1, 0)])  4.78 us
    dot_general x4, matrix products, partial(): jnp.einsum('rd,pud->pru', rows[:, first + j * width:first + (j + 1) * wid...  4.19 us
  transfers between devices with their start and end apart: 17, of which 7 were waited for; matrix products, arithmetic and copies ran while one was open for 8% of the time, Pallas kernels for 3%

profile of v10, /device:TPU:1, one launch (start us, length us, event | category | flops | bytes accessed | tf_op | source)
XLA Modules:
  0.0 174.2 jit_solution(1468259905904454171)
XLA Ops:
  0.7 0.8 pad_maximum_fusion.7
  1.5 0.8 broadcast_in_dim.93
  2.3 10.2 %all-to-all-start = ((bf16[16,32,512]{2,1,0:T(8,128)(2,1)}), bf16[16,32,512]{2,1,0:T(8,128)(2,1)S(1)}, u32[]{:S(2)}, u32[]{:S(2)}) async-start(bf16[16,32,512]{2,1,0:T(8,128)(2,1)} %broadcast_in_dim.93), calls=%async_computation | async-start | bytes 1048576 | tf_op jit(solution)/shard_map/token_blocks/all_to_all | solution.py:17
  13.0 0.2 select_reduce_fusion
  13.3 0.7 fusion.57
  18.4 5.7 %all-to-all-done = bf16[16,32,512]{2,1,0:T(8,128)(2,1)S(1)} async-done(((bf16[16,32,512]{2,1,0:T(8,128)(2,1)}), bf16[16,32,512]{2,1,0:T(8,128)(2,1)S(1)}, u32[]{:S(2)}, u32[]{:S(2)}) %all-to-all-start) | async-done | bytes 524320 | tf_op jit(solution)/shard_map/token_blocks/all_to_all | solution.py:17
  24.1 0.2 fusion.5
  24.4 0.8 broadcast_in_dim.100
  25.2 13.6 %all-to-all-start.1 = ((bf16[32,4,1024]{2,1,0:T(4,128)(2,1)}), bf16[32,4,1024]{2,1,0:T(4,128)(2,1)}, u32[]{:S(2)}, u32[]{:S(2)}) async-start(bf16[32,4,1024]{2,1,0:T(4,128)(2,1)} %bitcast.4), calls=%async_computation.1 | async-start | bytes 524288 | tf_op jit(solution)/shard_map/dispatch/all_to_all | solution.py:17
  38.8 0.6 gather_fusion
  39.4 3.3 %collective-permute-start.1 = (bf16[16,128,256]{2,1,0:T(8,128)(2,1)S(1)}, bf16[16,128,256]{2,1,0:T(8,128)(2,1)}, u32[]{:S(2)}, u32[]{:S(2)}) collective-permute-start(bf16[16,128,256]{2,1,0:T(8,128)(2,1)S(1)} %gather_fusion), channel_id=1, source_target_pairs={{0,1},{1,0},{2,3},{3,2},{4,5},{5,4},{6,7},{7,6},{8,9},{9,8},{10,11... | collective-permute-start | bytes 3145736 | tf_op jit(solution)/shard_map/weights/ppermute | solution.py:25
  42.7 1.8 %gather_fusion.1 = bf16[16,128,256]{2,1,0:T(8,128)(2,1)S(1)} fusion(bf16[16,128,256]{2,1,0:T(8,128)(2,1)} %bitcast.72, s32[1024]{0:T(1024)S(1)} %pad_clamp_fusion), kind=kCustom, calls=%fused_computation.1 | custom fusion | bytes 2097216 | tf_op jit(solution)/shard_map/weights/jit(_take)/gather | solution.py:33
  44.5 1.9 %collective-permute-start.2 = (bf16[16,128,256]{2,1,0:T(8,128)(2,1)S(1)}, bf16[16,128,256]{2,1,0:T(8,128)(2,1)}, u32[]{:S(2)}, u32[]{:S(2)}) collective-permute-start(bf16[16,128,256]{2,1,0:T(8,128)(2,1)S(1)} %gather_fusion.1), channel_id=1, source_target_pairs={{0,1},{1,0},{2,3},{3,2},{4,5},{5,4},{6,7},{7,6},{8,9},{9,8},{10,11... | collective-permute-start | bytes 3145736 | tf_op jit(solution)/shard_map/weights/ppermute | solution.py:25
  51.7 0.7 compare_convert_fusion
  52.4 5.4 %all-to-all-done.1 = bf16[32,4,1024]{2,1,0:T(4,128)(2,1)} async-done(((bf16[32,4,1024]{2,1,0:T(4,128)(2,1)}), bf16[32,4,1024]{2,1,0:T(4,128)(2,1)}, u32[]{:S(2)}, u32[]{:S(2)}) %all-to-all-start.1) | async-done | bytes 262176 | tf_op jit(solution)/shard_map/dispatch/all_to_all | solution.py:17
  57.8 1.0 reshape.129
  58.9 0.4 fusion.25
  59.3 0.4 fusion.28
  59.7 1.7 fusion.2
  61.4 1.7 fusion.3
  63.1 1.0 pad_maximum_fusion
  64.1 4.9 %all-to-all-start.2 = ((bf16[8,128,512]{1,2,0:T(8,128)(2,1)}), bf16[8,128,512]{1,2,0:T(8,128)(2,1)S(1)}, u32[]{:S(2)}, u32[]{:S(2)}) async-start(bf16[8,128,512]{1,2,0:T(8,128)(2,1)} %pad_maximum_fusion), calls=%async_computation.2 | async-start | bytes 2097152 | tf_op jit(solution)/shard_map/hidden/all_to_all | solution.py:17
  69.1 4.8 %collective-permute-start = (bf16[128,512]{1,0:T(8,128)(2,1)S(1)}, bf16[128,512]{1,0:T(8,128)(2,1)S(1)}, u32[]{:S(2)}, u32[]{:S(2)}) collective-permute-start(bf16[128,512]{1,0:T(8,128)(2,1)S(1)} %pad_maximum_fusion.4), channel_id=1, source_target_pairs={{0,1},{1,0},{2,3},{3,2},{4,5},{5,4},{6,7},{7,6},{8,9},{9,8},{10,11... | collective-permute-start | bytes 393224 | tf_op jit(solution)/shard_map/hidden/ppermute | solution.py:25
  73.9 1.0 collective-permute-done
  74.9 11.5 %all-to-all-done.2 = bf16[8,128,512]{1,2,0:T(8,128)(2,1)S(1)} async-done(((bf16[8,128,512]{1,2,0:T(8,128)(2,1)}), bf16[8,128,512]{1,2,0:T(8,128)(2,1)S(1)}, u32[]{:S(2)}, u32[]{:S(2)}) %all-to-all-start.2) | async-done | bytes 1048608 | tf_op jit(solution)/shard_map/hidden/all_to_all | solution.py:17
  86.3 0.1 convert_reduce_fusion
  86.6 0.1 copy.31
  86.7 1.1 broadcast_in_dim.102
  87.8 3.6 %all-to-all-start.3 = ((bf16[8,128,512]{2,1,0:T(8,128)(2,1)}), bf16[8,128,512]{2,1,0:T(8,128)(2,1)S(1)}, u32[]{:S(2)}, u32[]{:S(2)}) async-start(bf16[8,128,512]{2,1,0:T(8,128)(2,1)} %broadcast_in_dim.102), calls=%async_computation.3 | async-start | bytes 2097152 | tf_op jit(solution)/shard_map/hidden/all_to_all | solution.py:17
  91.3 4.8 %collective-permute-start.3 = (bf16[256,512]{1,0:T(8,128)(2,1)S(1)}, bf16[256,512]{1,0:T(8,128)(2,1)}, u32[]{:S(2)}, u32[]{:S(2)}) collective-permute-start(bf16[256,512]{1,0:T(8,128)(2,1)S(1)} %pad_maximum_fusion.2), channel_id=1, source_target_pairs={{0,8},{8,0},{1,9},{9,1},{2,10},{10,2},{3,11},{11,3},{4,12},{12,4},... | collective-permute-start | bytes 786440 | tf_op jit(solution)/shard_map/hidden/ppermute | solution.py:166
  96.2 3.4 %collective-permute-start.4 = (bf16[128,512]{0,1:T(8,128)(2,1)S(1)}, bf16[128,512]{0,1:T(8,128)(2,1)S(1)}, u32[]{:S(2)}, u32[]{:S(2)}) collective-permute-start(bf16[128,512]{0,1:T(8,128)(2,1)S(1)} %pad_maximum_fusion.6), channel_id=1, source_target_pairs={{0,1},{1,0},{2,3},{3,2},{4,5},{5,4},{6,7},{7,6},{8,9},{9,8},{10,11... | collective-permute-start | bytes 393224 | tf_op jit(solution)/shard_map/hidden/ppermute | solution.py:25
  99.6 1.0 collective-permute-done.4
  100.5 0.7 maximum_bitcast_fusion
  101.3 10.2 %collective-permute-done.3 = bf16[256,512]{1,0:T(8,128)(2,1)} collective-permute-done((bf16[256,512]{1,0:T(8,128)(2,1)S(1)}, bf16[256,512]{1,0:T(8,128)(2,1)}, u32[]{:S(2)}, u32[]{:S(2)}) %collective-permute-start.3) | collective-permute-done | bytes 262176 | tf_op jit(solution)/shard_map/hidden/ppermute | solution.py:166
  111.5 1.5 fusion.9
  113.1 1.5 fusion.8
  114.6 0.3 fusion.7
  114.9 0.9 copy-done.8
  115.8 0.3 fusion.6
  116.2 0.8 reshape.136
  117.0 6.1 %all-to-all-start.4 = ((bf16[32,4,1024]{2,1,0:T(4,128)(2,1)}), bf16[32,4,1024]{2,1,0:T(4,128)(2,1)S(1)}, u32[]{:S(2)}, u32[]{:S(2)}) async-start(bf16[32,4,1024]{2,1,0:T(4,128)(2,1)} %reshape.136), calls=%async_computation.4 | async-start | bytes 524288 | tf_op jit(solution)/shard_map/give_back/all_to_all | solution.py:17
  123.0 1.0 pad_maximum_fusion.1.first
  124.1 3.3 %collective-permute-start.6 = (bf16[2,256,512]{2,1,0:T(8,128)(2,1)S(1)}, bf16[2,256,512]{2,1,0:T(8,128)(2,1)S(1)}, u32[]{:S(2)}, u32[]{:S(2)}) collective-permute-start(bf16[2,256,512]{2,1,0:T(8,128)(2,1)S(1)} %pad_maximum_fusion.1.first), channel_id=1, source_target_pairs={{0,2},{2,4},{4,6},{6,0},{1,3},{3,5},{5,7},{7,1},{8,10},{10,12},{12... | collective-permute-start | bytes 1572872 | tf_op jit(solution)/shard_map/all_rows/ppermute | solution.py:202
  127.3 5.1 %collective-permute-start.8 = (bf16[2,256,512]{2,1,0:T(8,128)(2,1)S(1)}, bf16[2,256,512]{2,1,0:T(8,128)(2,1)S(1)}, u32[]{:S(2)}, u32[]{:S(2)}) collective-permute-start(bf16[2,256,512]{2,1,0:T(8,128)(2,1)S(1)} %pad_maximum_fusion.1.first), channel_id=1, source_target_pairs={{0,4},{2,6},{4,0},{6,2},{1,5},{3,7},{5,1},{7,3},{8,12},{10,14},{12... | collective-permute-start | bytes 1572872 | tf_op jit(solution)/shard_map/all_rows/ppermute | solution.py:202
  132.5 3.1 %collective-permute-start.9 = (bf16[2,256,512]{2,1,0:T(8,128)(2,1)S(1)}, bf16[2,256,512]{2,1,0:T(8,128)(2,1)S(1)}, u32[]{:S(2)}, u32[]{:S(2)}) collective-permute-start(bf16[2,256,512]{2,1,0:T(8,128)(2,1)S(1)} %pad_maximum_fusion.1.first), channel_id=1, source_target_pairs={{0,6},{2,0},{4,2},{6,4},{1,7},{3,1},{5,3},{7,5},{8,14},{10,8},{12,... | collective-permute-start | bytes 1572872 | tf_op jit(solution)/shard_map/all_rows/ppermute | solution.py:202
  135.6 6.1 %all-to-all-done.4 = bf16[32,4,1024]{2,1,0:T(4,128)(2,1)S(1)} async-done(((bf16[32,4,1024]{2,1,0:T(4,128)(2,1)}), bf16[32,4,1024]{2,1,0:T(4,128)(2,1)S(1)}, u32[]{:S(2)}, u32[]{:S(2)}) %all-to-all-start.4) | async-done | bytes 262176 | tf_op jit(solution)/shard_map/give_back/all_to_all | solution.py:17
  141.7 0.8 reshape.165
  142.5 1.2 fusion.4.after_ref
  143.7 0.9 broadcast_in_dim.106
  144.5 6.8 %all-to-all-start.5 = ((bf16[8,32,1024]{2,1,0:T(8,128)(2,1)}), bf16[8,32,1024]{2,1,0:T(8,128)(2,1)}, u32[]{:S(2)}, u32[]{:S(2)}) async-start(bf16[8,32,1024]{2,1,0:T(8,128)(2,1)} %broadcast_in_dim.106), calls=%async_computation.5 | async-start | bytes 1048576 | tf_op jit(solution)/shard_map/result/all_to_all | solution.py:17
  151.4 1.3 new_slices.3
  152.7 4.9 %collective-permute-start.7 = (bf16[4,256,256]{2,1,0:T(8,128)(2,1)}, bf16[4,256,256]{2,1,0:T(8,128)(2,1)S(1)}, u32[]{:S(2)}, u32[]{:S(2)}) collective-permute-start(bf16[4,256,256]{2,1,0:T(8,128)(2,1)} %get-tuple-element.45), channel_id=1, source_target_pairs={{0,1},{1,0},{2,3},{3,2},{4,5},{5,4},{6,7},{7,6},{8,9},{9,8},{10,11... | collective-permute-start | bytes 1572872 | tf_op jit(solution)/shard_map/new_slices/ppermute | solution.py:25
  157.7 1.4 new_slices.4
  159.1 0.7 copy-done.3
  159.8 0.7 copy-done.5
  160.5 1.9 %collective-permute-start.10 = (bf16[4,256,256]{2,1,0:T(8,128)(2,1)}, bf16[4,256,256]{2,1,0:T(8,128)(2,1)S(1)}, u32[]{:S(2)}, u32[]{:S(2)}) collective-permute-start(bf16[4,256,256]{2,1,0:T(8,128)(2,1)} %get-tuple-element.48), channel_id=1, source_target_pairs={{0,1},{1,0},{2,3},{3,2},{4,5},{5,4},{6,7},{7,6},{8,9},{9,8},{10,11... | collective-permute-start | bytes 1572872 | tf_op jit(solution)/shard_map/new_slices/ppermute | solution.py:25
  162.4 0.9 dynamic-slice_bitcast_fusion
  163.3 4.1 %collective-permute-start.5 = (bf16[32,512]{1,0:T(8,128)(2,1)S(1)}, bf16[32,512]{1,0:T(8,128)(2,1)S(1)}, u32[]{:S(2)}, u32[]{:S(2)}) collective-permute-start(bf16[32,512]{1,0:T(8,128)(2,1)S(1)} %dynamic-slice_bitcast_fusion), channel_id=1, source_target_pairs={{0,1},{1,0},{2,3},{3,2},{4,5},{5,4},{6,7},{7,6},{8,9},{9,8},{10,11... | collective-permute-start | bytes 98312 | tf_op jit(solution)/shard_map/result/ppermute | solution.py:25
  167.5 0.9 copy-done.2
  168.4 0.9 copy-done.4
  169.4 0.9 copy-done.6
  170.3 2.4 %new_slices.5 = (bf16[128,4096]{1,0:T(8,128)(2,1)}, bf16[128,4096]{1,0:T(8,128)(2,1)}) custom-call(s32[16]{0:T(128)S(1)} %fusion.38.source_ref, bf16[4,128,256]{2,1,0:T(8,128)(2,1)S(1)} %get-tuple-element.43.refs_0_, bf16[4,128,256]{2,1,0:T(8,128)(2,1)S(1)} %copy-done.2, bf16[4,256,256]{2,1,0:T(8,128)(2,1)S(1)} %collective-permute-done.7.refs_2_, ...), custom_call_target="tpu_custom_call" | custom-call | tf_op jit(solution)/shard_map/new_slices/pallas_call | solution.py:232
  172.8 0.8 fusion.23
  173.6 0.6 fusion.54
  (62 shorter events, 1.2 us)
Async XLA Ops:
  0.6 38.1 %copy-start = (bf16[2048,256]{1,0:T(8,128)(2,1)S(1)}, bf16[2048,256]{1,0:T(8,128)(2,1)}, u32[]{:S(2)}) copy-start(bf16[2048,256]{1,0:T(8,128)(2,1)} %param.11) | copy-start | bytes 3145732
  0.6 11.9 %copy-start.10 = (s32[32,2]{0,1:T(2,128)S(1)}, s32[32,2]{0,1:T(2,128)}, u32[]{:S(2)}) copy-start(s32[32,2]{0,1:T(2,128)} %param.9) | copy-start | bytes 772
  0.7 12.5 %copy-start.11 = (s32[16]{0:T(128)S(1)}, s32[16]{0:T(128)}, u32[]{:S(2)}) copy-start(s32[16]{0:T(128)} %param.13) | copy-start | bytes 196
  0.7 17.6 %copy-start.12 = (f32[32,2]{0,1:T(2,128)S(1)}, f32[32,2]{0,1:T(2,128)}, u32[]{:S(2)}) copy-start(f32[32,2]{0,1:T(2,128)} %param.10) | copy-start | bytes 772
  2.3 21.7 %all-to-all-start = ((bf16[16,32,512]{2,1,0:T(8,128)(2,1)}), bf16[16,32,512]{2,1,0:T(8,128)(2,1)S(1)}, u32[]{:S(2)}, u32[]{:S(2)}) async-start(bf16[16,32,512]{2,1,0:T(8,128)(2,1)} %broadcast_in_dim.93), calls=%async_computation | async-start | bytes 1048576 | tf_op jit(solution)/shard_map/token_blocks/all_to_all | solution.py:17
  12.8 25.9 %copy-start.13 = (s32[16]{0:T(128)S(1)}, s32[16]{0:T(128)}, u32[]{:S(2)}) copy-start(s32[16]{0:T(128)} %param.14) | copy-start | bytes 196
  25.2 32.7 %all-to-all-start.1 = ((bf16[32,4,1024]{2,1,0:T(4,128)(2,1)}), bf16[32,4,1024]{2,1,0:T(4,128)(2,1)}, u32[]{:S(2)}, u32[]{:S(2)}) async-start(bf16[32,4,1024]{2,1,0:T(4,128)(2,1)} %bitcast.4), calls=%async_computation.1 | async-start | bytes 524288 | tf_op jit(solution)/shard_map/dispatch/all_to_all | solution.py:17
  39.4 22.0 %collective-permute-start.1 = (bf16[16,128,256]{2,1,0:T(8,128)(2,1)S(1)}, bf16[16,128,256]{2,1,0:T(8,128)(2,1)}, u32[]{:S(2)}, u32[]{:S(2)}) collective-permute-start(bf16[16,128,256]{2,1,0:T(8,128)(2,1)S(1)} %gather_fusion), channel_id=1, source_target_pairs={{0,1},{1,0},{2,3},{3,2},{4,5},{5,4},{6,7},{7,6},{8,9},{9,8},{10,11... | collective-permute-start | bytes 3145736 | tf_op jit(solution)/shard_map/weights/ppermute | solution.py:25
  44.5 14.8 %copy-start.7 = (bf16[16,128,256]{2,1,0:T(8,128)(2,1)}, bf16[16,128,256]{2,1,0:T(8,128)(2,1)S(1)}, u32[]{:S(2)}) copy-start(bf16[16,128,256]{2,1,0:T(8,128)(2,1)S(1)} %gather_fusion.1) | copy-start | bytes 3145732
  44.5 15.2 %collective-permute-start.2 = (bf16[16,128,256]{2,1,0:T(8,128)(2,1)S(1)}, bf16[16,128,256]{2,1,0:T(8,128)(2,1)}, u32[]{:S(2)}, u32[]{:S(2)}) collective-permute-start(bf16[16,128,256]{2,1,0:T(8,128)(2,1)S(1)} %gather_fusion.1), channel_id=1, source_target_pairs={{0,1},{1,0},{2,3},{3,2},{4,5},{5,4},{6,7},{7,6},{8,9},{9,8},{10,11... | collective-permute-start | bytes 3145736 | tf_op jit(solution)/shard_map/weights/ppermute | solution.py:25
  64.1 22.2 %all-to-all-start.2 = ((bf16[8,128,512]{1,2,0:T(8,128)(2,1)}), bf16[8,128,512]{1,2,0:T(8,128)(2,1)S(1)}, u32[]{:S(2)}, u32[]{:S(2)}) async-start(bf16[8,128,512]{1,2,0:T(8,128)(2,1)} %pad_maximum_fusion), calls=%async_computation.2 | async-start | bytes 2097152 | tf_op jit(solution)/shard_map/hidden/all_to_all | solution.py:17
  69.1 5.7 %collective-permute-start = (bf16[128,512]{1,0:T(8,128)(2,1)S(1)}, bf16[128,512]{1,0:T(8,128)(2,1)S(1)}, u32[]{:S(2)}, u32[]{:S(2)}) collective-permute-start(bf16[128,512]{1,0:T(8,128)(2,1)S(1)} %pad_maximum_fusion.4), channel_id=1, source_target_pairs={{0,1},{1,0},{2,3},{3,2},{4,5},{5,4},{6,7},{7,6},{8,9},{9,8},{10,11... | collective-permute-start | bytes 393224 | tf_op jit(solution)/shard_map/hidden/ppermute | solution.py:25
  87.8 23.7 %all-to-all-start.3 = ((bf16[8,128,512]{2,1,0:T(8,128)(2,1)}), bf16[8,128,512]{2,1,0:T(8,128)(2,1)S(1)}, u32[]{:S(2)}, u32[]{:S(2)}) async-start(bf16[8,128,512]{2,1,0:T(8,128)(2,1)} %broadcast_in_dim.102), calls=%async_computation.3 | async-start | bytes 2097152 | tf_op jit(solution)/shard_map/hidden/all_to_all | solution.py:17
  91.3 20.2 %collective-permute-start.3 = (bf16[256,512]{1,0:T(8,128)(2,1)S(1)}, bf16[256,512]{1,0:T(8,128)(2,1)}, u32[]{:S(2)}, u32[]{:S(2)}) collective-permute-start(bf16[256,512]{1,0:T(8,128)(2,1)S(1)} %pad_maximum_fusion.2), channel_id=1, source_target_pairs={{0,8},{8,0},{1,9},{9,1},{2,10},{10,2},{3,11},{11,3},{4,12},{12,4},... | collective-permute-start | bytes 786440 | tf_op jit(solution)/shard_map/hidden/ppermute | solution.py:166
  96.2 4.4 %collective-permute-start.4 = (bf16[128,512]{0,1:T(8,128)(2,1)S(1)}, bf16[128,512]{0,1:T(8,128)(2,1)S(1)}, u32[]{:S(2)}, u32[]{:S(2)}) collective-permute-start(bf16[128,512]{0,1:T(8,128)(2,1)S(1)} %pad_maximum_fusion.6), channel_id=1, source_target_pairs={{0,1},{1,0},{2,3},{3,2},{4,5},{5,4},{6,7},{7,6},{8,9},{9,8},{10,11... | collective-permute-start | bytes 393224 | tf_op jit(solution)/shard_map/hidden/ppermute | solution.py:25
  114.6 1.2 copy-start.8
  117.0 24.7 %all-to-all-start.4 = ((bf16[32,4,1024]{2,1,0:T(4,128)(2,1)}), bf16[32,4,1024]{2,1,0:T(4,128)(2,1)S(1)}, u32[]{:S(2)}, u32[]{:S(2)}) async-start(bf16[32,4,1024]{2,1,0:T(4,128)(2,1)} %reshape.136), calls=%async_computation.4 | async-start | bytes 524288 | tf_op jit(solution)/shard_map/give_back/all_to_all | solution.py:17
  124.1 27.3 %collective-permute-start.6 = (bf16[2,256,512]{2,1,0:T(8,128)(2,1)S(1)}, bf16[2,256,512]{2,1,0:T(8,128)(2,1)S(1)}, u32[]{:S(2)}, u32[]{:S(2)}) collective-permute-start(bf16[2,256,512]{2,1,0:T(8,128)(2,1)S(1)} %pad_maximum_fusion.1.first), channel_id=1, source_target_pairs={{0,2},{2,4},{4,6},{6,0},{1,3},{3,5},{5,7},{7,1},{8,10},{10,12},{12... | collective-permute-start | bytes 1572872 | tf_op jit(solution)/shard_map/all_rows/ppermute | solution.py:202
  127.3 30.3 %collective-permute-start.8 = (bf16[2,256,512]{2,1,0:T(8,128)(2,1)S(1)}, bf16[2,256,512]{2,1,0:T(8,128)(2,1)S(1)}, u32[]{:S(2)}, u32[]{:S(2)}) collective-permute-start(bf16[2,256,512]{2,1,0:T(8,128)(2,1)S(1)} %pad_maximum_fusion.1.first), channel_id=1, source_target_pairs={{0,4},{2,6},{4,0},{6,2},{1,5},{3,7},{5,1},{7,3},{8,12},{10,14},{12... | collective-permute-start | bytes 1572872 | tf_op jit(solution)/shard_map/all_rows/ppermute | solution.py:202
  132.5 25.2 %collective-permute-start.9 = (bf16[2,256,512]{2,1,0:T(8,128)(2,1)S(1)}, bf16[2,256,512]{2,1,0:T(8,128)(2,1)S(1)}, u32[]{:S(2)}, u32[]{:S(2)}) collective-permute-start(bf16[2,256,512]{2,1,0:T(8,128)(2,1)S(1)} %pad_maximum_fusion.1.first), channel_id=1, source_target_pairs={{0,6},{2,0},{4,2},{6,4},{1,7},{3,1},{5,3},{7,5},{8,14},{10,8},{12,... | collective-permute-start | bytes 1572872 | tf_op jit(solution)/shard_map/all_rows/ppermute | solution.py:202
  142.5 8.9 %copy-start.9 = (bf16[512,256]{1,0:T(8,128)(2,1)S(1)}, bf16[512,256]{1,0:T(8,128)(2,1)}, u32[]{:S(2)}) copy-start(bf16[512,256]{1,0:T(8,128)(2,1)} %maximum_bitcast_fusion) | copy-start | bytes 786436
  144.5 17.9 %all-to-all-start.5 = ((bf16[8,32,1024]{2,1,0:T(8,128)(2,1)}), bf16[8,32,1024]{2,1,0:T(8,128)(2,1)}, u32[]{:S(2)}, u32[]{:S(2)}) async-start(bf16[8,32,1024]{2,1,0:T(8,128)(2,1)} %broadcast_in_dim.106), calls=%async_computation.5 | async-start | bytes 1048576 | tf_op jit(solution)/shard_map/result/all_to_all | solution.py:17
  152.7 6.3 %copy-start.1 = (bf16[4,128,256]{2,1,0:T(8,128)(2,1)}, bf16[4,128,256]{2,1,0:T(8,128)(2,1)S(1)}, u32[]{:S(2)}) copy-start(bf16[4,128,256]{2,1,0:T(8,128)(2,1)S(1)} %get-tuple-element.44.refs_1_) | copy-start | bytes 786436
  152.7 14.7 %collective-permute-start.7 = (bf16[4,256,256]{2,1,0:T(8,128)(2,1)}, bf16[4,256,256]{2,1,0:T(8,128)(2,1)S(1)}, u32[]{:S(2)}, u32[]{:S(2)}) collective-permute-start(bf16[4,256,256]{2,1,0:T(8,128)(2,1)} %get-tuple-element.45), channel_id=1, source_target_pairs={{0,1},{1,0},{2,3},{3,2},{4,5},{5,4},{6,7},{7,6},{8,9},{9,8},{10,11... | collective-permute-start | bytes 1572872 | tf_op jit(solution)/shard_map/new_slices/ppermute | solution.py:25
  159.1 0.7 copy-start.3
  159.8 0.7 copy-start.5
  160.5 7.0 %collective-permute-start.10 = (bf16[4,256,256]{2,1,0:T(8,128)(2,1)}, bf16[4,256,256]{2,1,0:T(8,128)(2,1)S(1)}, u32[]{:S(2)}, u32[]{:S(2)}) collective-permute-start(bf16[4,256,256]{2,1,0:T(8,128)(2,1)} %get-tuple-element.48), channel_id=1, source_target_pairs={{0,1},{1,0},{2,3},{3,2},{4,5},{5,4},{6,7},{7,6},{8,9},{9,8},{10,11... | collective-permute-start | bytes 1572872 | tf_op jit(solution)/shard_map/new_slices/ppermute | solution.py:25
  163.3 9.5 %collective-permute-start.5 = (bf16[32,512]{1,0:T(8,128)(2,1)S(1)}, bf16[32,512]{1,0:T(8,128)(2,1)S(1)}, u32[]{:S(2)}, u32[]{:S(2)}) collective-permute-start(bf16[32,512]{1,0:T(8,128)(2,1)S(1)} %dynamic-slice_bitcast_fusion), channel_id=1, source_target_pairs={{0,1},{1,0},{2,3},{3,2},{4,5},{5,4},{6,7},{7,6},{8,9},{9,8},{10,11... | collective-permute-start | bytes 98312 | tf_op jit(solution)/shard_map/result/ppermute | solution.py:25
  167.5 1.0 copy-start.2
  168.4 0.9 copy-start.4
  169.4 0.9 copy-start.6

commit v11 on v9

--- a/solution.py
+++ b/solution.py
@@ -10,7 +10,7 @@
 CUTS = ("y", "x", "core")
 VMEM = pl.BlockSpec(memory_space=pltpu.VMEM)
 ANY = pl.BlockSpec(memory_space=pl.ANY)
-LARGE = pltpu.CompilerParams(vmem_limit_bytes=24 * 2**20)
+LARGE = pltpu.CompilerParams(vmem_limit_bytes=8 * 2**20)
 
 
 def exchange(parts, axis):
@@ -203,6 +203,7 @@
 
         mine = of_slot(*places[4:6]) + of_slot(*places[6:8])
         theirs = swap(jnp.concatenate(mine[2:] + mine[:2], axis=1))
+        theirs = lax.optimization_barrier((theirs, own_result))[0]
         slot_units = jnp.concatenate([jnp.concatenate(mine, axis=1), theirs], axis=0).T
         own_units, other_units = slot_units[: 2 * unit_width], slot_units[2 * unit_width :]
 

time: 173 us -> 175 us (1.012)
  waiting for transfers between devices: 46.8 us -> 40.6 us
  starting transfers between devices: 83.6 us -> 89.3 us
  local copies, waits for them, and re-layouts: 10.1 us -> 12.2 us
    ppermute x3, waiting for transfers between devices: 6.94 us -> 1.13 us  [local(): lax.ppermute(pair, 'x', [(i, (i + s) % column) for i in range(column)])]
    ppermute x7, starting transfers between devices: 21 us -> 25.1 us  [swap(): return lax.ppermute(block, 'core', [(0, 1), (1, 0)])]
    unnamed x15 -> x27, local copies, waits for them, and re-layouts: 1.02 us -> 3.11 us
  transfers between devices with their start and end apart: 17 -> 17, of which waited for: 7 -> 8; matrix products, arithmetic and copies ran while one was open for 5% -> 5% of each run, Pallas kernels for 3% -> 3%
where the time goes in v11:
time: 175 us; the launch traced here: 173 us
  starting transfers between devices  89.3 us (51%)
  waiting for transfers between devices  40.6 us (23%)
  between operations  15.6 us (9%)
  local copies, waits for them, and re-layouts  12.2 us (7%)
  matrix products  6.72 us (4%)
  other arithmetic  4.41 us (3%)
  Pallas kernels  4.41 us (3%)
    all_to_all x6, starting transfers between devices, exchange(): return lax.all_to_all(parts, axis, split_axis=0, concat_axis=0, tiled=True)  48.6 us
    ppermute x7, starting transfers between devices, swap(): return lax.ppermute(block, 'core', [(0, 1), (1, 0)])  25.1 us
    all_to_all x6, waiting for transfers between devices, exchange(): return lax.all_to_all(parts, axis, split_axis=0, concat_axis=0, tiled=True)  23.2 us
    ppermute x1, waiting for transfers between devices, local(): rows_y = lax.ppermute(later_rows, 'y', [(0, 1), (1, 0)])  15.3 us
    ppermute x3, starting transfers between devices, local(): lax.ppermute(pair, 'x', [(i, (i + s) % column) for i in range(column)])  10.9 us
    ppermute x1, starting transfers between devices, local(): rows_y = lax.ppermute(later_rows, 'y', [(0, 1), (1, 0)])  4.77 us
  transfers between devices with their start and end apart: 17, of which 8 were waited for; matrix products, arithmetic and copies ran while one was open for 5% of the time, Pallas kernels for 3%

profile of v11, /device:TPU:1, one launch (start us, length us, event | category | flops | bytes accessed | tf_op | source)
XLA Modules:
  0.0 173.2 jit_solution(1766764346047630673)
XLA Ops:
  0.7 0.8 pad_maximum_fusion.7
  1.4 0.8 broadcast_in_dim.88
  2.3 10.2 %all-to-all-start = ((bf16[16,32,512]{2,1,0:T(8,128)(2,1)}), bf16[16,32,512]{2,1,0:T(8,128)(2,1)S(1)}, u32[]{:S(2)}, u32[]{:S(2)}) async-start(bf16[16,32,512]{2,1,0:T(8,128)(2,1)} %broadcast_in_dim.88), calls=%async_computation | async-start | bytes 1048576 | tf_op jit(solution)/shard_map/token_blocks/all_to_all | solution.py:17
  12.6 0.1 eq.83
  12.9 0.2 select_reduce_fusion
  13.1 0.6 fusion.59
  18.0 6.0 %all-to-all-done = bf16[16,32,512]{2,1,0:T(8,128)(2,1)S(1)} async-done(((bf16[16,32,512]{2,1,0:T(8,128)(2,1)}), bf16[16,32,512]{2,1,0:T(8,128)(2,1)S(1)}, u32[]{:S(2)}, u32[]{:S(2)}) %all-to-all-start) | async-done | bytes 524320 | tf_op jit(solution)/shard_map/token_blocks/all_to_all | solution.py:17
  24.0 0.2 fusion.5
  24.3 0.8 broadcast_in_dim.95
  25.1 13.6 %all-to-all-start.1 = ((bf16[32,4,1024]{2,1,0:T(4,128)(2,1)}), bf16[32,4,1024]{2,1,0:T(4,128)(2,1)}, u32[]{:S(2)}, u32[]{:S(2)}) async-start(bf16[32,4,1024]{2,1,0:T(4,128)(2,1)} %bitcast.4), calls=%async_computation.1 | async-start | bytes 524288 | tf_op jit(solution)/shard_map/dispatch/all_to_all | solution.py:17
  38.7 3.3 %collective-permute-start.1 = (bf16[2048,256]{1,0:T(8,128)(2,1)S(1)}, bf16[2048,256]{1,0:T(8,128)(2,1)S(1)}, u32[]{:S(2)}, u32[]{:S(2)}) collective-permute-start(bf16[2048,256]{1,0:T(8,128)(2,1)S(1)} %copy-done.1), channel_id=1, source_target_pairs={{0,1},{1,0},{2,3},{3,2},{4,5},{5,4},{6,7},{7,6},{8,9},{9,8},{10,11... | collective-permute-start | bytes 3145736 | tf_op jit(solution)/shard_map/weights/ppermute | solution.py:25
  41.9 1.9 %collective-permute-start.2 = (bf16[2048,256]{1,0:T(8,128)(2,1)S(1)}, bf16[2048,256]{1,0:T(8,128)(2,1)}, u32[]{:S(2)}, u32[]{:S(2)}) collective-permute-start(bf16[2048,256]{1,0:T(8,128)(2,1)S(1)} %copy-done), channel_id=1, source_target_pairs={{0,1},{1,0},{2,3},{3,2},{4,5},{5,4},{6,7},{7,6},{8,9},{9,8},{10,11... | collective-permute-start | bytes 3145736 | tf_op jit(solution)/shard_map/weights/ppermute | solution.py:25
  44.0 0.6 fusion.57
  55.0 0.7 compare_convert_fusion
  55.7 2.0 %all-to-all-done.1 = bf16[32,4,1024]{2,1,0:T(4,128)(2,1)} async-done(((bf16[32,4,1024]{2,1,0:T(4,128)(2,1)}), bf16[32,4,1024]{2,1,0:T(4,128)(2,1)}, u32[]{:S(2)}, u32[]{:S(2)}) %all-to-all-start.1) | async-done | bytes 262176 | tf_op jit(solution)/shard_map/dispatch/all_to_all | solution.py:17
  57.7 1.0 reshape.123
  58.8 0.5 fusion.28
  59.2 0.5 fusion.25
  59.7 0.5 fusion.3
  60.2 0.5 copy-done.3
  60.7 1.7 fusion.2
  62.4 1.1 pad_maximum_fusion
  63.5 4.9 %all-to-all-start.2 = ((bf16[8,128,512]{2,1,0:T(8,128)(2,1)}), bf16[8,128,512]{2,1,0:T(8,128)(2,1)S(1)}, u32[]{:S(2)}, u32[]{:S(2)}) async-start(bf16[8,128,512]{2,1,0:T(8,128)(2,1)} %pad_maximum_fusion), calls=%async_computation.2 | async-start | bytes 2097152 | tf_op jit(solution)/shard_map/hidden/all_to_all | solution.py:17
  68.5 4.8 %collective-permute-start = (bf16[128,512]{1,0:T(8,128)(2,1)S(1)}, bf16[128,512]{1,0:T(8,128)(2,1)S(1)}, u32[]{:S(2)}, u32[]{:S(2)}) collective-permute-start(bf16[128,512]{1,0:T(8,128)(2,1)S(1)} %pad_maximum_fusion.4), channel_id=1, source_target_pairs={{0,1},{1,0},{2,3},{3,2},{4,5},{5,4},{6,7},{7,6},{8,9},{9,8},{10,11... | collective-permute-start | bytes 393224 | tf_op jit(solution)/shard_map/hidden/ppermute | solution.py:25
  73.2 1.0 collective-permute-done
  74.2 11.5 %all-to-all-done.2 = bf16[8,128,512]{2,1,0:T(8,128)(2,1)S(1)} async-done(((bf16[8,128,512]{2,1,0:T(8,128)(2,1)}), bf16[8,128,512]{2,1,0:T(8,128)(2,1)S(1)}, u32[]{:S(2)}, u32[]{:S(2)}) %all-to-all-start.2) | async-done | bytes 1048608 | tf_op jit(solution)/shard_map/hidden/all_to_all | solution.py:17
  85.7 0.2 convert_reduce_fusion
  85.9 1.1 broadcast_in_dim.96
  87.0 3.6 %all-to-all-start.3 = ((bf16[8,128,512]{2,1,0:T(8,128)(2,1)}), bf16[8,128,512]{2,1,0:T(8,128)(2,1)S(1)}, u32[]{:S(2)}, u32[]{:S(2)}) async-start(bf16[8,128,512]{2,1,0:T(8,128)(2,1)} %broadcast_in_dim.96), calls=%async_computation.3 | async-start | bytes 2097152 | tf_op jit(solution)/shard_map/hidden/all_to_all | solution.py:17
  90.5 4.8 %collective-permute-start.3 = (bf16[256,512]{1,0:T(8,128)(2,1)S(1)}, bf16[256,512]{1,0:T(8,128)(2,1)S(1)}, u32[]{:S(2)}, u32[]{:S(2)}) collective-permute-start(bf16[256,512]{1,0:T(8,128)(2,1)S(1)} %pad_maximum_fusion.2), channel_id=1, source_target_pairs={{0,8},{8,0},{1,9},{9,1},{2,10},{10,2},{3,11},{11,3},{4,12},{12,4},... | collective-permute-start | bytes 786440 | tf_op jit(solution)/shard_map/hidden/ppermute | solution.py:167
  95.3 15.3 %collective-permute-done.3 = bf16[256,512]{1,0:T(8,128)(2,1)S(1)} collective-permute-done((bf16[256,512]{1,0:T(8,128)(2,1)S(1)}, bf16[256,512]{1,0:T(8,128)(2,1)S(1)}, u32[]{:S(2)}, u32[]{:S(2)}) %collective-permute-start.3) | collective-permute-done | bytes 262176 | tf_op jit(solution)/shard_map/hidden/ppermute | solution.py:167
  110.6 0.7 copy-done.7
  111.3 1.5 fusion.8
  112.8 0.3 fusion.6
  113.1 0.9 copy-done.2
  114.1 0.3 fusion.7
  114.4 0.9 copy-done.4
  115.3 0.3 fusion.9
  115.6 0.8 reshape.128
  116.5 9.5 %all-to-all-start.4 = ((bf16[32,4,1024]{2,1,0:T(4,128)(2,1)}), bf16[32,4,1024]{2,1,0:T(4,128)(2,1)S(1)}, u32[]{:S(2)}, u32[]{:S(2)}) async-start(bf16[32,4,1024]{2,1,0:T(4,128)(2,1)} %reshape.128), calls=%async_computation.4 | async-start | bytes 524288 | tf_op jit(solution)/shard_map/give_back/all_to_all | solution.py:17
  126.1 5.6 %collective-permute-start.8 = (bf16[2,256,512]{2,1,0:T(8,128)(2,1)S(1)}, bf16[2,256,512]{2,1,0:T(8,128)(2,1)S(1)}, u32[]{:S(2)}, u32[]{:S(2)}) collective-permute-start(bf16[2,256,512]{2,1,0:T(8,128)(2,1)S(1)} %pad_maximum_fusion.1.first), channel_id=1, source_target_pairs={{0,4},{2,6},{4,0},{6,2},{1,5},{3,7},{5,1},{7,3},{8,12},{10,14},{12... | collective-permute-start | bytes 1572872 | tf_op jit(solution)/shard_map/all_rows/ppermute | solution.py:213
  131.7 2.0 %collective-permute-start.9 = (bf16[2,256,512]{2,1,0:T(8,128)(2,1)S(1)}, bf16[2,256,512]{2,1,0:T(8,128)(2,1)S(1)}, u32[]{:S(2)}, u32[]{:S(2)}) collective-permute-start(bf16[2,256,512]{2,1,0:T(8,128)(2,1)S(1)} %pad_maximum_fusion.1.first), channel_id=1, source_target_pairs={{0,6},{2,0},{4,2},{6,4},{1,7},{3,1},{5,3},{7,5},{8,14},{10,8},{12,... | collective-permute-start | bytes 1572872 | tf_op jit(solution)/shard_map/all_rows/ppermute | solution.py:213
  133.6 3.3 %collective-permute-start.6 = (bf16[2,256,512]{2,1,0:T(8,128)(2,1)S(1)}, bf16[2,256,512]{2,1,0:T(8,128)(2,1)S(1)}, u32[]{:S(2)}, u32[]{:S(2)}) collective-permute-start(bf16[2,256,512]{2,1,0:T(8,128)(2,1)S(1)} %pad_maximum_fusion.1.first), channel_id=1, source_target_pairs={{0,2},{2,4},{4,6},{6,0},{1,3},{3,5},{5,7},{7,1},{8,10},{10,12},{12... | collective-permute-start | bytes 1572872 | tf_op jit(solution)/shard_map/all_rows/ppermute | solution.py:213
  137.0 0.1 constant_dynamic-slice_fusion
  137.1 0.1 copy.41
  137.2 0.1 copy.42
  137.4 0.1 copy.43
  137.5 0.1 copy.44
  137.6 3.5 %collective-permute-start.5 = (bf16[128,512]{0,1:T(8,128)(2,1)S(1)}, bf16[128,512]{0,1:T(8,128)(2,1)S(1)}, u32[]{:S(2)}, u32[]{:S(2)}) collective-permute-start(bf16[128,512]{0,1:T(8,128)(2,1)S(1)} %pad_maximum_fusion.6), channel_id=1, source_target_pairs={{0,1},{1,0},{2,3},{3,2},{4,5},{5,4},{6,7},{7,6},{8,9},{9,8},{10,11... | collective-permute-start | bytes 393224 | tf_op jit(solution)/shard_map/slot_units/ppermute | solution.py:25
  141.2 3.5 %all-to-all-done.4 = bf16[32,4,1024]{2,1,0:T(4,128)(2,1)S(1)} async-done(((bf16[32,4,1024]{2,1,0:T(4,128)(2,1)}), bf16[32,4,1024]{2,1,0:T(4,128)(2,1)S(1)}, u32[]{:S(2)}, u32[]{:S(2)}) %all-to-all-start.4) | async-done | bytes 262176 | tf_op jit(solution)/shard_map/give_back/all_to_all | solution.py:17
  144.7 0.9 fusion.4.after_ref
  145.6 0.9 broadcast_in_dim.100
  146.5 6.9 %all-to-all-start.5 = ((bf16[8,32,1024]{2,1,0:T(8,128)(2,1)}), bf16[8,32,1024]{2,1,0:T(8,128)(2,1)}, u32[]{:S(2)}, u32[]{:S(2)}) async-start(bf16[8,32,1024]{2,1,0:T(8,128)(2,1)} %broadcast_in_dim.100), calls=%async_computation.5 | async-start | bytes 1048576 | tf_op jit(solution)/shard_map/result/all_to_all | solution.py:17
  153.4 1.1 collective-permute-done.9.second
  154.5 0.6 new_slices.4
  155.1 3.7 %collective-permute-start.10 = (bf16[4,256,256]{2,1,0:T(8,128)(2,1)S(1)}, bf16[4,256,256]{2,1,0:T(8,128)(2,1)S(1)}, u32[]{:S(2)}, u32[]{:S(2)}) collective-permute-start(bf16[4,256,256]{2,1,0:T(8,128)(2,1)S(1)} %get-tuple-element.56), channel_id=1, source_target_pairs={{0,1},{1,0},{2,3},{3,2},{4,5},{5,4},{6,7},{7,6},{8,9},{9,8},{10,11... | collective-permute-start | bytes 1572872 | tf_op jit(solution)/shard_map/new_slices/ppermute | solution.py:25
  158.9 1.3 new_slices.3
  160.2 1.9 %collective-permute-start.7 = (bf16[4,256,256]{2,1,0:T(8,128)(2,1)}, bf16[4,256,256]{2,1,0:T(8,128)(2,1)S(1)}, u32[]{:S(2)}, u32[]{:S(2)}) collective-permute-start(bf16[4,256,256]{2,1,0:T(8,128)(2,1)} %get-tuple-element.53), channel_id=1, source_target_pairs={{0,1},{1,0},{2,3},{3,2},{4,5},{5,4},{6,7},{7,6},{8,9},{9,8},{10,11... | collective-permute-start | bytes 1572872 | tf_op jit(solution)/shard_map/new_slices/ppermute | solution.py:25
  162.2 0.3 all-to-all-done.5
  162.5 0.8 dynamic-slice_bitcast_fusion
  163.3 6.0 %collective-permute-start.4 = (bf16[32,512]{1,0:T(8,128)(2,1)S(1)}, bf16[32,512]{1,0:T(8,128)(2,1)S(1)}, u32[]{:S(2)}, u32[]{:S(2)}) collective-permute-start(bf16[32,512]{1,0:T(8,128)(2,1)S(1)} %dynamic-slice_bitcast_fusion), channel_id=1, source_target_pairs={{0,1},{1,0},{2,3},{3,2},{4,5},{5,4},{6,7},{7,6},{8,9},{9,8},{10,11... | collective-permute-start | bytes 98312 | tf_op jit(solution)/shard_map/result/ppermute | solution.py:25
  169.3 2.4 %new_slices.5 = (bf16[128,4096]{1,0:T(8,128)(2,1)}, bf16[128,4096]{1,0:T(8,128)(2,1)}) custom-call(s32[16]{0:T(128)S(1)} %fusion.38.source_ref, bf16[4,128,256]{2,1,0:T(8,128)(2,1)S(1)} %get-tuple-element.51.refs_0_, bf16[4,128,256]{2,1,0:T(8,128)(2,1)S(1)} %get-tuple-element.52.refs_1_, bf16[4,256,256]{2,1,0:T(8,128)(2,1)S(1)} %collective-permute-done.7.refs_2_, ...), custom_call_target="tpu_custom_call" | custom-call | tf_op jit(solution)/shard_map/new_slices/pallas_call | solution.py:242
  171.8 0.9 fusion.23
  172.6 0.6 fusion.54
  (60 shorter events, 1.2 us)
Async XLA Ops:
  0.6 11.9 %copy-start.9 = (s32[32,2]{0,1:T(2,128)S(1)}, s32[32,2]{0,1:T(2,128)}, u32[]{:S(2)}) copy-start(s32[32,2]{0,1:T(2,128)} %param.9) | copy-start | bytes 772
  0.6 12.5 %copy-start.10 = (s32[16]{0:T(128)S(1)}, s32[16]{0:T(128)}, u32[]{:S(2)}) copy-start(s32[16]{0:T(128)} %param.13) | copy-start | bytes 196
  0.7 17.3 %copy-start.12 = (f32[32,2]{0,1:T(2,128)S(1)}, f32[32,2]{0,1:T(2,128)}, u32[]{:S(2)}) copy-start(f32[32,2]{0,1:T(2,128)} %param.10) | copy-start | bytes 772
  2.3 21.7 %all-to-all-start = ((bf16[16,32,512]{2,1,0:T(8,128)(2,1)}), bf16[16,32,512]{2,1,0:T(8,128)(2,1)S(1)}, u32[]{:S(2)}, u32[]{:S(2)}) async-start(bf16[16,32,512]{2,1,0:T(8,128)(2,1)} %broadcast_in_dim.88), calls=%async_computation | async-start | bytes 1048576 | tf_op jit(solution)/shard_map/token_blocks/all_to_all | solution.py:17
  12.6 26.0 %copy-start.1 = (bf16[2048,256]{1,0:T(8,128)(2,1)S(1)}, bf16[2048,256]{1,0:T(8,128)(2,1)}, u32[]{:S(2)}) copy-start(bf16[2048,256]{1,0:T(8,128)(2,1)} %param.11) | copy-start | bytes 3145732
  12.7 29.2 %copy-start = (bf16[2048,256]{1,0:T(8,128)(2,1)S(1)}, bf16[2048,256]{1,0:T(8,128)(2,1)}, u32[]{:S(2)}) copy-start(bf16[2048,256]{1,0:T(8,128)(2,1)} %param.12) | copy-start | bytes 3145732
  12.7 31.2 %copy-start.11 = (s32[16]{0:T(128)S(1)}, s32[16]{0:T(128)}, u32[]{:S(2)}) copy-start(s32[16]{0:T(128)} %param.14) | copy-start | bytes 196
  25.1 32.7 %all-to-all-start.1 = ((bf16[32,4,1024]{2,1,0:T(4,128)(2,1)}), bf16[32,4,1024]{2,1,0:T(4,128)(2,1)}, u32[]{:S(2)}, u32[]{:S(2)}) async-start(bf16[32,4,1024]{2,1,0:T(4,128)(2,1)} %bitcast.4), calls=%async_computation.1 | async-start | bytes 524288 | tf_op jit(solution)/shard_map/dispatch/all_to_all | solution.py:17
  38.7 21.1 %collective-permute-start.1 = (bf16[2048,256]{1,0:T(8,128)(2,1)S(1)}, bf16[2048,256]{1,0:T(8,128)(2,1)S(1)}, u32[]{:S(2)}, u32[]{:S(2)}) collective-permute-start(bf16[2048,256]{1,0:T(8,128)(2,1)S(1)} %copy-done.1), channel_id=1, source_target_pairs={{0,1},{1,0},{2,3},{3,2},{4,5},{5,4},{6,7},{7,6},{8,9},{9,8},{10,11... | collective-permute-start | bytes 3145736 | tf_op jit(solution)/shard_map/weights/ppermute | solution.py:25
  41.9 18.8 %collective-permute-start.2 = (bf16[2048,256]{1,0:T(8,128)(2,1)S(1)}, bf16[2048,256]{1,0:T(8,128)(2,1)}, u32[]{:S(2)}, u32[]{:S(2)}) collective-permute-start(bf16[2048,256]{1,0:T(8,128)(2,1)S(1)} %copy-done), channel_id=1, source_target_pairs={{0,1},{1,0},{2,3},{3,2},{4,5},{5,4},{6,7},{7,6},{8,9},{9,8},{10,11... | collective-permute-start | bytes 3145736 | tf_op jit(solution)/shard_map/weights/ppermute | solution.py:25
  59.7 1.0 copy-start.3
  63.5 22.2 %all-to-all-start.2 = ((bf16[8,128,512]{2,1,0:T(8,128)(2,1)}), bf16[8,128,512]{2,1,0:T(8,128)(2,1)S(1)}, u32[]{:S(2)}, u32[]{:S(2)}) async-start(bf16[8,128,512]{2,1,0:T(8,128)(2,1)} %pad_maximum_fusion), calls=%async_computation.2 | async-start | bytes 2097152 | tf_op jit(solution)/shard_map/hidden/all_to_all | solution.py:17
  68.5 5.7 %collective-permute-start = (bf16[128,512]{1,0:T(8,128)(2,1)S(1)}, bf16[128,512]{1,0:T(8,128)(2,1)S(1)}, u32[]{:S(2)}, u32[]{:S(2)}) collective-permute-start(bf16[128,512]{1,0:T(8,128)(2,1)S(1)} %pad_maximum_fusion.4), channel_id=1, source_target_pairs={{0,1},{1,0},{2,3},{3,2},{4,5},{5,4},{6,7},{7,6},{8,9},{9,8},{10,11... | collective-permute-start | bytes 393224 | tf_op jit(solution)/shard_map/hidden/ppermute | solution.py:25
  74.2 16.3 %copy-start.5 = (bf16[256,512]{1,0:T(8,128)(2,1)}, bf16[256,512]{1,0:T(8,128)(2,1)S(1)}, u32[]{:S(2)}) copy-start(bf16[256,512]{1,0:T(8,128)(2,1)S(1)} %pad_maximum_fusion.2) | copy-start | bytes 786436
  87.0 23.6 %all-to-all-start.3 = ((bf16[8,128,512]{2,1,0:T(8,128)(2,1)}), bf16[8,128,512]{2,1,0:T(8,128)(2,1)S(1)}, u32[]{:S(2)}, u32[]{:S(2)}) async-start(bf16[8,128,512]{2,1,0:T(8,128)(2,1)} %broadcast_in_dim.96), calls=%async_computation.3 | async-start | bytes 2097152 | tf_op jit(solution)/shard_map/hidden/all_to_all | solution.py:17
  90.5 20.1 %collective-permute-start.3 = (bf16[256,512]{1,0:T(8,128)(2,1)S(1)}, bf16[256,512]{1,0:T(8,128)(2,1)S(1)}, u32[]{:S(2)}, u32[]{:S(2)}) collective-permute-start(bf16[256,512]{1,0:T(8,128)(2,1)S(1)} %pad_maximum_fusion.2), channel_id=1, source_target_pairs={{0,8},{8,0},{1,9},{9,1},{2,10},{10,2},{3,11},{11,3},{4,12},{12,4},... | collective-permute-start | bytes 786440 | tf_op jit(solution)/shard_map/hidden/ppermute | solution.py:167
  110.6 0.7 copy-start.7
  112.8 1.2 copy-start.2
  114.0 1.2 copy-start.4
  115.6 10.4 %copy-start.6 = (bf16[256,512]{1,0:T(8,128)(2,1)S(1)}, bf16[256,512]{1,0:T(8,128)(2,1)}, u32[]{:S(2)}) copy-start(bf16[256,512]{1,0:T(8,128)(2,1)} %copy-done.5) | copy-start | bytes 786436
  115.6 10.4 %copy-start.8 = (bf16[256,512]{1,0:T(8,128)(2,1)S(1)}, bf16[256,512]{1,0:T(8,128)(2,1)}, u32[]{:S(2)}) copy-start(bf16[256,512]{1,0:T(8,128)(2,1)} %copy-done.7) | copy-start | bytes 786436
  116.5 28.2 %all-to-all-start.4 = ((bf16[32,4,1024]{2,1,0:T(4,128)(2,1)}), bf16[32,4,1024]{2,1,0:T(4,128)(2,1)S(1)}, u32[]{:S(2)}, u32[]{:S(2)}) async-start(bf16[32,4,1024]{2,1,0:T(4,128)(2,1)} %reshape.128), calls=%async_computation.4 | async-start | bytes 524288 | tf_op jit(solution)/shard_map/give_back/all_to_all | solution.py:17
  126.1 27.3 %collective-permute-start.8 = (bf16[2,256,512]{2,1,0:T(8,128)(2,1)S(1)}, bf16[2,256,512]{2,1,0:T(8,128)(2,1)S(1)}, u32[]{:S(2)}, u32[]{:S(2)}) collective-permute-start(bf16[2,256,512]{2,1,0:T(8,128)(2,1)S(1)} %pad_maximum_fusion.1.first), channel_id=1, source_target_pairs={{0,4},{2,6},{4,0},{6,2},{1,5},{3,7},{5,1},{7,3},{8,12},{10,14},{12... | collective-permute-start | bytes 1572872 | tf_op jit(solution)/shard_map/all_rows/ppermute | solution.py:213
  131.7 22.9 %collective-permute-start.9 = (bf16[2,256,512]{2,1,0:T(8,128)(2,1)S(1)}, bf16[2,256,512]{2,1,0:T(8,128)(2,1)S(1)}, u32[]{:S(2)}, u32[]{:S(2)}) collective-permute-start(bf16[2,256,512]{2,1,0:T(8,128)(2,1)S(1)} %pad_maximum_fusion.1.first), channel_id=1, source_target_pairs={{0,6},{2,0},{4,2},{6,4},{1,7},{3,1},{5,3},{7,5},{8,14},{10,8},{12,... | collective-permute-start | bytes 1572872 | tf_op jit(solution)/shard_map/all_rows/ppermute | solution.py:213
  133.6 25.2 %collective-permute-start.6 = (bf16[2,256,512]{2,1,0:T(8,128)(2,1)S(1)}, bf16[2,256,512]{2,1,0:T(8,128)(2,1)S(1)}, u32[]{:S(2)}, u32[]{:S(2)}) collective-permute-start(bf16[2,256,512]{2,1,0:T(8,128)(2,1)S(1)} %pad_maximum_fusion.1.first), channel_id=1, source_target_pairs={{0,2},{2,4},{4,6},{6,0},{1,3},{3,5},{5,7},{7,1},{8,10},{10,12},{12... | collective-permute-start | bytes 1572872 | tf_op jit(solution)/shard_map/all_rows/ppermute | solution.py:213
  137.6 8.0 %collective-permute-start.5 = (bf16[128,512]{0,1:T(8,128)(2,1)S(1)}, bf16[128,512]{0,1:T(8,128)(2,1)S(1)}, u32[]{:S(2)}, u32[]{:S(2)}) collective-permute-start(bf16[128,512]{0,1:T(8,128)(2,1)S(1)} %pad_maximum_fusion.6), channel_id=1, source_target_pairs={{0,1},{1,0},{2,3},{3,2},{4,5},{5,4},{6,7},{7,6},{8,9},{9,8},{10,11... | collective-permute-start | bytes 393224 | tf_op jit(solution)/shard_map/slot_units/ppermute | solution.py:25
  146.5 16.0 %all-to-all-start.5 = ((bf16[8,32,1024]{2,1,0:T(8,128)(2,1)}), bf16[8,32,1024]{2,1,0:T(8,128)(2,1)}, u32[]{:S(2)}, u32[]{:S(2)}) async-start(bf16[8,32,1024]{2,1,0:T(8,128)(2,1)} %broadcast_in_dim.100), calls=%async_computation.5 | async-start | bytes 1048576 | tf_op jit(solution)/shard_map/result/all_to_all | solution.py:17
  155.1 14.1 %collective-permute-start.10 = (bf16[4,256,256]{2,1,0:T(8,128)(2,1)S(1)}, bf16[4,256,256]{2,1,0:T(8,128)(2,1)S(1)}, u32[]{:S(2)}, u32[]{:S(2)}) collective-permute-start(bf16[4,256,256]{2,1,0:T(8,128)(2,1)S(1)} %get-tuple-element.56), channel_id=1, source_target_pairs={{0,1},{1,0},{2,3},{3,2},{4,5},{5,4},{6,7},{7,6},{8,9},{9,8},{10,11... | collective-permute-start | bytes 1572872 | tf_op jit(solution)/shard_map/new_slices/ppermute | solution.py:25
  160.2 9.1 %collective-permute-start.7 = (bf16[4,256,256]{2,1,0:T(8,128)(2,1)}, bf16[4,256,256]{2,1,0:T(8,128)(2,1)S(1)}, u32[]{:S(2)}, u32[]{:S(2)}) collective-permute-start(bf16[4,256,256]{2,1,0:T(8,128)(2,1)} %get-tuple-element.53), channel_id=1, source_target_pairs={{0,1},{1,0},{2,3},{3,2},{4,5},{5,4},{6,7},{7,6},{8,9},{9,8},{10,11... | collective-permute-start | bytes 1572872 | tf_op jit(solution)/shard_map/new_slices/ppermute | solution.py:25
  163.3 8.4 %collective-permute-start.4 = (bf16[32,512]{1,0:T(8,128)(2,1)S(1)}, bf16[32,512]{1,0:T(8,128)(2,1)S(1)}, u32[]{:S(2)}, u32[]{:S(2)}) collective-permute-start(bf16[32,512]{1,0:T(8,128)(2,1)S(1)} %dynamic-slice_bitcast_fusion), channel_id=1, source_target_pairs={{0,1},{1,0},{2,3},{3,2},{4,5},{5,4},{6,7},{7,6},{8,9},{9,8},{10,11... | collective-permute-start | bytes 98312 | tf_op jit(solution)/shard_map/result/ppermute | solution.py:25

commit v12 on v10

--- a/solution.py
+++ b/solution.py
@@ -31,6 +31,51 @@
 
 def rows_at(blocks, places):
     return jnp.take(blocks, places, axis=0, mode="clip")
+
+
+def joined(refs):
+    return [
+        jnp.concatenate([refs[i][...], refs[i + 1][...]], axis=0) for i in range(0, len(refs), 2)
+    ]
+
+
+def partial_kernel(slots_ref, rows_ref, *refs):
+    weights, out_ref = joined(refs[:-1]), refs[-1]
+    width = weights[0].shape[1]
+    units = out_ref.shape[2] // 2
+    for i in range(2):
+        part = sum(
+            lax.dot_general(
+                rows_ref[:, (2 * i + j) * width : (2 * i + j + 1) * width],
+                weights[2 * i + j],
+                (((1,), (1,)), ((), ())),
+                preferred_element_type=F32,
+            )
+            for j in range(2)
+        )
+        out_ref[0, :, i * units : (i + 1) * units] = part.astype(BF16)
+
+
+def rows_kernel(slots_ref, units_ref, *refs):
+    up, other_up, down, other_down = joined(refs[:-2])
+    out_ref, total = refs[-2:]
+    width = up.shape[1]
+    count = units_ref.shape[2] // 2
+
+    @pl.when(pl.program_id(0) == 0)
+    def _():
+        total[...] = jnp.zeros_like(total)
+
+    hidden, pre_grad = units_ref[0, :, :count], units_ref[0, :, count:]
+    products = ((hidden, down), (pre_grad, up), (hidden, other_down), (pre_grad, other_up))
+    for i, (left, right) in enumerate(products):
+        total[:, i * width : (i + 1) * width] += jnp.dot(
+            left, right, preferred_element_type=F32
+        )
+
+    @pl.when(pl.program_id(0) == pl.num_programs(0) - 1)
+    def _():
+        out_ref[...] = total[...].astype(BF16)
 
 
 def gradient_kernel(own_units, other_units, first, second, after_ref, up_ref, down_ref, theirs_ref):
@@ -49,8 +94,16 @@
 
 
 def layout_kernel(source_ref, *refs):
-    groups, (up_ref, down_ref) = (refs[:3], refs[3:6]), refs[6:]
-    blocks, unit_width, width = refs[0].shape
+    held, (up_ref, down_ref), parts, sems = refs[:6], refs[6:8], refs[8:14], refs[14]
+    copies = [
+        pltpu.make_async_copy(held[i], parts[i], sems.at[i]) for i in range(len(held))
+    ]
+    for copy in copies:
+        copy.start()
+    for copy in copies:
+        copy.wait()
+    groups = (parts[:3], parts[3:])
+    blocks, unit_width, width = parts[0].shape
     for p in range(4 * blocks):
         columns = pl.ds(p * width, width)
         source = source_ref[p]
@@ -85,13 +138,25 @@
         cut_list[:, None] * (old_rows[:, None] == cut_list[None, :]).astype(jnp.int32), axis=0
     )
 
-    def in_slots(weights):
-        blocks = rows_at(weights.reshape(cut_count, unit_width, width), new_slots)
-        shape = (chips, 2 * unit_width, width)
-        return [blocks.reshape(shape), swap(blocks).reshape(shape)]
-
     with jax.named_scope("weights"):
-        up, down = in_slots(old_up), in_slots(old_down)
+        weights = [old_up, swap(old_up), old_down, swap(old_down)]
+
+    def over_chips(kernel, first, first_spec, out_shape, out_spec, scratch=()):
+        unit_specs = [
+            pl.BlockSpec((unit_width, width), lambda p, slots, i=i: (slots[2 * p + i], 0))
+            for i in range(2)
+        ]
+        return pl.pallas_call(
+            kernel,
+            grid_spec=pltpu.PrefetchScalarGridSpec(
+                num_scalar_prefetch=1,
+                grid=(chips,),
+                in_specs=[first_spec] + unit_specs * 4,
+                out_specs=out_spec,
+                scratch_shapes=scratch,
+            ),
+            out_shape=out_shape,
+        )(new_slots, first, *[half for block in weights for half in (block, block)])
 
     with jax.named_scope("token_blocks"):
         blocks = everywhere(jnp.concatenate([tokens, cotangent], axis=1), CUTS)
@@ -137,19 +202,14 @@
     places = [*found(cut), *found(other_cut)]
     rows, source, picker, places = lax.optimization_barrier((rows, source, picker, places))
 
-    def partial(weights, first):
-        return sum(
-            jnp.einsum(
-                "rd,pud->pru",
-                rows[:, first + j * width : first + (j + 1) * width],
-                weights[j],
-                preferred_element_type=F32,
-            )
-            for j in range(2)
-        ).astype(BF16)
-
     with jax.named_scope("hidden"):
-        parts = jnp.concatenate([partial(up, 0), partial(down, 2 * width)], axis=2)
+        parts = over_chips(
+            partial_kernel,
+            rows,
+            pl.BlockSpec((core_rows, 4 * width), lambda p, slots: (0, 0)),
+            jax.ShapeDtypeStruct((chips, core_rows, 4 * unit_width), BF16),
+            pl.BlockSpec((1, core_rows, 4 * unit_width), lambda p, slots: (p, 0, 0)),
+        )
         sums = jnp.sum(exchange(parts, CHIP).astype(F32), axis=0)
         pre_act, hidden_grad = sums[:, : 2 * unit_width], sums[:, 2 * unit_width :]
         sig = jax.nn.sigmoid(pre_act)
@@ -171,15 +231,15 @@
         slot_units = jnp.concatenate([jnp.concatenate(mine, axis=1), theirs], axis=0).T
         units = everywhere(own_units, CHIP)
         units, rows_y, slot_units = lax.optimization_barrier((units, rows_y, slot_units))
-        hidden, pre_grad = units[:, :, : 2 * unit_width], units[:, :, 2 * unit_width :]
-
-    def rows_of(units, weights):
-        return jnp.einsum("pru,pud->rd", units, weights, preferred_element_type=F32).astype(BF16)
 
     with jax.named_scope("give_back"):
-        half_rows = jnp.concatenate(
-            [rows_of(part, weights[j]) for j in range(2) for part, weights in ((hidden, down), (pre_grad, up))],
-            axis=1,
+        half_rows = over_chips(
+            rows_kernel,
+            units,
+            pl.BlockSpec((1, core_rows, 4 * unit_width), lambda p, slots: (p, 0, 0)),
+            jax.ShapeDtypeStruct((core_rows, 4 * width), BF16),
+            pl.BlockSpec((core_rows, 4 * width), lambda p, slots: (0, 0)),
+            [pltpu.VMEM((core_rows, 4 * width), F32)],
         )
         sent_rows = half_rows.reshape(group_count, held_slots, 4 * width)
         half_rows = exchange(sent_rows, "expert")
@@ -232,8 +292,10 @@
         up_grad, down_grad = pl.pallas_call(
             layout_kernel,
             out_shape=(grad, grad),
-            in_specs=[pl.BlockSpec(memory_space=pltpu.SMEM)] + [VMEM] * 6,
+            in_specs=[pl.BlockSpec(memory_space=pltpu.SMEM)] + [ANY] * 6,
             out_specs=(VMEM, VMEM),
+            scratch_shapes=[pltpu.VMEM(part.shape, BF16) for part in held]
+            + [pltpu.SemaphoreType.DMA((6,))],
             compiler_params=LARGE,
         )(source, *held)
         their_share, up_grad, down_grad = lax.optimization_barrier(

time: 176 us -> 180 us (1.023)
  Pallas kernels: 5.15 us -> 19.8 us
  matrix products: 9.28 us -> 0.41 us
  waiting for transfers between devices: 40.9 us -> 48.8 us
  local copies, waits for them, and re-layouts: 16.6 us -> 11 us
  other arithmetic: 6.12 us -> 2.82 us
    pallas_call x0 -> x2, Pallas kernels: none -> 15.2 us  [over_chips(): pl.pallas_call(kernel, grid_spec=pltpu.PrefetchScalarGridSpec(num_scalar_...]
    dot_general x8 -> x0, matrix products: 7.86 us -> none  [the longest x4 4.19 us: partial(): jnp.einsum('rd,pud->pru', rows[:, first + j * width:first + (j + 1) * wid...]
    all_to_all x6, waiting for transfers between devices: 28.7 us -> 33.9 us  [exchange(): return lax.all_to_all(parts, axis, split_axis=0, concat_axis=0, tiled=True)]
    unnamed x29 -> x17, local copies, waits for them, and re-layouts: 5.32 us -> 2.23 us
    gather x2 -> x0, local copies, waits for them, and re-layouts: 2.45 us -> none  [rows_at(): return jnp.take(blocks, places, axis=0, mode='clip')]
    ppermute x3, waiting for transfers between devices: 0.01 us -> 2.22 us  [local(): lax.ppermute(pair, 'x', [(i, (i + s) % column) for i in range(column)])]
  transfers between devices with their start and end apart: 17 -> 17, of which waited for: 7 -> 8; matrix products, arithmetic and copies ran while one was open for 8% -> 3% of each run, Pallas kernels for 3% -> 3%
where the time goes in v12:
time: 180 us; the launch traced here: 178 us
  starting transfers between devices  85.3 us (47%)
  waiting for transfers between devices  48.8 us (27%)
  Pallas kernels  19.8 us (11%)
  local copies, waits for them, and re-layouts  11 us (6%)
  between operations  10.3 us (6%)
  other arithmetic  2.82 us (2%)
    all_to_all x6, starting transfers between devices, exchange(): return lax.all_to_all(parts, axis, split_axis=0, concat_axis=0, tiled=True)  45.9 us
    all_to_all x6, waiting for transfers between devices, exchange(): return lax.all_to_all(parts, axis, split_axis=0, concat_axis=0, tiled=True)  33.9 us
    ppermute x7, starting transfers between devices, swap(): return lax.ppermute(block, 'core', [(0, 1), (1, 0)])  23.7 us
    pallas_call x2, Pallas kernels, over_chips(): pl.pallas_call(kernel, grid_spec=pltpu.PrefetchScalarGridSpec(num_scalar_...  15.2 us
    ppermute x3, starting transfers between devices, local(): lax.ppermute(pair, 'x', [(i, (i + s) % column) for i in range(column)])  10.9 us
    ppermute x1, waiting for transfers between devices, local(): rows_y = lax.ppermute(later_rows, 'y', [(0, 1), (1, 0)])  10.7 us
    ppermute x1, starting transfers between devices, local(): rows_y = lax.ppermute(later_rows, 'y', [(0, 1), (1, 0)])  4.78 us
  transfers between devices with their start and end apart: 17, of which 8 were waited for; matrix products, arithmetic and copies ran while one was open for 3% of the time, Pallas kernels for 3%

profile of v12, /device:TPU:1, one launch (start us, length us, event | category | flops | bytes accessed | tf_op | source)
XLA Modules:
  0.0 178.4 jit_solution(8414917291490751126)
XLA Ops:
  0.7 0.8 pad_maximum_fusion.5
  1.5 0.8 broadcast_in_dim.88
  2.3 10.2 %all-to-all-start = ((bf16[16,32,512]{2,1,0:T(8,128)(2,1)}), bf16[16,32,512]{2,1,0:T(8,128)(2,1)S(1)}, u32[]{:S(2)}, u32[]{:S(2)}) async-start(bf16[16,32,512]{2,1,0:T(8,128)(2,1)} %broadcast_in_dim.88), calls=%async_computation | async-start | bytes 1048576 | tf_op jit(solution)/shard_map/token_blocks/all_to_all | solution.py:17
  12.6 2.1 %collective-permute-start.1 = (bf16[2048,256]{1,0:T(8,128)(2,1)S(1)}, bf16[2048,256]{1,0:T(8,128)(2,1)S(1)}, u32[]{:S(2)}, u32[]{:S(2)}) collective-permute-start(bf16[2048,256]{1,0:T(8,128)(2,1)S(1)} %copy-done), channel_id=1, source_target_pairs={{0,1},{1,0},{2,3},{3,2},{4,5},{5,4},{6,7},{7,6},{8,9},{9,8},{10,11... | collective-permute-start | bytes 3145736 | tf_op jit(solution)/shard_map/weights/ppermute | solution.py:25
  14.7 2.2 %collective-permute-start.2 = (bf16[2048,256]{1,0:T(8,128)(2,1)}, bf16[2048,256]{1,0:T(8,128)(2,1)}, u32[]{:S(2)}, u32[]{:S(2)}) collective-permute-start(bf16[2048,256]{1,0:T(8,128)(2,1)} %refs_5_.3), channel_id=1, source_target_pairs={{0,1},{1,0},{2,3},{3,2},{4,5},{5,4},{6,7},{7,6},{8,9},{9,8},{10,11... | collective-permute-start | bytes 3145736 | tf_op jit(solution)/shard_map/weights/ppermute | solution.py:25
  17.0 0.1 select_reduce_fusion.1
  17.1 0.1 copy.39
  17.1 0.1 eq.87
  17.2 0.1 fusion.11
  17.3 0.1 reduce_window_sum.11
  17.4 0.2 select_reduce_fusion
  17.6 0.7 fusion.34
  20.9 0.1 reduce_sum.48
  21.0 0.1 copy.40
  22.5 0.1 compare_reduce_fusion
  22.6 0.1 fusion.10
  22.7 1.4 all-to-all-done
  24.1 0.2 fusion.1
  24.3 0.1 broadcast_in_dim.94
  24.4 0.8 broadcast_in_dim.95
  25.2 13.4 %all-to-all-start.1 = ((bf16[32,4,1024]{2,1,0:T(4,128)(2,1)}), bf16[32,4,1024]{2,1,0:T(4,128)(2,1)S(1)}, u32[]{:S(2)}, u32[]{:S(2)}) async-start(bf16[32,4,1024]{2,1,0:T(4,128)(2,1)} %bitcast.4), calls=%async_computation.1 | async-start | bytes 524288 | tf_op jit(solution)/shard_map/dispatch/all_to_all | solution.py:17
  43.9 0.1 compare_convert_fusion
  44.0 13.8 %all-to-all-done.1 = bf16[32,4,1024]{2,1,0:T(4,128)(2,1)S(1)} async-done(((bf16[32,4,1024]{2,1,0:T(4,128)(2,1)}), bf16[32,4,1024]{2,1,0:T(4,128)(2,1)S(1)}, u32[]{:S(2)}, u32[]{:S(2)}) %all-to-all-start.1) | async-done | bytes 262176 | tf_op jit(solution)/shard_map/dispatch/all_to_all | solution.py:17
  57.7 0.8 reshape.111.rows_ref
  58.5 1.0 copy-done.1
  59.5 7.8 %hidden.1 = bf16[8,128,512]{2,1,0:T(8,128)(2,1)} custom-call(s32[16]{0:T(128)} %slots_ref.3, bf16[128,1024]{1,0:T(8,128)(2,1)} %reshape.111.rows_ref, bf16[2048,256]{1,0:T(8,128)(2,1)} %refs_1_.3, bf16[2048,256]{1,0:T(8,128)(2,1)} %refs_1_.3, bf16[2048,256]{1,0:T(8,128)(2,1)} %copy-done.1, bf16[2048,256]{1,0:T(8,128)(2,1)} %copy-done.1, ...), custom_call_target="tpu_custom_call" | custom-call | tf_op jit(solution)/shard_map/hidden/pallas_call | solution.py:149
  67.2 7.3 %all-to-all-start.2 = ((bf16[8,128,512]{2,1,0:T(8,128)(2,1)}), bf16[8,128,512]{2,1,0:T(8,128)(2,1)S(1)}, u32[]{:S(2)}, u32[]{:S(2)}) async-start(bf16[8,128,512]{2,1,0:T(8,128)(2,1)} %hidden.1), calls=%async_computation.2 | async-start | bytes 2097152 | tf_op jit(solution)/shard_map/hidden/all_to_all | solution.py:17
  74.6 4.9 %collective-permute-start = (bf16[128,512]{1,0:T(8,128)(2,1)S(1)}, bf16[128,512]{1,0:T(8,128)(2,1)S(1)}, u32[]{:S(2)}, u32[]{:S(2)}) collective-permute-start(bf16[128,512]{1,0:T(8,128)(2,1)S(1)} %pad_maximum_fusion.2), channel_id=1, source_target_pairs={{0,1},{1,0},{2,3},{3,2},{4,5},{5,4},{6,7},{7,6},{8,9},{9,8},{10,11... | collective-permute-start | bytes 393224 | tf_op jit(solution)/shard_map/hidden/ppermute | solution.py:25
  79.6 1.0 collective-permute-done
  80.6 11.1 %all-to-all-done.2 = bf16[8,128,512]{2,1,0:T(8,128)(2,1)S(1)} async-done(((bf16[8,128,512]{2,1,0:T(8,128)(2,1)}), bf16[8,128,512]{2,1,0:T(8,128)(2,1)S(1)}, u32[]{:S(2)}, u32[]{:S(2)}) %all-to-all-start.2) | async-done | bytes 1048608 | tf_op jit(solution)/shard_map/hidden/all_to_all | solution.py:17
  91.7 0.1 convert_reduce_fusion
  91.8 0.1 copy.45
  91.9 0.1 copy.46
  92.0 0.1 multiply_convert_fusion.1
  92.1 0.1 copy.43
  92.2 1.1 broadcast_in_dim.96
  93.3 3.6 %all-to-all-start.3 = ((bf16[8,128,512]{2,1,0:T(8,128)(2,1)}), bf16[8,128,512]{2,1,0:T(8,128)(2,1)S(1)}, u32[]{:S(2)}, u32[]{:S(2)}) async-start(bf16[8,128,512]{2,1,0:T(8,128)(2,1)} %broadcast_in_dim.96), calls=%async_computation.3 | async-start | bytes 2097152 | tf_op jit(solution)/shard_map/hidden/all_to_all | solution.py:17
  96.9 4.8 %collective-permute-start.3 = (bf16[256,512]{1,0:T(8,128)(2,1)S(1)}, bf16[256,512]{1,0:T(8,128)(2,1)S(1)}, u32[]{:S(2)}, u32[]{:S(2)}) collective-permute-start(bf16[256,512]{1,0:T(8,128)(2,1)S(1)} %pad_maximum_fusion.1), channel_id=1, source_target_pairs={{0,8},{8,0},{1,9},{9,1},{2,10},{10,2},{3,11},{11,3},{4,12},{12,4},... | collective-permute-start | bytes 786440 | tf_op jit(solution)/shard_map/hidden/ppermute | solution.py:226
  101.7 3.6 %collective-permute-start.4 = (bf16[128,512]{0,1:T(8,128)(2,1)S(1)}, bf16[128,512]{0,1:T(8,128)(2,1)S(1)}, u32[]{:S(2)}, u32[]{:S(2)}) collective-permute-start(bf16[128,512]{0,1:T(8,128)(2,1)S(1)} %pad_maximum_fusion.4), channel_id=1, source_target_pairs={{0,1},{1,0},{2,3},{3,2},{4,5},{5,4},{6,7},{7,6},{8,9},{9,8},{10,11... | collective-permute-start | bytes 393224 | tf_op jit(solution)/shard_map/hidden/ppermute | solution.py:25
  105.4 1.0 collective-permute-done.4
  106.4 10.7 %collective-permute-done.3 = bf16[256,512]{1,0:T(8,128)(2,1)S(1)} collective-permute-done((bf16[256,512]{1,0:T(8,128)(2,1)S(1)}, bf16[256,512]{1,0:T(8,128)(2,1)S(1)}, u32[]{:S(2)}, u32[]{:S(2)}) %collective-permute-start.3) | collective-permute-done | bytes 262176 | tf_op jit(solution)/shard_map/hidden/ppermute | solution.py:226
  117.0 1.0 copy-done.2
  118.0 7.4 %give_back.1 = bf16[128,1024]{1,0:T(8,128)(2,1)} custom-call(s32[16]{0:T(128)} %slots_ref.3, bf16[8,128,512]{2,1,0:T(8,128)(2,1)} %copy-done.2, bf16[2048,256]{1,0:T(8,128)(2,1)} %refs_1_.3, bf16[2048,256]{1,0:T(8,128)(2,1)} %refs_1_.3, bf16[2048,256]{1,0:T(8,128)(2,1)} %copy-done.1, bf16[2048,256]{1,0:T(8,128)(2,1)} %copy-done.1, ...), custom_call_target="tpu_custom_call" | custom-call | tf_op jit(solution)/shard_map/give_back/pallas_call | solution.py:149
  125.4 1.8 reshape.112
  127.2 4.8 %all-to-all-start.4 = ((bf16[32,4,1024]{2,1,0:T(4,128)(2,1)}), bf16[32,4,1024]{2,1,0:T(4,128)(2,1)S(1)}, u32[]{:S(2)}, u32[]{:S(2)}) async-start(bf16[32,4,1024]{2,1,0:T(4,128)(2,1)} %reshape.112), calls=%async_computation.4 | async-start | bytes 524288 | tf_op jit(solution)/shard_map/give_back/all_to_all | solution.py:17
  132.0 0.1 pad_maximum_fusion.first
  132.0 5.6 %collective-permute-start.8 = (bf16[2,256,512]{2,1,0:T(8,128)(2,1)S(1)}, bf16[2,256,512]{2,1,0:T(8,128)(2,1)S(1)}, u32[]{:S(2)}, u32[]{:S(2)}) collective-permute-start(bf16[2,256,512]{2,1,0:T(8,128)(2,1)S(1)} %pad_maximum_fusion.first), channel_id=1, source_target_pairs={{0,4},{2,6},{4,0},{6,2},{1,5},{3,7},{5,1},{7,3},{8,12},{10,14},{12... | collective-permute-start | bytes 1572872 | tf_op jit(solution)/shard_map/all_rows/ppermute | solution.py:262
  137.6 2.0 %collective-permute-start.9 = (bf16[2,256,512]{2,1,0:T(8,128)(2,1)S(1)}, bf16[2,256,512]{2,1,0:T(8,128)(2,1)S(1)}, u32[]{:S(2)}, u32[]{:S(2)}) collective-permute-start(bf16[2,256,512]{2,1,0:T(8,128)(2,1)S(1)} %pad_maximum_fusion.first), channel_id=1, source_target_pairs={{0,6},{2,0},{4,2},{6,4},{1,7},{3,1},{5,3},{7,5},{8,14},{10,8},{12,... | collective-permute-start | bytes 1572872 | tf_op jit(solution)/shard_map/all_rows/ppermute | solution.py:262
  139.6 3.3 %collective-permute-start.6 = (bf16[2,256,512]{2,1,0:T(8,128)(2,1)S(1)}, bf16[2,256,512]{2,1,0:T(8,128)(2,1)S(1)}, u32[]{:S(2)}, u32[]{:S(2)}) collective-permute-start(bf16[2,256,512]{2,1,0:T(8,128)(2,1)S(1)} %pad_maximum_fusion.first), channel_id=1, source_target_pairs={{0,2},{2,4},{4,6},{6,0},{1,3},{3,5},{5,7},{7,1},{8,10},{10,12},{12... | collective-permute-start | bytes 1572872 | tf_op jit(solution)/shard_map/all_rows/ppermute | solution.py:262
  142.9 7.7 %all-to-all-done.4 = bf16[32,4,1024]{2,1,0:T(4,128)(2,1)S(1)} async-done(((bf16[32,4,1024]{2,1,0:T(4,128)(2,1)}), bf16[32,4,1024]{2,1,0:T(4,128)(2,1)S(1)}, u32[]{:S(2)}, u32[]{:S(2)}) %all-to-all-start.4) | async-done | bytes 262176 | tf_op jit(solution)/shard_map/give_back/all_to_all | solution.py:17
  150.6 0.1 reshape.115
  150.7 0.2 fusion.after_ref
  150.9 0.9 broadcast_in_dim.100
  151.7 6.5 %all-to-all-start.5 = ((bf16[8,32,1024]{2,1,0:T(8,128)(2,1)}), bf16[8,32,1024]{2,1,0:T(8,128)(2,1)}, u32[]{:S(2)}, u32[]{:S(2)}) async-start(bf16[8,32,1024]{2,1,0:T(8,128)(2,1)} %broadcast_in_dim.100), calls=%async_computation.5 | async-start | bytes 1048576 | tf_op jit(solution)/shard_map/result/all_to_all | solution.py:17
  158.3 2.2 %collective-permute-done.9.second = bf16[2,256,512]{2,1,0:T(8,128)(2,1)S(1)} collective-permute-done((bf16[2,256,512]{2,1,0:T(8,128)(2,1)S(1)}, bf16[2,256,512]{2,1,0:T(8,128)(2,1)S(1)}, u32[]{:S(2)}, u32[]{:S(2)}) %collective-permute-start.9) | collective-permute-done | bytes 524320 | tf_op jit(solution)/shard_map/all_rows/ppermute | solution.py:262
  160.5 0.6 new_slices.4
  161.1 3.9 %collective-permute-start.10 = (bf16[4,256,256]{2,1,0:T(8,128)(2,1)S(1)}, bf16[4,256,256]{2,1,0:T(8,128)(2,1)S(1)}, u32[]{:S(2)}, u32[]{:S(2)}) collective-permute-start(bf16[4,256,256]{2,1,0:T(8,128)(2,1)S(1)} %get-tuple-element.48), channel_id=1, source_target_pairs={{0,1},{1,0},{2,3},{3,2},{4,5},{5,4},{6,7},{7,6},{8,9},{9,8},{10,11... | collective-permute-start | bytes 1572872 | tf_op jit(solution)/shard_map/new_slices/ppermute | solution.py:25
  165.0 1.3 new_slices.3
  166.4 1.9 %collective-permute-start.7 = (bf16[4,256,256]{2,1,0:T(8,128)(2,1)}, bf16[4,256,256]{2,1,0:T(8,128)(2,1)S(1)}, u32[]{:S(2)}, u32[]{:S(2)}) collective-permute-start(bf16[4,256,256]{2,1,0:T(8,128)(2,1)} %get-tuple-element.45), channel_id=1, source_target_pairs={{0,1},{1,0},{2,3},{3,2},{4,5},{5,4},{6,7},{7,6},{8,9},{9,8},{10,11... | collective-permute-start | bytes 1572872 | tf_op jit(solution)/shard_map/new_slices/ppermute | solution.py:25
  168.3 0.9 dynamic-slice_bitcast_fusion
  169.2 5.0 %collective-permute-start.5 = (bf16[32,512]{1,0:T(8,128)(2,1)S(1)}, bf16[32,512]{1,0:T(8,128)(2,1)S(1)}, u32[]{:S(2)}, u32[]{:S(2)}) collective-permute-start(bf16[32,512]{1,0:T(8,128)(2,1)S(1)} %dynamic-slice_bitcast_fusion), channel_id=1, source_target_pairs={{0,1},{1,0},{2,3},{3,2},{4,5},{5,4},{6,7},{7,6},{8,9},{9,8},{10,11... | collective-permute-start | bytes 98312 | tf_op jit(solution)/shard_map/result/ppermute | solution.py:25
  174.2 2.6 %new_slices.5 = (bf16[128,4096]{1,0:T(8,128)(2,1)}, bf16[128,4096]{1,0:T(8,128)(2,1)}) custom-call(s32[16]{0:T(128)S(1)} %fusion.18.source_ref, bf16[4,128,256]{2,1,0:T(8,128)(2,1)S(1)} %get-tuple-element.43.refs_0_, bf16[4,128,256]{2,1,0:T(8,128)(2,1)S(1)} %get-tuple-element.44.refs_1_, bf16[4,256,256]{2,1,0:T(8,128)(2,1)S(1)} %collective-permute-done.7.refs_2_, ...), custom_call_target="tpu_custom_call" | custom-call | tf_op jit(solution)/shard_map/new_slices/pallas_call | solution.py:292
  176.9 0.9 fusion.9
  177.8 0.6 fusion.31
  (40 shorter events, 0.3 us)
Async XLA Ops:
  0.6 12.0 %copy-start = (bf16[2048,256]{1,0:T(8,128)(2,1)S(1)}, bf16[2048,256]{1,0:T(8,128)(2,1)}, u32[]{:S(2)}) copy-start(bf16[2048,256]{1,0:T(8,128)(2,1)} %refs_1_.3) | copy-start | bytes 3145732
  0.6 16.3 %copy-start.5 = (s32[16]{0:T(128)S(1)}, s32[16]{0:T(128)}, u32[]{:S(2)}) copy-start(s32[16]{0:T(128)} %param.13) | copy-start | bytes 196
  0.7 16.4 %copy-start.4 = (s32[32,2]{0,1:T(2,128)S(1)}, s32[32,2]{0,1:T(2,128)}, u32[]{:S(2)}) copy-start(s32[32,2]{0,1:T(2,128)} %param.9) | copy-start | bytes 772
  0.7 21.9 %copy-start.6 = (f32[32,2]{0,1:T(2,128)S(1)}, f32[32,2]{0,1:T(2,128)}, u32[]{:S(2)}) copy-start(f32[32,2]{0,1:T(2,128)} %param.10) | copy-start | bytes 772
  2.3 21.7 %all-to-all-start = ((bf16[16,32,512]{2,1,0:T(8,128)(2,1)}), bf16[16,32,512]{2,1,0:T(8,128)(2,1)S(1)}, u32[]{:S(2)}, u32[]{:S(2)}) async-start(bf16[16,32,512]{2,1,0:T(8,128)(2,1)} %broadcast_in_dim.88), calls=%async_computation | async-start | bytes 1048576 | tf_op jit(solution)/shard_map/token_blocks/all_to_all | solution.py:17
  12.6 45.9 %collective-permute-start.1 = (bf16[2048,256]{1,0:T(8,128)(2,1)S(1)}, bf16[2048,256]{1,0:T(8,128)(2,1)S(1)}, u32[]{:S(2)}, u32[]{:S(2)}) collective-permute-start(bf16[2048,256]{1,0:T(8,128)(2,1)S(1)} %copy-done), channel_id=1, source_target_pairs={{0,1},{1,0},{2,3},{3,2},{4,5},{5,4},{6,7},{7,6},{8,9},{9,8},{10,11... | collective-permute-start | bytes 3145736 | tf_op jit(solution)/shard_map/weights/ppermute | solution.py:25
  14.7 43.8 %collective-permute-start.2 = (bf16[2048,256]{1,0:T(8,128)(2,1)}, bf16[2048,256]{1,0:T(8,128)(2,1)}, u32[]{:S(2)}, u32[]{:S(2)}) collective-permute-start(bf16[2048,256]{1,0:T(8,128)(2,1)} %refs_5_.3), channel_id=1, source_target_pairs={{0,1},{1,0},{2,3},{3,2},{4,5},{5,4},{6,7},{7,6},{8,9},{9,8},{10,11... | collective-permute-start | bytes 3145736 | tf_op jit(solution)/shard_map/weights/ppermute | solution.py:25
  25.2 32.6 %all-to-all-start.1 = ((bf16[32,4,1024]{2,1,0:T(4,128)(2,1)}), bf16[32,4,1024]{2,1,0:T(4,128)(2,1)S(1)}, u32[]{:S(2)}, u32[]{:S(2)}) async-start(bf16[32,4,1024]{2,1,0:T(4,128)(2,1)} %bitcast.4), calls=%async_computation.1 | async-start | bytes 524288 | tf_op jit(solution)/shard_map/dispatch/all_to_all | solution.py:17
  58.5 1.0 copy-start.1
  67.2 7.4 %copy-start.3 = (bf16[128,1024]{1,0:T(8,128)(2,1)S(1)}, bf16[128,1024]{1,0:T(8,128)(2,1)}, u32[]{:S(2)}) copy-start(bf16[128,1024]{1,0:T(8,128)(2,1)} %reshape.111.rows_ref) | copy-start | bytes 786436
  67.2 24.4 %all-to-all-start.2 = ((bf16[8,128,512]{2,1,0:T(8,128)(2,1)}), bf16[8,128,512]{2,1,0:T(8,128)(2,1)S(1)}, u32[]{:S(2)}, u32[]{:S(2)}) async-start(bf16[8,128,512]{2,1,0:T(8,128)(2,1)} %hidden.1), calls=%async_computation.2 | async-start | bytes 2097152 | tf_op jit(solution)/shard_map/hidden/all_to_all | solution.py:17
  74.6 5.9 %collective-permute-start = (bf16[128,512]{1,0:T(8,128)(2,1)S(1)}, bf16[128,512]{1,0:T(8,128)(2,1)S(1)}, u32[]{:S(2)}, u32[]{:S(2)}) collective-permute-start(bf16[128,512]{1,0:T(8,128)(2,1)S(1)} %pad_maximum_fusion.2), channel_id=1, source_target_pairs={{0,1},{1,0},{2,3},{3,2},{4,5},{5,4},{6,7},{7,6},{8,9},{9,8},{10,11... | collective-permute-start | bytes 393224 | tf_op jit(solution)/shard_map/hidden/ppermute | solution.py:25
  93.3 23.7 %all-to-all-start.3 = ((bf16[8,128,512]{2,1,0:T(8,128)(2,1)}), bf16[8,128,512]{2,1,0:T(8,128)(2,1)S(1)}, u32[]{:S(2)}, u32[]{:S(2)}) async-start(bf16[8,128,512]{2,1,0:T(8,128)(2,1)} %broadcast_in_dim.96), calls=%async_computation.3 | async-start | bytes 2097152 | tf_op jit(solution)/shard_map/hidden/all_to_all | solution.py:17
  96.9 20.2 %collective-permute-start.3 = (bf16[256,512]{1,0:T(8,128)(2,1)S(1)}, bf16[256,512]{1,0:T(8,128)(2,1)S(1)}, u32[]{:S(2)}, u32[]{:S(2)}) collective-permute-start(bf16[256,512]{1,0:T(8,128)(2,1)S(1)} %pad_maximum_fusion.1), channel_id=1, source_target_pairs={{0,8},{8,0},{1,9},{9,1},{2,10},{10,2},{3,11},{11,3},{4,12},{12,4},... | collective-permute-start | bytes 786440 | tf_op jit(solution)/shard_map/hidden/ppermute | solution.py:226
  101.7 4.6 %collective-permute-start.4 = (bf16[128,512]{0,1:T(8,128)(2,1)S(1)}, bf16[128,512]{0,1:T(8,128)(2,1)S(1)}, u32[]{:S(2)}, u32[]{:S(2)}) collective-permute-start(bf16[128,512]{0,1:T(8,128)(2,1)S(1)} %pad_maximum_fusion.4), channel_id=1, source_target_pairs={{0,1},{1,0},{2,3},{3,2},{4,5},{5,4},{6,7},{7,6},{8,9},{9,8},{10,11... | collective-permute-start | bytes 393224 | tf_op jit(solution)/shard_map/hidden/ppermute | solution.py:25
  117.0 1.0 copy-start.2
  127.2 23.5 %all-to-all-start.4 = ((bf16[32,4,1024]{2,1,0:T(4,128)(2,1)}), bf16[32,4,1024]{2,1,0:T(4,128)(2,1)S(1)}, u32[]{:S(2)}, u32[]{:S(2)}) async-start(bf16[32,4,1024]{2,1,0:T(4,128)(2,1)} %reshape.112), calls=%async_computation.4 | async-start | bytes 524288 | tf_op jit(solution)/shard_map/give_back/all_to_all | solution.py:17
  132.0 26.3 %collective-permute-start.8 = (bf16[2,256,512]{2,1,0:T(8,128)(2,1)S(1)}, bf16[2,256,512]{2,1,0:T(8,128)(2,1)S(1)}, u32[]{:S(2)}, u32[]{:S(2)}) collective-permute-start(bf16[2,256,512]{2,1,0:T(8,128)(2,1)S(1)} %pad_maximum_fusion.first), channel_id=1, source_target_pairs={{0,4},{2,6},{4,0},{6,2},{1,5},{3,7},{5,1},{7,3},{8,12},{10,14},{12... | collective-permute-start | bytes 1572872 | tf_op jit(solution)/shard_map/all_rows/ppermute | solution.py:262
  137.6 22.9 %collective-permute-start.9 = (bf16[2,256,512]{2,1,0:T(8,128)(2,1)S(1)}, bf16[2,256,512]{2,1,0:T(8,128)(2,1)S(1)}, u32[]{:S(2)}, u32[]{:S(2)}) collective-permute-start(bf16[2,256,512]{2,1,0:T(8,128)(2,1)S(1)} %pad_maximum_fusion.first), channel_id=1, source_target_pairs={{0,6},{2,0},{4,2},{6,4},{1,7},{3,1},{5,3},{7,5},{8,14},{10,8},{12,... | collective-permute-start | bytes 1572872 | tf_op jit(solution)/shard_map/all_rows/ppermute | solution.py:262
  139.6 25.4 %collective-permute-start.6 = (bf16[2,256,512]{2,1,0:T(8,128)(2,1)S(1)}, bf16[2,256,512]{2,1,0:T(8,128)(2,1)S(1)}, u32[]{:S(2)}, u32[]{:S(2)}) collective-permute-start(bf16[2,256,512]{2,1,0:T(8,128)(2,1)S(1)} %pad_maximum_fusion.first), channel_id=1, source_target_pairs={{0,2},{2,4},{4,6},{6,0},{1,3},{3,5},{5,7},{7,1},{8,10},{10,12},{12... | collective-permute-start | bytes 1572872 | tf_op jit(solution)/shard_map/all_rows/ppermute | solution.py:262
  151.7 16.6 %all-to-all-start.5 = ((bf16[8,32,1024]{2,1,0:T(8,128)(2,1)}), bf16[8,32,1024]{2,1,0:T(8,128)(2,1)}, u32[]{:S(2)}, u32[]{:S(2)}) async-start(bf16[8,32,1024]{2,1,0:T(8,128)(2,1)} %broadcast_in_dim.100), calls=%async_computation.5 | async-start | bytes 1048576 | tf_op jit(solution)/shard_map/result/all_to_all | solution.py:17
  161.1 13.1 %collective-permute-start.10 = (bf16[4,256,256]{2,1,0:T(8,128)(2,1)S(1)}, bf16[4,256,256]{2,1,0:T(8,128)(2,1)S(1)}, u32[]{:S(2)}, u32[]{:S(2)}) collective-permute-start(bf16[4,256,256]{2,1,0:T(8,128)(2,1)S(1)} %get-tuple-element.48), channel_id=1, source_target_pairs={{0,1},{1,0},{2,3},{3,2},{4,5},{5,4},{6,7},{7,6},{8,9},{9,8},{10,11... | collective-permute-start | bytes 1572872 | tf_op jit(solution)/shard_map/new_slices/ppermute | solution.py:25
  166.4 7.9 %collective-permute-start.7 = (bf16[4,256,256]{2,1,0:T(8,128)(2,1)}, bf16[4,256,256]{2,1,0:T(8,128)(2,1)S(1)}, u32[]{:S(2)}, u32[]{:S(2)}) collective-permute-start(bf16[4,256,256]{2,1,0:T(8,128)(2,1)} %get-tuple-element.45), channel_id=1, source_target_pairs={{0,1},{1,0},{2,3},{3,2},{4,5},{5,4},{6,7},{7,6},{8,9},{9,8},{10,11... | collective-permute-start | bytes 1572872 | tf_op jit(solution)/shard_map/new_slices/ppermute | solution.py:25
  169.2 7.7 %collective-permute-start.5 = (bf16[32,512]{1,0:T(8,128)(2,1)S(1)}, bf16[32,512]{1,0:T(8,128)(2,1)S(1)}, u32[]{:S(2)}, u32[]{:S(2)}) collective-permute-start(bf16[32,512]{1,0:T(8,128)(2,1)S(1)} %dynamic-slice_bitcast_fusion), channel_id=1, source_target_pairs={{0,1},{1,0},{2,3},{3,2},{4,5},{5,4},{6,7},{7,6},{8,9},{9,8},{10,11... | collective-permute-start | bytes 98312 | tf_op jit(solution)/shard_map/result/ppermute | solution.py:25

commit v13 on v11

--- a/solution.py
+++ b/solution.py
@@ -33,39 +33,27 @@
     return jnp.take(blocks, places, axis=0, mode="clip")
 
 
-def gradient_kernel(own_units, other_units, first, second, after_ref, up_ref, down_ref, theirs_ref):
-    unit_width, width = up_ref.shape[1:]
-    hidden, pre_grad = [
-        jnp.concatenate([own_units[part], other_units[part]], axis=0)
-        for part in (pl.ds(0, unit_width), pl.ds(unit_width, unit_width))
-    ]
-    for j, rows in enumerate((first, second)):
-        up = jnp.dot(pre_grad, rows[0, :, :width], preferred_element_type=F32).astype(BF16)
-        down = jnp.dot(hidden, rows[0, :, width:], preferred_element_type=F32).astype(BF16)
-        up_ref[j] = up[:unit_width]
-        down_ref[j] = down[:unit_width]
-        theirs_ref[j, :unit_width] = up[unit_width:]
-        theirs_ref[j, unit_width:] = down[unit_width:]
+def gradient_kernel(own_units, other_units, *refs):
+    rows, (own_ref, theirs_ref) = refs[:-3], refs[-2:]
+    unit_width = own_units.shape[0]
+    units = jnp.concatenate([own_units[...], other_units[...]], axis=0)
+    for s, block in enumerate(rows):
+        grad = jnp.dot(units, block[...], preferred_element_type=F32).astype(BF16)
+        own_ref[0, s] = grad[:unit_width]
+        theirs_ref[0, s] = grad[unit_width:]
 
 
 def layout_kernel(source_ref, *refs):
-    groups, (up_ref, down_ref) = (refs[:3], refs[3:6]), refs[6:]
-    blocks, unit_width, width = refs[0].shape
-    for p in range(4 * blocks):
-        columns = pl.ds(p * width, width)
+    held, outs = refs[:-2], refs[-2:]
+    _, blocks, _, width = held[0].shape
+    for p in range(len(held) * blocks):
         source = source_ref[p]
-        place = source % blocks
-        for g, (own_up, own_down, theirs) in enumerate(groups):
-
-            @pl.when(source // blocks == 2 * g)
+        for g, part in enumerate(held):
+
+            @pl.when(source // blocks == g)
             def _():
-                up_ref[:, columns] = own_up[place]
-                down_ref[:, columns] = own_down[place]
-
-            @pl.when(source // blocks == 2 * g + 1)
-            def _():
-                up_ref[:, columns] = theirs[place, :unit_width]
-                down_ref[:, columns] = theirs[place, unit_width:]
+                for i, out_ref in enumerate(outs):
+                    out_ref[:, p * width : (p + 1) * width] = part[i, source % blocks]
 
 
 def local(tokens, expert_ids, gate_weights, old_up, old_down, old_rows, new_slots, cotangent):
@@ -131,7 +119,7 @@
     back = (lax.axis_index("x") - source % column) % column
     other_y = (source // column != lax.axis_index("y")).astype(jnp.int32)
     other_core = (inverse % 2 != core).astype(jnp.int32)
-    source = 8 * (back // 2) + 4 * other_core + 2 * other_y + back % 2
+    source = (2 * other_y + other_core) * column + back
     row_list = jnp.arange(core_rows, dtype=jnp.int32)
     row_slot = row_list // capacity * capacity + row_list % held_slots * 2 + core
     picker = (target.reshape(-1)[:, None] == row_slot[None, :]).astype(BF16)
@@ -163,10 +151,7 @@
         )
         routed = jnp.concatenate([rows[:, :width], rows[:, 2 * width : 3 * width]], axis=1)
         routed = jnp.concatenate([routed, others], axis=0)
-        later_rows, own_units = lax.optimization_barrier((routed, own_units))
-        rows_y = lax.ppermute(later_rows, "y", [(0, 1), (1, 0)])
         units = everywhere(own_units, CHIP)
-        units, rows_y = lax.optimization_barrier((units, rows_y))
         hidden, pre_grad = units[:, :, : 2 * unit_width], units[:, :, 2 * unit_width :]
 
     def rows_of(units, weights):
@@ -179,6 +164,16 @@
         )
         sent_rows = half_rows.reshape(group_count, held_slots, 4 * width)
         half_rows = exchange(sent_rows, "expert")
+
+        def along_x(start):
+            return [start] + [
+                lax.ppermute(start, "x", [(i, (i + s) % column) for i in range(column)])
+                for s in range(1, column)
+            ]
+
+        own_y = lax.optimization_barrier((routed, sent_rows))[0]
+        all_rows = [along_x(own_y), along_x(lax.ppermute(own_y, "y", [(0, 1), (1, 0)]))]
+        half_rows, all_rows = lax.optimization_barrier((half_rows, all_rows))
         entries = jnp.dot(picker, half_rows.reshape(core_rows, 4 * width), preferred_element_type=F32)
         is_out = jnp.arange(4 * width) // width % 2 == 0
         factor = jnp.where(is_out[None, None, :], gate_weights[:, :, None], 1.0)
@@ -207,42 +202,27 @@
         slot_units = jnp.concatenate([jnp.concatenate(mine, axis=1), theirs], axis=0).T
         own_units, other_units = slot_units[: 2 * unit_width], slot_units[2 * unit_width :]
 
-    with jax.named_scope("all_rows"):
-        pair = jnp.stack(lax.optimization_barrier((routed, rows_y, sent_rows))[:2])
-        pairs = [pair] + [
-            lax.ppermute(pair, "x", [(i, (i + s) % column) for i in range(column)])
-            for s in range(1, column)
-        ]
-
     with jax.named_scope("new_slices"):
-        units_spec = pl.BlockSpec((2 * unit_width, slot_rows), lambda t: (0, 0))
-        rows_spec = pl.BlockSpec((1, slot_rows, 2 * width), lambda t: (t, 0, 0))
-        part_spec = pl.BlockSpec((2, unit_width, width), lambda t: (t, 0, 0))
-        part = jax.ShapeDtypeStruct((chips // 2, unit_width, width), BF16)
+        units_spec = pl.BlockSpec((unit_width, slot_rows), lambda t: (1 - t, 0))
+        rows_spec = pl.BlockSpec((slot_rows, width), lambda t: (0, t))
+        part_spec = pl.BlockSpec((1, column, unit_width, width), lambda t: (t, 0, 0, 0))
+        part = jax.ShapeDtypeStruct((2, column, unit_width, width), BF16)
         held = []
-        for g in range(2):
-            up_part, down_part, theirs = pl.pallas_call(
+        for rows in all_rows:
+            own, theirs = pl.pallas_call(
                 gradient_kernel,
                 grid=(2,),
-                out_shape=(
-                    part,
-                    part,
-                    jax.ShapeDtypeStruct((chips // 2, 2 * unit_width, width), BF16),
-                ),
-                in_specs=[units_spec, units_spec, rows_spec, rows_spec, ANY],
-                out_specs=(
-                    part_spec,
-                    part_spec,
-                    pl.BlockSpec((2, 2 * unit_width, width), lambda t: (t, 0, 0)),
-                ),
+                out_shape=(part, part),
+                in_specs=[units_spec] * 2 + [rows_spec] * column + [ANY],
+                out_specs=(part_spec, part_spec),
                 compiler_params=LARGE,
-            )(own_units, other_units, *pairs[2 * g : 2 * g + 2], own_result)
-            held += [up_part, down_part, swap(theirs)]
+            )(own_units, other_units, *rows, own_result)
+            held += [own, swap(theirs)]
         grad = jax.ShapeDtypeStruct((unit_width, cut_count * width), BF16)
         up_grad, down_grad = pl.pallas_call(
             layout_kernel,
             out_shape=(grad, grad),
-            in_specs=[pl.BlockSpec(memory_space=pltpu.SMEM)] + [VMEM] * 6,
+            in_specs=[pl.BlockSpec(memory_space=pltpu.SMEM)] + [VMEM] * 4,
             out_specs=(VMEM, VMEM),
             compiler_params=LARGE,
         )(source, *held)

time: 175 us -> 182 us (1.040)
  blocking collectives: 0 us -> 35 us
  waiting for transfers between devices: 40.6 us -> 20.2 us
  local copies, waits for them, and re-layouts: 12.2 us -> 8.19 us
  starting transfers between devices: 89.3 us -> 85.4 us
  matrix products: 6.72 us -> 8.82 us
    all_to_all x0 -> x2, blocking collectives: none -> 35 us  [exchange(): return lax.all_to_all(parts, axis, split_axis=0, concat_axis=0, tiled=True)]
    ppermute x4 -> x7, waiting for transfers between devices: 16.4 us -> 5.39 us  [the longest x6 5.06 us: along_x(): lax.ppermute(start, 'x', [(i, (i + s) % column) for i in range(column)])]
    all_to_all x6 -> x4, waiting for transfers between devices: 23.2 us -> 13.8 us  [exchange(): return lax.all_to_all(parts, axis, split_axis=0, concat_axis=0, tiled=True)]
    ppermute x4 -> x7, starting transfers between devices: 15.6 us -> 21 us  [the longest x6 18.2 us: along_x(): lax.ppermute(start, 'x', [(i, (i + s) % column) for i in range(column)])]
    all_to_all x6 -> x4, starting transfers between devices: 48.6 us -> 43.5 us  [exchange(): return lax.all_to_all(parts, axis, split_axis=0, concat_axis=0, tiled=True)]
    ppermute x7, starting transfers between devices: 25.1 us -> 20.8 us  [swap(): return lax.ppermute(block, 'core', [(0, 1), (1, 0)])]
    unnamed x27 -> x15, local copies, waits for them, and re-layouts: 3.11 us -> 0.12 us
  transfers between devices with their start and end apart: 17 -> 18, of which waited for: 8 -> 7; matrix products, arithmetic and copies ran while one was open for 5% -> 4% of each run, Pallas kernels for 3% -> 3%
where the time goes in v13:
time: 182 us; the launch traced here: 180 us
  starting transfers between devices  85.4 us (47%)
  blocking collectives  35 us (19%)
  waiting for transfers between devices  20.2 us (11%)
  between operations  15.3 us (8%)
  matrix products  8.82 us (5%)
  local copies, waits for them, and re-layouts  8.19 us (4%)
  Pallas kernels  4.66 us (3%)
  other arithmetic  2.77 us (2%)
    all_to_all x4, starting transfers between devices, exchange(): return lax.all_to_all(parts, axis, split_axis=0, concat_axis=0, tiled=True)  43.5 us
    all_to_all x2, blocking collectives, exchange(): return lax.all_to_all(parts, axis, split_axis=0, concat_axis=0, tiled=True)  35 us
    ppermute x7, starting transfers between devices, swap(): return lax.ppermute(block, 'core', [(0, 1), (1, 0)])  20.8 us
    ppermute x6, starting transfers between devices, along_x(): lax.ppermute(start, 'x', [(i, (i + s) % column) for i in range(column)])  18.2 us
    all_to_all x4, waiting for transfers between devices, exchange(): return lax.all_to_all(parts, axis, split_axis=0, concat_axis=0, tiled=True)  13.8 us
    ppermute x6, waiting for transfers between devices, along_x(): lax.ppermute(start, 'x', [(i, (i + s) % column) for i in range(column)])  5.06 us
    dot_general x4, matrix products, partial(): jnp.einsum('rd,pud->pru', rows[:, first + j * width:first + (j + 1) * wid...  4.35 us
    dot_general x4, matrix products, rows_of(): jnp.einsum('pru,pud->rd', units, weights, preferred_element_type=F32)  4.06 us
  transfers between devices with their start and end apart: 18, of which 7 were waited for; matrix products, arithmetic and copies ran while one was open for 4% of the time, Pallas kernels for 3%

profile of v13, /device:TPU:1, one launch (start us, length us, event | category | flops | bytes accessed | tf_op | source)
XLA Modules:
  0.0 180.3 jit_solution(6157600812909700717)
XLA Ops:
  0.7 0.8 pad_maximum_fusion.6
  1.4 0.8 broadcast_in_dim.88
  2.3 10.2 %all-to-all-start = ((bf16[16,32,512]{2,1,0:T(8,128)(2,1)}), bf16[16,32,512]{2,1,0:T(8,128)(2,1)S(1)}, u32[]{:S(2)}, u32[]{:S(2)}) async-start(bf16[16,32,512]{2,1,0:T(8,128)(2,1)} %broadcast_in_dim.88), calls=%async_computation | async-start | bytes 1048576 | tf_op jit(solution)/shard_map/token_blocks/all_to_all | solution.py:17
  12.5 0.1 copy.38
  12.6 0.1 eq.82
  12.8 0.1 reduce_window_sum.11
  12.9 0.2 select_reduce_fusion
  13.1 0.6 fusion.58
  16.3 0.1 reduce_sum.48
  17.9 0.1 fusion.30
  18.0 6.0 %all-to-all-done = bf16[16,32,512]{2,1,0:T(8,128)(2,1)S(1)} async-done(((bf16[16,32,512]{2,1,0:T(8,128)(2,1)}), bf16[16,32,512]{2,1,0:T(8,128)(2,1)S(1)}, u32[]{:S(2)}, u32[]{:S(2)}) %all-to-all-start) | async-done | bytes 524320 | tf_op jit(solution)/shard_map/token_blocks/all_to_all | solution.py:17
  24.0 0.2 fusion.5
  24.3 0.8 broadcast_in_dim.95
  25.1 13.4 %all-to-all-start.1 = ((bf16[32,4,1024]{2,1,0:T(4,128)(2,1)}), bf16[32,4,1024]{2,1,0:T(4,128)(2,1)S(1)}, u32[]{:S(2)}, u32[]{:S(2)}) async-start(bf16[32,4,1024]{2,1,0:T(4,128)(2,1)} %bitcast.4), calls=%async_computation.1 | async-start | bytes 524288 | tf_op jit(solution)/shard_map/dispatch/all_to_all | solution.py:17
  38.5 3.3 %collective-permute-start = (bf16[2048,256]{1,0:T(8,128)(2,1)S(1)}, bf16[2048,256]{1,0:T(8,128)(2,1)}, u32[]{:S(2)}, u32[]{:S(2)}) collective-permute-start(bf16[2048,256]{1,0:T(8,128)(2,1)S(1)} %copy-done.2), channel_id=1, source_target_pairs={{0,1},{1,0},{2,3},{3,2},{4,5},{5,4},{6,7},{7,6},{8,9},{9,8},{10,11... | collective-permute-start | bytes 3145736 | tf_op jit(solution)/shard_map/weights/ppermute | solution.py:25
  41.8 1.9 %collective-permute-start.1 = (bf16[2048,256]{1,0:T(8,128)(2,1)S(1)}, bf16[2048,256]{1,0:T(8,128)(2,1)}, u32[]{:S(2)}, u32[]{:S(2)}) collective-permute-start(bf16[2048,256]{1,0:T(8,128)(2,1)S(1)} %copy-done.1), channel_id=1, source_target_pairs={{0,1},{1,0},{2,3},{3,2},{4,5},{5,4},{6,7},{7,6},{8,9},{9,8},{10,11... | collective-permute-start | bytes 3145736 | tf_op jit(solution)/shard_map/weights/ppermute | solution.py:25
  43.7 0.1 select_reduce_fusion.1
  43.9 0.6 fusion.56
  54.7 2.9 %all-to-all-done.1 = bf16[32,4,1024]{2,1,0:T(4,128)(2,1)S(1)} async-done(((bf16[32,4,1024]{2,1,0:T(4,128)(2,1)}), bf16[32,4,1024]{2,1,0:T(4,128)(2,1)S(1)}, u32[]{:S(2)}, u32[]{:S(2)}) %all-to-all-start.1) | async-done | bytes 262176 | tf_op jit(solution)/shard_map/dispatch/all_to_all | solution.py:17
  57.7 0.5 fusion.28
  58.2 0.5 fusion.25
  58.7 1.7 fusion.3
  60.4 1.7 fusion.2
  62.1 0.1 pad_maximum_fusion
  62.2 19.2 %all_to_all.30 = bf16[8,128,512]{2,1,0:T(8,128)(2,1)S(1)} all-to-all(bf16[8,128,512]{2,1,0:T(8,128)(2,1)S(1)} %pad_maximum_fusion), channel_id=1, replica_groups=mesh['expert'=32,'y'=2,'x'=4,'core'=2] {'y','x'}, dimensions={0} | all-to-all | bytes 2097152 | tf_op jit(solution)/shard_map/hidden/all_to_all | solution.py:17
  81.4 0.1 convert_reduce_fusion
  81.7 15.9 %all_to_all.31 = bf16[8,128,512]{2,1,0:T(8,128)(2,1)S(1)} all-to-all(bf16[8,128,512]{2,1,0:T(8,128)(2,1)S(1)} %broadcast_in_dim.96), channel_id=1, replica_groups=mesh['expert'=32,'y'=2,'x'=4,'core'=2] {'y','x'}, dimensions={0} | all-to-all | bytes 2097152 | tf_op jit(solution)/shard_map/hidden/all_to_all | solution.py:17
  97.6 1.9 %fusion.8 = bf16[128,256]{1,0:T(8,128)(2,1)S(1)} fusion(bf16[8,256,256]{2,1,0:T(8,128)(2,1)} %bitcast.18, bf16[8,128,512]{2,1,0:T(8,128)(2,1)S(1)} %all_to_all.31), kind=kOutput, calls=%fused_computation.17 | convolution fusion | flops 134250496 | bytes 1638400 | tf_op jit(solution)/shard_map/give_back/pru,pud->rd/dot_general | solution.py:158
  99.5 0.3 fusion.6
  99.8 0.3 fusion.7
  100.1 1.5 fusion.9
  101.7 0.8 reshape.128
  102.5 13.4 %all-to-all-start.4 = ((bf16[32,4,1024]{2,1,0:T(4,128)(2,1)}), bf16[32,4,1024]{2,1,0:T(4,128)(2,1)S(1)}, u32[]{:S(2)}, u32[]{:S(2)}) async-start(bf16[32,4,1024]{2,1,0:T(4,128)(2,1)} %reshape.128), calls=%async_computation.4 | async-start | bytes 524288 | tf_op jit(solution)/shard_map/give_back/all_to_all | solution.py:17
  115.9 4.0 %collective-permute-start.2 = (bf16[128,512]{1,0:T(8,128)(2,1)S(1)}, bf16[128,512]{1,0:T(8,128)(2,1)S(1)}, u32[]{:S(2)}, u32[]{:S(2)}) collective-permute-start(bf16[128,512]{1,0:T(8,128)(2,1)S(1)} %pad_maximum_fusion.4), channel_id=1, source_target_pairs={{0,1},{1,0},{2,3},{3,2},{4,5},{5,4},{6,7},{7,6},{8,9},{9,8},{10,11... | collective-permute-start | bytes 393224 | tf_op jit(solution)/shard_map/hidden/ppermute | solution.py:25
  120.0 1.0 collective-permute-done.2
  120.9 2.8 %collective-permute-start.6 = (bf16[256,512]{1,0:T(8,128)(2,1)S(1)}, bf16[256,512]{1,0:T(8,128)(2,1)S(1)}, u32[]{:S(2)}, u32[]{:S(2)}) collective-permute-start(bf16[256,512]{1,0:T(8,128)(2,1)S(1)} %pad_maximum_fusion.2.refs_0_), channel_id=1, source_target_pairs={{0,8},{8,0},{1,9},{9,1},{2,10},{10,2},{3,11},{11,3},{4,12},{12,4},... | collective-permute-start | bytes 786440 | tf_op jit(solution)/shard_map/give_back/ppermute | solution.py:175
  123.7 2.6 %collective-permute-start.3 = (bf16[256,512]{1,0:T(8,128)(2,1)S(1)}, bf16[256,512]{1,0:T(8,128)(2,1)S(1)}, u32[]{:S(2)}, u32[]{:S(2)}) collective-permute-start(bf16[256,512]{1,0:T(8,128)(2,1)S(1)} %pad_maximum_fusion.2.refs_0_), channel_id=1, source_target_pairs={{0,2},{2,4},{4,6},{6,0},{1,3},{3,5},{5,7},{7,1},{8,10},{10,12},{12... | collective-permute-start | bytes 786440 | tf_op jit(solution)/shard_map/give_back/ppermute | solution.py:170
  126.3 3.7 %collective-permute-start.4 = (bf16[256,512]{1,0:T(8,128)(2,1)S(1)}, bf16[256,512]{1,0:T(8,128)(2,1)S(1)}, u32[]{:S(2)}, u32[]{:S(2)}) collective-permute-start(bf16[256,512]{1,0:T(8,128)(2,1)S(1)} %pad_maximum_fusion.2.refs_0_), channel_id=1, source_target_pairs={{0,4},{2,6},{4,0},{6,2},{1,5},{3,7},{5,1},{7,3},{8,12},{10,14},{12... | collective-permute-start | bytes 786440 | tf_op jit(solution)/shard_map/give_back/ppermute | solution.py:170
  130.1 2.5 %collective-permute-start.5 = (bf16[256,512]{1,0:T(8,128)(2,1)S(1)}, bf16[256,512]{1,0:T(8,128)(2,1)S(1)}, u32[]{:S(2)}, u32[]{:S(2)}) collective-permute-start(bf16[256,512]{1,0:T(8,128)(2,1)S(1)} %pad_maximum_fusion.2.refs_0_), channel_id=1, source_target_pairs={{0,6},{2,0},{4,2},{6,4},{1,7},{3,1},{5,3},{7,5},{8,14},{10,8},{12,... | collective-permute-start | bytes 786440 | tf_op jit(solution)/shard_map/give_back/ppermute | solution.py:170
  132.6 0.3 collective-permute-done.6.refs_0_
  132.9 2.6 %collective-permute-start.7 = (bf16[256,512]{1,0:T(8,128)(2,1)S(1)}, bf16[256,512]{1,0:T(8,128)(2,1)S(1)}, u32[]{:S(2)}, u32[]{:S(2)}) collective-permute-start(bf16[256,512]{1,0:T(8,128)(2,1)S(1)} %collective-permute-done.6.refs_0_), channel_id=1, source_target_pairs={{0,2},{2,4},{4,6},{6,0},{1,3},{3,5},{5,7},{7,1},{8,10},{10,12},{12... | collective-permute-start | bytes 786440 | tf_op jit(solution)/shard_map/give_back/ppermute | solution.py:170
  135.5 3.2 %collective-permute-start.8 = (bf16[256,512]{1,0:T(8,128)(2,1)S(1)}, bf16[256,512]{1,0:T(8,128)(2,1)S(1)}, u32[]{:S(2)}, u32[]{:S(2)}) collective-permute-start(bf16[256,512]{1,0:T(8,128)(2,1)S(1)} %collective-permute-done.6.refs_0_), channel_id=1, source_target_pairs={{0,4},{2,6},{4,0},{6,2},{1,5},{3,7},{5,1},{7,3},{8,12},{10,14},{12... | collective-permute-start | bytes 786440 | tf_op jit(solution)/shard_map/give_back/ppermute | solution.py:170
  138.7 3.7 %collective-permute-start.9 = (bf16[256,512]{1,0:T(8,128)(2,1)S(1)}, bf16[256,512]{1,0:T(8,128)(2,1)S(1)}, u32[]{:S(2)}, u32[]{:S(2)}) collective-permute-start(bf16[256,512]{1,0:T(8,128)(2,1)S(1)} %collective-permute-done.6.refs_0_), channel_id=1, source_target_pairs={{0,6},{2,0},{4,2},{6,4},{1,7},{3,1},{5,3},{7,5},{8,14},{10,8},{12,... | collective-permute-start | bytes 786440 | tf_op jit(solution)/shard_map/give_back/ppermute | solution.py:170
  142.4 1.0 constant_dynamic-slice_fusion
  143.4 0.1 copy.41
  143.6 0.1 copy.42
  143.7 0.1 copy.43
  143.8 0.1 copy.44
  144.0 4.2 %collective-permute-start.11 = (bf16[128,512]{0,1:T(8,128)(2,1)S(1)}, bf16[128,512]{0,1:T(8,128)(2,1)S(1)}, u32[]{:S(2)}, u32[]{:S(2)}) collective-permute-start(bf16[128,512]{0,1:T(8,128)(2,1)S(1)} %pad_maximum_fusion.5), channel_id=1, source_target_pairs={{0,1},{1,0},{2,3},{3,2},{4,5},{5,4},{6,7},{7,6},{8,9},{9,8},{10,11... | collective-permute-start | bytes 393224 | tf_op jit(solution)/shard_map/slot_units/ppermute | solution.py:25
  148.2 2.5 %collective-permute-done.8.refs_2_ = bf16[256,512]{1,0:T(8,128)(2,1)S(1)} collective-permute-done((bf16[256,512]{1,0:T(8,128)(2,1)S(1)}, bf16[256,512]{1,0:T(8,128)(2,1)S(1)}, u32[]{:S(2)}, u32[]{:S(2)}) %collective-permute-start.8) | collective-permute-done | bytes 262176 | tf_op jit(solution)/shard_map/give_back/ppermute | solution.py:170
  150.8 2.5 %collective-permute-done.9.refs_3_ = bf16[256,512]{1,0:T(8,128)(2,1)S(1)} collective-permute-done((bf16[256,512]{1,0:T(8,128)(2,1)S(1)}, bf16[256,512]{1,0:T(8,128)(2,1)S(1)}, u32[]{:S(2)}, u32[]{:S(2)}) %collective-permute-start.9) | collective-permute-done | bytes 262176 | tf_op jit(solution)/shard_map/give_back/ppermute | solution.py:170
  153.4 0.2 fusion.4.refs_4_
  153.6 0.9 broadcast_in_dim.100
  154.5 6.5 %all-to-all-start.5 = ((bf16[8,32,1024]{2,1,0:T(8,128)(2,1)}), bf16[8,32,1024]{2,1,0:T(8,128)(2,1)}, u32[]{:S(2)}, u32[]{:S(2)}) async-start(bf16[8,32,1024]{2,1,0:T(8,128)(2,1)} %broadcast_in_dim.100), calls=%async_computation.5 | async-start | bytes 1048576 | tf_op jit(solution)/shard_map/result/all_to_all | solution.py:17
  161.0 0.7 new_slices.4
  161.7 2.8 %collective-permute-start.13 = (bf16[2,4,128,256]{3,2,1,0:T(8,128)(2,1)S(1)}, bf16[2,4,128,256]{3,2,1,0:T(8,128)(2,1)S(1)}, u32[]{:S(2)}, u32[]{:S(2)}) collective-permute-start(bf16[2,4,128,256]{3,2,1,0:T(8,128)(2,1)S(1)} %get-tuple-element.60), channel_id=1, source_target_pairs={{0,1},{1,0},{2,3},{3,2},{4,5},{5,4},{6,7},{7,6},{8,9},{9,8},{10,11... | collective-permute-start | bytes 1572872 | tf_op jit(solution)/shard_map/new_slices/ppermute | solution.py:25
  164.5 1.4 new_slices.3
  166.0 1.9 %collective-permute-start.12 = (bf16[2,4,128,256]{3,2,1,0:T(8,128)(2,1)}, bf16[2,4,128,256]{3,2,1,0:T(8,128)(2,1)S(1)}, u32[]{:S(2)}, u32[]{:S(2)}) collective-permute-start(bf16[2,4,128,256]{3,2,1,0:T(8,128)(2,1)} %get-tuple-element.54), channel_id=1, source_target_pairs={{0,1},{1,0},{2,3},{3,2},{4,5},{5,4},{6,7},{7,6},{8,9},{9,8},{10,11... | collective-permute-start | bytes 1572872 | tf_op jit(solution)/shard_map/new_slices/ppermute | solution.py:25
  167.9 4.9 %all-to-all-done.5 = bf16[8,32,1024]{2,1,0:T(8,128)(2,1)} async-done(((bf16[8,32,1024]{2,1,0:T(8,128)(2,1)}), bf16[8,32,1024]{2,1,0:T(8,128)(2,1)}, u32[]{:S(2)}, u32[]{:S(2)}) %all-to-all-start.5) | async-done | bytes 524320 | tf_op jit(solution)/shard_map/result/all_to_all | solution.py:17
  172.8 0.9 dynamic-slice_bitcast_fusion
  173.6 2.7 %collective-permute-start.10 = (bf16[32,512]{1,0:T(8,128)(2,1)S(1)}, bf16[32,512]{1,0:T(8,128)(2,1)S(1)}, u32[]{:S(2)}, u32[]{:S(2)}) collective-permute-start(bf16[32,512]{1,0:T(8,128)(2,1)S(1)} %dynamic-slice_bitcast_fusion), channel_id=1, source_target_pairs={{0,1},{1,0},{2,3},{3,2},{4,5},{5,4},{6,7},{7,6},{8,9},{9,8},{10,11... | collective-permute-start | bytes 98312 | tf_op jit(solution)/shard_map/result/ppermute | solution.py:25
  176.4 2.5 %new_slices.5 = (bf16[128,4096]{1,0:T(8,128)(2,1)}, bf16[128,4096]{1,0:T(8,128)(2,1)}) custom-call(s32[16]{0:T(128)S(1)} %fusion.38.source_ref, bf16[2,4,128,256]{3,2,1,0:T(8,128)(2,1)S(1)} %get-tuple-element.53.refs_0_, bf16[2,4,128,256]{3,2,1,0:T(8,128)(2,1)S(1)} %collective-permute-done.12.refs_1_, ...), custom_call_target="tpu_custom_call" | custom-call | tf_op jit(solution)/shard_map/new_slices/pallas_call | solution.py:222
  178.8 0.9 fusion.23
  179.7 0.6 fusion.53
  (51 shorter events, 0.9 us)
Async XLA Ops:
  0.6 11.9 %copy-start.3 = (s32[32,2]{0,1:T(2,128)S(1)}, s32[32,2]{0,1:T(2,128)}, u32[]{:S(2)}) copy-start(s32[32,2]{0,1:T(2,128)} %param.9) | copy-start | bytes 772
  0.6 12.5 %copy-start.4 = (s32[16]{0:T(128)S(1)}, s32[16]{0:T(128)}, u32[]{:S(2)}) copy-start(s32[16]{0:T(128)} %param.13) | copy-start | bytes 196
  0.7 17.3 %copy-start.6 = (f32[32,2]{0,1:T(2,128)S(1)}, f32[32,2]{0,1:T(2,128)}, u32[]{:S(2)}) copy-start(f32[32,2]{0,1:T(2,128)} %param.10) | copy-start | bytes 772
  2.3 21.7 %all-to-all-start = ((bf16[16,32,512]{2,1,0:T(8,128)(2,1)}), bf16[16,32,512]{2,1,0:T(8,128)(2,1)S(1)}, u32[]{:S(2)}, u32[]{:S(2)}) async-start(bf16[16,32,512]{2,1,0:T(8,128)(2,1)} %broadcast_in_dim.88), calls=%async_computation | async-start | bytes 1048576 | tf_op jit(solution)/shard_map/token_blocks/all_to_all | solution.py:17
  12.6 25.9 %copy-start.2 = (bf16[2048,256]{1,0:T(8,128)(2,1)S(1)}, bf16[2048,256]{1,0:T(8,128)(2,1)}, u32[]{:S(2)}) copy-start(bf16[2048,256]{1,0:T(8,128)(2,1)} %param.11) | copy-start | bytes 3145732
  12.7 29.1 %copy-start.1 = (bf16[2048,256]{1,0:T(8,128)(2,1)S(1)}, bf16[2048,256]{1,0:T(8,128)(2,1)}, u32[]{:S(2)}) copy-start(bf16[2048,256]{1,0:T(8,128)(2,1)} %param.12) | copy-start | bytes 3145732
  12.7 31.1 %copy-start.5 = (s32[16]{0:T(128)S(1)}, s32[16]{0:T(128)}, u32[]{:S(2)}) copy-start(s32[16]{0:T(128)} %param.14) | copy-start | bytes 196
  25.1 32.5 %all-to-all-start.1 = ((bf16[32,4,1024]{2,1,0:T(4,128)(2,1)}), bf16[32,4,1024]{2,1,0:T(4,128)(2,1)S(1)}, u32[]{:S(2)}, u32[]{:S(2)}) async-start(bf16[32,4,1024]{2,1,0:T(4,128)(2,1)} %bitcast.4), calls=%async_computation.1 | async-start | bytes 524288 | tf_op jit(solution)/shard_map/dispatch/all_to_all | solution.py:17
  38.5 20.1 %collective-permute-start = (bf16[2048,256]{1,0:T(8,128)(2,1)S(1)}, bf16[2048,256]{1,0:T(8,128)(2,1)}, u32[]{:S(2)}, u32[]{:S(2)}) collective-permute-start(bf16[2048,256]{1,0:T(8,128)(2,1)S(1)} %copy-done.2), channel_id=1, source_target_pairs={{0,1},{1,0},{2,3},{3,2},{4,5},{5,4},{6,7},{7,6},{8,9},{9,8},{10,11... | collective-permute-start | bytes 3145736 | tf_op jit(solution)/shard_map/weights/ppermute | solution.py:25
  41.8 18.6 %collective-permute-start.1 = (bf16[2048,256]{1,0:T(8,128)(2,1)S(1)}, bf16[2048,256]{1,0:T(8,128)(2,1)}, u32[]{:S(2)}, u32[]{:S(2)}) collective-permute-start(bf16[2048,256]{1,0:T(8,128)(2,1)S(1)} %copy-done.1), channel_id=1, source_target_pairs={{0,1},{1,0},{2,3},{3,2},{4,5},{5,4},{6,7},{7,6},{8,9},{9,8},{10,11... | collective-permute-start | bytes 3145736 | tf_op jit(solution)/shard_map/weights/ppermute | solution.py:25
  97.6 4.1 %copy-start = (bf16[8,128,512]{2,1,0:T(8,128)(2,1)}, bf16[8,128,512]{2,1,0:T(8,128)(2,1)S(1)}, u32[]{:S(2)}) copy-start(bf16[8,128,512]{2,1,0:T(8,128)(2,1)S(1)} %all_to_all.31) | copy-start | bytes 3145732
  102.5 50.8 %all-to-all-start.4 = ((bf16[32,4,1024]{2,1,0:T(4,128)(2,1)}), bf16[32,4,1024]{2,1,0:T(4,128)(2,1)S(1)}, u32[]{:S(2)}, u32[]{:S(2)}) async-start(bf16[32,4,1024]{2,1,0:T(4,128)(2,1)} %reshape.128), calls=%async_computation.4 | async-start | bytes 524288 | tf_op jit(solution)/shard_map/give_back/all_to_all | solution.py:17
  115.9 5.0 %collective-permute-start.2 = (bf16[128,512]{1,0:T(8,128)(2,1)S(1)}, bf16[128,512]{1,0:T(8,128)(2,1)S(1)}, u32[]{:S(2)}, u32[]{:S(2)}) collective-permute-start(bf16[128,512]{1,0:T(8,128)(2,1)S(1)} %pad_maximum_fusion.4), channel_id=1, source_target_pairs={{0,1},{1,0},{2,3},{3,2},{4,5},{5,4},{6,7},{7,6},{8,9},{9,8},{10,11... | collective-permute-start | bytes 393224 | tf_op jit(solution)/shard_map/hidden/ppermute | solution.py:25
  120.9 12.0 %collective-permute-start.6 = (bf16[256,512]{1,0:T(8,128)(2,1)S(1)}, bf16[256,512]{1,0:T(8,128)(2,1)S(1)}, u32[]{:S(2)}, u32[]{:S(2)}) collective-permute-start(bf16[256,512]{1,0:T(8,128)(2,1)S(1)} %pad_maximum_fusion.2.refs_0_), channel_id=1, source_target_pairs={{0,8},{8,0},{1,9},{9,1},{2,10},{10,2},{3,11},{11,3},{4,12},{12,4},... | collective-permute-start | bytes 786440 | tf_op jit(solution)/shard_map/give_back/ppermute | solution.py:175
  123.7 14.9 %collective-permute-start.3 = (bf16[256,512]{1,0:T(8,128)(2,1)S(1)}, bf16[256,512]{1,0:T(8,128)(2,1)S(1)}, u32[]{:S(2)}, u32[]{:S(2)}) collective-permute-start(bf16[256,512]{1,0:T(8,128)(2,1)S(1)} %pad_maximum_fusion.2.refs_0_), channel_id=1, source_target_pairs={{0,2},{2,4},{4,6},{6,0},{1,3},{3,5},{5,7},{7,1},{8,10},{10,12},{12... | collective-permute-start | bytes 786440 | tf_op jit(solution)/shard_map/give_back/ppermute | solution.py:170
  126.3 17.6 %collective-permute-start.4 = (bf16[256,512]{1,0:T(8,128)(2,1)S(1)}, bf16[256,512]{1,0:T(8,128)(2,1)S(1)}, u32[]{:S(2)}, u32[]{:S(2)}) collective-permute-start(bf16[256,512]{1,0:T(8,128)(2,1)S(1)} %pad_maximum_fusion.2.refs_0_), channel_id=1, source_target_pairs={{0,4},{2,6},{4,0},{6,2},{1,5},{3,7},{5,1},{7,3},{8,12},{10,14},{12... | collective-permute-start | bytes 786440 | tf_op jit(solution)/shard_map/give_back/ppermute | solution.py:170
  130.1 18.2 %collective-permute-start.5 = (bf16[256,512]{1,0:T(8,128)(2,1)S(1)}, bf16[256,512]{1,0:T(8,128)(2,1)S(1)}, u32[]{:S(2)}, u32[]{:S(2)}) collective-permute-start(bf16[256,512]{1,0:T(8,128)(2,1)S(1)} %pad_maximum_fusion.2.refs_0_), channel_id=1, source_target_pairs={{0,6},{2,0},{4,2},{6,4},{1,7},{3,1},{5,3},{7,5},{8,14},{10,8},{12,... | collective-permute-start | bytes 786440 | tf_op jit(solution)/shard_map/give_back/ppermute | solution.py:170
  132.9 15.3 %collective-permute-start.7 = (bf16[256,512]{1,0:T(8,128)(2,1)S(1)}, bf16[256,512]{1,0:T(8,128)(2,1)S(1)}, u32[]{:S(2)}, u32[]{:S(2)}) collective-permute-start(bf16[256,512]{1,0:T(8,128)(2,1)S(1)} %collective-permute-done.6.refs_0_), channel_id=1, source_target_pairs={{0,2},{2,4},{4,6},{6,0},{1,3},{3,5},{5,7},{7,1},{8,10},{10,12},{12... | collective-permute-start | bytes 786440 | tf_op jit(solution)/shard_map/give_back/ppermute | solution.py:170
  135.5 15.3 %collective-permute-start.8 = (bf16[256,512]{1,0:T(8,128)(2,1)S(1)}, bf16[256,512]{1,0:T(8,128)(2,1)S(1)}, u32[]{:S(2)}, u32[]{:S(2)}) collective-permute-start(bf16[256,512]{1,0:T(8,128)(2,1)S(1)} %collective-permute-done.6.refs_0_), channel_id=1, source_target_pairs={{0,4},{2,6},{4,0},{6,2},{1,5},{3,7},{5,1},{7,3},{8,12},{10,14},{12... | collective-permute-start | bytes 786440 | tf_op jit(solution)/shard_map/give_back/ppermute | solution.py:170
  138.7 14.6 %collective-permute-start.9 = (bf16[256,512]{1,0:T(8,128)(2,1)S(1)}, bf16[256,512]{1,0:T(8,128)(2,1)S(1)}, u32[]{:S(2)}, u32[]{:S(2)}) collective-permute-start(bf16[256,512]{1,0:T(8,128)(2,1)S(1)} %collective-permute-done.6.refs_0_), channel_id=1, source_target_pairs={{0,6},{2,0},{4,2},{6,4},{1,7},{3,1},{5,3},{7,5},{8,14},{10,8},{12,... | collective-permute-start | bytes 786440 | tf_op jit(solution)/shard_map/give_back/ppermute | solution.py:170
  144.0 9.6 %collective-permute-start.11 = (bf16[128,512]{0,1:T(8,128)(2,1)S(1)}, bf16[128,512]{0,1:T(8,128)(2,1)S(1)}, u32[]{:S(2)}, u32[]{:S(2)}) collective-permute-start(bf16[128,512]{0,1:T(8,128)(2,1)S(1)} %pad_maximum_fusion.5), channel_id=1, source_target_pairs={{0,1},{1,0},{2,3},{3,2},{4,5},{5,4},{6,7},{7,6},{8,9},{9,8},{10,11... | collective-permute-start | bytes 393224 | tf_op jit(solution)/shard_map/slot_units/ppermute | solution.py:25
  154.5 18.3 %all-to-all-start.5 = ((bf16[8,32,1024]{2,1,0:T(8,128)(2,1)}), bf16[8,32,1024]{2,1,0:T(8,128)(2,1)}, u32[]{:S(2)}, u32[]{:S(2)}) async-start(bf16[8,32,1024]{2,1,0:T(8,128)(2,1)} %broadcast_in_dim.100), calls=%async_computation.5 | async-start | bytes 1048576 | tf_op jit(solution)/shard_map/result/all_to_all | solution.py:17
  161.7 14.6 %collective-permute-start.13 = (bf16[2,4,128,256]{3,2,1,0:T(8,128)(2,1)S(1)}, bf16[2,4,128,256]{3,2,1,0:T(8,128)(2,1)S(1)}, u32[]{:S(2)}, u32[]{:S(2)}) collective-permute-start(bf16[2,4,128,256]{3,2,1,0:T(8,128)(2,1)S(1)} %get-tuple-element.60), channel_id=1, source_target_pairs={{0,1},{1,0},{2,3},{3,2},{4,5},{5,4},{6,7},{7,6},{8,9},{9,8},{10,11... | collective-permute-start | bytes 1572872 | tf_op jit(solution)/shard_map/new_slices/ppermute | solution.py:25
  166.0 10.4 %collective-permute-start.12 = (bf16[2,4,128,256]{3,2,1,0:T(8,128)(2,1)}, bf16[2,4,128,256]{3,2,1,0:T(8,128)(2,1)S(1)}, u32[]{:S(2)}, u32[]{:S(2)}) collective-permute-start(bf16[2,4,128,256]{3,2,1,0:T(8,128)(2,1)} %get-tuple-element.54), channel_id=1, source_target_pairs={{0,1},{1,0},{2,3},{3,2},{4,5},{5,4},{6,7},{7,6},{8,9},{9,8},{10,11... | collective-permute-start | bytes 1572872 | tf_op jit(solution)/shard_map/new_slices/ppermute | solution.py:25
  173.6 5.2 %collective-permute-start.10 = (bf16[32,512]{1,0:T(8,128)(2,1)S(1)}, bf16[32,512]{1,0:T(8,128)(2,1)S(1)}, u32[]{:S(2)}, u32[]{:S(2)}) collective-permute-start(bf16[32,512]{1,0:T(8,128)(2,1)S(1)} %dynamic-slice_bitcast_fusion), channel_id=1, source_target_pairs={{0,1},{1,0},{2,3},{3,2},{4,5},{5,4},{6,7},{7,6},{8,9},{9,8},{10,11... | collective-permute-start | bytes 98312 | tf_op jit(solution)/shard_map/result/ppermute | solution.py:25
